TPU v7x, 128 devices: a whole 4x4x4 slice. The times are simulated.
128 devices in a mesh: seq: 16 (over z_lo, y, core), slot: 8 (over x, z_hi).
Axes of the slice: x: 4, y: 4, z: 4 (z_hi: 2, z_lo: 2; z = z_hi * 2 + z_lo), core: 2. Of those that a mesh axis runs over, the one named last changes fastest.
Arguments:
- tokens: bfloat16 [32768, 1280], P('seq'), may hold values from -6 to 6
- slot_keys: bfloat16 [1280, 1024], P(None, 'slot'), may hold values from -0.4375 to 0.4375
- w_in: bfloat16 [64, 3072, 1280], P('slot', 'seq'), may hold values from -0.15625 to 0.15625
- w_out: bfloat16 [64, 3072, 1280], P('slot', 'seq'), may hold values from -0.109375 to 0.109375
- out_grad: bfloat16 [32768, 1280], P('seq'), may hold values from -6 to 6
Outputs:
- grad_tokens: bfloat16 [32768, 1280], P('seq', 'slot')
- grad_keys: float32 [1280, 1024], P('seq', 'slot')
- grad_w_in: bfloat16 [64, 3072, 1280], P('slot', 'seq')
- grad_w_out: bfloat16 [64, 3072, 1280], P('slot', 'seq')
All inputs are finite; a program needn't handle non-finite values.
Results may differ from a plain program's by a relative error of at most 0.04.
Values may be sent and summed in bfloat16 or wider, within the bound.
No kernel may reach another device: no remote copies, remote signals or barrier semaphores. Data moves between devices by JAX's collectives and lax.ppermute only.
A program may use at most 128 MiB of HBM per device.

v0:
```python
import jax
import jax.numpy as jnp
from jax import lax
from jax.sharding import PartitionSpec as P

gelu_scale = 0.7978845608
gelu_cubic = 0.044715
rows_contract = (((0,), (0,)), ((), ()))
cols_contract = (((1,), (1,)), ((), ()))


def gelu_tanh(values):
    return (
        0.5
        * values
        * (1.0 + jnp.tanh(gelu_scale * (values + gelu_cubic * values * values * values)))
    )


def gelu_slope(values):
    bent = jnp.tanh(gelu_scale * (values + gelu_cubic * values * values * values))
    return 0.5 * (1.0 + bent) + 0.5 * values * (1.0 - bent * bent) * gelu_scale * (
        1.0 + 3.0 * gelu_cubic * values * values
    )


def per_device(tokens, slot_keys, w_in, w_out, out_grad):
    features = tokens.shape[1]
    experts = w_in.shape[0]
    logits = jnp.dot(tokens, slot_keys, preferred_element_type=jnp.float32)
    exp_logits = jnp.exp(logits)
    column_total = lax.psum(jnp.sum(exp_logits, axis=0), "seq")
    row_total = lax.psum(jnp.sum(exp_logits, axis=1), "slot")
    dispatch = exp_logits / column_total[None, :]
    combine = exp_logits / row_total[:, None]
    dispatch_low = dispatch.astype(jnp.bfloat16)
    combine_low = combine.astype(jnp.bfloat16)
    slot_in = lax.psum(
        lax.dot_general(
            dispatch_low, tokens, rows_contract, preferred_element_type=jnp.float32
        ).astype(jnp.bfloat16),
        "seq",
    )
    slot_grad = lax.psum(
        lax.dot_general(
            combine_low, out_grad, rows_contract, preferred_element_type=jnp.float32
        ).astype(jnp.bfloat16),
        "seq",
    )
    grouped_in = slot_in.reshape(experts, -1, features)
    hidden_pre = jnp.einsum("esd,ehd->esh", grouped_in, w_in, preferred_element_type=jnp.float32)
    hidden_act = gelu_tanh(hidden_pre).astype(jnp.bfloat16)
    out_terms = jnp.einsum(
        "esh,ehd->esd", hidden_act, w_out, preferred_element_type=jnp.float32
    ).reshape(-1, features)
    slot_out = lax.psum(out_terms.astype(jnp.bfloat16), "seq")
    grouped_grad = slot_grad.reshape(experts, -1, features)
    grad_w_out = jnp.einsum(
        "esh,esd->ehd", hidden_act, grouped_grad, preferred_element_type=jnp.float32
    ).astype(jnp.bfloat16)
    act_grad = jnp.einsum("esd,ehd->esh", grouped_grad, w_out, preferred_element_type=jnp.float32)
    pre_grad = (act_grad * gelu_slope(hidden_pre)).astype(jnp.bfloat16)
    grad_w_in = jnp.einsum(
        "esh,esd->ehd", pre_grad, grouped_in, preferred_element_type=jnp.float32
    ).astype(jnp.bfloat16)
    in_terms = jnp.einsum(
        "esh,ehd->esd", pre_grad, w_in, preferred_element_type=jnp.float32
    ).reshape(-1, features)
    slot_in_grad = lax.psum(in_terms.astype(jnp.bfloat16), "seq")
    comb_dot = lax.dot_general(
        out_grad, slot_out, cols_contract, preferred_element_type=jnp.float32
    )
    comb_row = lax.psum(jnp.sum(combine * comb_dot, axis=1), "slot")
    comb_logit_grad = combine * (comb_dot - comb_row[:, None])
    disp_dot = lax.dot_general(
        tokens, slot_in_grad, cols_contract, preferred_element_type=jnp.float32
    )
    disp_total = lax.psum(jnp.sum(dispatch_low.astype(jnp.float32) * disp_dot, axis=0), "seq")
    disp_logit_grad = dispatch * (disp_dot - disp_total[None, :])
    logit_grad_low = (disp_logit_grad + comb_logit_grad).astype(jnp.bfloat16)
    grad_keys = lax.psum_scatter(
        lax.dot_general(
            tokens, logit_grad_low, rows_contract, preferred_element_type=jnp.float32
        ).astype(jnp.bfloat16),
        "seq",
        scatter_dimension=0,
        tiled=True,
    ).astype(jnp.float32)
    partial_sum = lax.dot_general(
        logit_grad_low, slot_keys, cols_contract, preferred_element_type=jnp.float32
    )
    partial_sum = partial_sum + jnp.dot(
        dispatch_low, slot_in_grad, preferred_element_type=jnp.float32
    )
    token_sum = lax.psum_scatter(
        partial_sum.astype(jnp.bfloat16), "slot", scatter_dimension=1, tiled=True
    )
    return (token_sum, grad_keys, grad_w_in, grad_w_out)


def solution(mesh):
    placed = (
        P("seq", None),
        P(None, "slot"),
        P("slot", "seq", None),
        P("slot", "seq", None),
        P("seq", None),
    )
    return jax.shard_map(
        per_device,
        mesh=mesh,
        in_specs=placed,
        out_specs=(
            P("seq", "slot"),
            P("seq", "slot"),
            P("slot", "seq", None),
            P("slot", "seq", None),
        ),
        check_vma=False,
    )
```

profile of v0, /device:TPU:1, one launch (start us, length us, event | category | flops | bytes accessed | tf_op | source)
XLA Modules:
  0.0 544.8 jit_solution(14423384498551287804)
XLA Ops:
  7.2 0.0 copy-start
  7.2 0.0 all-reduce.7.cloned.1.call-start
  7.2 0.9 copy-done
  8.1 4.1 fusion.9
  12.2 28.6 %psum.56 = f32[128]{0:T(128)S(1)} all-reduce(f32[128]{0:T(128)S(1)} %get-tuple-element.13), channel_id=1, replica_groups=mesh['seq'=16,'slot'=8] {'seq'}, use_global_device_ids=true, to_apply=%region_1.0 | all-reduce | flops 128 | bytes 1024 | tf_op jit(solution)/shard_map/psum | solution.py:32
  40.9 0.0 copy-start.9
  40.9 0.1 fusion.3
  41.0 4.1 convolution_convert_fusion.5
  45.1 21.2 %psum.57 = f32[2048]{0:T(1024)S(1)} all-reduce(f32[2048]{0:T(1024)S(1)} %get-tuple-element.12), channel_id=1, replica_groups=mesh['seq'=16,'slot'=8] {'slot'}, use_global_device_ids=true, to_apply=%region_3.0 | all-reduce | flops 2048 | bytes 16384 | tf_op jit(solution)/shard_map/psum | solution.py:33
  66.3 4.3 convolution_convert_fusion.6
  70.6 0.0 copy-done.9
  70.6 0.0 all-reduce.7.cloned.1.call-update
  70.7 0.0 all-reduce.5.cloned.1.call-start
  70.7 118.8 %all-reduce.7.cloned.1.call-done = (bf16[8,16,1280]{2,1,0:T(8,128)(2,1)}, bf16[8,16,1280]{2,1,0:T(8,128)(2,1)}) async-done(((bf16[8,16,1280]{2,1,0:T(8,128)(2,1)}, bf16[8,16,1280]{2,1,0:T(8,128)(2,1)}), (bf16[8,16,1280]{2,1,0:T(8,128)(2,1)}, bf16[8,16,1280]{2,1,0:T(8,128)(2,1)})) %all-reduce.7.cloned.1.call-update) | async-done | bytes 655376 | tf_op jit(solution)/shard_map/psum | solution.py:38
  189.5 0.0 copy-start.1
  189.5 0.0 copy-start.6
  189.5 3.5 fusion.10
  193.0 0.0 copy-start.4
  193.0 0.0 copy-start.2
  193.0 3.6 convolution_convert_fusion.2
  196.6 0.0 copy-done.1
  196.6 0.0 copy-done.6
  196.7 1.1 fusion.1
  197.8 0.0 copy-done.2
  197.8 1.4 convolution_convert_fusion.3
  199.1 0.0 copy-done.4
  199.1 0.0 all-reduce.5.cloned.1.call-update
  199.2 0.0 reduce-scatter.7.cloned.1.call-start
  199.2 119.7 %all-reduce.5.cloned.1.call-done = (bf16[128,1280]{1,0:T(8,128)(2,1)}, bf16[128,1280]{1,0:T(8,128)(2,1)}) async-done(((bf16[128,1280]{1,0:T(8,128)(2,1)}, bf16[128,1280]{1,0:T(8,128)(2,1)}), (bf16[128,1280]{1,0:T(8,128)(2,1)}, bf16[128,1280]{1,0:T(8,128)(2,1)})) %all-reduce.5.cloned.1.call-update) | async-done | bytes 655376 | tf_op jit(solution)/shard_map/psum | solution.py:56
  318.9 0.0 copy-start.10
  318.9 4.2 multiply_reduce_fusion.1
  323.1 27.8 %psum.61 = f32[128]{0:T(128)} all-reduce(f32[128]{0:T(128)S(1)} %get-tuple-element.21), channel_id=1, replica_groups=mesh['seq'=16,'slot'=8] {'seq'}, use_global_device_ids=true, to_apply=%region_8.0 | all-reduce | flops 128 | bytes 1024 | tf_op jit(solution)/shard_map/psum | solution.py:78
  350.9 0.0 copy-done.10
  350.9 5.0 multiply_reduce_fusion
  355.8 20.7 %psum.63 = f32[2048]{0:T(1024)S(1)} all-reduce(f32[2048]{0:T(1024)S(1)} %get-tuple-element.19), channel_id=1, replica_groups=mesh['seq'=16,'slot'=8] {'slot'}, use_global_device_ids=true, to_apply=%region_11.0 | all-reduce | flops 2048 | bytes 16384 | tf_op jit(solution)/shard_map/psum | solution.py:73
  376.5 1.8 add_convert_fusion.1
  378.3 3.4 fusion
  381.7 0.9 copy.17
  382.6 0.0 reduce-scatter.7.cloned.1.call-update
  382.6 0.0 copy-start.3
  382.6 0.2 reduce-scatter.5.cloned.1.call-start
  382.8 1.5 fusion.11
  384.4 0.0 copy-done.3
  384.4 3.9 add_convert_fusion
  388.3 0.0 copy-start.8
  388.3 0.0 copy-start.5
  388.3 0.0 copy-start.7
  388.3 0.0 reduce-scatter.5.cloned.1.call-update
  388.3 0.9 copy-done.8
  389.2 3.1 convolution_convert_fusion.1
  392.4 0.0 copy-done.5
  392.4 0.0 copy-done.7
  392.4 3.2 convolution_convert_fusion
  395.5 44.5 %reduce-scatter.7.cloned.1.call-done = bf16[80,128]{1,0:T(8,128)(2,1)} async-done(((bf16[1280,128]{1,0:T(8,128)(2,1)}), bf16[80,128]{1,0:T(8,128)(2,1)}) %reduce-scatter.7.cloned.1.call-update) | async-done | bytes 20496
  440.1 0.8 copy.18
  440.9 0.7 copy.14
  441.6 96.6 %reduce-scatter.5.cloned.1.call-done = bf16[2048,160]{0,1:T(8,128)(2,1)} async-done(((bf16[2048,1280]{0,1:T(8,128)(2,1)}), bf16[2048,160]{0,1:T(8,128)(2,1)}) %reduce-scatter.5.cloned.1.call-update) | async-done | bytes 655376 | tf_op jit(solution)/shard_map/reduce_scatter | solution.py:95
Async XLA Ops:
  7.2 1.0 copy-start
  7.2 182.3 %all-reduce.7.cloned.1.call-start = ((), (), s32[]{:S(2)}) async-start(), calls=%async_computation.5 | async-start | bytes 1310720 | tf_op jit(solution)/shard_map/psum | solution.py:38
  40.9 29.8 %copy-start.9 = (f32[128]{0:T(128)}, f32[128]{0:T(128)S(1)}, u32[]{:S(2)}) copy-start(f32[128]{0:T(128)S(1)} %psum.56) | copy-start | bytes 1540
  70.7 248.2 %all-reduce.5.cloned.1.call-start = ((), (), s32[]{:S(2)}) async-start(), calls=%async_computation.4 | async-start | bytes 1310720 | tf_op jit(solution)/shard_map/psum | solution.py:56
  189.5 7.1 %copy-start.1 = (bf16[8,192,1280]{2,1,0:T(8,128)(2,1)S(1)}, bf16[8,192,1280]{2,1,0:T(8,128)(2,1)}, u32[]{:S(2)}) copy-start(bf16[8,192,1280]{2,1,0:T(8,128)(2,1)} %param.8) | copy-start | bytes 11796484
  189.5 7.1 %copy-start.6 = (bf16[8,16,1280]{2,1,0:T(8,128)(2,1)S(1)}, bf16[8,16,1280]{2,1,0:T(8,128)(2,1)}, u32[]{:S(2)}) copy-start(bf16[8,16,1280]{2,1,0:T(8,128)(2,1)} %get-tuple-element.17) | copy-start | bytes 983044
  193.0 6.1 %copy-start.4 = (f32[8,16,192]{2,1,0:T(8,128)}, f32[8,16,192]{2,1,0:T(8,128)S(1)}, u32[]{:S(2)}) copy-start(f32[8,16,192]{2,1,0:T(8,128)S(1)} %fusion.10) | copy-start | bytes 294916
  193.0 4.8 copy-start.2
  199.2 240.9 %reduce-scatter.7.cloned.1.call-start = ((), (), s32[]{:S(2)}) async-start(), calls=%async_computation.3 | async-start | bytes 348160
  318.9 32.0 %copy-start.10 = (bf16[128,1280]{1,0:T(8,128)(2,1)S(1)}, bf16[128,1280]{1,0:T(8,128)(2,1)}, u32[]{:S(2)}) copy-start(bf16[128,1280]{1,0:T(8,128)(2,1)} %get-tuple-element.14) | copy-start | bytes 983044
  382.6 1.8 copy-start.3
  382.6 155.7 %reduce-scatter.5.cloned.1.call-start = ((), (), s32[]{:S(2)}) async-start(), calls=%async_computation.2 | async-start | bytes 5898240 | tf_op jit(solution)/shard_map/reduce_scatter | solution.py:95
  388.3 1.0 copy-start.8
  388.3 4.1 copy-start.5
  388.3 4.1 copy-start.7
Sparse Core Ops, SparseCore 0:
  70.8 118.6 all-reduce.6
  199.3 119.5 all-reduce.4
  382.7 57.3 reduce-scatter.6
  444.9 93.3 reduce-scatter.4
where the time goes:
time: 545 us
  waiting for transfers between devices  380 us (70%)
  blocking collectives  98.3 us (18%)
  matrix products  46.4 us (9%)
  between operations  13.8 us (3%)
    psum x1, waiting for transfers between devices, per_device(): slot_out = lax.psum(out_terms.astype(jnp.bfloat16), 'seq')  120 us
    psum x1, waiting for transfers between devices, per_device(): lax.psum(lax.dot_general(dispatch_low, tokens, rows_contract, preferred_e...  119 us
    reduce_scatter x1, waiting for transfers between devices, per_device(): lax.psum_scatter(partial_sum.astype(jnp.bfloat16), 'slot', scatter_dimens...  96.6 us
    unnamed x5, waiting for transfers between devices  44.6 us
    psum x1, blocking collectives, per_device(): column_total = lax.psum(jnp.sum(exp_logits, axis=0), 'seq')  28.6 us
    psum x1, blocking collectives, per_device(): lax.psum(jnp.sum(dispatch_low.astype(jnp.float32) * disp_dot, axis=0), 's...  27.8 us
    psum x1, blocking collectives, per_device(): row_total = lax.psum(jnp.sum(exp_logits, axis=1), 'slot')  21.2 us
    psum x1, blocking collectives, per_device(): comb_row = lax.psum(jnp.sum(combine * comb_dot, axis=1), 'slot')  20.7 us
  transfers between devices with their start and end apart: 4, of which 4 were waited for; matrix products, arithmetic and copies ran while one was open for 2% of the time, Pallas kernels for 0%

commit v1 on v0

v1 whole, which is shorter than its diff:
```python
import jax
import jax.numpy as jnp
from jax import lax
from jax.sharding import Mesh, PartitionSpec as P

gelu_scale = 0.7978845608
gelu_cubic = 0.044715
rows_contract = (((0,), (0,)), ((), ()))
cols_contract = (((1,), (1,)), ((), ()))

SEQ = ("zl", "y", "c")
SLOT = ("x", "zh")
SAME_CORE = ("x", "zh", "zl", "y")
f32 = jnp.float32
bf16 = jnp.bfloat16


def gelu_tanh(values):
    return (
        0.5
        * values
        * (1.0 + jnp.tanh(gelu_scale * (values + gelu_cubic * values * values * values)))
    )


def gelu_slope(values):
    bent = jnp.tanh(gelu_scale * (values + gelu_cubic * values * values * values))
    return 0.5 * (1.0 + bent) + 0.5 * values * (1.0 - bent * bent) * gelu_scale * (
        1.0 + 3.0 * gelu_cubic * values * values
    )


def to_blocks(first, second, groups):
    slots, width = first.shape
    both = jnp.stack([first, second]).reshape(2, groups, slots // groups, 2, width // 2)
    return both.transpose(1, 3, 0, 2, 4).reshape(groups * 2, 2, slots // groups, width // 2)


def per_device(tokens, slot_keys, w_in, w_out, out_grad):
    token_count, features = tokens.shape
    experts = w_in.shape[0]
    own_slots = slot_keys.shape[1]
    core = lax.axis_index("c")
    slot_at = lax.axis_index(SLOT)
    half = features // 2
    slot_devices = lax.axis_size(SLOT)
    seq_devices = lax.axis_size(SEQ)
    groups = seq_devices // 2
    block = own_slots // groups
    everyone = slot_devices * groups

    keys_all = lax.all_gather(slot_keys, SLOT, axis=0, tiled=False)

    logits = jnp.dot(tokens, slot_keys, preferred_element_type=f32)
    exp_logits = jnp.exp(logits)
    own_column = jnp.sum(exp_logits, axis=0)
    own_row = jnp.sum(exp_logits, axis=1)
    row_parts = lax.all_to_all(
        jnp.broadcast_to(own_row.reshape(1, -1, 128), (slot_devices, token_count // 128, 128)),
        SLOT, 0, 0,
    )
    row_total = jnp.sum(row_parts, axis=0).reshape(-1)
    safe_column = jnp.where(own_column > 0, own_column, 1.0)
    dispatch_own = (exp_logits / safe_column[None, :]).astype(bf16)
    slot_in_part = lax.dot_general(
        dispatch_own, tokens, rows_contract, preferred_element_type=f32
    ).astype(bf16)
    combine_own = (exp_logits / row_total[:, None]).astype(bf16)
    slot_grad_part = lax.dot_general(
        combine_own, out_grad, rows_contract, preferred_element_type=f32
    ).astype(bf16)
    parts = lax.all_to_all(to_blocks(slot_in_part, slot_grad_part, groups), SEQ, 0, 0)
    column_sent = jnp.broadcast_to(
        own_column.reshape(groups, 1, 1, block), (groups, 2, 8, block)
    ).reshape(seq_devices, 8, block)
    column_parts = lax.all_to_all(column_sent, SEQ, 0, 0)[:, 0, :]
    column_total = jnp.sum(column_parts, axis=0)
    share = column_parts / column_total[None, :]
    slot_in_block = jnp.sum(parts[:, 0].astype(f32) * share[:, :, None], axis=0)
    slot_grad_block = jnp.sum(parts[:, 1].astype(f32), axis=0)
    sent = jnp.stack([slot_in_block, slot_grad_block]).astype(bf16)
    whole = lax.all_to_all(
        jnp.broadcast_to(sent[None], (seq_devices,) + sent.shape), SEQ, 0, 0
    )
    whole = whole.reshape(groups, 2, 2, block, half).transpose(2, 0, 3, 1, 4)
    whole = whole.reshape(2, experts, own_slots // experts, features)
    grouped_in, grouped_grad = whole[0], whole[1]

    hidden_pre = jnp.einsum("esd,ehd->esh", grouped_in, w_in, preferred_element_type=f32)
    hidden_act = gelu_tanh(hidden_pre).astype(bf16)
    out_terms = jnp.einsum("esh,ehd->esd", hidden_act, w_out, preferred_element_type=f32)
    act_grad = jnp.einsum("esd,ehd->esh", grouped_grad, w_out, preferred_element_type=f32)
    pre_grad = (act_grad * gelu_slope(hidden_pre)).astype(bf16)
    in_terms = jnp.einsum("esh,ehd->esd", pre_grad, w_in, preferred_element_type=f32)
    grad_w_out = jnp.einsum(
        "esh,esd->ehd", hidden_act, grouped_grad, preferred_element_type=f32
    ).astype(bf16)
    grad_w_in = jnp.einsum(
        "esh,esd->ehd", pre_grad, grouped_in, preferred_element_type=f32
    ).astype(bf16)
    terms = lax.all_to_all(
        to_blocks(
            out_terms.reshape(-1, features).astype(bf16),
            in_terms.reshape(-1, features).astype(bf16),
            groups,
        ),
        SEQ, 0, 0,
    )
    summed = jnp.sum(terms.astype(f32), axis=0).astype(bf16)
    disp_half = jnp.sum(slot_in_block * summed[1].astype(f32), axis=1)
    extra = jnp.concatenate([column_total, disp_half]).reshape(1, -1)
    gathered = lax.all_to_all(
        jnp.broadcast_to(summed[None], (everyone,) + summed.shape), SAME_CORE, 0, 0
    )
    extras = lax.all_to_all(
        jnp.broadcast_to(extra[None], (everyone, 8, extra.shape[1])), SAME_CORE, 0, 0
    )[:, 0, :]
    swap = [(0, 1), (1, 0)]
    gathered_other = lax.ppermute(gathered, "c", swap)
    extras_other = lax.ppermute(extras, "c", swap)
    column_all = extras[:, :block].reshape(-1)
    disp_total = (extras[:, block:] + extras_other[:, block:]).reshape(-1)

    def whole_width(of):
        mine = gathered[:, of].reshape(-1, half)
        other = gathered_other[:, of].reshape(-1, half)
        low = jnp.where(core == 0, mine, other)
        high = jnp.where(core == 0, other, mine)
        return jnp.concatenate([low, high], axis=1)

    slot_out = whole_width(0)
    in_grad = whole_width(1)
    keys = keys_all.transpose(1, 0, 2).reshape(features, -1)

    exp_all = jnp.exp(jnp.dot(tokens, keys, preferred_element_type=f32))
    combine = exp_all / row_total[:, None]
    dispatch = exp_all / column_all[None, :]
    comb_dot = lax.dot_general(out_grad, slot_out, cols_contract, preferred_element_type=f32)
    disp_dot = lax.dot_general(tokens, in_grad, cols_contract, preferred_element_type=f32)
    comb_row = jnp.sum(combine * comb_dot, axis=1)
    logit_grad = (
        dispatch * (disp_dot - disp_total[None, :]) + combine * (comb_dot - comb_row[:, None])
    ).astype(bf16)
    dispatch_low = dispatch.astype(bf16)
    own_logit_grad = lax.dynamic_slice_in_dim(logit_grad, slot_at * own_slots, own_slots, 1)
    keys_part = lax.dot_general(
        tokens, own_logit_grad, rows_contract, preferred_element_type=f32
    ).astype(bf16)
    keys_parts = lax.all_to_all(
        keys_part.reshape(seq_devices, features // seq_devices, own_slots), SEQ, 0, 0
    )
    grad_keys = jnp.sum(keys_parts.astype(f32), axis=0)
    width = features // slot_devices
    keys_rows = lax.dynamic_slice_in_dim(keys, slot_at * width, width, 0)
    in_grad_cols = lax.dynamic_slice_in_dim(in_grad, slot_at * width, width, 1)
    grad_tokens = lax.dot_general(logit_grad, keys_rows, cols_contract, preferred_element_type=f32)
    grad_tokens = grad_tokens + jnp.dot(dispatch_low, in_grad_cols, preferred_element_type=f32)
    return (grad_tokens.astype(bf16), grad_keys, grad_w_in, grad_w_out)


def solution(mesh):
    fine = Mesh(mesh.devices.reshape(2, 4, 2, 4, 2), ("zl", "y", "c", "x", "zh"))
    placed = (
        P(SEQ, None),
        P(None, SLOT),
        P(SLOT, SEQ, None),
        P(SLOT, SEQ, None),
        P(SEQ, None),
    )
    return jax.shard_map(
        per_device,
        mesh=fine,
        in_specs=placed,
        out_specs=(
            P(SEQ, SLOT),
            P(SEQ, SLOT),
            P(SLOT, SEQ, None),
            P(SLOT, SEQ, None),
        ),
        check_vma=False,
    )
```

time: 545 us -> 235 us (0.43)
  waiting for transfers between devices: 380 us -> 28.6 us
  starting transfers between devices: 0.35 us -> 38.2 us
  blocking collectives: 98.3 us -> 62.2 us
  matrix products: 46.4 us -> 64.2 us
  local copies, waits for them, and re-layouts: 4.36 us -> 15.2 us
  other arithmetic: 1.87 us -> 11 us
    psum x2 -> x0, waiting for transfers between devices: 238 us -> none  [the longest x1 120 us: per_device(): slot_out = lax.psum(out_terms.astype(jnp.bfloat16), 'seq')]
    psum x4 -> x0, blocking collectives: 98.3 us -> none  [the longest x1 28.6 us: per_device(): column_total = lax.psum(jnp.sum(exp_logits, axis=0), 'seq')]
    reduce_scatter x1 -> x0, waiting for transfers between devices: 96.6 us -> none  [per_device(): lax.psum_scatter(partial_sum.astype(jnp.bfloat16), 'slot', scatter_dimens...]
    all_to_all x0 -> x2, blocking collectives: none -> 62.2 us  [the longest x1 47.1 us: per_device(): lax.all_to_all(jnp.broadcast_to(summed[None], (everyone,) + summed.shape)...]
    unnamed x5 -> x1, waiting for transfers between devices: 44.6 us -> 0.68 us
    all_to_all x0 -> x6, starting transfers between devices: none -> 35.3 us  [the longest x1 8.16 us: per_device(): lax.all_to_all(jnp.broadcast_to(own_row.reshape(1, -1, 128), (slot_device...]
    all_to_all x0 -> x6, waiting for transfers between devices: none -> 27.9 us  [the longest x1 10.8 us: per_device(): lax.all_to_all(to_blocks(out_terms.reshape(-1, features).astype(bf16), in...]
    dot_general x12 -> x13, matrix products: 38.2 us -> 50.4 us  [the longest x1 12.5 us: per_device(): lax.dot_general(tokens, in_grad, cols_contract, preferred_element_type=f32)]
  transfers between devices with their start and end apart: 4 -> 9, of which waited for: 4 -> 5; matrix products, arithmetic and copies ran while one was open for 2% -> 18% of each run, Pallas kernels for 0% -> 0%
where the time goes in v1:
time: 235 us; the launch traced here: 234 us
  matrix products  64.2 us (27%)
  blocking collectives  62.2 us (26%)
  starting transfers between devices  38.2 us (16%)
  waiting for transfers between devices  28.6 us (12%)
  local copies, waits for them, and re-layouts  15.2 us (6%)
  between operations  14.4 us (6%)
  other arithmetic  11 us (5%)
    all_to_all x1, blocking collectives, per_device(): lax.all_to_all(jnp.broadcast_to(summed[None], (everyone,) + summed.shape)...  47.1 us
    all_to_all x1, blocking collectives, per_device(): lax.all_to_all(jnp.broadcast_to(sent[None], (seq_devices,) + sent.shape),...  15.1 us
    dot_general x1, matrix products, per_device(): lax.dot_general(tokens, in_grad, cols_contract, preferred_element_type=f32)  12.5 us
    all_to_all x1, waiting for transfers between devices, per_device(): lax.all_to_all(to_blocks(out_terms.reshape(-1, features).astype(bf16), in...  10.8 us
    dot_general x1, matrix products, per_device(): lax.dot_general(out_grad, slot_out, cols_contract, preferred_element_type...  10.7 us
    all_to_all x1, waiting for transfers between devices, per_device(): lax.all_to_all(to_blocks(slot_in_part, slot_grad_part, groups), SEQ, 0, 0)  9.59 us
    dot_general x1, matrix products, per_device(): exp_all = jnp.exp(jnp.dot(tokens, keys, preferred_element_type=f32))  8.35 us
    all_to_all x1, starting transfers between devices, per_device(): lax.all_to_all(jnp.broadcast_to(own_row.reshape(1, -1, 128), (slot_device...  8.16 us
  transfers between devices with their start and end apart: 9, of which 5 were waited for; matrix products, arithmetic and copies ran while one was open for 18% of the time, Pallas kernels for 0%

profile of v1, /device:TPU:1, one launch (start us, length us, event | category | flops | bytes accessed | tf_op | source)
XLA Modules:
  0.0 233.8 jit_solution(11430800361528859925)
XLA Ops:
  7.2 4.1 %fusion.33 = (f32[128]{0:T(128)S(1)}, f32[2048]{0:T(1024)S(1)}, f32[2048,128]{1,0:T(8,128)S(1)}) fusion(bf16[2048,1280]{1,0:T(8,128)(2,1)} %param.5, bf16[1280,128]{1,0:T(8,128)(2,1)} %param.6), kind=kOutput, calls=%fused_computation.74 | convolution fusion | flops 671610752 | bytes 6627840 | tf_op jit(solution)/shard_map/dot_general | solution.py:54
  11.3 0.6 broadcast_in_dim.49
  12.0 8.2 %all-to-all-start.1 = ((f32[8,16,128]{2,1,0:T(8,128)}), f32[8,16,128]{2,1,0:T(8,128)S(1)}, u32[]{:S(2)}, u32[]{:S(2)}) async-start(f32[8,16,128]{2,1,0:T(8,128)} %broadcast_in_dim.49), calls=%async_computation.1 | async-start | bytes 131072 | tf_op jit(solution)/shard_map/all_to_all | solution.py:58
  20.1 3.4 %convolution_convert_fusion.6 = bf16[128,1280]{1,0:T(8,128)(2,1)S(1)} fusion(bf16[2048,1280]{1,0:T(8,128)(2,1)} %param.5, f32[2048,128]{1,0:T(8,128)S(1)} %get-tuple-element.16, f32[128]{0:T(128)S(1)} %compare_select_fusion), kind=kOutput, calls=%fused_computation.28 | convolution fusion | flops 671776768 | bytes 6619648 | tf_op jit(solution)/shard_map/dot_general | solution.py:65
  23.5 0.1 broadcast_in_dim.22
  23.6 0.1 stack.23
  23.8 0.7 reshape.134
  24.5 2.3 all-to-all-done.1
  26.7 7.0 %all-to-all-start = ((f32[16,1,128]{2,1,0:T(1,128)}), f32[16,1,128]{2,1,0:T(1,128)S(1)}, u32[]{:S(2)}, u32[]{:S(2)}) async-start(f32[16,1,128]{2,1,0:T(1,128)} %reshape.134), calls=%async_computation | async-start | bytes 16384 | tf_op jit(solution)/shard_map/all_to_all | solution.py:76
  33.8 0.6 copy-done.4
  34.4 3.6 %convolution_convert_fusion.5 = bf16[128,1280]{1,0:T(8,128)(2,1)S(1)} fusion(bf16[2048,1280]{1,0:T(8,128)(2,1)} %param.9, f32[2048,128]{1,0:T(8,128)S(1)} %get-tuple-element.16, f32[2048]{0:T(1024)S(1)} %bitcast.90), kind=kOutput, calls=%fused_computation.27 | convolution fusion | flops 671776768 | bytes 6627328 | tf_op jit(solution)/shard_map/dot_general | solution.py:69
  38.0 0.1 stack.24
  38.2 0.9 pad_maximum_fusion.4
  39.1 0.1 all-to-all-done
  39.2 5.6 %all-to-all-start.2 = ((bf16[16,2,16,640]{3,2,1,0:T(8,128)(2,1)}), bf16[16,2,16,640]{3,2,1,0:T(8,128)(2,1)S(1)}, u32[]{:S(2)}, u32[]{:S(2)}) async-start(bf16[16,2,16,640]{3,2,1,0:T(8,128)(2,1)} %bitcast.7), calls=%async_computation.2 | async-start | bytes 1310720 | tf_op jit(solution)/shard_map/all_to_all | solution.py:72
  44.8 0.5 broadcast.58
  45.3 0.7 reduce.5
  46.1 0.5 copy-done.6
  46.6 9.6 %all-to-all-done.2 = bf16[16,2,16,640]{3,2,1,0:T(8,128)(2,1)S(1)} async-done(((bf16[16,2,16,640]{3,2,1,0:T(8,128)(2,1)}), bf16[16,2,16,640]{3,2,1,0:T(8,128)(2,1)S(1)}, u32[]{:S(2)}, u32[]{:S(2)}) %all-to-all-start.2) | async-done | bytes 655392 | tf_op jit(solution)/shard_map/all_to_all | solution.py:72
  56.2 0.1 fusion.14
  56.5 15.1 %all_to_all.40 = bf16[16,2,16,640]{3,2,1,0:T(8,128)(2,1)S(1)} all-to-all(bf16[16,2,16,640]{3,2,1,0:T(8,128)(2,1)S(1)} %broadcast_in_dim.50), channel_id=1, replica_groups=mesh['zl'=2,'y'=4,'c'=2,'x'=4,'zh'=2] {'zl','y','c'}, dimensions={0} | all-to-all | bytes 1310720 | tf_op jit(solution)/shard_map/all_to_all | solution.py:82
  71.7 0.3 copy.35
  72.0 0.2 squeeze.16
  72.2 0.3 copy.36
  72.4 0.2 squeeze.17
  72.7 3.4 %fusion.36 = f32[8,16,192]{2,1,0:T(8,128)S(1)} fusion(bf16[8,16,1280]{2,1,0:T(8,128)(2,1)S(1)} %squeeze.16, bf16[8,192,1280]{2,1,0:T(8,128)(2,1)} %param.7), kind=kOutput, calls=%fused_computation.77 | convolution fusion | flops 62914560 | bytes 4358144 | tf_op jit(solution)/shard_map/esd,ehd->esh/dot_general | solution.py:89
  76.0 0.6 convolution_convert_fusion.3
  76.7 1.1 fusion.13
  77.8 0.3 copy-done.1
  78.2 0.6 convolution_convert_fusion.2
  78.8 0.1 convert_element_type.105
  78.9 0.1 convert_element_type.102
  79.1 0.9 pad_maximum_fusion.5
  80.0 3.8 %all-to-all-start.4 = ((bf16[16,2,16,640]{3,2,1,0:T(8,128)(2,1)}), bf16[16,2,16,640]{3,2,1,0:T(8,128)(2,1)S(1)}, u32[]{:S(2)}, u32[]{:S(2)}) async-start(bf16[16,2,16,640]{3,2,1,0:T(8,128)(2,1)} %bitcast.16), calls=%async_computation.4 | async-start | bytes 1310720 | tf_op jit(solution)/shard_map/all_to_all | solution.py:101
  83.8 0.7 all-gather.3.cloned.1.call-update
  84.5 10.8 %all-to-all-done.4 = bf16[16,2,16,640]{3,2,1,0:T(8,128)(2,1)S(1)} async-done(((bf16[16,2,16,640]{3,2,1,0:T(8,128)(2,1)}), bf16[16,2,16,640]{3,2,1,0:T(8,128)(2,1)S(1)}, u32[]{:S(2)}, u32[]{:S(2)}) %all-to-all-start.4) | async-done | bytes 655392 | tf_op jit(solution)/shard_map/all_to_all | solution.py:101
  95.4 0.1 reduce_sum.99
  95.4 0.2 broadcast_in_dim.52
  95.7 47.1 %all_to_all.41 = bf16[64,2,16,640]{3,2,1,0:T(8,128)(2,1)S(1)} all-to-all(bf16[64,2,16,640]{3,2,1,0:T(8,128)(2,1)S(1)} %broadcast_in_dim.52), channel_id=1, replica_groups=mesh['zl'=2,'y'=4,'c'=2,'x'=4,'zh'=2] {'x','zh','zl','y'}, dimensions={0} | all-to-all | bytes 5242880 | tf_op jit(solution)/shard_map/all_to_all | solution.py:112
  142.7 1.4 collective-permute-start
  144.1 0.1 fusion.26
  144.3 0.7 pad_maximum_fusion.7
  145.0 0.7 broadcast_in_dim.51
  145.7 1.7 reshape.136
  147.5 7.0 %all-to-all-start.5 = ((f32[64,1,256]{2,1,0:T(1,128)}), f32[64,1,256]{2,1,0:T(1,128)S(1)}, u32[]{:S(2)}, u32[]{:S(2)}) async-start(f32[64,1,256]{2,1,0:T(1,128)} %reshape.136), calls=%async_computation.5 | async-start | bytes 131072 | tf_op jit(solution)/shard_map/all_to_all | solution.py:115
  154.4 3.2 %convolution_convert_fusion = bf16[8,192,1280]{2,1,0:T(8,128)(2,1)} fusion(bf16[8,16,1280]{2,1,0:T(8,128)(2,1)S(1)} %squeeze.17, f32[8,16,192]{2,1,0:T(8,128)S(1)} %fusion.36), kind=kOutput, calls=%fused_computation.9 | convolution fusion | flops 65101824 | bytes 4358144 | tf_op jit(solution)/shard_map/esh,esd->ehd/dot_general | solution.py:95
  157.6 5.1 %all-to-all-done.5 = f32[64,1,256]{2,1,0:T(1,128)S(1)} async-done(((f32[64,1,256]{2,1,0:T(1,128)}), f32[64,1,256]{2,1,0:T(1,128)S(1)}, u32[]{:S(2)}, u32[]{:S(2)}) %all-to-all-start.5) | async-done | bytes 65568 | tf_op jit(solution)/shard_map/all_to_all | solution.py:115
  162.7 0.8 reduce.6
  163.5 0.1 reshape.137
  163.7 1.5 collective-permute-start.1
  165.2 3.1 %convolution_convert_fusion.1 = bf16[8,192,1280]{2,1,0:T(8,128)(2,1)} fusion(bf16[8,16,192]{2,1,0:T(8,128)(2,1)S(1)} %fusion.13, bf16[8,16,1280]{2,1,0:T(8,128)(2,1)S(1)} %squeeze.16), kind=kOutput, calls=%fused_computation.10 | convolution fusion | flops 64880640 | bytes 4308992 | tf_op jit(solution)/shard_map/esh,esd->ehd/dot_general | solution.py:98
  168.3 0.1 slice_add_fusion
  168.6 4.4 %copy.32 = bf16[1280,8,128]{0,2,1:T(8,128)(2,1)} copy(bf16[1280,8,128]{2,0,1:T(8,128)(2,1)} %bitcast.77) | data formatting | bytes 5242880 | tf_op jit(solution)/shard_map/transpose | solution.py:133
  172.9 8.4 %fusion.35 = f32[2048,1024]{0,1:T(8,128)S(1)} fusion(bf16[2048,1280]{1,0:T(8,128)(2,1)} %param.5, bf16[1280,1024]{0,1:T(8,128)(2,1)} %bitcast.75), kind=kOutput, calls=%fused_computation.76 | convolution fusion | flops 5368709120 | bytes 16252928 | tf_op jit(solution)/shard_map/dot_general | solution.py:135
  181.3 5.7 %broadcast_select_fusion.1 = (bf16[64,1,16,640]{3,2,1,0:T(8,128)(2,1)S(1)}, bf16[64,1,16,640]{3,2,1,0:T(8,128)(2,1)}, bf16[64,1,16,640]{3,2,1,0:T(8,128)(2,1)S(1)}, bf16[64,1,16,640]{3,2,1,0:T(8,128)(2,1)}) fusion(pred[]{:T(512)S(6)} %eq.2, bf16[64,2,16,640]{3,2,1,0:T(8,128)(2,1)} %collective-permute-done, bf16[64,2,16,640]{3,2,1,0:T(8,128)(2,1)S(1)} %all_to_all.41), kind=kLoop, calls=%fused_computation.31 | loop fusion | flops 2621440 | bytes 10485761 | tf_op jit(solution)/shard_map/jit(_where)/select_n | solution.py:127
  187.1 10.7 %fusion = (f32[2048]{0:T(1024)S(1)}, f32[1024,2048]{1,0:T(8,128)}) fusion(f32[2048]{0:T(1024)S(1)} %bitcast.91, f32[2048,1024]{0,1:T(8,128)S(1)} %fusion.35, bf16[2048,1280]{1,0:T(8,128)(2,1)} %param.9, bf16[1024,640]{1,0:T(8,128)(2,1)S(1)} %bitcast.84, bf16[1024,640]{1,0:T(8,128)(2,1)S(1)} %bitcast.83), kind=kOutput, calls=%fused_computation.2 | convolution fusion | flops 5380241408 | bytes 24657920 | tf_op jit(solution)/shard_map/dot_general | solution.py:138
  197.8 12.5 %fusion.3 = bf16[2048,1024]{0,1:T(8,128)(2,1)S(1)} fusion(f32[1024,2048]{1,0:T(8,128)} %get-tuple-element.18, f32[2048]{0:T(1024)S(1)} %get-tuple-element.17, f32[1024]{0:T(1024)S(1)} %sub.25, f32[2048]{0:T(1024)S(1)} %bitcast.92, f32[2048,1024]{0,1:T(8,128)} %copy-done.7, bf16[2048,1280]{1,0:T(8,128)(2,1)} %param.5, bf16[1024,640]{1,0:T(8,128)(2,1)} %bitcast.79, ...), kind=kOutput, calls=%fused_computation.5 | convolution fusion | flops 5390729216 | bytes 28860416 | tf_op jit(solution)/shard_map/dot_general | solution.py:139
  210.3 2.0 copy-done.2
  212.3 0.9 fusion.12
  213.2 0.9 copy.39
  214.1 3.7 %all-to-all-start.7 = ((bf16[16,80,128]{2,1,0:T(8,128)(2,1)}), bf16[16,80,128]{2,1,0:T(8,128)(2,1)S(1)}, u32[]{:S(2)}, u32[]{:S(2)}) async-start(bf16[16,80,128]{2,1,0:T(8,128)(2,1)} %bitcast.26), calls=%async_computation.7 | async-start | bytes 655360 | tf_op jit(solution)/shard_map/all_to_all | solution.py:149
  217.8 5.6 %fusion.4 = f32[2048,160]{0,1:T(8,128)S(1)} fusion(f32[2048,1024]{0,1:T(8,128)} %copy-done.7, f32[1024]{0:T(1024)S(1)} %div.55, s32[]{:T(128)S(6)} %select_n.57, bf16[1024,640]{1,0:T(8,128)(2,1)} %bitcast.82, bf16[1024,640]{1,0:T(8,128)(2,1)} %bitcast.80), kind=kOutput, calls=%fused_computation.11 | convolution fusion | flops 675938304 | bytes 12324868 | tf_op jit(solution)/shard_map/dot_general | solution.py:157
  223.3 3.0 %fusion.11 = bf16[2048,160]{0,1:T(8,128)(2,1)} fusion(f32[2048,160]{0,1:T(8,128)S(1)} %fusion.4, bf16[2048,1024]{0,1:T(8,128)(2,1)S(1)} %copy-done.3, bf16[1280,1024]{0,1:T(8,128)(2,1)} %bitcast.76, s32[]{:T(128)S(6)} %select_n.57), kind=kOutput, calls=%fused_computation.23 | convolution fusion | flops 671744000 | bytes 6684676 | tf_op jit(solution)/shard_map/dot_general | solution.py:156
  226.3 0.7 convert_reduce_fusion
  (41 shorter events, 0.7 us)
Async XLA Ops:
  12.0 14.8 %all-to-all-start.1 = ((f32[8,16,128]{2,1,0:T(8,128)}), f32[8,16,128]{2,1,0:T(8,128)S(1)}, u32[]{:S(2)}, u32[]{:S(2)}) async-start(f32[8,16,128]{2,1,0:T(8,128)} %broadcast_in_dim.49), calls=%async_computation.1 | async-start | bytes 131072 | tf_op jit(solution)/shard_map/all_to_all | solution.py:58
  26.7 12.4 %all-to-all-start = ((f32[16,1,128]{2,1,0:T(1,128)}), f32[16,1,128]{2,1,0:T(1,128)S(1)}, u32[]{:S(2)}, u32[]{:S(2)}) async-start(f32[16,1,128]{2,1,0:T(1,128)} %reshape.134), calls=%async_computation | async-start | bytes 16384 | tf_op jit(solution)/shard_map/all_to_all | solution.py:76
  33.8 0.6 copy-start.4
  39.2 17.0 %all-to-all-start.2 = ((bf16[16,2,16,640]{3,2,1,0:T(8,128)(2,1)}), bf16[16,2,16,640]{3,2,1,0:T(8,128)(2,1)S(1)}, u32[]{:S(2)}, u32[]{:S(2)}) async-start(bf16[16,2,16,640]{3,2,1,0:T(8,128)(2,1)} %bitcast.7), calls=%async_computation.2 | async-start | bytes 1310720 | tf_op jit(solution)/shard_map/all_to_all | solution.py:72
  46.1 0.5 copy-start.6
  72.7 3.4 %copy-start = (bf16[8,192,1280]{2,1,0:T(8,128)(2,1)S(1)}, bf16[8,192,1280]{2,1,0:T(8,128)(2,1)}, u32[]{:S(2)}) copy-start(bf16[8,192,1280]{2,1,0:T(8,128)(2,1)} %param.8) | copy-start | bytes 11796484
  76.0 2.1 copy-start.1
  80.0 15.4 %all-to-all-start.4 = ((bf16[16,2,16,640]{3,2,1,0:T(8,128)(2,1)}), bf16[16,2,16,640]{3,2,1,0:T(8,128)(2,1)S(1)}, u32[]{:S(2)}, u32[]{:S(2)}) async-start(bf16[16,2,16,640]{3,2,1,0:T(8,128)(2,1)} %bitcast.16), calls=%async_computation.4 | async-start | bytes 1310720 | tf_op jit(solution)/shard_map/all_to_all | solution.py:101
  83.8 84.8 %all-gather.3.cloned.1.call-start = ((), (), s32[]{:S(2)}) async-start(), calls=%async_computation.8 | async-start | bytes 2949120 | tf_op jit(solution)/shard_map/all_gather | solution.py:52
  142.7 38.6 %collective-permute-start = (bf16[64,2,16,640]{3,2,1,0:T(8,128)(2,1)S(1)}, bf16[64,2,16,640]{3,2,1,0:T(8,128)(2,1)}, u32[]{:S(2)}, u32[]{:S(2)}) collective-permute-start(bf16[64,2,16,640]{3,2,1,0:T(8,128)(2,1)S(1)} %all_to_all.41), channel_id=1, source_target_pairs={{0,8},{8,0},{1,9},{9,1},{2,10},{10,2},{3,11},{11,3},{4,12},{12,4},... | collective-permute-start | bytes 7864328 | tf_op jit(solution)/shard_map/ppermute | solution.py:119
  147.5 15.2 %all-to-all-start.5 = ((f32[64,1,256]{2,1,0:T(1,128)}), f32[64,1,256]{2,1,0:T(1,128)S(1)}, u32[]{:S(2)}, u32[]{:S(2)}) async-start(f32[64,1,256]{2,1,0:T(1,128)} %reshape.136), calls=%async_computation.5 | async-start | bytes 131072 | tf_op jit(solution)/shard_map/all_to_all | solution.py:115
  163.7 4.7 %collective-permute-start.1 = (f32[64,32]{1,0:T(8,128)S(1)}, f32[64,32]{1,0:T(8,128)S(1)}, u32[]{:S(2)}, u32[]{:S(2)}) collective-permute-start(f32[64,32]{1,0:T(8,128)S(1)} %bitcast.85), channel_id=1, source_target_pairs={{0,8},{8,0},{1,9},{9,1},{2,10},{10,2},{3,11},{11,3},{4,12},{12,4},... | collective-permute-start | bytes 24584 | tf_op jit(solution)/shard_map/ppermute | solution.py:120
  181.3 5.8 %copy-start.7 = (f32[2048,1024]{0,1:T(8,128)}, f32[2048,1024]{0,1:T(8,128)S(1)}, u32[]{:S(2)}) copy-start(f32[2048,1024]{0,1:T(8,128)S(1)} %fusion.35) | copy-start | bytes 25165828
  181.3 5.8 %copy-start.5 = (f32[16,128]{1,0:T(8,128)S(1)}, f32[16,128]{1,0:T(8,128)}, u32[]{:S(2)}) copy-start(f32[16,128]{1,0:T(8,128)} %copy-done.4) | copy-start | bytes 24580
  187.1 25.2 %slice-start = ((s8[5242880]{0:T(1024)(128)(4,1)}), s8[4194304]{0:T(1024)(128)(4,1)S(1)}, s32[]{:S(2)}) async-start(s8[5242880]{0:T(1024)(128)(4,1)} %bitcast.73), calls=%async_computation.9 | async-start | bytes 8388608
  197.8 14.5 %slice-start.1 = ((s8[5242880]{0:T(1024)(128)(4,1)}), s8[1048576]{0:T(1024)(128)(4,1)S(1)}, s32[]{:S(2)}) async-start(s8[5242880]{0:T(1024)(128)(4,1)} %bitcast.73), calls=%async_computation.10 | async-start | bytes 2097152
  210.3 2.0 copy-start.2
  214.1 12.2 %all-to-all-start.7 = ((bf16[16,80,128]{2,1,0:T(8,128)(2,1)}), bf16[16,80,128]{2,1,0:T(8,128)(2,1)S(1)}, u32[]{:S(2)}, u32[]{:S(2)}) async-start(bf16[16,80,128]{2,1,0:T(8,128)(2,1)} %bitcast.26), calls=%async_computation.7 | async-start | bytes 655360 | tf_op jit(solution)/shard_map/all_to_all | solution.py:149
  217.8 5.6 %copy-start.3 = (bf16[2048,1024]{0,1:T(8,128)(2,1)S(1)}, bf16[2048,1024]{0,1:T(8,128)(2,1)}, u32[]{:S(2)}) copy-start(bf16[2048,1024]{0,1:T(8,128)(2,1)} %copy-done.2) | copy-start | bytes 12582916
Sparse Core Ops, SparseCore 0:
  86.9 70.9 all-gather.2

commit v2 on v1

v2 whole, which is shorter than its diff:
```python
import jax
import jax.numpy as jnp
from jax import lax
from jax.experimental import pallas as pl
from jax.experimental.pallas import tpu as pltpu
from jax.sharding import Mesh, PartitionSpec as P

gelu_scale = 0.7978845608
gelu_cubic = 0.044715
rows_contract = (((0,), (0,)), ((), ()))
cols_contract = (((1,), (1,)), ((), ()))

SEQ = ("zl", "y", "c")
SLOT = ("x", "zh")
SAME_CORE = ("x", "zh", "zl", "y")
f32 = jnp.float32
bf16 = jnp.bfloat16
LANES = 128
MIB = 1 << 20


def gelu_tanh(values):
    return (
        0.5
        * values
        * (1.0 + jnp.tanh(gelu_scale * (values + gelu_cubic * values * values * values)))
    )


def gelu_slope(values):
    bent = jnp.tanh(gelu_scale * (values + gelu_cubic * values * values * values))
    return 0.5 * (1.0 + bent) + 0.5 * values * (1.0 - bent * bent) * gelu_scale * (
        1.0 + 3.0 * gelu_cubic * values * values
    )


def guarded(total):
    power = jnp.where(total > 2.0**64, 2.0**-32, jnp.where(total < 2.0**-64, 2.0**32, 1.0))
    return power, 1.0 / (total * power)


def two_parts(values):
    high = values.astype(bf16).astype(f32)
    return high, values - high


def in_lanes(rows, columns):
    lane = lax.broadcasted_iota(jnp.int32, (rows, LANES), 1)
    laid = jnp.zeros((rows, LANES), f32)
    for at, column in enumerate(columns):
        laid = jnp.where(lane == at, column, laid)
    return laid.astype(bf16)


def params(mib):
    return pltpu.CompilerParams(vmem_limit_bytes=mib * MIB)


def cost(flops, nbytes):
    return pl.CostEstimate(flops=flops, bytes_accessed=nbytes, transcendentals=0)


def whole_in_vmem():
    return pl.BlockSpec(memory_space=pltpu.VMEM)


def own_logits(keys_t, tokens, copies, tile=512):
    slots, features = keys_t.shape
    count = tokens.shape[0]

    def kernel(keys_ref, tokens_ref, exp_ref, row_ref, column_ref):
        exps = jnp.exp(
            lax.dot_general(keys_ref[...], tokens_ref[...], cols_contract, preferred_element_type=f32)
        )
        exp_ref[...] = exps
        row_ref[...] = jnp.broadcast_to(
            jnp.sum(exps, axis=0, keepdims=True)[None], (copies, 1, tile)
        )
        by_lane = exps[:, :LANES]
        for at in range(1, tile // LANES):
            by_lane = by_lane + exps[:, at * LANES : (at + 1) * LANES]

        @pl.when(pl.program_id(0) == 0)
        def _():
            column_ref[...] = by_lane

        @pl.when(pl.program_id(0) > 0)
        def _():
            column_ref[...] += by_lane

    return pl.pallas_call(
        kernel,
        grid=(count // tile,),
        in_specs=[
            pl.BlockSpec((slots, features), lambda i: (0, 0)),
            pl.BlockSpec((tile, features), lambda i: (i, 0)),
        ],
        out_specs=[
            pl.BlockSpec((slots, tile), lambda i: (0, i)),
            pl.BlockSpec((copies, 1, tile), lambda i: (0, 0, i)),
            pl.BlockSpec((slots, LANES), lambda i: (0, 0)),
        ],
        out_shape=[
            jax.ShapeDtypeStruct((slots, count), f32),
            jax.ShapeDtypeStruct((copies, 1, count), f32),
            jax.ShapeDtypeStruct((slots, LANES), f32),
        ],
        compiler_params=params(32),
        cost_estimate=cost(2 * slots * features * count, 2 * features * count + 4 * slots * count),
        name="own_logits",
    )(keys_t, tokens)


def dispatch_part(exps, column, tokens, tile=512):
    slots, count = exps.shape
    features = tokens.shape[1]

    def kernel(exp_ref, column_ref, tokens_ref, out_ref, total_ref):
        total = jnp.sum(column_ref[...], axis=1, keepdims=True)
        power, inverse = guarded(jnp.where(total > 0, total, 1.0))
        weights = ((exp_ref[...] * power) * inverse).astype(bf16)
        term = jnp.dot(weights, tokens_ref[...], preferred_element_type=f32)

        @pl.when(pl.program_id(0) == 0)
        def _():
            total_ref[...] = term

        @pl.when(pl.program_id(0) > 0)
        def _():
            total_ref[...] += term

        @pl.when(pl.program_id(0) == pl.num_programs(0) - 1)
        def _():
            out_ref[...] = total_ref[...].astype(bf16)

    return pl.pallas_call(
        kernel,
        grid=(count // tile,),
        in_specs=[
            pl.BlockSpec((slots, tile), lambda i: (0, i)),
            pl.BlockSpec((slots, LANES), lambda i: (0, 0)),
            pl.BlockSpec((tile, features), lambda i: (i, 0)),
        ],
        out_specs=pl.BlockSpec((slots, features), lambda i: (0, 0)),
        out_shape=jax.ShapeDtypeStruct((slots, features), bf16),
        scratch_shapes=[pltpu.VMEM((slots, features), f32)],
        compiler_params=params(32),
        cost_estimate=cost(2 * slots * features * count, 2 * features * count + 4 * slots * count),
        name="dispatch_part",
    )(exps, column, tokens)


def combine_part(exps, row_parts, column, slot_in_part, out_grad, groups, tile=512):
    slots, count = exps.shape
    features = out_grad.shape[1]
    half = features // 2
    block = slots // groups
    width = features + LANES
    copies = row_parts.shape[0]

    def kernel(exp_ref, row_ref, column_ref, in_ref, grad_ref, sent_ref, total_ref):
        power, inverse = guarded(jnp.sum(row_ref[...], axis=0))
        weights = ((exp_ref[...] * power) * inverse).astype(bf16)
        term = jnp.dot(weights, grad_ref[...], preferred_element_type=f32)

        @pl.when(pl.program_id(0) == 0)
        def _():
            total_ref[...] = term

        @pl.when(pl.program_id(0) > 0)
        def _():
            total_ref[...] += term

        @pl.when(pl.program_id(0) == pl.num_programs(0) - 1)
        def _():
            total = jnp.sum(column_ref[...], axis=1, keepdims=True)
            shift, _unused = guarded(total)
            high, low = two_parts(total * shift)
            lanes = in_lanes(slots, (high, low, 1.0 / shift))
            grad = total_ref[...].astype(bf16)
            for group in range(groups):
                rows = slice(group * block, (group + 1) * block)
                for side in range(2):
                    cut = slice(side * half, (side + 1) * half)
                    sent_ref[group * 2 + side, :, :half] = in_ref[rows, cut]
                    sent_ref[group * 2 + side, :, half:features] = grad[rows, cut]
                    sent_ref[group * 2 + side, :, features:] = lanes[rows]

    return pl.pallas_call(
        kernel,
        grid=(count // tile,),
        in_specs=[
            pl.BlockSpec((slots, tile), lambda i: (0, i)),
            pl.BlockSpec((copies, 1, tile), lambda i: (0, 0, i)),
            pl.BlockSpec((slots, LANES), lambda i: (0, 0)),
            pl.BlockSpec((slots, features), lambda i: (0, 0)),
            pl.BlockSpec((tile, features), lambda i: (i, 0)),
        ],
        out_specs=pl.BlockSpec((groups * 2, block, width), lambda i: (0, 0, 0)),
        out_shape=jax.ShapeDtypeStruct((groups * 2, block, width), bf16),
        scratch_shapes=[pltpu.VMEM((slots, features), f32)],
        compiler_params=params(32),
        cost_estimate=cost(2 * slots * features * count, 2 * features * count + 4 * slots * count),
        name="combine_part",
    )(exps, row_parts, column, slot_in_part, out_grad)


def sum_slots(parts, copies):
    sources, block, width = parts.shape
    features = width - LANES
    half = features // 2

    def kernel(parts_ref, sent_ref, in_ref, column_ref):
        lanes = parts_ref[:, :, features:].astype(f32)
        columns = (lanes[:, :, 0:1] + lanes[:, :, 1:2]) * lanes[:, :, 2:3]
        total = jnp.sum(columns, axis=0)
        power, inverse = guarded(total)
        share = (columns * power[None]) * inverse[None]
        slot_in = jnp.zeros((block, half), f32)
        slot_grad = jnp.zeros((block, half), f32)
        for source in range(sources):
            slot_in = slot_in + parts_ref[source, :, :half].astype(f32) * share[source]
            slot_grad = slot_grad + parts_ref[source, :, half:features].astype(f32)
        in_ref[...] = slot_in
        column_ref[...] = jnp.broadcast_to(total, (block, LANES))
        in_low = slot_in.astype(bf16)
        grad_low = slot_grad.astype(bf16)
        for copy in range(copies):
            sent_ref[copy, :, :half] = in_low
            sent_ref[copy, :, half:] = grad_low

    return pl.pallas_call(
        kernel,
        in_specs=[whole_in_vmem()],
        out_specs=[whole_in_vmem()] * 3,
        out_shape=[
            jax.ShapeDtypeStruct((copies, block, features), bf16),
            jax.ShapeDtypeStruct((block, half), f32),
            jax.ShapeDtypeStruct((block, LANES), f32),
        ],
        compiler_params=params(32),
        name="sum_slots",
    )(parts)


def experts_part(whole, w_in, w_out):
    experts, hidden, features = w_in.shape
    block = whole.shape[1]
    half = features // 2

    def kernel(whole_ref, w_in_ref, w_out_ref, terms_ref, act_ref, pre_ref):
        slots = jnp.concatenate([whole_ref[0, :, :half], whole_ref[1, :, :half]], axis=1)
        grads = jnp.concatenate([whole_ref[0, :, half:], whole_ref[1, :, half:]], axis=1)
        hidden_pre = lax.dot_general(slots, w_in_ref[0], cols_contract, preferred_element_type=f32)
        act_grad = lax.dot_general(grads, w_out_ref[0], cols_contract, preferred_element_type=f32)
        act = gelu_tanh(hidden_pre).astype(bf16)
        pre = (act_grad * gelu_slope(hidden_pre)).astype(bf16)
        out_terms = jnp.dot(act, w_out_ref[0], preferred_element_type=f32).astype(bf16)
        in_terms = jnp.dot(pre, w_in_ref[0], preferred_element_type=f32).astype(bf16)
        for side in range(2):
            cut = slice(side * half, (side + 1) * half)
            terms_ref[side, :, :half] = out_terms[:, cut]
            terms_ref[side, :, half:] = in_terms[:, cut]
        act_ref[0] = act
        pre_ref[0] = pre

    return pl.pallas_call(
        kernel,
        grid=(experts,),
        in_specs=[
            pl.BlockSpec((2, block, features), lambda e: (e, 0, 0)),
            pl.BlockSpec((1, hidden, features), lambda e: (e, 0, 0)),
            pl.BlockSpec((1, hidden, features), lambda e: (e, 0, 0)),
        ],
        out_specs=[
            pl.BlockSpec((2, block, features), lambda e: (e, 0, 0)),
            pl.BlockSpec((1, block, hidden), lambda e: (e, 0, 0)),
            pl.BlockSpec((1, block, hidden), lambda e: (e, 0, 0)),
        ],
        out_shape=[
            jax.ShapeDtypeStruct(whole.shape, bf16),
            jax.ShapeDtypeStruct((experts, block, hidden), bf16),
            jax.ShapeDtypeStruct((experts, block, hidden), bf16),
        ],
        compiler_params=params(32),
        cost_estimate=cost(8 * experts * block * hidden * features, 4 * experts * hidden * features),
        name="experts_part",
    )(whole, w_in, w_out)


def weight_grads(whole, act, pre, hidden_shape):
    experts, hidden, features = hidden_shape
    block = whole.shape[1]
    half = features // 2

    def kernel(whole_ref, act_ref, pre_ref, in_ref, out_ref):
        for side in range(2):
            cut = slice(side * half, (side + 1) * half)
            in_ref[0, :, cut] = lax.dot_general(
                pre_ref[0], whole_ref[side, :, :half], rows_contract, preferred_element_type=f32
            ).astype(bf16)
            out_ref[0, :, cut] = lax.dot_general(
                act_ref[0], whole_ref[side, :, half:], rows_contract, preferred_element_type=f32
            ).astype(bf16)

    return pl.pallas_call(
        kernel,
        grid=(experts,),
        in_specs=[
            pl.BlockSpec((2, block, features), lambda e: (e, 0, 0)),
            pl.BlockSpec((1, block, hidden), lambda e: (e, 0, 0)),
            pl.BlockSpec((1, block, hidden), lambda e: (e, 0, 0)),
        ],
        out_specs=[pl.BlockSpec((1, hidden, features), lambda e: (e, 0, 0))] * 2,
        out_shape=[jax.ShapeDtypeStruct(hidden_shape, bf16)] * 2,
        compiler_params=params(32),
        cost_estimate=cost(4 * experts * block * hidden * features, 4 * experts * hidden * features),
        name="weight_grads",
    )(whole, act, pre)


def sum_terms(terms, slot_in, column, copies):
    sources, block, features = terms.shape
    half = features // 2
    width = features + LANES

    def kernel(terms_ref, in_ref, column_ref, sent_ref):
        total = terms_ref[0].astype(f32)
        for source in range(1, sources):
            total = total + terms_ref[source].astype(f32)
        low = total.astype(bf16)
        inner = jnp.sum(in_ref[...] * low[:, half:].astype(f32), axis=1, keepdims=True)
        power, inverse = guarded(column_ref[:, 0:1])
        lanes = in_lanes(block, two_parts(inverse) + (power,) + two_parts(inner))
        for copy in range(copies):
            sent_ref[copy, :, :features] = low
            sent_ref[copy, :, features:] = lanes

    return pl.pallas_call(
        kernel,
        in_specs=[whole_in_vmem()] * 3,
        out_specs=whole_in_vmem(),
        out_shape=jax.ShapeDtypeStruct((copies, block, width), bf16),
        compiler_params=params(32),
        name="sum_terms",
    )(terms, slot_in, column)


def all_exps(keys_t, tokens, tile=256):
    slots, features = keys_t.shape
    count = tokens.shape[0]

    def kernel(keys_ref, tokens_ref, exp_ref):
        exp_ref[...] = jnp.exp(
            lax.dot_general(keys_ref[...], tokens_ref[...], cols_contract, preferred_element_type=f32)
        )

    return pl.pallas_call(
        kernel,
        grid=(count // tile,),
        in_specs=[
            pl.BlockSpec((slots, features), lambda i: (0, 0)),
            pl.BlockSpec((tile, features), lambda i: (i, 0)),
        ],
        out_specs=pl.BlockSpec((slots, tile), lambda i: (0, i)),
        out_shape=jax.ShapeDtypeStruct((slots, count), f32),
        compiler_params=params(32),
        cost_estimate=cost(2 * slots * features * count, 2 * features * count + 4 * slots * count),
        name="all_exps",
    )(keys_t, tokens)


def logit_grads(place, exps, tokens, out_grad, row_parts, mine, other, own_slots, tile=256):
    slots, count = exps.shape
    features = tokens.shape[1]
    half = features // 2
    blocks, block, width = mine.shape
    copies = row_parts.shape[0]

    def kernel(
        place_ref, exp_ref, tokens_ref, grad_ref, row_ref, mine_ref, other_ref,
        logit_ref, dispatch_ref, keys_ref, power_ref, inverse_ref, total_ref, sum_ref,
    ):
        core = place_ref[0]
        here = pl.multiple_of(core * half, LANES)
        there = pl.multiple_of((1 - core) * half, LANES)
        step = pl.program_id(0)

        @pl.when(step == 0)
        def _():
            lanes = mine_ref[:, :, features:].reshape(slots, LANES).astype(f32)
            apart = other_ref[:, :, features:].reshape(slots, LANES).astype(f32)
            inner = lanes[:, 3:4] + lanes[:, 4:5] + apart[:, 3:4] + apart[:, 4:5]
            power_ref[...] = jnp.broadcast_to(lanes[:, 2:3], (slots, tile))
            inverse_ref[...] = jnp.broadcast_to(lanes[:, 0:1] + lanes[:, 1:2], (slots, tile))
            total_ref[...] = jnp.broadcast_to(inner, (slots, tile))

        def dot(at, ref):
            near = lax.dot_general(
                mine_ref[:, :, at * half : (at + 1) * half].reshape(slots, half),
                ref[:, pl.ds(here, half)],
                cols_contract,
                preferred_element_type=f32,
            )
            far = lax.dot_general(
                other_ref[:, :, at * half : (at + 1) * half].reshape(slots, half),
                ref[:, pl.ds(there, half)],
                cols_contract,
                preferred_element_type=f32,
            )
            return near + far

        power, inverse = guarded(jnp.sum(row_ref[...], axis=0))
        exps_here = exp_ref[...]
        combine = (exps_here * power) * inverse
        comb_dot = dot(0, grad_ref)
        comb_row = jnp.sum(combine * comb_dot, axis=0, keepdims=True)
        dispatch = (exps_here * power_ref[...]) * inverse_ref[...]
        disp_dot = dot(1, tokens_ref)
        logit = combine * (comb_dot - comb_row) + dispatch * (disp_dot - total_ref[...])
        logit_ref[...] = logit.astype(bf16)
        dispatch_ref[...] = dispatch.astype(bf16)
        own = logit_ref[pl.ds(pl.multiple_of(place_ref[1] * own_slots, own_slots), own_slots), :]
        term = jnp.dot(own, tokens_ref[...], preferred_element_type=f32)

        @pl.when(step == 0)
        def _():
            sum_ref[...] = term

        @pl.when(step > 0)
        def _():
            sum_ref[...] += term

        @pl.when(step == pl.num_programs(0) - 1)
        def _():
            keys_ref[...] = sum_ref[...].T.astype(bf16)

    return pl.pallas_call(
        kernel,
        grid_spec=pltpu.PrefetchScalarGridSpec(
            num_scalar_prefetch=1,
            grid=(count // tile,),
            in_specs=[
                pl.BlockSpec((slots, tile), lambda i, place: (0, i)),
                pl.BlockSpec((tile, features), lambda i, place: (i, 0)),
                pl.BlockSpec((tile, features), lambda i, place: (i, 0)),
                pl.BlockSpec((copies, 1, tile), lambda i, place: (0, 0, i)),
                pl.BlockSpec((blocks, block, width), lambda i, place: (0, 0, 0)),
                pl.BlockSpec((blocks, block, width), lambda i, place: (0, 0, 0)),
            ],
            out_specs=[
                pl.BlockSpec((slots, tile), lambda i, place: (0, i)),
                pl.BlockSpec((slots, tile), lambda i, place: (0, i)),
                pl.BlockSpec((features, own_slots), lambda i, place: (0, 0)),
            ],
            scratch_shapes=[
                pltpu.VMEM((slots, tile), f32),
                pltpu.VMEM((slots, tile), f32),
                pltpu.VMEM((slots, tile), f32),
                pltpu.VMEM((own_slots, features), f32),
            ],
        ),
        out_shape=[
            jax.ShapeDtypeStruct((slots, count), bf16),
            jax.ShapeDtypeStruct((slots, count), bf16),
            jax.ShapeDtypeStruct((features, own_slots), bf16),
        ],
        compiler_params=params(56),
        cost_estimate=cost(4 * slots * features * count, 4 * features * count + 8 * slots * count),
        name="logit_grads",
    )(place, exps, tokens, out_grad, row_parts, mine, other)


def token_grads(keys_rows, in_grad_rows, logit_grad, dispatch, tile=512):
    width, slots = keys_rows.shape
    count = logit_grad.shape[1]

    def kernel(keys_ref, in_ref, logit_ref, dispatch_ref, out_ref):
        total = jnp.dot(keys_ref[...], logit_ref[...], preferred_element_type=f32)
        total = total + jnp.dot(in_ref[...], dispatch_ref[...], preferred_element_type=f32)
        out_ref[...] = total.T.astype(bf16)

    return pl.pallas_call(
        kernel,
        grid=(count // tile,),
        in_specs=[
            pl.BlockSpec((width, slots), lambda i: (0, 0)),
            pl.BlockSpec((width, slots), lambda i: (0, 0)),
            pl.BlockSpec((slots, tile), lambda i: (0, i)),
            pl.BlockSpec((slots, tile), lambda i: (0, i)),
        ],
        out_specs=pl.BlockSpec((tile, width), lambda i: (i, 0)),
        out_shape=jax.ShapeDtypeStruct((count, width), bf16),
        compiler_params=params(32),
        cost_estimate=cost(4 * slots * width * count, 4 * slots * count),
        name="token_grads",
    )(keys_rows, in_grad_rows, logit_grad, dispatch)


def per_device(tokens, slot_keys, w_in, w_out, out_grad):
    features = tokens.shape[1]
    own_slots = slot_keys.shape[1]
    core = lax.axis_index("c")
    slot_at = lax.axis_index(SLOT)
    half = features // 2
    slot_devices = lax.axis_size(SLOT)
    seq_devices = lax.axis_size(SEQ)
    groups = seq_devices // 2
    everyone = slot_devices * groups

    keys_t = slot_keys.T
    keys_all = lax.all_gather(keys_t, SLOT, axis=0, tiled=True)

    exps, own_row, column = own_logits(keys_t, tokens, slot_devices)
    row_parts = lax.all_to_all(own_row, SLOT, 0, 0)
    slot_in_part = dispatch_part(exps, column, tokens)
    parts = lax.all_to_all(
        combine_part(exps, row_parts, column, slot_in_part, out_grad, groups), SEQ, 0, 0
    )
    sent, slot_in, column_total = sum_slots(parts, seq_devices)
    whole = lax.all_to_all(sent, SEQ, 0, 0)

    sent, act, pre = experts_part(whole, w_in, w_out)
    terms = lax.all_to_all(sent, SEQ, 0, 0)
    grad_w_in, grad_w_out = weight_grads(whole, act, pre, w_in.shape)
    mine = lax.all_to_all(
        sum_terms(terms, slot_in, column_total, everyone), SAME_CORE, 0, 0
    )
    other = lax.ppermute(mine, "c", [(0, 1), (1, 0)])

    all_exp = all_exps(keys_all, tokens)
    place = jnp.stack([core, slot_at]).astype(jnp.int32)
    logit_grad, dispatch, keys_part = logit_grads(
        place, all_exp, tokens, out_grad, row_parts, mine, other, own_slots
    )
    keys_parts = lax.all_to_all(
        keys_part.reshape(seq_devices, features // seq_devices, own_slots), SEQ, 0, 0
    )
    grad_keys = jnp.sum(keys_parts.astype(f32), axis=0)

    width = features // slot_devices
    keys_rows = lax.dynamic_slice_in_dim(keys_all, slot_at * width, width, 1).T
    side = (slot_at * width) // half
    at = half + slot_at * width - side * half
    in_grad_cols = jnp.where(
        side == core,
        lax.dynamic_slice_in_dim(mine, at, width, 2),
        lax.dynamic_slice_in_dim(other, at, width, 2),
    )
    in_grad_rows = in_grad_cols.reshape(-1, width).T
    grad_tokens = token_grads(keys_rows, in_grad_rows, logit_grad, dispatch)
    return (grad_tokens, grad_keys, grad_w_in, grad_w_out)


def solution(mesh):
    fine = Mesh(mesh.devices.reshape(2, 4, 2, 4, 2), ("zl", "y", "c", "x", "zh"))
    placed = (
        P(SEQ, None),
        P(None, SLOT),
        P(SLOT, SEQ, None),
        P(SLOT, SEQ, None),
        P(SEQ, None),
    )
    return jax.shard_map(
        per_device,
        mesh=fine,
        in_specs=placed,
        out_specs=(
            P(SEQ, SLOT),
            P(SEQ, SLOT),
            P(SLOT, SEQ, None),
            P(SLOT, SEQ, None),
        ),
        check_vma=False,
    )
```

time: 235 us -> 246 us (1.047)
  matrix products: 64.2 us -> 0 us
  Pallas kernels: 0 us -> 56.6 us
  waiting for transfers between devices: 28.6 us -> 75.8 us
  starting transfers between devices: 38.2 us -> 22.8 us
  blocking collectives: 62.2 us -> 48.6 us
  local copies, waits for them, and re-layouts: 15.2 us -> 24 us
  other arithmetic: 11 us -> 3.25 us
    dot_general x15 -> x0, matrix products: 64.2 us -> none  [the longest x1 12.5 us: per_device(): lax.dot_general(tokens, in_grad, cols_contract, preferred_element_type=f32)]
    pallas_call x0 -> x10, Pallas kernels: none -> 56.6 us  [the longest x1 26.1 us: logit_grads(): pl.pallas_call(kernel, grid_spec=pltpu.PrefetchScalarGridSpec(num_scalar_...]
    all_gather x1, waiting for transfers between devices: 0.01 us -> 34 us  [per_device(): keys_all = lax.all_gather(keys_t, SLOT, axis=0, tiled=True)]
    all_to_all x5 -> x2, starting transfers between devices: 31.6 us -> 14.5 us  [the longest x1 8.17 us: per_device(): row_parts = lax.all_to_all(own_row, SLOT, 0, 0)]
    all_to_all x2 -> x3, blocking collectives: 62.2 us -> 48.6 us  [the longest x1 19.2 us: per_device(): lax.all_to_all(combine_part(exps, row_parts, column, slot_in_part, out_gr...]
    all_to_all x5 -> x2, waiting for transfers between devices: 27.9 us -> 41.1 us  [the longest x1 39 us: per_device(): lax.all_to_all(sum_terms(terms, slot_in, column_total, everyone), SAME_CO...]
    unnamed x24 -> x21, local copies, waits for them, and re-layouts: 6.06 us -> 18.8 us
    select_n x2 -> x1, other arithmetic: 5.74 us -> 1.92 us  [per_device(): jnp.where(side == core, lax.dynamic_slice_in_dim(mine, at, width, 2), lax...]
  transfers between devices with their start and end apart: 9 -> 5, of which waited for: 5 -> 3; matrix products, arithmetic and copies ran while one was open for 18% -> 3% of each run, Pallas kernels for 0% -> 8%
where the time goes in v2:
time: 246 us; the launch traced here: 245 us
  waiting for transfers between devices  75.8 us (31%)
  Pallas kernels  56.6 us (23%)
  blocking collectives  48.6 us (20%)
  local copies, waits for them, and re-layouts  24 us (10%)
  starting transfers between devices  22.8 us (9%)
  between operations  14.1 us (6%)
  other arithmetic  3.25 us (1%)
    all_to_all x1, waiting for transfers between devices, per_device(): lax.all_to_all(sum_terms(terms, slot_in, column_total, everyone), SAME_CO...  39 us
    all_gather x1, waiting for transfers between devices, per_device(): keys_all = lax.all_gather(keys_t, SLOT, axis=0, tiled=True)  34 us
    pallas_call x1, Pallas kernels, logit_grads(): pl.pallas_call(kernel, grid_spec=pltpu.PrefetchScalarGridSpec(num_scalar_...  26.1 us
    all_to_all x1, blocking collectives, per_device(): lax.all_to_all(combine_part(exps, row_parts, column, slot_in_part, out_gr...  19.2 us
    unnamed x21, local copies, waits for them, and re-layouts  18.8 us
    all_to_all x1, blocking collectives, per_device(): whole = lax.all_to_all(sent, SEQ, 0, 0)  14.7 us
    all_to_all x1, blocking collectives, per_device(): terms = lax.all_to_all(sent, SEQ, 0, 0)  14.6 us
    all_to_all x1, starting transfers between devices, per_device(): row_parts = lax.all_to_all(own_row, SLOT, 0, 0)  8.17 us
  transfers between devices with their start and end apart: 5, of which 3 were waited for; matrix products, arithmetic and copies ran while one was open for 3% of the time, Pallas kernels for 8%

profile of v2, /device:TPU:1, one launch (start us, length us, event | category | flops | bytes accessed | tf_op | source)
XLA Modules:
  0.0 245.2 jit_solution(17996238145638994432)
XLA Ops:
  7.2 1.1 copy.13.keys_ref
  8.3 0.0 copy-start
  8.3 2.5 %copy-done = bf16[2048,1280]{1,0:T(8,128)(2,1)S(1)} copy-done((bf16[2048,1280]{1,0:T(8,128)(2,1)S(1)}, bf16[2048,1280]{1,0:T(8,128)(2,1)}, u32[]{:S(2)}) %copy-start) | copy-done | bytes 5242904
  10.8 3.1 %own_logits.1 = (f32[128,2048]{1,0:T(8,128)S(1)}, f32[8,1,2048]{2,1,0:T(1,128)}, f32[128,128]{1,0:T(8,128)S(1)}) custom-call(bf16[128,1280]{1,0:T(8,128)(2,1)S(1)} %copy.13.keys_ref, bf16[2048,1280]{1,0:T(8,128)(2,1)S(1)} %copy-done), custom_call_target="tpu_custom_call" | custom-call | flops 671088640 | bytes 6291456 | tf_op jit(solution)/shard_map/own_logits/pallas_call | solution.py:91
  13.9 8.2 %all-to-all-start = ((f32[8,1,2048]{2,1,0:T(1,128)}), f32[8,1,2048]{2,1,0:T(1,128)S(1)}, u32[]{:S(2)}, u32[]{:S(2)}) async-start(f32[8,1,2048]{2,1,0:T(1,128)} %get-tuple-element.19), calls=%async_computation | async-start | bytes 131072 | tf_op jit(solution)/shard_map/all_to_all | solution.py:515
  22.0 0.0 copy-start.1
  22.0 2.5 %copy-done.1 = bf16[2048,1280]{1,0:T(8,128)(2,1)S(1)} copy-done((bf16[2048,1280]{1,0:T(8,128)(2,1)S(1)}, bf16[2048,1280]{1,0:T(8,128)(2,1)}, u32[]{:S(2)}) %copy-start.1) | copy-done | bytes 5242904
  24.5 2.0 dispatch_part.1.in_ref
  26.5 2.1 all-to-all-done.row_ref
  28.6 0.0 copy-start.3
  28.6 2.5 %copy-done.3 = bf16[2048,1280]{1,0:T(8,128)(2,1)S(1)} copy-done((bf16[2048,1280]{1,0:T(8,128)(2,1)S(1)}, bf16[2048,1280]{1,0:T(8,128)(2,1)}, u32[]{:S(2)}) %copy-start.3) | copy-done | bytes 5242904
  31.1 0.0 copy-start.8
  31.1 0.0 copy-start.6
  31.1 0.0 copy-start.7
  31.1 1.9 combine_part.1
  33.0 19.2 %all_to_all.30.parts_ref = bf16[16,16,1408]{2,1,0:T(8,128)(2,1)S(1)} all-to-all(bf16[16,16,1408]{2,1,0:T(8,128)(2,1)S(1)} %combine_part.1), channel_id=1, replica_groups=mesh['zl'=2,'y'=4,'c'=2,'x'=4,'zh'=2] {'zl','y','c'}, dimensions={0} | all-to-all | bytes 1441792 | tf_op jit(solution)/shard_map/all_to_all | solution.py:517
  52.3 0.0 copy-done.8
  52.3 0.3 sum_slots.1
  52.6 14.7 %all_to_all.31.whole_ref = bf16[16,16,1280]{2,1,0:T(8,128)(2,1)S(1)} all-to-all(bf16[16,16,1280]{2,1,0:T(8,128)(2,1)S(1)} %get-tuple-element.21), channel_id=1, replica_groups=mesh['zl'=2,'y'=4,'c'=2,'x'=4,'zh'=2] {'zl','y','c'}, dimensions={0} | all-to-all | bytes 1310720 | tf_op jit(solution)/shard_map/all_to_all | solution.py:521
  67.3 0.0 copy-done.6
  67.3 0.0 copy-done.7
  67.3 4.8 %experts_part.1 = (bf16[16,16,1280]{2,1,0:T(8,128)(2,1)S(1)}, bf16[8,16,192]{2,1,0:T(8,128)(2,1)S(1)}, bf16[8,16,192]{2,1,0:T(8,128)(2,1)S(1)}) custom-call(bf16[16,16,1280]{2,1,0:T(8,128)(2,1)S(1)} %all_to_all.31.whole_ref, bf16[8,192,1280]{2,1,0:T(8,128)(2,1)S(1)} %copy-done.6, bf16[8,192,1280]{2,1,0:T(8,128)(2,1)S(1)} %copy-done.7), custom_call_target="tpu_custom_call" | custom-call | flops 251658240 | bytes 7864320 | tf_op jit(solution)/shard_map/experts_part/pallas_call | solution.py:267
  72.1 14.6 %all_to_all.32.terms_ref = bf16[16,16,1280]{2,1,0:T(8,128)(2,1)S(1)} all-to-all(bf16[16,16,1280]{2,1,0:T(8,128)(2,1)S(1)} %get-tuple-element.22), channel_id=1, replica_groups=mesh['zl'=2,'y'=4,'c'=2,'x'=4,'zh'=2] {'zl','y','c'}, dimensions={0} | all-to-all | bytes 1310720 | tf_op jit(solution)/shard_map/all_to_all | solution.py:524
  86.7 1.9 sum_terms.1
  88.6 6.3 %all-to-all-start.4 = ((bf16[64,16,1408]{2,1,0:T(8,128)(2,1)}), bf16[64,16,1408]{2,1,0:T(8,128)(2,1)}, u32[]{:S(2)}, u32[]{:S(2)}) async-start(bf16[64,16,1408]{2,1,0:T(8,128)(2,1)} %sum_terms.1), calls=%async_computation.4 | async-start | bytes 5767168 | tf_op jit(solution)/shard_map/all_to_all | solution.py:526
  94.9 0.0 all-gather.2.cloned.1.call-start
  95.0 0.7 all-gather.2.cloned.1.call-update
  95.7 39.0 %all-to-all-done.4.mine_ref = bf16[64,16,1408]{2,1,0:T(8,128)(2,1)} async-done(((bf16[64,16,1408]{2,1,0:T(8,128)(2,1)}), bf16[64,16,1408]{2,1,0:T(8,128)(2,1)}, u32[]{:S(2)}, u32[]{:S(2)}) %all-to-all-start.4) | async-done | bytes 2883616 | tf_op jit(solution)/shard_map/all_to_all | solution.py:526
  134.7 2.3 collective-permute-start
  137.0 0.7 pad_add_fusion.place_ref
  137.7 5.7 %weight_grads.1 = (bf16[8,192,1280]{2,1,0:T(8,128)(2,1)}, bf16[8,192,1280]{2,1,0:T(8,128)(2,1)}) custom-call(bf16[16,16,1280]{2,1,0:T(8,128)(2,1)S(1)} %all_to_all.31.whole_ref, bf16[8,16,192]{2,1,0:T(8,128)(2,1)S(1)} %get-tuple-element.28.act_ref, bf16[8,16,192]{2,1,0:T(8,128)(2,1)S(1)} %get-tuple-element.29.pre_ref), custom_call_target="tpu_custom_call" | custom-call | flops 125829120 | bytes 7864320 | tf_op jit(solution)/shard_map/weight_grads/pallas_call | solution.py:306
  143.4 34.0 %all-gather.2.cloned.1.call-done = bf16[1024,1280]{0,1:T(8,128)(2,1)} async-done(((bf16[128,1280]{0,1:T(8,128)(2,1)}), bf16[1024,1280]{0,1:T(8,128)(2,1)}) %all-gather.2.cloned.1.call-update) | async-done | bytes 2621456 | tf_op jit(solution)/shard_map/all_gather | solution.py:512
  177.4 3.0 %copy.15.keys_ref = bf16[1024,1280]{1,0:T(8,128)(2,1)S(1)} copy(bf16[1024,1280]{0,1:T(8,128)(2,1)} %all-gather.2.cloned.1.call-done) | data formatting | bytes 5242880 | tf_op jit(solution)/shard_map/all_gather | solution.py:512
  180.4 0.0 copy-start.2
  180.4 2.5 %copy-done.2 = bf16[2048,1280]{1,0:T(8,128)(2,1)S(1)} copy-done((bf16[2048,1280]{1,0:T(8,128)(2,1)S(1)}, bf16[2048,1280]{1,0:T(8,128)(2,1)}, u32[]{:S(2)}) %copy-start.2) | copy-done | bytes 5242904
  182.9 7.7 %all_exps.1.exp_ref = f32[1024,2048]{1,0:T(8,128)S(1)} custom-call(bf16[1024,1280]{1,0:T(8,128)(2,1)S(1)} %copy.15.keys_ref, bf16[2048,1280]{1,0:T(8,128)(2,1)S(1)} %copy-done.2), custom_call_target="tpu_custom_call" | custom-call | flops 5368709120 | bytes 13631488 | tf_op jit(solution)/shard_map/all_exps/pallas_call | solution.py:358
  190.6 0.0 copy-start.9
  190.6 3.2 %copy-done.9 = f32[1024,2048]{1,0:T(8,128)} copy-done((f32[1024,2048]{1,0:T(8,128)}, f32[1024,2048]{1,0:T(8,128)S(1)}, u32[]{:S(2)}) %copy-start.9) | copy-done | bytes 8388632
  193.8 0.0 collective-permute-done.other_ref
  193.8 26.1 %logit_grads.1 = (bf16[1024,2048]{1,0:T(8,128)(2,1)}, bf16[1024,2048]{1,0:T(8,128)(2,1)}, bf16[1280,128]{1,0:T(8,128)(2,1)}) custom-call(s32[2]{0:T(128)} %pad_add_fusion.place_ref, f32[1024,2048]{1,0:T(8,128)} %copy-done.9, bf16[2048,1280]{1,0:T(8,128)(2,1)} %tokens_ref.7, bf16[2048,1280]{1,0:T(8,128)(2,1)} %grad_ref.3, f32[8,1,2048]{2,1,0:T(1,128)} %copy-done.8, ...), custom_call_target="tpu_custom_call" | custom-call | flops 10737418240 | bytes 27262976 | tf_op jit(solution)/shard_map/logit_grads/pallas_call | solution.py:438
  219.9 5.9 %all-to-all-start.5 = ((bf16[16,80,128]{2,1,0:T(8,128)(2,1)}), bf16[16,80,128]{2,1,0:T(8,128)(2,1)S(1)}, u32[]{:S(2)}, u32[]{:S(2)}) async-start(bf16[16,80,128]{2,1,0:T(8,128)(2,1)} %bitcast.12), calls=%async_computation.5 | async-start | bytes 655360 | tf_op jit(solution)/shard_map/all_to_all | solution.py:536
  225.9 1.0 dynamic-slice_bitcast_fusion.keys_ref
  226.9 1.9 dynamic-slice_select_fusion
  228.8 0.2 copy.14
  229.0 0.0 copy-start.4
  229.0 2.2 copy-done.4
  231.2 0.0 copy-start.5
  231.2 2.2 copy-done.5
  233.3 3.2 %token_grads.1 = bf16[2048,160]{1,0:T(8,128)(2,1)S(1)} custom-call(bf16[160,1024]{1,0:T(8,128)(2,1)S(1)} %dynamic-slice_bitcast_fusion.keys_ref, bf16[160,1024]{1,0:T(8,128)(2,1)S(1)} %bitcast.8, bf16[1024,2048]{1,0:T(8,128)(2,1)S(1)} %copy-done.4, bf16[1024,2048]{1,0:T(8,128)(2,1)S(1)} %copy-done.5), custom_call_target="tpu_custom_call" | custom-call | flops 1342177280 | bytes 8388608 | tf_op jit(solution)/shard_map/token_grads/pallas_call | solution.py:483
  236.5 1.2 copy.16
  237.7 0.0 all-to-all-done.5
  237.7 0.7 convert_reduce_fusion
Async XLA Ops:
  8.3 2.5 %copy-start = (bf16[2048,1280]{1,0:T(8,128)(2,1)S(1)}, bf16[2048,1280]{1,0:T(8,128)(2,1)}, u32[]{:S(2)}) copy-start(bf16[2048,1280]{1,0:T(8,128)(2,1)} %tokens_ref.7) | copy-start | bytes 15728644
  13.9 14.8 %all-to-all-start = ((f32[8,1,2048]{2,1,0:T(1,128)}), f32[8,1,2048]{2,1,0:T(1,128)S(1)}, u32[]{:S(2)}, u32[]{:S(2)}) async-start(f32[8,1,2048]{2,1,0:T(1,128)} %get-tuple-element.19), calls=%async_computation | async-start | bytes 131072 | tf_op jit(solution)/shard_map/all_to_all | solution.py:515
  22.0 2.5 %copy-start.1 = (bf16[2048,1280]{1,0:T(8,128)(2,1)S(1)}, bf16[2048,1280]{1,0:T(8,128)(2,1)}, u32[]{:S(2)}) copy-start(bf16[2048,1280]{1,0:T(8,128)(2,1)} %tokens_ref.7) | copy-start | bytes 15728644
  28.6 2.5 %copy-start.3 = (bf16[2048,1280]{1,0:T(8,128)(2,1)S(1)}, bf16[2048,1280]{1,0:T(8,128)(2,1)}, u32[]{:S(2)}) copy-start(bf16[2048,1280]{1,0:T(8,128)(2,1)} %grad_ref.3) | copy-start | bytes 15728644
  31.1 21.2 %copy-start.8 = (f32[8,1,2048]{2,1,0:T(1,128)}, f32[8,1,2048]{2,1,0:T(1,128)S(1)}, u32[]{:S(2)}) copy-start(f32[8,1,2048]{2,1,0:T(1,128)S(1)} %all-to-all-done.row_ref) | copy-start | bytes 196612
  31.1 36.2 %copy-start.6 = (bf16[8,192,1280]{2,1,0:T(8,128)(2,1)S(1)}, bf16[8,192,1280]{2,1,0:T(8,128)(2,1)}, u32[]{:S(2)}) copy-start(bf16[8,192,1280]{2,1,0:T(8,128)(2,1)} %w_in_ref.1) | copy-start | bytes 11796484
  31.1 36.2 %copy-start.7 = (bf16[8,192,1280]{2,1,0:T(8,128)(2,1)S(1)}, bf16[8,192,1280]{2,1,0:T(8,128)(2,1)}, u32[]{:S(2)}) copy-start(bf16[8,192,1280]{2,1,0:T(8,128)(2,1)} %w_out_ref.1) | copy-start | bytes 11796484
  88.6 46.1 %all-to-all-start.4 = ((bf16[64,16,1408]{2,1,0:T(8,128)(2,1)}), bf16[64,16,1408]{2,1,0:T(8,128)(2,1)}, u32[]{:S(2)}, u32[]{:S(2)}) async-start(bf16[64,16,1408]{2,1,0:T(8,128)(2,1)} %sum_terms.1), calls=%async_computation.4 | async-start | bytes 5767168 | tf_op jit(solution)/shard_map/all_to_all | solution.py:526
  94.9 82.5 %all-gather.2.cloned.1.call-start = ((), (), s32[]{:S(2)}) async-start(), calls=%async_computation.6 | async-start | bytes 2949120 | tf_op jit(solution)/shard_map/all_gather | solution.py:512
  134.7 59.1 %collective-permute-start = (bf16[64,16,1408]{2,1,0:T(8,128)(2,1)}, bf16[64,16,1408]{2,1,0:T(8,128)(2,1)}, u32[]{:S(2)}, u32[]{:S(2)}) collective-permute-start(bf16[64,16,1408]{2,1,0:T(8,128)(2,1)} %all-to-all-done.4.mine_ref), channel_id=1, source_target_pairs={{0,8},{8,0},{1,9},{9,1},{2,10},{10,2},{3,11},{11,3},{4,12},{12,4},... | collective-permute-start | bytes 8650760 | tf_op jit(solution)/shard_map/ppermute | solution.py:529
  180.4 2.5 %copy-start.2 = (bf16[2048,1280]{1,0:T(8,128)(2,1)S(1)}, bf16[2048,1280]{1,0:T(8,128)(2,1)}, u32[]{:S(2)}) copy-start(bf16[2048,1280]{1,0:T(8,128)(2,1)} %tokens_ref.7) | copy-start | bytes 15728644
  190.6 3.3 %copy-start.9 = (f32[1024,2048]{1,0:T(8,128)}, f32[1024,2048]{1,0:T(8,128)S(1)}, u32[]{:S(2)}) copy-start(f32[1024,2048]{1,0:T(8,128)S(1)} %all_exps.1.exp_ref) | copy-start | bytes 25165828
  219.9 17.8 %all-to-all-start.5 = ((bf16[16,80,128]{2,1,0:T(8,128)(2,1)}), bf16[16,80,128]{2,1,0:T(8,128)(2,1)S(1)}, u32[]{:S(2)}, u32[]{:S(2)}) async-start(bf16[16,80,128]{2,1,0:T(8,128)(2,1)} %bitcast.12), calls=%async_computation.5 | async-start | bytes 655360 | tf_op jit(solution)/shard_map/all_to_all | solution.py:536
  229.0 2.2 copy-start.4
  231.2 2.2 copy-start.5
Sparse Core Ops, SparseCore 0:
  97.9 79.4 all-gather.1

commit v3 on v2

--- a/solution.py
+++ b/solution.py
@@ -12,7 +12,7 @@
 
 SEQ = ("zl", "y", "c")
 SLOT = ("x", "zh")
-SAME_CORE = ("x", "zh", "zl", "y")
+GATHERED = ("x", "zl", "y")
 f32 = jnp.float32
 bf16 = jnp.bfloat16
 LANES = 128
@@ -370,23 +370,78 @@
     )(keys_t, tokens)
 
 
-def logit_grads(place, exps, tokens, out_grad, row_parts, mine, other, own_slots, tile=256):
+def whole_block(shape):
+    return pl.BlockSpec(shape, lambda i: (0,) * len(shape), pipeline_mode=pl.Buffered(1))
+
+
+def width_dot(place_ref, mine_ref, other_ref, ref, at):
+    blocks, block, width = mine_ref.shape
+    half = ref.shape[1] // 2
+    core = place_ref[0]
+    here = pl.multiple_of(core * half, LANES)
+    there = pl.multiple_of((1 - core) * half, LANES)
+    near = lax.dot_general(
+        mine_ref[:, :, at * half : (at + 1) * half].reshape(blocks * block, half),
+        ref[:, pl.ds(here, half)],
+        cols_contract,
+        preferred_element_type=f32,
+    )
+    far = lax.dot_general(
+        other_ref[:, :, at * half : (at + 1) * half].reshape(blocks * block, half),
+        ref[:, pl.ds(there, half)],
+        cols_contract,
+        preferred_element_type=f32,
+    )
+    return near + far
+
+
+def comb_dots(place, exps, out_grad, row_parts, mine, other, tile=512):
+    slots, count = exps.shape
+    features = out_grad.shape[1]
+    copies = row_parts.shape[0]
+
+    def kernel(place_ref, exp_ref, grad_ref, row_ref, mine_ref, other_ref, dot_ref, sum_ref):
+        power, inverse = guarded(jnp.sum(row_ref[...], axis=0))
+        dots = width_dot(place_ref, mine_ref, other_ref, grad_ref, 0)
+        dot_ref[...] = dots
+        combine = (exp_ref[...] * power) * inverse
+        sum_ref[...] = jnp.sum(combine * dots, axis=0, keepdims=True)
+
+    return pl.pallas_call(
+        kernel,
+        grid=(count // tile,),
+        in_specs=[
+            pl.BlockSpec(memory_space=pltpu.SMEM),
+            pl.BlockSpec((slots, tile), lambda i: (0, i)),
+            pl.BlockSpec((tile, features), lambda i: (i, 0)),
+            pl.BlockSpec((copies, 1, tile), lambda i: (0, 0, i)),
+            whole_block(mine.shape),
+            whole_block(other.shape),
+        ],
+        out_specs=[
+            pl.BlockSpec((slots, tile), lambda i: (0, i)),
+            pl.BlockSpec((1, tile), lambda i: (0, i)),
+        ],
+        out_shape=[
+            jax.ShapeDtypeStruct((slots, count), f32),
+            jax.ShapeDtypeStruct((1, count), f32),
+        ],
+        compiler_params=params(24),
+        cost_estimate=cost(2 * slots * features * count, 2 * features * count),
+        name="comb_dots",
+    )(place, exps, out_grad, row_parts, mine, other)
+
+
+def disp_dots(place, exps, dots, tokens, row_parts, mine, other, tile=512):
     slots, count = exps.shape
     features = tokens.shape[1]
-    half = features // 2
-    blocks, block, width = mine.shape
     copies = row_parts.shape[0]
 
     def kernel(
-        place_ref, exp_ref, tokens_ref, grad_ref, row_ref, mine_ref, other_ref,
-        logit_ref, dispatch_ref, keys_ref, power_ref, inverse_ref, total_ref, sum_ref,
+        place_ref, exp_ref, dot_ref, tokens_ref, row_ref, mine_ref, other_ref,
+        terms_ref, dispatch_ref, power_ref, inverse_ref, total_ref,
     ):
-        core = place_ref[0]
-        here = pl.multiple_of(core * half, LANES)
-        there = pl.multiple_of((1 - core) * half, LANES)
-        step = pl.program_id(0)
-
-        @pl.when(step == 0)
+        @pl.when(pl.program_id(0) == 0)
         def _():
             lanes = mine_ref[:, :, features:].reshape(slots, LANES).astype(f32)
             apart = other_ref[:, :, features:].reshape(slots, LANES).astype(f32)
@@ -395,121 +450,160 @@
             inverse_ref[...] = jnp.broadcast_to(lanes[:, 0:1] + lanes[:, 1:2], (slots, tile))
             total_ref[...] = jnp.broadcast_to(inner, (slots, tile))
 
-        def dot(at, ref):
-            near = lax.dot_general(
-                mine_ref[:, :, at * half : (at + 1) * half].reshape(slots, half),
-                ref[:, pl.ds(here, half)],
-                cols_contract,
-                preferred_element_type=f32,
-            )
-            far = lax.dot_general(
-                other_ref[:, :, at * half : (at + 1) * half].reshape(slots, half),
-                ref[:, pl.ds(there, half)],
-                cols_contract,
-                preferred_element_type=f32,
-            )
-            return near + far
-
         power, inverse = guarded(jnp.sum(row_ref[...], axis=0))
-        exps_here = exp_ref[...]
-        combine = (exps_here * power) * inverse
-        comb_dot = dot(0, grad_ref)
-        comb_row = jnp.sum(combine * comb_dot, axis=0, keepdims=True)
-        dispatch = (exps_here * power_ref[...]) * inverse_ref[...]
-        disp_dot = dot(1, tokens_ref)
-        logit = combine * (comb_dot - comb_row) + dispatch * (disp_dot - total_ref[...])
-        logit_ref[...] = logit.astype(bf16)
+        here = exp_ref[...]
+        dispatch = (here * power_ref[...]) * inverse_ref[...]
         dispatch_ref[...] = dispatch.astype(bf16)
+        disp_dot = width_dot(place_ref, mine_ref, other_ref, tokens_ref, 1)
+        combine = (here * power) * inverse
+        terms_ref[...] = combine * dot_ref[...] + dispatch * (disp_dot - total_ref[...])
+
+    return pl.pallas_call(
+        kernel,
+        grid=(count // tile,),
+        in_specs=[
+            pl.BlockSpec(memory_space=pltpu.SMEM),
+            pl.BlockSpec((slots, tile), lambda i: (0, i)),
+            pl.BlockSpec((slots, tile), lambda i: (0, i)),
+            pl.BlockSpec((tile, features), lambda i: (i, 0)),
+            pl.BlockSpec((copies, 1, tile), lambda i: (0, 0, i)),
+            whole_block(mine.shape),
+            whole_block(other.shape),
+        ],
+        out_specs=[
+            pl.BlockSpec((slots, tile), lambda i: (0, i)),
+            pl.BlockSpec((slots, tile), lambda i: (0, i)),
+        ],
+        out_shape=[
+            jax.ShapeDtypeStruct((slots, count), f32),
+            jax.ShapeDtypeStruct((slots, count), bf16),
+        ],
+        scratch_shapes=[pltpu.VMEM((slots, tile), f32)] * 3,
+        compiler_params=params(24),
+        cost_estimate=cost(2 * slots * features * count, 2 * features * count),
+        name="disp_dots",
+    )(place, exps, dots, tokens, row_parts, mine, other)
+
+
+def logit_grads(place, exps, terms, dispatch, tokens, row_parts, row, row_other, rows_other, own_slots, tile=512):
+    slots, count = exps.shape
+    features = tokens.shape[1]
+    copies = row_parts.shape[0]
+    width = rows_other.shape[0]
+
+    def kernel(
+        place_ref, exp_ref, terms_ref, dispatch_ref, tokens_ref, row_ref, sum_ref, other_ref, rows_ref,
+        logit_ref, keys_ref, sent_ref, total_ref,
+    ):
+        step = pl.program_id(0)
+        power, inverse = guarded(jnp.sum(row_ref[...], axis=0))
+        weight = (sum_ref[...] + other_ref[...]) * inverse
+        logit_ref[...] = (terms_ref[...] - (exp_ref[...] * power) * weight).astype(bf16)
         own = logit_ref[pl.ds(pl.multiple_of(place_ref[1] * own_slots, own_slots), own_slots), :]
         term = jnp.dot(own, tokens_ref[...], preferred_element_type=f32)
 
         @pl.when(step == 0)
         def _():
-            sum_ref[...] = term
+            total_ref[...] = term
 
         @pl.when(step > 0)
         def _():
-            sum_ref[...] += term
+            total_ref[...] += term
 
         @pl.when(step == pl.num_programs(0) - 1)
         def _():
-            keys_ref[...] = sum_ref[...].T.astype(bf16)
-
-    return pl.pallas_call(
-        kernel,
-        grid_spec=pltpu.PrefetchScalarGridSpec(
-            num_scalar_prefetch=1,
-            grid=(count // tile,),
-            in_specs=[
-                pl.BlockSpec((slots, tile), lambda i, place: (0, i)),
-                pl.BlockSpec((tile, features), lambda i, place: (i, 0)),
-                pl.BlockSpec((tile, features), lambda i, place: (i, 0)),
-                pl.BlockSpec((copies, 1, tile), lambda i, place: (0, 0, i)),
-                pl.BlockSpec((blocks, block, width), lambda i, place: (0, 0, 0)),
-                pl.BlockSpec((blocks, block, width), lambda i, place: (0, 0, 0)),
-            ],
-            out_specs=[
-                pl.BlockSpec((slots, tile), lambda i, place: (0, i)),
-                pl.BlockSpec((slots, tile), lambda i, place: (0, i)),
-                pl.BlockSpec((features, own_slots), lambda i, place: (0, 0)),
-            ],
-            scratch_shapes=[
-                pltpu.VMEM((slots, tile), f32),
-                pltpu.VMEM((slots, tile), f32),
-                pltpu.VMEM((slots, tile), f32),
-                pltpu.VMEM((own_slots, features), f32),
-            ],
-        ),
+            keys_ref[...] = total_ref[...].T.astype(bf16)
+
+        sent = jnp.dot(rows_ref[:, :slots], logit_ref[...], preferred_element_type=f32)
+        sent = sent + jnp.dot(rows_ref[:, slots:], dispatch_ref[...], preferred_element_type=f32)
+        sent_ref[...] = sent.astype(bf16)
+
+    return pl.pallas_call(
+        kernel,
+        grid=(count // tile,),
+        in_specs=[
+            pl.BlockSpec(memory_space=pltpu.SMEM),
+            pl.BlockSpec((slots, tile), lambda i: (0, i)),
+            pl.BlockSpec((slots, tile), lambda i: (0, i)),
+            pl.BlockSpec((slots, tile), lambda i: (0, i)),
+            pl.BlockSpec((tile, features), lambda i: (i, 0)),
+            pl.BlockSpec((copies, 1, tile), lambda i: (0, 0, i)),
+            pl.BlockSpec((1, tile), lambda i: (0, i)),
+            pl.BlockSpec((1, tile), lambda i: (0, i)),
+            whole_block(rows_other.shape),
+        ],
+        out_specs=[
+            pl.BlockSpec((slots, tile), lambda i: (0, i)),
+            pl.BlockSpec((features, own_slots), lambda i: (0, 0)),
+            pl.BlockSpec((width, tile), lambda i: (0, i)),
+        ],
         out_shape=[
             jax.ShapeDtypeStruct((slots, count), bf16),
-            jax.ShapeDtypeStruct((slots, count), bf16),
             jax.ShapeDtypeStruct((features, own_slots), bf16),
-        ],
-        compiler_params=params(56),
-        cost_estimate=cost(4 * slots * features * count, 4 * features * count + 8 * slots * count),
+            jax.ShapeDtypeStruct((width, count), bf16),
+        ],
+        scratch_shapes=[pltpu.VMEM((own_slots, features), f32)],
+        compiler_params=params(24),
+        cost_estimate=cost(2 * own_slots * features * count, 2 * features * count),
         name="logit_grads",
-    )(place, exps, tokens, out_grad, row_parts, mine, other)
-
-
-def token_grads(keys_rows, in_grad_rows, logit_grad, dispatch, tile=512):
-    width, slots = keys_rows.shape
-    count = logit_grad.shape[1]
-
-    def kernel(keys_ref, in_ref, logit_ref, dispatch_ref, out_ref):
-        total = jnp.dot(keys_ref[...], logit_ref[...], preferred_element_type=f32)
-        total = total + jnp.dot(in_ref[...], dispatch_ref[...], preferred_element_type=f32)
-        out_ref[...] = total.T.astype(bf16)
-
-    return pl.pallas_call(
-        kernel,
-        grid=(count // tile,),
-        in_specs=[
-            pl.BlockSpec((width, slots), lambda i: (0, 0)),
-            pl.BlockSpec((width, slots), lambda i: (0, 0)),
-            pl.BlockSpec((slots, tile), lambda i: (0, i)),
-            pl.BlockSpec((slots, tile), lambda i: (0, i)),
-        ],
-        out_specs=pl.BlockSpec((tile, width), lambda i: (i, 0)),
-        out_shape=jax.ShapeDtypeStruct((count, width), bf16),
-        compiler_params=params(32),
+    )(place, exps, terms, dispatch, tokens, row_parts, row, row_other, rows_other)
+
+
+def token_grads(rows, logit_grad, dispatch, tile=512):
+    slots, count = logit_grad.shape
+    width = rows.shape[0]
+
+    def kernel(rows_ref, logit_ref, dispatch_ref, out_ref):
+        total = jnp.dot(rows_ref[:, :slots], logit_ref[...], preferred_element_type=f32)
+        out_ref[...] = total + jnp.dot(
+            rows_ref[:, slots:], dispatch_ref[...], preferred_element_type=f32
+        )
+
+    return pl.pallas_call(
+        kernel,
+        grid=(count // tile,),
+        in_specs=[
+            whole_block(rows.shape),
+            pl.BlockSpec((slots, tile), lambda i: (0, i)),
+            pl.BlockSpec((slots, tile), lambda i: (0, i)),
+        ],
+        out_specs=pl.BlockSpec((width, tile), lambda i: (0, i)),
+        out_shape=jax.ShapeDtypeStruct((width, count), f32),
+        compiler_params=params(24),
         cost_estimate=cost(4 * slots * width * count, 4 * slots * count),
         name="token_grads",
-    )(keys_rows, in_grad_rows, logit_grad, dispatch)
+    )(rows, logit_grad, dispatch)
+
+
+def transposed(keys):
+    def kernel(keys_ref, out_ref):
+        out_ref[...] = keys_ref[...].T
+
+    return pl.pallas_call(
+        kernel,
+        in_specs=[whole_in_vmem()],
+        out_specs=whole_in_vmem(),
+        out_shape=jax.ShapeDtypeStruct(keys.shape[::-1], keys.dtype),
+        compiler_params=params(24),
+        name="transposed",
+    )(keys)
 
 
 def per_device(tokens, slot_keys, w_in, w_out, out_grad):
     features = tokens.shape[1]
     own_slots = slot_keys.shape[1]
     core = lax.axis_index("c")
-    slot_at = lax.axis_index(SLOT)
+    column_at = lax.axis_index("x")
+    pair_at = lax.axis_index("zh")
     half = features // 2
     slot_devices = lax.axis_size(SLOT)
     seq_devices = lax.axis_size(SEQ)
     groups = seq_devices // 2
-    everyone = slot_devices * groups
-
-    keys_t = slot_keys.T
-    keys_all = lax.all_gather(keys_t, SLOT, axis=0, tiled=True)
+    everyone = lax.axis_size(GATHERED)
+    swap = [(0, 1), (1, 0)]
+
+    keys_t = transposed(slot_keys)
+    keys_all = lax.all_gather(keys_t, "x", axis=0, tiled=True)
 
     exps, own_row, column = own_logits(keys_t, tokens, slot_devices)
     row_parts = lax.all_to_all(own_row, SLOT, 0, 0)
@@ -521,34 +615,45 @@
     whole = lax.all_to_all(sent, SEQ, 0, 0)
 
     sent, act, pre = experts_part(whole, w_in, w_out)
+    sent, keys_all = lax.optimization_barrier((sent, keys_all))
     terms = lax.all_to_all(sent, SEQ, 0, 0)
+    all_exp = all_exps(keys_all, tokens)
+    terms, all_exp, act, pre = lax.optimization_barrier((terms, all_exp, act, pre))
+    sent = sum_terms(terms, slot_in, column_total, everyone)
+    mine = lax.all_to_all(sent, GATHERED, 0, 0)
     grad_w_in, grad_w_out = weight_grads(whole, act, pre, w_in.shape)
-    mine = lax.all_to_all(
-        sum_terms(terms, slot_in, column_total, everyone), SAME_CORE, 0, 0
-    )
-    other = lax.ppermute(mine, "c", [(0, 1), (1, 0)])
-
-    all_exp = all_exps(keys_all, tokens)
-    place = jnp.stack([core, slot_at]).astype(jnp.int32)
-    logit_grad, dispatch, keys_part = logit_grads(
-        place, all_exp, tokens, out_grad, row_parts, mine, other, own_slots
-    )
+    mine, grad_w_in, grad_w_out = lax.optimization_barrier((mine, grad_w_in, grad_w_out))
+    other = lax.ppermute(mine, "c", swap)
+
+    place = jnp.stack([core, column_at]).astype(jnp.int32)
+    dots, row = comb_dots(place, all_exp, out_grad, row_parts, mine, other)
+    row_other = lax.ppermute(row, "zh", swap)
+    terms, dispatch = disp_dots(place, all_exp, dots, tokens, row_parts, mine, other)
+
+    width = features // slot_devices
+    pair = 2 * width
+    keys_cols = lax.dynamic_slice_in_dim(keys_all, column_at * pair, pair, 1)
+    side = (column_at * pair) // half
+    at = half + column_at * pair - side * half
+    in_grad_cols = jnp.where(
+        side == core,
+        lax.dynamic_slice_in_dim(mine, at, pair, 2),
+        lax.dynamic_slice_in_dim(other, at, pair, 2),
+    ).reshape(-1, pair)
+    pair_rows = jnp.concatenate([keys_cols.T, in_grad_cols.T], axis=1)
+    rows_own = lax.dynamic_slice_in_dim(pair_rows, pair_at * width, width, 0)
+    rows_other = lax.dynamic_slice_in_dim(pair_rows, (1 - pair_at) * width, width, 0)
+
+    logit_grad, keys_part, sent = logit_grads(
+        place, all_exp, terms, dispatch, tokens, row_parts, row, row_other, rows_other, own_slots
+    )
+    received = lax.ppermute(sent, "zh", swap)
     keys_parts = lax.all_to_all(
         keys_part.reshape(seq_devices, features // seq_devices, own_slots), SEQ, 0, 0
     )
     grad_keys = jnp.sum(keys_parts.astype(f32), axis=0)
-
-    width = features // slot_devices
-    keys_rows = lax.dynamic_slice_in_dim(keys_all, slot_at * width, width, 1).T
-    side = (slot_at * width) // half
-    at = half + slot_at * width - side * half
-    in_grad_cols = jnp.where(
-        side == core,
-        lax.dynamic_slice_in_dim(mine, at, width, 2),
-        lax.dynamic_slice_in_dim(other, at, width, 2),
-    )
-    in_grad_rows = in_grad_cols.reshape(-1, width).T
-    grad_tokens = token_grads(keys_rows, in_grad_rows, logit_grad, dispatch)
+    own_grads = token_grads(rows_own, logit_grad, dispatch)
+    grad_tokens = (own_grads + received.astype(f32)).astype(bf16).T
     return (grad_tokens, grad_keys, grad_w_in, grad_w_out)
 
 

time: 246 us -> 182 us (0.74)
  waiting for transfers between devices: 75.8 us -> 28.5 us
  blocking collectives: 48.6 us -> 34 us
  Pallas kernels: 56.6 us -> 45 us
  starting transfers between devices: 22.8 us -> 27.7 us
  other arithmetic: 3.25 us -> 6.02 us
    all_gather x1, waiting for transfers between devices: 34 us -> 0.01 us  [per_device(): keys_all = lax.all_gather(keys_t, 'x', axis=0, tiled=True)]
    all_to_all x1 -> x2, waiting for transfers between devices: 39 us -> 14.6 us  [the longest x1 13.8 us: per_device(): mine = lax.all_to_all(sent, GATHERED, 0, 0)]
    all_to_all x1 -> x0, blocking collectives: 14.6 us -> none  [per_device(): terms = lax.all_to_all(sent, SEQ, 0, 0)]
    all_to_all x1, waiting for transfers between devices: 0.01 us -> 10.6 us  [per_device(): lax.all_to_all(keys_part.reshape(seq_devices, features // seq_devices, ow...]
    pallas_call x2 -> x5, Pallas kernels: 29.2 us -> 21.6 us  [the longest x1 7.23 us: disp_dots(): pl.pallas_call(kernel, grid=(count // tile,), in_specs=[pl.BlockSpec(memo...]
    all_to_all x1 -> x2, starting transfers between devices: 6.3 us -> 9.6 us  [the longest x1 5.77 us: per_device(): mine = lax.all_to_all(sent, GATHERED, 0, 0)]
    pallas_call x1, Pallas kernels: 7.68 us -> 4.66 us  [all_exps(): pl.pallas_call(kernel, grid=(count // tile,), in_specs=[pl.BlockSpec((slo...]
    all_gather x1 -> x0, local copies, waits for them, and re-layouts: 2.98 us -> none  [per_device(): keys_all = lax.all_gather(keys_t, SLOT, axis=0, tiled=True)]
  transfers between devices with their start and end apart: 5 -> 8, of which waited for: 3 -> 5; matrix products, arithmetic and copies ran while one was open for 3% -> 3% of each run, Pallas kernels for 8% -> 18%
where the time goes in v3:
time: 182 us; the launch traced here: 181 us
  Pallas kernels  45 us (25%)
  blocking collectives  34 us (19%)
  waiting for transfers between devices  28.5 us (16%)
  starting transfers between devices  27.7 us (15%)
  local copies, waits for them, and re-layouts  25.8 us (14%)
  between operations  14.2 us (8%)
  other arithmetic  6.02 us (3%)
    unnamed x36, local copies, waits for them, and re-layouts  21.5 us
    all_to_all x1, blocking collectives, per_device(): lax.all_to_all(combine_part(exps, row_parts, column, slot_in_part, out_gr...  19.3 us
    all_to_all x1, blocking collectives, per_device(): whole = lax.all_to_all(sent, SEQ, 0, 0)  14.7 us
    all_to_all x1, waiting for transfers between devices, per_device(): mine = lax.all_to_all(sent, GATHERED, 0, 0)  13.8 us
    all_to_all x1, waiting for transfers between devices, per_device(): lax.all_to_all(keys_part.reshape(seq_devices, features // seq_devices, ow...  10.6 us
    all_to_all x1, starting transfers between devices, per_device(): row_parts = lax.all_to_all(own_row, SLOT, 0, 0)  8.17 us
    pallas_call x1, Pallas kernels, disp_dots(): pl.pallas_call(kernel, grid=(count // tile,), in_specs=[pl.BlockSpec(memo...  7.23 us
    pallas_call x1, Pallas kernels, logit_grads(): pl.pallas_call(kernel, grid=(count // tile,), in_specs=[pl.BlockSpec(memo...  6.25 us
  transfers between devices with their start and end apart: 8, of which 5 were waited for; matrix products, arithmetic and copies ran while one was open for 3% of the time, Pallas kernels for 18%

profile of v3, /device:TPU:1, one launch (start us, length us, event | category | flops | bytes accessed | tf_op | source)
XLA Modules:
  0.0 181.3 jit_solution(8304759005423228740)
XLA Ops:
  7.2 0.0 all-gather.2.cloned.1.call-start
  7.2 0.0 copy-start.13
  7.2 1.0 copy-done.13
  8.2 0.1 transposed.1.keys_ref
  8.3 0.9 copy.12
  9.2 0.0 all-gather.2.cloned.1.call-update
  9.2 0.0 copy-start
  9.3 2.5 %copy-done = bf16[2048,1280]{1,0:T(8,128)(2,1)S(1)} copy-done((bf16[2048,1280]{1,0:T(8,128)(2,1)S(1)}, bf16[2048,1280]{1,0:T(8,128)(2,1)}, u32[]{:S(2)}) %copy-start) | copy-done | bytes 5242904
  11.7 3.1 %own_logits.1 = (f32[128,2048]{1,0:T(8,128)S(1)}, f32[8,1,2048]{2,1,0:T(1,128)}, f32[128,128]{1,0:T(8,128)S(1)}) custom-call(bf16[128,1280]{1,0:T(8,128)(2,1)S(1)} %transposed.1.keys_ref, bf16[2048,1280]{1,0:T(8,128)(2,1)S(1)} %copy-done), custom_call_target="tpu_custom_call" | custom-call | flops 671088640 | bytes 6291456 | tf_op jit(solution)/shard_map/own_logits/pallas_call | solution.py:91
  14.8 8.2 %all-to-all-start = ((f32[8,1,2048]{2,1,0:T(1,128)}), f32[8,1,2048]{2,1,0:T(1,128)S(1)}, u32[]{:S(2)}, u32[]{:S(2)}) async-start(f32[8,1,2048]{2,1,0:T(1,128)} %get-tuple-element.32), calls=%async_computation | async-start | bytes 131072 | tf_op jit(solution)/shard_map/all_to_all | solution.py:609
  23.0 2.6 %copy-done.1 = bf16[2048,1280]{1,0:T(8,128)(2,1)S(1)} copy-done((bf16[2048,1280]{1,0:T(8,128)(2,1)S(1)}, bf16[2048,1280]{1,0:T(8,128)(2,1)}, u32[]{:S(2)}) %copy-start.1) | copy-done | bytes 5242904
  25.5 2.0 %dispatch_part.1.in_ref = bf16[128,1280]{1,0:T(8,128)(2,1)S(1)} custom-call(f32[128,2048]{1,0:T(8,128)S(1)} %get-tuple-element.31.exp_ref, f32[128,128]{1,0:T(8,128)S(1)} %get-tuple-element.33.column_ref, bf16[2048,1280]{1,0:T(8,128)(2,1)S(1)} %copy-done.1), custom_call_target="tpu_custom_call" | custom-call | flops 671088640 | bytes 6291456 | tf_op jit(solution)/shard_map/dispatch_part/pallas_call | solution.py:136
  27.6 2.1 %all-to-all-done.row_ref = f32[8,1,2048]{2,1,0:T(1,128)S(1)} async-done(((f32[8,1,2048]{2,1,0:T(1,128)}), f32[8,1,2048]{2,1,0:T(1,128)S(1)}, u32[]{:S(2)}, u32[]{:S(2)}) %all-to-all-start) | async-done | bytes 65568 | tf_op jit(solution)/shard_map/all_to_all | solution.py:609
  29.7 2.5 %copy-done.5 = bf16[2048,1280]{1,0:T(8,128)(2,1)S(1)} copy-done((bf16[2048,1280]{1,0:T(8,128)(2,1)S(1)}, bf16[2048,1280]{1,0:T(8,128)(2,1)}, u32[]{:S(2)}) %copy-start.5) | copy-done | bytes 5242904
  32.2 1.9 %combine_part.1 = bf16[16,16,1408]{2,1,0:T(8,128)(2,1)S(1)} custom-call(f32[128,2048]{1,0:T(8,128)S(1)} %get-tuple-element.31.exp_ref, f32[8,1,2048]{2,1,0:T(1,128)S(1)} %all-to-all-done.row_ref, f32[128,128]{1,0:T(8,128)S(1)} %get-tuple-element.33.column_ref, bf16[128,1280]{1,0:T(8,128)(2,1)S(1)} %dispatch_part.1.in_ref, bf16[2048,1280]{1,0:T(8,128)(2,1)S(1)} %copy-done.5), custom_call_target="tpu_custom_call" | custom-call | flops 671088640 | bytes 6291456 | tf_op jit(solution)/shard_map/combine_part/pallas_call | solution.py:189
  34.1 19.3 %all_to_all.30.parts_ref = bf16[16,16,1408]{2,1,0:T(8,128)(2,1)S(1)} all-to-all(bf16[16,16,1408]{2,1,0:T(8,128)(2,1)S(1)} %combine_part.1), channel_id=1, replica_groups=mesh['zl'=2,'y'=4,'c'=2,'x'=4,'zh'=2] {'zl','y','c'}, dimensions={0} | all-to-all | bytes 1441792 | tf_op jit(solution)/shard_map/all_to_all | solution.py:611
  53.4 0.3 sum_slots.1
  53.7 14.7 %all_to_all.31.whole_ref = bf16[16,16,1280]{2,1,0:T(8,128)(2,1)S(1)} all-to-all(bf16[16,16,1280]{2,1,0:T(8,128)(2,1)S(1)} %get-tuple-element.34), channel_id=1, replica_groups=mesh['zl'=2,'y'=4,'c'=2,'x'=4,'zh'=2] {'zl','y','c'}, dimensions={0} | all-to-all | bytes 1310720 | tf_op jit(solution)/shard_map/all_to_all | solution.py:615
  68.4 0.0 copy-done.10
  68.4 0.0 copy-done.11
  68.4 5.5 %experts_part.1 = (bf16[16,16,1280]{2,1,0:T(8,128)(2,1)}, bf16[8,16,192]{2,1,0:T(8,128)(2,1)S(1)}, bf16[8,16,192]{2,1,0:T(8,128)(2,1)S(1)}) custom-call(bf16[16,16,1280]{2,1,0:T(8,128)(2,1)S(1)} %all_to_all.31.whole_ref, bf16[8,192,1280]{2,1,0:T(8,128)(2,1)S(1)} %copy-done.10, bf16[8,192,1280]{2,1,0:T(8,128)(2,1)S(1)} %copy-done.11), custom_call_target="tpu_custom_call" | custom-call | flops 251658240 | bytes 7864320 | tf_op jit(solution)/shard_map/experts_part/pallas_call | solution.py:267
  74.0 3.8 %all-to-all-start.3 = ((bf16[16,16,1280]{2,1,0:T(8,128)(2,1)}), bf16[16,16,1280]{2,1,0:T(8,128)(2,1)S(1)}, u32[]{:S(2)}, u32[]{:S(2)}) async-start(bf16[16,16,1280]{2,1,0:T(8,128)(2,1)} %get-tuple-element.37), calls=%async_computation.3 | async-start | bytes 1310720 | tf_op jit(solution)/shard_map/all_to_all | solution.py:619
  77.8 1.6 copy.13.keys_ref
  79.4 0.0 copy-start.2
  79.4 2.5 %copy-done.2 = bf16[2048,1280]{1,0:T(8,128)(2,1)S(1)} copy-done((bf16[2048,1280]{1,0:T(8,128)(2,1)S(1)}, bf16[2048,1280]{1,0:T(8,128)(2,1)}, u32[]{:S(2)}) %copy-start.2) | copy-done | bytes 5242904
  81.9 4.7 %all_exps.1.exp_ref = f32[512,2048]{1,0:T(8,128)S(1)} custom-call(bf16[512,1280]{1,0:T(8,128)(2,1)S(1)} %copy.13.keys_ref, bf16[2048,1280]{1,0:T(8,128)(2,1)S(1)} %copy-done.2), custom_call_target="tpu_custom_call" | custom-call | flops 2684354560 | bytes 9437184 | tf_op jit(solution)/shard_map/all_exps/pallas_call | solution.py:358
  86.6 0.0 copy-start.3
  86.6 2.0 %copy-done.3 = f32[512,2048]{1,0:T(8,128)} copy-done((f32[512,2048]{1,0:T(8,128)}, f32[512,2048]{1,0:T(8,128)S(1)}, u32[]{:S(2)}) %copy-start.3) | copy-done | bytes 4194328
  88.6 0.8 all-to-all-done.3.terms_ref
  89.4 0.2 sum_terms.1
  89.5 0.0 copy-start.9
  89.6 1.1 copy-done.9
  90.7 5.8 %all-to-all-start.4 = ((bf16[32,16,1408]{2,1,0:T(8,128)(2,1)}), bf16[32,16,1408]{2,1,0:T(8,128)(2,1)S(1)}, u32[]{:S(2)}, u32[]{:S(2)}) async-start(bf16[32,16,1408]{2,1,0:T(8,128)(2,1)} %copy-done.9), calls=%async_computation.4 | async-start | bytes 2883584 | tf_op jit(solution)/shard_map/all_to_all | solution.py:623
  96.5 5.8 %weight_grads.1 = (bf16[8,192,1280]{2,1,0:T(8,128)(2,1)}, bf16[8,192,1280]{2,1,0:T(8,128)(2,1)}) custom-call(bf16[16,16,1280]{2,1,0:T(8,128)(2,1)S(1)} %all_to_all.31.whole_ref, bf16[8,16,192]{2,1,0:T(8,128)(2,1)S(1)} %get-tuple-element.43.act_ref, bf16[8,16,192]{2,1,0:T(8,128)(2,1)S(1)} %get-tuple-element.44.pre_ref), custom_call_target="tpu_custom_call" | custom-call | flops 125829120 | bytes 7864320 | tf_op jit(solution)/shard_map/weight_grads/pallas_call | solution.py:306
  102.2 13.8 %all-to-all-done.4.mine_ref = bf16[32,16,1408]{2,1,0:T(8,128)(2,1)S(1)} async-done(((bf16[32,16,1408]{2,1,0:T(8,128)(2,1)}), bf16[32,16,1408]{2,1,0:T(8,128)(2,1)S(1)}, u32[]{:S(2)}, u32[]{:S(2)}) %all-to-all-start.4) | async-done | bytes 1441824 | tf_op jit(solution)/shard_map/all_to_all | solution.py:623
  116.0 2.0 %collective-permute-start = (bf16[32,16,1408]{2,1,0:T(8,128)(2,1)S(1)}, bf16[32,16,1408]{2,1,0:T(8,128)(2,1)}, u32[]{:S(2)}, u32[]{:S(2)}) collective-permute-start(bf16[32,16,1408]{2,1,0:T(8,128)(2,1)S(1)} %all-to-all-done.4.mine_ref), channel_id=1, source_target_pairs={{0,8},{8,0},{1,9},{9,1},{2,10},{10,2},{3,11},{11,3},{4,12},{12,4},... | collective-permute-start | bytes 4325384 | tf_op jit(solution)/shard_map/ppermute | solution.py:626
  118.0 0.1 pad_add_fusion.place_ref
  118.1 1.7 dynamic-slice_bitcast_fusion
  119.8 1.2 collective-permute-done.other_ref
  121.0 1.4 dynamic-slice_select_fusion
  122.4 0.0 slice-start
  122.4 0.2 copy.14
  122.6 0.0 copy-start.4
  122.6 2.3 %copy-done.4 = f32[512,2048]{1,0:T(8,128)S(1)} copy-done((f32[512,2048]{1,0:T(8,128)S(1)}, f32[512,2048]{1,0:T(8,128)}, u32[]{:S(2)}) %copy-start.4) | copy-done | bytes 4194328
  124.8 2.5 %copy-done.6 = bf16[2048,1280]{1,0:T(8,128)(2,1)S(1)} copy-done((bf16[2048,1280]{1,0:T(8,128)(2,1)S(1)}, bf16[2048,1280]{1,0:T(8,128)(2,1)}, u32[]{:S(2)}) %copy-start.6) | copy-done | bytes 5242904
  127.3 6.2 %comb_dots.1 = (f32[512,2048]{1,0:T(8,128)S(1)}, f32[1,2048]{1,0:T(1,128)S(1)}) custom-call(s32[2]{0:T(128)S(1)} %pad_add_fusion.place_ref, f32[512,2048]{1,0:T(8,128)S(1)} %copy-done.4, bf16[2048,1280]{1,0:T(8,128)(2,1)S(1)} %copy-done.6, f32[8,1,2048]{2,1,0:T(1,128)S(1)} %all-to-all-done.row_ref, bf16[32,16,1408]{2,1,0:T(8,128)(2,1)S(1)} %all-to-all-done.4.mine_ref, ...), custom_call_target="tpu_custom_call" | custom-call | flops 2684354560 | bytes 5242880 | tf_op jit(solution)/shard_map/comb_dots/pallas_call | solution.py:410
  133.5 2.0 %collective-permute-start.1 = (f32[1,2048]{1,0:T(1,128)S(1)}, f32[1,2048]{1,0:T(1,128)S(1)}, u32[]{:S(2)}, u32[]{:S(2)}) collective-permute-start(f32[1,2048]{1,0:T(1,128)S(1)} %get-tuple-element.52.sum_ref), channel_id=1, source_target_pairs={{0,1},{1,0},{2,3},{3,2},{4,5},{5,4},{6,7},{7,6},{8,9},{9,8},{10,11... | collective-permute-start | bytes 24584 | tf_op jit(solution)/shard_map/ppermute | solution.py:630
  135.5 7.2 %disp_dots.1 = (f32[512,2048]{1,0:T(8,128)S(1)}, bf16[512,2048]{1,0:T(8,128)(2,1)S(1)}) custom-call(s32[2]{0:T(128)S(1)} %pad_add_fusion.place_ref, f32[512,2048]{1,0:T(8,128)S(1)} %copy-done.4, f32[512,2048]{1,0:T(8,128)S(1)} %get-tuple-element.49.dot_ref, bf16[2048,1280]{1,0:T(8,128)(2,1)S(1)} %bitcast.10, f32[8,1,2048]{2,1,0:T(1,128)S(1)} %all-to-all-done.row_ref, ...), custom_call_target="tpu_custom_call" | custom-call | flops 2684354560 | bytes 5242880 | tf_op jit(solution)/shard_map/disp_dots/pallas_call | solution.py:461
  142.7 0.0 copy-start.7
  142.7 0.0 copy-done.15
  142.7 0.9 fusion.1
  143.6 0.0 collective-permute-done.1.other_ref
  143.6 6.3 %logit_grads.1 = (bf16[512,2048]{1,0:T(8,128)(2,1)S(1)}, bf16[1280,128]{1,0:T(8,128)(2,1)S(1)}, bf16[160,2048]{1,0:T(8,128)(2,1)}) custom-call(s32[2]{0:T(128)S(1)} %pad_add_fusion.place_ref, f32[512,2048]{1,0:T(8,128)S(1)} %copy-done.4, f32[512,2048]{1,0:T(8,128)S(1)} %get-tuple-element.50.terms_ref, bf16[512,2048]{1,0:T(8,128)(2,1)S(1)} %get-tuple-element.51.dispatch_ref, ...), custom_call_target="tpu_custom_call" | custom-call | flops 671088640 | bytes 5242880 | tf_op jit(solution)/shard_map/logit_grads/pallas_call | solution.py:521
  149.8 0.0 copy-done.7
  149.9 1.1 collective-permute-start.2
  151.0 0.0 copy-done.14
  151.0 4.9 %all-to-all-start.5 = ((bf16[16,80,128]{2,1,0:T(8,128)(2,1)}), bf16[16,80,128]{2,1,0:T(8,128)(2,1)}, u32[]{:S(2)}, u32[]{:S(2)}) async-start(bf16[16,80,128]{2,1,0:T(8,128)(2,1)} %bitcast.11), calls=%async_computation.5 | async-start | bytes 655360 | tf_op jit(solution)/shard_map/all_to_all | solution.py:651
  155.8 1.6 copy-done.8
  157.4 1.0 copy-done.12
  158.4 1.8 token_grads.1
  160.2 10.6 %all-to-all-done.5 = bf16[16,80,128]{2,1,0:T(8,128)(2,1)} async-done(((bf16[16,80,128]{2,1,0:T(8,128)(2,1)}), bf16[16,80,128]{2,1,0:T(8,128)(2,1)}, u32[]{:S(2)}, u32[]{:S(2)}) %all-to-all-start.5) | async-done | bytes 327712 | tf_op jit(solution)/shard_map/all_to_all | solution.py:651
  170.8 1.6 convert_reduce_fusion
  172.4 0.0 collective-permute-done.2
  172.4 2.1 %fusion = bf16[2048,160]{0,1:T(8,128)(2,1)} fusion(f32[160,2048]{1,0:T(8,128)S(1)} %token_grads.1, bf16[160,2048]{1,0:T(8,128)(2,1)} %collective-permute-done.2), kind=kLoop, calls=%fused_computation.5 | loop fusion | flops 983040 | bytes 2621440 | tf_op jit(solution)/shard_map/transpose | solution.py:656
  (14 shorter events, 0.0 us)
Async XLA Ops:
  7.2 66.8 %all-gather.2.cloned.1.call-start = ((), (), s32[]{:S(2)}) async-start(), calls=%async_computation.6 | async-start | bytes 1638400 | tf_op jit(solution)/shard_map/all_gather | solution.py:606
  7.2 1.0 copy-start.13
  9.2 2.5 %copy-start = (bf16[2048,1280]{1,0:T(8,128)(2,1)S(1)}, bf16[2048,1280]{1,0:T(8,128)(2,1)}, u32[]{:S(2)}) copy-start(bf16[2048,1280]{1,0:T(8,128)(2,1)} %tokens_ref.9) | copy-start | bytes 15728644
  14.8 14.9 %all-to-all-start = ((f32[8,1,2048]{2,1,0:T(1,128)}), f32[8,1,2048]{2,1,0:T(1,128)S(1)}, u32[]{:S(2)}, u32[]{:S(2)}) async-start(f32[8,1,2048]{2,1,0:T(1,128)} %get-tuple-element.32), calls=%async_computation | async-start | bytes 131072 | tf_op jit(solution)/shard_map/all_to_all | solution.py:609
  23.0 2.6 %copy-start.1 = (bf16[2048,1280]{1,0:T(8,128)(2,1)S(1)}, bf16[2048,1280]{1,0:T(8,128)(2,1)}, u32[]{:S(2)}) copy-start(bf16[2048,1280]{1,0:T(8,128)(2,1)} %tokens_ref.9) | copy-start | bytes 15728644
  29.7 2.5 %copy-start.5 = (bf16[2048,1280]{1,0:T(8,128)(2,1)S(1)}, bf16[2048,1280]{1,0:T(8,128)(2,1)}, u32[]{:S(2)}) copy-start(bf16[2048,1280]{1,0:T(8,128)(2,1)} %grad_ref.3) | copy-start | bytes 15728644
  32.2 36.3 %copy-start.10 = (bf16[8,192,1280]{2,1,0:T(8,128)(2,1)S(1)}, bf16[8,192,1280]{2,1,0:T(8,128)(2,1)}, u32[]{:S(2)}) copy-start(bf16[8,192,1280]{2,1,0:T(8,128)(2,1)} %w_in_ref.1) | copy-start | bytes 11796484
  32.2 36.3 %copy-start.11 = (bf16[8,192,1280]{2,1,0:T(8,128)(2,1)S(1)}, bf16[8,192,1280]{2,1,0:T(8,128)(2,1)}, u32[]{:S(2)}) copy-start(bf16[8,192,1280]{2,1,0:T(8,128)(2,1)} %w_out_ref.1) | copy-start | bytes 11796484
  74.0 15.4 %all-to-all-start.3 = ((bf16[16,16,1280]{2,1,0:T(8,128)(2,1)}), bf16[16,16,1280]{2,1,0:T(8,128)(2,1)S(1)}, u32[]{:S(2)}, u32[]{:S(2)}) async-start(bf16[16,16,1280]{2,1,0:T(8,128)(2,1)} %get-tuple-element.37), calls=%async_computation.3 | async-start | bytes 1310720 | tf_op jit(solution)/shard_map/all_to_all | solution.py:619
  79.4 2.5 %copy-start.2 = (bf16[2048,1280]{1,0:T(8,128)(2,1)S(1)}, bf16[2048,1280]{1,0:T(8,128)(2,1)}, u32[]{:S(2)}) copy-start(bf16[2048,1280]{1,0:T(8,128)(2,1)} %tokens_ref.9) | copy-start | bytes 15728644
  86.6 2.0 %copy-start.3 = (f32[512,2048]{1,0:T(8,128)}, f32[512,2048]{1,0:T(8,128)S(1)}, u32[]{:S(2)}) copy-start(f32[512,2048]{1,0:T(8,128)S(1)} %all_exps.1.exp_ref) | copy-start | bytes 12582916
  89.5 1.1 copy-start.9
  90.7 25.3 %all-to-all-start.4 = ((bf16[32,16,1408]{2,1,0:T(8,128)(2,1)}), bf16[32,16,1408]{2,1,0:T(8,128)(2,1)S(1)}, u32[]{:S(2)}, u32[]{:S(2)}) async-start(bf16[32,16,1408]{2,1,0:T(8,128)(2,1)} %copy-done.9), calls=%async_computation.4 | async-start | bytes 2883584 | tf_op jit(solution)/shard_map/all_to_all | solution.py:623
  116.0 5.0 %collective-permute-start = (bf16[32,16,1408]{2,1,0:T(8,128)(2,1)S(1)}, bf16[32,16,1408]{2,1,0:T(8,128)(2,1)}, u32[]{:S(2)}, u32[]{:S(2)}) collective-permute-start(bf16[32,16,1408]{2,1,0:T(8,128)(2,1)S(1)} %all-to-all-done.4.mine_ref), channel_id=1, source_target_pairs={{0,8},{8,0},{1,9},{9,1},{2,10},{10,2},{3,11},{11,3},{4,12},{12,4},... | collective-permute-start | bytes 4325384 | tf_op jit(solution)/shard_map/ppermute | solution.py:626
  122.4 13.1 %slice-start = ((s8[5242880]{0:T(1024)(128)(4,1)}), s8[1048576]{0:T(1024)(128)(4,1)S(1)}, s32[]{:S(2)}) async-start(s8[5242880]{0:T(1024)(128)(4,1)} %bitcast.9), calls=%async_computation.7 | async-start | bytes 2097152
  122.6 2.3 %copy-start.4 = (f32[512,2048]{1,0:T(8,128)S(1)}, f32[512,2048]{1,0:T(8,128)}, u32[]{:S(2)}) copy-start(f32[512,2048]{1,0:T(8,128)} %copy-done.3) | copy-start | bytes 12582916
  124.8 2.5 %copy-start.6 = (bf16[2048,1280]{1,0:T(8,128)(2,1)S(1)}, bf16[2048,1280]{1,0:T(8,128)(2,1)}, u32[]{:S(2)}) copy-start(bf16[2048,1280]{1,0:T(8,128)(2,1)} %grad_ref.3) | copy-start | bytes 15728644
  127.3 8.1 %slice-start.1 = ((s8[5242880]{0:T(1024)(128)(4,1)}), s8[4194304]{0:T(1024)(128)(4,1)S(1)}, s32[]{:S(2)}) async-start(s8[5242880]{0:T(1024)(128)(4,1)} %bitcast.9), calls=%async_computation.8 | async-start | bytes 8388608
  133.5 10.1 %collective-permute-start.1 = (f32[1,2048]{1,0:T(1,128)S(1)}, f32[1,2048]{1,0:T(1,128)S(1)}, u32[]{:S(2)}, u32[]{:S(2)}) collective-permute-start(f32[1,2048]{1,0:T(1,128)S(1)} %get-tuple-element.52.sum_ref), channel_id=1, source_target_pairs={{0,1},{1,0},{2,3},{3,2},{4,5},{5,4},{6,7},{7,6},{8,9},{9,8},{10,11... | collective-permute-start | bytes 24584 | tf_op jit(solution)/shard_map/ppermute | solution.py:630
  135.5 7.3 %copy-start.15 = (bf16[320,512]{1,0:T(8,128)(2,1)S(1)}, bf16[320,512]{1,0:T(8,128)(2,1)}, u32[]{:S(2)}) copy-start(bf16[320,512]{1,0:T(8,128)(2,1)} %dynamic-slice_bitcast_fusion) | copy-start | bytes 983044
  142.7 7.1 %copy-start.7 = (bf16[512,2048]{1,0:T(8,128)(2,1)}, bf16[512,2048]{1,0:T(8,128)(2,1)S(1)}, u32[]{:S(2)}) copy-start(bf16[512,2048]{1,0:T(8,128)(2,1)S(1)} %get-tuple-element.51.dispatch_ref) | copy-start | bytes 6291460
  149.8 1.1 copy-start.14
  149.9 22.5 %collective-permute-start.2 = (bf16[160,2048]{1,0:T(8,128)(2,1)}, bf16[160,2048]{1,0:T(8,128)(2,1)}, u32[]{:S(2)}, u32[]{:S(2)}) collective-permute-start(bf16[160,2048]{1,0:T(8,128)(2,1)} %get-tuple-element.54), channel_id=1, source_target_pairs={{0,1},{1,0},{2,3},{3,2},{4,5},{5,4},{6,7},{7,6},{8,9},{9,8},{10,11... | collective-permute-start | bytes 1966088 | tf_op jit(solution)/shard_map/ppermute | solution.py:650
  151.0 19.8 %all-to-all-start.5 = ((bf16[16,80,128]{2,1,0:T(8,128)(2,1)}), bf16[16,80,128]{2,1,0:T(8,128)(2,1)}, u32[]{:S(2)}, u32[]{:S(2)}) async-start(bf16[16,80,128]{2,1,0:T(8,128)(2,1)} %bitcast.11), calls=%async_computation.5 | async-start | bytes 655360 | tf_op jit(solution)/shard_map/all_to_all | solution.py:651
  155.8 1.6 copy-start.8
  157.4 1.0 copy-start.12
Sparse Core Ops, SparseCore 0:
  10.2 31.3 all-gather.1

commit v4 on v0

v4 whole, which is shorter than its diff:
```python
import jax
import jax.numpy as jnp
from jax import lax
from jax.experimental import pallas as pl
from jax.experimental.pallas import tpu as pltpu
from jax.sharding import Mesh, PartitionSpec as P

gelu_scale = 0.7978845608
gelu_cubic = 0.044715
rows_contract = (((0,), (0,)), ((), ()))
cols_contract = (((1,), (1,)), ((), ()))

SEQ = ("zl", "y", "c")
SLOT = ("xa", "xb", "zh")
KEYS = ("xb", "zh")
CHIPS = ("zl", "y")
GATHERED = ("xb", "zh", "zl", "y")
f32 = jnp.float32
bf16 = jnp.bfloat16
LANES = 128
MIB = 1 << 20
GRANT = 16
SCALE = 1


def gelu_tanh(values):
    return (
        0.5
        * values
        * (1.0 + jnp.tanh(gelu_scale * (values + gelu_cubic * values * values * values)))
    )


def gelu_slope(values):
    bent = jnp.tanh(gelu_scale * (values + gelu_cubic * values * values * values))
    return 0.5 * (1.0 + bent) + 0.5 * values * (1.0 - bent * bent) * gelu_scale * (
        1.0 + 3.0 * gelu_cubic * values * values
    )


def guarded(total):
    power = jnp.where(total > 2.0**64, 2.0**-32, jnp.where(total < 2.0**-64, 2.0**32, 1.0))
    return power, 1.0 / (total * power)


def two_parts(values):
    high = values.astype(bf16).astype(f32)
    return high, values - high


def in_lanes(rows, columns):
    lane = lax.broadcasted_iota(jnp.int32, (rows, LANES), 1)
    laid = jnp.zeros((rows, LANES), f32)
    for at, column in enumerate(columns):
        laid = jnp.where(lane == at, column, laid)
    return laid.astype(bf16)


def params(mib):
    return pltpu.CompilerParams(vmem_limit_bytes=mib * MIB)


def cost(flops, nbytes):
    return pl.CostEstimate(flops=SCALE * flops, bytes_accessed=nbytes, transcendentals=0)


def whole_in_vmem():
    return pl.BlockSpec(memory_space=pltpu.VMEM)


def in_smem():
    return pl.BlockSpec(memory_space=pltpu.SMEM)


def halves(place_ref, half):
    core = place_ref[0]
    here = pl.ds(pl.multiple_of(core * half, LANES), half)
    there = pl.ds(pl.multiple_of((1 - core) * half, LANES), half)
    return here, there


def own_logits(slot_keys, tokens, copies, tile=512):
    features, slots = slot_keys.shape
    count = tokens.shape[0]

    def kernel(slot_keys_ref, tokens_ref, exp_ref, row_ref, column_ref):
        keys = slot_keys_ref[...].T
        by_lane = jnp.zeros((slots, LANES), f32)
        for at in range(0, count, tile):
            cut = slice(at, at + tile)
            exps = jnp.exp(
                lax.dot_general(keys, tokens_ref[cut, :], cols_contract, preferred_element_type=f32)
            )
            exp_ref[:, cut] = exps
            row_ref[:, :, cut] = jnp.broadcast_to(
                jnp.sum(exps, axis=0, keepdims=True)[None], (copies, 1, tile)
            )
            for lanes in range(0, tile, LANES):
                by_lane = by_lane + exps[:, lanes : lanes + LANES]
        column_ref[...] = by_lane

    return pl.pallas_call(
        kernel,
        in_specs=[whole_in_vmem()] * 2,
        out_specs=[whole_in_vmem()] * 3,
        out_shape=[
            jax.ShapeDtypeStruct((slots, count), f32),
            jax.ShapeDtypeStruct((copies, 1, count), f32),
            jax.ShapeDtypeStruct((slots, LANES), f32),
        ],
        compiler_params=params(GRANT),
        cost_estimate=cost(2 * slots * features * count, 2 * features * count),
        name="own_logits",
    )(slot_keys, tokens)


def dispatch_part(exps, column, column_other, tokens):
    slots, count = exps.shape
    features = tokens.shape[1]

    def kernel(exp_ref, column_ref, other_ref, tokens_ref, out_ref, weights_ref):
        total = jnp.sum(column_ref[...] + other_ref[...], axis=1, keepdims=True)
        power, inverse = guarded(jnp.where(total > 0, total, 1.0))
        weights_ref[...] = ((exp_ref[...] * power) * inverse).astype(bf16)
        out_ref[...] = jnp.dot(
            weights_ref[...], tokens_ref[...], preferred_element_type=f32
        ).astype(bf16)

    return pl.pallas_call(
        kernel,
        in_specs=[whole_in_vmem()] * 4,
        out_specs=whole_in_vmem(),
        out_shape=jax.ShapeDtypeStruct((slots, features), bf16),
        scratch_shapes=[pltpu.VMEM((slots, count), bf16)],
        compiler_params=params(GRANT),
        cost_estimate=cost(2 * slots * features * count, 2 * features * count),
        name="dispatch_part",
    )(exps, column, column_other, tokens)


def combine_part(place, exps, row_parts, column, column_other, slot_in_part, out_grad, groups):
    slots, count = exps.shape
    features = out_grad.shape[1]
    half = features // 2
    block = slots // groups

    def kernel(
        place_ref, exp_ref, row_ref, column_ref, other_ref, in_ref, grad_ref,
        keep_ref, give_ref, weights_ref, total_ref,
    ):
        power, inverse = guarded(jnp.sum(row_ref[...], axis=0))
        weights_ref[...] = ((exp_ref[...] * power) * inverse).astype(bf16)
        total = jnp.sum(column_ref[...] + other_ref[...], axis=1, keepdims=True)
        shift, _unused = guarded(total)
        high, low = two_parts(total * shift)
        lanes = in_lanes(slots, (high, low, 1.0 / shift))
        total_ref[...] = jnp.dot(
            weights_ref[...], grad_ref[...], preferred_element_type=f32
        ).astype(bf16)
        here, there = halves(place_ref, half)
        for group in range(groups):
            rows = slice(group * block, (group + 1) * block)
            keep_ref[group, :, :half] = in_ref[rows, here]
            keep_ref[group, :, half:features] = total_ref[rows, here]
            keep_ref[group, :, features:] = lanes[rows]
            give_ref[group, :, :half] = in_ref[rows, there]
            give_ref[group, :, half:] = total_ref[rows, there]

    return pl.pallas_call(
        kernel,
        in_specs=[in_smem()] + [whole_in_vmem()] * 6,
        out_specs=[whole_in_vmem()] * 2,
        out_shape=[
            jax.ShapeDtypeStruct((groups, block, features + LANES), bf16),
            jax.ShapeDtypeStruct((groups, block, features), bf16),
        ],
        scratch_shapes=[
            pltpu.VMEM((slots, count), bf16),
            pltpu.VMEM((slots, features), bf16),
        ],
        compiler_params=params(GRANT),
        cost_estimate=cost(2 * slots * features * count, 2 * features * count),
        name="combine_part",
    )(place, exps, row_parts, column, column_other, slot_in_part, out_grad)


def pair_sum(keep, received):
    features = received.shape[2]

    def kernel(keep_ref, received_ref, out_ref):
        total = keep_ref[:, :, :features].astype(f32) + received_ref[...].astype(f32)
        out_ref[:, :, :features] = total.astype(bf16)
        if keep_ref.shape[2] > features:
            out_ref[:, :, features:] = keep_ref[:, :, features:]

    return pl.pallas_call(
        kernel,
        in_specs=[whole_in_vmem()] * 2,
        out_specs=whole_in_vmem(),
        out_shape=jax.ShapeDtypeStruct(keep.shape, bf16),
        compiler_params=params(GRANT),
        name="pair_sum",
    )(keep, received)


def sum_slots(parts, copies):
    sources, block, width = parts.shape
    features = width - LANES
    half = features // 2

    def kernel(parts_ref, sent_ref, in_ref, column_ref):
        lanes = parts_ref[:, :, features:].astype(f32)
        columns = (lanes[:, :, 0:1] + lanes[:, :, 1:2]) * lanes[:, :, 2:3]
        total = jnp.sum(columns, axis=0)
        power, inverse = guarded(total)
        share = (columns * power[None]) * inverse[None]
        slot_in = jnp.zeros((block, half), f32)
        slot_grad = jnp.zeros((block, half), f32)
        for source in range(sources):
            slot_in = slot_in + parts_ref[source, :, :half].astype(f32) * share[source]
            slot_grad = slot_grad + parts_ref[source, :, half:features].astype(f32)
        in_ref[...] = slot_in
        column_ref[...] = jnp.broadcast_to(total, (block, LANES))
        in_low = slot_in.astype(bf16)
        grad_low = slot_grad.astype(bf16)
        for copy in range(copies):
            sent_ref[copy, :, :half] = in_low
            sent_ref[copy, :, half:] = grad_low

    return pl.pallas_call(
        kernel,
        in_specs=[whole_in_vmem()],
        out_specs=[whole_in_vmem()] * 3,
        out_shape=[
            jax.ShapeDtypeStruct((copies, block, features), bf16),
            jax.ShapeDtypeStruct((block, half), f32),
            jax.ShapeDtypeStruct((block, LANES), f32),
        ],
        compiler_params=params(GRANT),
        name="sum_slots",
    )(parts)


def experts_part(place, mine, other, w_in, w_out):
    experts, hidden, features = w_in.shape
    block = mine.shape[1]
    half = features // 2

    def kernel(place_ref, mine_ref, other_ref, w_in_ref, w_out_ref, keep_ref, give_ref, act_ref, pre_ref):
        here, there = halves(place_ref, half)

        def inward(at, weights_ref, e):
            cut = slice(at * half, (at + 1) * half)
            near = lax.dot_general(
                mine_ref[e, :, cut], weights_ref[e, :, here], cols_contract, preferred_element_type=f32
            )
            far = lax.dot_general(
                other_ref[e, :, cut], weights_ref[e, :, there], cols_contract, preferred_element_type=f32
            )
            return near + far

        for e in range(experts):
            hidden_pre = inward(0, w_in_ref, e)
            act_grad = inward(1, w_out_ref, e)
            act = gelu_tanh(hidden_pre).astype(bf16)
            pre = (act_grad * gelu_slope(hidden_pre)).astype(bf16)
            for cut, out_ref in ((here, keep_ref), (there, give_ref)):
                out_ref[e, :, :half] = jnp.dot(
                    act, w_out_ref[e, :, cut], preferred_element_type=f32
                ).astype(bf16)
                out_ref[e, :, half:] = jnp.dot(
                    pre, w_in_ref[e, :, cut], preferred_element_type=f32
                ).astype(bf16)
            act_ref[e] = act
            pre_ref[e] = pre

    return pl.pallas_call(
        kernel,
        in_specs=[in_smem()] + [whole_in_vmem()] * 4,
        out_specs=[whole_in_vmem()] * 4,
        out_shape=[
            jax.ShapeDtypeStruct((experts, block, features), bf16),
            jax.ShapeDtypeStruct((experts, block, features), bf16),
            jax.ShapeDtypeStruct((experts, block, hidden), bf16),
            jax.ShapeDtypeStruct((experts, block, hidden), bf16),
        ],
        compiler_params=params(GRANT),
        cost_estimate=cost(8 * experts * block * hidden * features, 4 * experts * hidden * features),
        name="experts_part",
    )(place, mine, other, w_in, w_out)


def weight_grads(place, mine, other, act, pre):
    experts, block, hidden = act.shape
    features = mine.shape[2]
    half = features // 2

    def kernel(place_ref, mine_ref, other_ref, act_ref, pre_ref, in_ref, out_ref):
        here, there = halves(place_ref, half)
        for cut, from_ref in ((here, mine_ref), (there, other_ref)):
            in_ref[0, :, cut] = lax.dot_general(
                pre_ref[0], from_ref[0, :, :half], rows_contract, preferred_element_type=f32
            ).astype(bf16)
            out_ref[0, :, cut] = lax.dot_general(
                act_ref[0], from_ref[0, :, half:], rows_contract, preferred_element_type=f32
            ).astype(bf16)

    return pl.pallas_call(
        kernel,
        grid=(experts,),
        in_specs=[
            in_smem(),
            pl.BlockSpec((1, block, features), lambda e: (e, 0, 0)),
            pl.BlockSpec((1, block, features), lambda e: (e, 0, 0)),
            pl.BlockSpec((1, block, hidden), lambda e: (e, 0, 0)),
            pl.BlockSpec((1, block, hidden), lambda e: (e, 0, 0)),
        ],
        out_specs=[pl.BlockSpec((1, hidden, features), lambda e: (e, 0, 0))] * 2,
        out_shape=[jax.ShapeDtypeStruct((experts, hidden, features), bf16)] * 2,
        compiler_params=params(GRANT),
        cost_estimate=cost(4 * experts * block * hidden * features, 4 * experts * hidden * features),
        name="weight_grads",
    )(place, mine, other, act, pre)


def sum_terms(terms, slot_in, column, copies):
    sources, block, features = terms.shape
    half = features // 2
    width = features + LANES

    def kernel(terms_ref, in_ref, column_ref, sent_ref):
        total = terms_ref[0].astype(f32)
        for source in range(1, sources):
            total = total + terms_ref[source].astype(f32)
        low = total.astype(bf16)
        inner = jnp.sum(in_ref[...] * low[:, half:].astype(f32), axis=1, keepdims=True)
        power, inverse = guarded(column_ref[:, 0:1])
        lanes = in_lanes(block, two_parts(inverse) + (power,) + two_parts(inner))
        for copy in range(copies):
            sent_ref[copy, :, :features] = low
            sent_ref[copy, :, features:] = lanes

    return pl.pallas_call(
        kernel,
        in_specs=[whole_in_vmem()] * 3,
        out_specs=whole_in_vmem(),
        out_shape=jax.ShapeDtypeStruct((copies, block, width), bf16),
        compiler_params=params(GRANT),
        name="sum_terms",
    )(terms, slot_in, column)


def all_exps(place, keys_all, tokens, width, tile=256):
    blocks, features, block = keys_all.shape
    slots = blocks * block
    count = tokens.shape[0]
    half = features // 2

    def kernel(place_ref, keys_ref, tokens_ref, exp_ref, rows_ref, turned_ref):
        for at in range(blocks):
            cut = slice(at * block, (at + 1) * block)
            turned_ref[cut, :] = keys_ref[at].T
            for side in range(2):
                first = pl.multiple_of(place_ref[1] * width + side * half, 16)
                rows_ref[side, :, cut] = keys_ref[at, pl.ds(first, width), :]
        for at in range(0, count, tile):
            exp_ref[:, at : at + tile] = jnp.exp(
                lax.dot_general(
                    turned_ref[...], tokens_ref[at : at + tile, :], cols_contract,
                    preferred_element_type=f32,
                )
            ).astype(bf16)

    return pl.pallas_call(
        kernel,
        in_specs=[in_smem()] + [whole_in_vmem()] * 2,
        out_specs=[whole_in_vmem()] * 2,
        out_shape=[
            jax.ShapeDtypeStruct((slots, count), bf16),
            jax.ShapeDtypeStruct((2, width, slots), bf16),
        ],
        scratch_shapes=[pltpu.VMEM((slots, features), bf16)],
        compiler_params=params(GRANT),
        cost_estimate=cost(2 * slots * features * count, 2 * features * count),
        name="all_exps",
    )(place, keys_all, tokens)


def width_dot(place_ref, mine_ref, other_ref, ref, at, rows):
    blocks, block, _unused = mine_ref.shape
    half = ref.shape[1] // 2
    here, there = halves(place_ref, half)
    near = lax.dot_general(
        mine_ref[:, :, at * half : (at + 1) * half].reshape(blocks * block, half),
        ref[rows, here],
        cols_contract,
        preferred_element_type=f32,
    )
    far = lax.dot_general(
        other_ref[:, :, at * half : (at + 1) * half].reshape(blocks * block, half),
        ref[rows, there],
        cols_contract,
        preferred_element_type=f32,
    )
    return near + far


def comb_dots(place, exps, out_grad, row_parts, mine, other, tile=256):
    slots, count = exps.shape
    features = out_grad.shape[1]

    def kernel(place_ref, exp_ref, grad_ref, row_ref, mine_ref, other_ref, dot_ref, sum_ref):
        for at in range(0, count, tile):
            cut = slice(at, at + tile)
            power, inverse = guarded(jnp.sum(row_ref[:, :, cut], axis=0))
            dots = width_dot(place_ref, mine_ref, other_ref, grad_ref, 0, cut)
            dot_ref[:, cut] = dots
            terms = (exp_ref[:, cut].astype(f32) * power) * dots
            sum_ref[:, cut] = jnp.sum(terms, axis=0, keepdims=True) * inverse

    return pl.pallas_call(
        kernel,
        in_specs=[in_smem()] + [whole_in_vmem()] * 5,
        out_specs=[whole_in_vmem()] * 2,
        out_shape=[
            jax.ShapeDtypeStruct((slots, count), f32),
            jax.ShapeDtypeStruct((1, count), f32),
        ],
        compiler_params=params(GRANT),
        cost_estimate=cost(2 * slots * features * count, 2 * features * count),
        name="comb_dots",
    )(place, exps, out_grad, row_parts, mine, other)


def disp_dots(place, exps, dots, tokens, row_parts, mine, other, width, tile=256):
    slots, count = exps.shape
    features = tokens.shape[1]
    half = features // 2

    def kernel(
        place_ref, exp_ref, dot_ref, tokens_ref, row_ref, mine_ref, other_ref,
        terms_ref, dispatch_ref, rows_ref, power_ref, inverse_ref, total_ref, turned_ref,
    ):
        lanes = mine_ref[:, :, features:].reshape(slots, LANES).astype(f32)
        apart = other_ref[:, :, features:].reshape(slots, LANES).astype(f32)
        inner = lanes[:, 3:4] + lanes[:, 4:5] + apart[:, 3:4] + apart[:, 4:5]
        power_ref[...] = jnp.broadcast_to(lanes[:, 2:3], (slots, tile))
        inverse_ref[...] = jnp.broadcast_to(lanes[:, 0:1] + lanes[:, 1:2], (slots, tile))
        total_ref[...] = jnp.broadcast_to(inner, (slots, tile))
        rows = pl.ds(pl.multiple_of(place_ref[1] * width, 16), width)
        for at, ref in enumerate((mine_ref, other_ref)):
            turned_ref[...] = ref[:, :, half:features].reshape(slots, half).T
            rows_ref[at] = turned_ref[rows, :]
        for at in range(0, count, tile):
            cut = slice(at, at + tile)
            power, inverse = guarded(jnp.sum(row_ref[:, :, cut], axis=0))
            exps_here = exp_ref[:, cut].astype(f32)
            dispatch = (exps_here * power_ref[...]) * inverse_ref[...]
            dispatch_ref[:, cut] = dispatch.astype(bf16)
            disp_dot = width_dot(place_ref, mine_ref, other_ref, tokens_ref, 1, cut)
            combine = (exps_here * power) * inverse
            terms_ref[:, cut] = combine * dot_ref[:, cut] + dispatch * (disp_dot - total_ref[...])

    return pl.pallas_call(
        kernel,
        in_specs=[in_smem()] + [whole_in_vmem()] * 6,
        out_specs=[whole_in_vmem()] * 3,
        out_shape=[
            jax.ShapeDtypeStruct((slots, count), f32),
            jax.ShapeDtypeStruct((slots, count), bf16),
            jax.ShapeDtypeStruct((2, width, slots), bf16),
        ],
        scratch_shapes=[pltpu.VMEM((slots, tile), f32)] * 3 + [pltpu.VMEM((half, slots), bf16)],
        compiler_params=params(GRANT),
        cost_estimate=cost(2 * slots * features * count, 2 * features * count),
        name="disp_dots",
    )(place, exps, dots, tokens, row_parts, mine, other)


def logit_grads(place, exps, terms, dispatch, tokens, row_parts, row, row_other, keys_rows, grad_rows, own_slots, tile=256):
    slots, count = exps.shape
    features = tokens.shape[1]
    width = keys_rows.shape[1]

    def kernel(
        place_ref, exp_ref, terms_ref, dispatch_ref, tokens_ref, row_ref, sum_ref, other_ref, keys_rows_ref, grad_rows_ref,
        keys_ref, sent_ref, own_ref, logit_ref,
    ):
        core, half_at = place_ref[0], place_ref[2]
        near = jnp.where(core == half_at, 0, 1)
        for at in range(0, count, tile):
            cut = slice(at, at + tile)
            power, inverse = guarded(jnp.sum(row_ref[:, :, cut], axis=0))
            weight = (sum_ref[:, cut] + other_ref[:, cut]) * inverse
            exps_here = exp_ref[:, cut].astype(f32)
            logit_ref[:, cut] = (terms_ref[:, cut] - (exps_here * power) * weight).astype(bf16)
            for out_ref, at_keys, at_grad in (
                (sent_ref, 1 - half_at, 1 - near),
                (own_ref, half_at, near),
            ):
                total = jnp.dot(keys_rows_ref[at_keys], logit_ref[:, cut], preferred_element_type=f32)
                total = total + jnp.dot(
                    grad_rows_ref[at_grad], dispatch_ref[:, cut], preferred_element_type=f32
                )
                out_ref[:, cut] = total.astype(out_ref.dtype)
        own = pl.ds(pl.multiple_of(place_ref[1] * own_slots, own_slots), own_slots)
        total = jnp.dot(logit_ref[own, :], tokens_ref[...], preferred_element_type=f32)
        keys_ref[...] = total.T.astype(bf16)

    return pl.pallas_call(
        kernel,
        in_specs=[in_smem()] + [whole_in_vmem()] * 9,
        out_specs=[whole_in_vmem()] * 3,
        out_shape=[
            jax.ShapeDtypeStruct((features, own_slots), bf16),
            jax.ShapeDtypeStruct((width, count), bf16),
            jax.ShapeDtypeStruct((width, count), f32),
        ],
        scratch_shapes=[pltpu.VMEM((slots, count), bf16)],
        compiler_params=params(GRANT),
        cost_estimate=cost(2 * own_slots * features * count, 2 * features * count),
        name="logit_grads",
    )(place, exps, terms, dispatch, tokens, row_parts, row, row_other, keys_rows, grad_rows)


def per_device(tokens, slot_keys, w_in, w_out, out_grad):
    features = tokens.shape[1]
    own_slots = slot_keys.shape[1]
    slot_devices = lax.axis_size(SLOT)
    seq_devices = lax.axis_size(SEQ)
    groups = lax.axis_size(CHIPS)
    everyone = lax.axis_size(GATHERED)
    width = features // slot_devices
    swap = [(0, 1), (1, 0)]
    place = jnp.stack(
        [lax.axis_index("c"), lax.axis_index(KEYS), lax.axis_index("xa")]
    ).astype(jnp.int32)

    keys_all = lax.all_gather(slot_keys, KEYS, axis=0, tiled=False)
    exps, own_row, column = own_logits(slot_keys, tokens, slot_devices)
    column_other = lax.ppermute(column, "c", swap)
    row_parts = lax.all_to_all(own_row, SLOT, 0, 0)
    slot_in_part = dispatch_part(exps, column, column_other, tokens)
    keep, give = combine_part(
        place, exps, row_parts, column, column_other, slot_in_part, out_grad, groups
    )
    parts = lax.all_to_all(pair_sum(keep, lax.ppermute(give, "c", swap)), CHIPS, 0, 0)
    sent, slot_in, column_total = sum_slots(parts, groups)
    mine = lax.all_to_all(sent, CHIPS, 0, 0)
    other = lax.ppermute(mine, "c", swap)

    keep, give, act, pre = experts_part(place, mine, other, w_in, w_out)
    sent = pair_sum(keep, lax.ppermute(give, "c", swap))
    sent, keys_all = lax.optimization_barrier((sent, keys_all))
    terms = lax.all_to_all(sent, CHIPS, 0, 0)
    all_exp, keys_rows = all_exps(place, keys_all, tokens, width)
    terms, all_exp, act, pre = lax.optimization_barrier((terms, all_exp, act, pre))
    sent = sum_terms(terms, slot_in, column_total, everyone)
    gathered = lax.all_to_all(sent, GATHERED, 0, 0)
    grad_w_in, grad_w_out = weight_grads(place, mine, other, act, pre)
    gathered, grad_w_in, grad_w_out = lax.optimization_barrier((gathered, grad_w_in, grad_w_out))
    gathered_other = lax.ppermute(gathered, "c", swap)

    dots, row = comb_dots(place, all_exp, out_grad, row_parts, gathered, gathered_other)
    row_other = lax.ppermute(row, "xa", swap)
    terms, dispatch, grad_rows = disp_dots(
        place, all_exp, dots, tokens, row_parts, gathered, gathered_other, width
    )
    keys_part, sent, own_grads = logit_grads(
        place, all_exp, terms, dispatch, tokens, row_parts, row, row_other, keys_rows, grad_rows, own_slots
    )
    received = lax.ppermute(sent, "xa", swap)
    keys_parts = lax.all_to_all(
        keys_part.reshape(seq_devices, features // seq_devices, own_slots), SEQ, 0, 0
    )
    grad_tokens = (own_grads + received.astype(f32)).astype(bf16).T
    grad_keys = jnp.sum(keys_parts.astype(f32), axis=0)
    return (grad_tokens, grad_keys, grad_w_in, grad_w_out)


def solution(mesh):
    fine = Mesh(mesh.devices.reshape(2, 4, 2, 2, 2, 2), ("zl", "y", "c", "xa", "xb", "zh"))
    placed = (
        P(SEQ, None),
        P(None, SLOT),
        P(SLOT, SEQ, None),
        P(SLOT, SEQ, None),
        P(SEQ, None),
    )
    return jax.shard_map(
        per_device,
        mesh=fine,
        in_specs=placed,
        out_specs=(
            P(SEQ, SLOT),
            P(SEQ, SLOT),
            P(SLOT, SEQ, None),
            P(SLOT, SEQ, None),
        ),
        check_vma=False,
    )
```

time: 545 us -> 163 us (0.30)
  waiting for transfers between devices: 380 us -> 23.7 us
  blocking collectives: 98.3 us -> 39.4 us
  matrix products: 46.4 us -> 0 us
  Pallas kernels: 0 us -> 34.8 us
  starting transfers between devices: 0.35 us -> 28.1 us
  local copies, waits for them, and re-layouts: 4.36 us -> 19.8 us
    psum x2 -> x0, waiting for transfers between devices: 238 us -> none  [the longest x1 120 us: per_device(): slot_out = lax.psum(out_terms.astype(jnp.bfloat16), 'seq')]
    psum x4 -> x0, blocking collectives: 98.3 us -> none  [the longest x1 28.6 us: per_device(): column_total = lax.psum(jnp.sum(exp_logits, axis=0), 'seq')]
    reduce_scatter x1 -> x0, waiting for transfers between devices: 96.6 us -> none  [per_device(): lax.psum_scatter(partial_sum.astype(jnp.bfloat16), 'slot', scatter_dimens...]
    dot_general x14 -> x0, matrix products: 46.4 us -> none  [the longest x1 4.98 us: per_device(): lax.dot_general(out_grad, slot_out, cols_contract, preferred_element_type...]
    unnamed x5 -> x1, waiting for transfers between devices: 44.6 us -> 0.68 us
    all_to_all x0 -> x3, blocking collectives: none -> 39.4 us  [the longest x1 15.1 us: per_device(): lax.all_to_all(pair_sum(keep, lax.ppermute(give, 'c', swap)), CHIPS, 0, 0)]
    pallas_call x0 -> x13, Pallas kernels: none -> 34.8 us  [the longest x1 6.32 us: weight_grads(): pl.pallas_call(kernel, grid=(experts,), in_specs=[in_smem(), pl.BlockSpec...]
    all_to_all x0 -> x3, starting transfers between devices: none -> 17 us  [the longest x1 8.16 us: per_device(): row_parts = lax.all_to_all(own_row, SLOT, 0, 0)]
  transfers between devices with their start and end apart: 4 -> 11, of which waited for: 4 -> 9; matrix products, arithmetic and copies ran while one was open for 2% -> 0% of each run, Pallas kernels for 0% -> 16%
where the time goes in v4:
time: 163 us; the launch traced here: 162 us
  blocking collectives  39.4 us (24%)
  Pallas kernels  34.8 us (21%)
  starting transfers between devices  28.1 us (17%)
  waiting for transfers between devices  23.7 us (15%)
  local copies, waits for them, and re-layouts  19.8 us (12%)
  between operations  14.2 us (9%)
  other arithmetic  1.78 us (1%)
    unnamed x40, local copies, waits for them, and re-layouts  19.8 us
    all_to_all x1, blocking collectives, per_device(): lax.all_to_all(pair_sum(keep, lax.ppermute(give, 'c', swap)), CHIPS, 0, 0)  15.1 us
    all_to_all x1, blocking collectives, per_device(): mine = lax.all_to_all(sent, CHIPS, 0, 0)  12.5 us
    all_to_all x1, blocking collectives, per_device(): lax.all_to_all(keys_part.reshape(seq_devices, features // seq_devices, ow...  11.7 us
    all_to_all x1, waiting for transfers between devices, per_device(): gathered = lax.all_to_all(sent, GATHERED, 0, 0)  9.89 us
    all_to_all x1, starting transfers between devices, per_device(): row_parts = lax.all_to_all(own_row, SLOT, 0, 0)  8.16 us
    pallas_call x1, Pallas kernels, weight_grads(): pl.pallas_call(kernel, grid=(experts,), in_specs=[in_smem(), pl.BlockSpec...  6.32 us
    pallas_call x1, Pallas kernels, disp_dots(): pl.pallas_call(kernel, in_specs=[in_smem()] + [whole_in_vmem()] * 6, out_...  5.43 us
  transfers between devices with their start and end apart: 11, of which 9 were waited for; matrix products, arithmetic and copies ran while one was open for 0% of the time, Pallas kernels for 16%

profile of v4, /device:TPU:1, one launch (start us, length us, event | category | flops | bytes accessed | tf_op | source)
XLA Modules:
  0.0 161.7 jit_solution(2981667748149225743)
XLA Ops:
  7.2 0.0 all-gather.3.cloned.1.call-start
  7.2 0.7 all-gather.3.cloned.1.call-update
  7.9 0.0 copy-start
  7.9 2.5 %copy-done = bf16[2048,1280]{1,0:T(8,128)(2,1)S(1)} copy-done((bf16[2048,1280]{1,0:T(8,128)(2,1)S(1)}, bf16[2048,1280]{1,0:T(8,128)(2,1)}, u32[]{:S(2)}) %copy-start) | copy-done | bytes 5242904
  10.4 1.0 copy-done.10
  11.4 2.5 %own_logits.1 = (f32[128,2048]{1,0:T(8,128)S(1)}, f32[8,1,2048]{2,1,0:T(1,128)}, f32[128,128]{1,0:T(8,128)S(1)}) custom-call(bf16[1280,128]{1,0:T(8,128)(2,1)S(1)} %copy-done.10, bf16[2048,1280]{1,0:T(8,128)(2,1)S(1)} %copy-done), custom_call_target="tpu_custom_call" | custom-call | flops 671088640 | bytes 5242880 | tf_op jit(solution)/shard_map/own_logits/pallas_call | solution.py:102
  13.8 8.2 %all-to-all-start = ((f32[8,1,2048]{2,1,0:T(1,128)}), f32[8,1,2048]{2,1,0:T(1,128)S(1)}, u32[]{:S(2)}, u32[]{:S(2)}) async-start(f32[8,1,2048]{2,1,0:T(1,128)} %get-tuple-element.38), calls=%async_computation | async-start | bytes 131072 | tf_op jit(solution)/shard_map/all_to_all | solution.py:542
  22.0 1.0 collective-permute-start
  22.9 0.1 pad_add_fusion.place_ref
  23.0 0.8 collective-permute-done.other_ref
  23.8 2.5 %copy-done.1 = bf16[2048,1280]{1,0:T(8,128)(2,1)S(1)} copy-done((bf16[2048,1280]{1,0:T(8,128)(2,1)S(1)}, bf16[2048,1280]{1,0:T(8,128)(2,1)}, u32[]{:S(2)}) %copy-start.1) | copy-done | bytes 5242904
  26.3 0.9 dispatch_part.1.in_ref
  27.3 1.4 all-to-all-done.row_ref
  28.6 2.5 %copy-done.3 = bf16[2048,1280]{1,0:T(8,128)(2,1)S(1)} copy-done((bf16[2048,1280]{1,0:T(8,128)(2,1)S(1)}, bf16[2048,1280]{1,0:T(8,128)(2,1)}, u32[]{:S(2)}) %copy-start.3) | copy-done | bytes 5242904
  31.1 1.5 combine_part.1
  32.6 2.3 %collective-permute-start.1 = (bf16[8,16,1280]{2,1,0:T(8,128)(2,1)S(1)}, bf16[8,16,1280]{2,1,0:T(8,128)(2,1)S(1)}, u32[]{:S(2)}, u32[]{:S(2)}) collective-permute-start(bf16[8,16,1280]{2,1,0:T(8,128)(2,1)S(1)} %get-tuple-element.41), channel_id=1, source_target_pairs={{0,8},{8,0},{1,9},{9,1},{2,10},{10,2},{3,11},{11,3},{4,12},{12,4},... | collective-permute-start | bytes 983048 | tf_op jit(solution)/shard_map/ppermute | solution.py:547
  35.0 1.3 collective-permute-done.1.received_ref
  36.2 0.1 pair_sum.2
  36.3 15.1 %all_to_all.30.parts_ref = bf16[8,16,1408]{2,1,0:T(8,128)(2,1)S(1)} all-to-all(bf16[8,16,1408]{2,1,0:T(8,128)(2,1)S(1)} %pair_sum.2), channel_id=1, replica_groups=mesh['zl'=2,'y'=4,'c'=2,'xa'=2,'xb'=2,'zh'=2] {'zl','y'}, dimensions={0} | all-to-all | bytes 720896 | tf_op jit(solution)/shard_map/all_to_all | solution.py:547
  51.5 0.2 sum_slots.1
  51.7 12.5 %all_to_all.31.mine_ref = bf16[8,16,1280]{2,1,0:T(8,128)(2,1)S(1)} all-to-all(bf16[8,16,1280]{2,1,0:T(8,128)(2,1)S(1)} %get-tuple-element.42), channel_id=1, replica_groups=mesh['zl'=2,'y'=4,'c'=2,'xa'=2,'xb'=2,'zh'=2] {'zl','y'}, dimensions={0} | all-to-all | bytes 655360 | tf_op jit(solution)/shard_map/all_to_all | solution.py:549
  64.2 1.1 collective-permute-start.2
  65.3 1.3 collective-permute-done.2.other_ref
  66.6 0.0 copy-done.6
  66.6 0.0 copy-done.7
  66.6 5.2 %experts_part.1 = (bf16[8,16,1280]{2,1,0:T(8,128)(2,1)S(1)}, bf16[8,16,1280]{2,1,0:T(8,128)(2,1)S(1)}, bf16[8,16,192]{2,1,0:T(8,128)(2,1)S(1)}, bf16[8,16,192]{2,1,0:T(8,128)(2,1)S(1)}) custom-call(s32[3]{0:T(128)S(1)} %pad_add_fusion.place_ref, bf16[8,16,1280]{2,1,0:T(8,128)(2,1)S(1)} %all_to_all.31.mine_ref, ...), custom_call_target="tpu_custom_call" | custom-call | flops 251658240 | bytes 7864320 | tf_op jit(solution)/shard_map/experts_part/pallas_call | solution.py:277
  71.7 0.0 copy-done.8
  71.7 0.6 copy-done.13
  72.4 0.6 copy-done.15
  73.0 0.4 collective-permute-start.3
  73.4 1.3 collective-permute-done.3.received_ref
  74.6 0.8 pair_sum.3
  75.4 3.4 %all-to-all-start.3 = ((bf16[8,16,1280]{2,1,0:T(8,128)(2,1)}), bf16[8,16,1280]{2,1,0:T(8,128)(2,1)S(1)}, u32[]{:S(2)}, u32[]{:S(2)}) async-start(bf16[8,16,1280]{2,1,0:T(8,128)(2,1)} %pair_sum.3), calls=%async_computation.3 | async-start | bytes 655360 | tf_op jit(solution)/shard_map/all_to_all | solution.py:555
  78.9 0.0 copy-start.2
  78.9 2.5 %copy-done.2 = bf16[2048,1280]{1,0:T(8,128)(2,1)S(1)} copy-done((bf16[2048,1280]{1,0:T(8,128)(2,1)S(1)}, bf16[2048,1280]{1,0:T(8,128)(2,1)}, u32[]{:S(2)}) %copy-start.2) | copy-done | bytes 5242904
  81.4 1.3 copy-done.17
  82.7 3.5 %all_exps.1 = (bf16[512,2048]{1,0:T(8,128)(2,1)S(1)}, bf16[2,160,512]{2,1,0:T(8,128)(2,1)S(1)}) custom-call(s32[3]{0:T(128)S(1)} %pad_add_fusion.place_ref, bf16[4,1280,128]{2,1,0:T(8,128)(2,1)S(1)} %bitcast.10, bf16[2048,1280]{1,0:T(8,128)(2,1)S(1)} %copy-done.2), custom_call_target="tpu_custom_call" | custom-call | flops 2684354560 | bytes 5242880 | tf_op jit(solution)/shard_map/all_exps/pallas_call | solution.py:374
  86.2 0.0 copy-start.11
  86.2 0.8 all-to-all-done.3.terms_ref
  87.0 0.1 sum_terms.1
  87.1 0.0 copy-start.5
  87.1 1.1 copy-done.5
  88.2 0.0 copy-done.11
  88.2 5.4 %all-to-all-start.4 = ((bf16[32,16,1408]{2,1,0:T(8,128)(2,1)}), bf16[32,16,1408]{2,1,0:T(8,128)(2,1)}, u32[]{:S(2)}, u32[]{:S(2)}) async-start(bf16[32,16,1408]{2,1,0:T(8,128)(2,1)} %copy-done.5), calls=%async_computation.4 | async-start | bytes 2883584 | tf_op jit(solution)/shard_map/all_to_all | solution.py:559
  93.6 0.0 copy-start.9
  93.6 1.0 copy-done.9
  94.6 0.8 copy-done.14
  95.5 0.8 copy-done.16
  96.3 6.3 %weight_grads.1 = (bf16[8,192,1280]{2,1,0:T(8,128)(2,1)}, bf16[8,192,1280]{2,1,0:T(8,128)(2,1)}) custom-call(s32[3]{0:T(128)S(1)} %pad_add_fusion.place_ref, bf16[8,16,1280]{2,1,0:T(8,128)(2,1)S(1)} %all_to_all.31.mine_ref, bf16[8,16,1280]{2,1,0:T(8,128)(2,1)S(1)} %copy-done.9, bf16[8,16,192]{2,1,0:T(8,128)(2,1)S(1)} %copy-done.14, ...), custom_call_target="tpu_custom_call" | custom-call | flops 125829120 | bytes 7864320 | tf_op jit(solution)/shard_map/weight_grads/pallas_call | solution.py:308
  102.6 9.9 %all-to-all-done.4.mine_ref = bf16[32,16,1408]{2,1,0:T(8,128)(2,1)} async-done(((bf16[32,16,1408]{2,1,0:T(8,128)(2,1)}), bf16[32,16,1408]{2,1,0:T(8,128)(2,1)}, u32[]{:S(2)}, u32[]{:S(2)}) %all-to-all-start.4) | async-done | bytes 1441824 | tf_op jit(solution)/shard_map/all_to_all | solution.py:559
  112.5 3.2 %collective-permute-start.4 = (bf16[32,16,1408]{2,1,0:T(8,128)(2,1)}, bf16[32,16,1408]{2,1,0:T(8,128)(2,1)S(1)}, u32[]{:S(2)}, u32[]{:S(2)}) collective-permute-start(bf16[32,16,1408]{2,1,0:T(8,128)(2,1)} %all-to-all-done.4.mine_ref), channel_id=1, source_target_pairs={{0,8},{8,0},{1,9},{9,1},{2,10},{10,2},{3,11},{11,3},{4,12},{12,4},... | collective-permute-start | bytes 4325384 | tf_op jit(solution)/shard_map/ppermute | solution.py:562
  115.7 3.1 %collective-permute-done.4.other_ref = bf16[32,16,1408]{2,1,0:T(8,128)(2,1)S(1)} collective-permute-done((bf16[32,16,1408]{2,1,0:T(8,128)(2,1)}, bf16[32,16,1408]{2,1,0:T(8,128)(2,1)S(1)}, u32[]{:S(2)}, u32[]{:S(2)}) %collective-permute-start.4) | collective-permute-done | bytes 1441824 | tf_op jit(solution)/shard_map/ppermute | solution.py:562
  118.7 2.5 %copy-done.4 = bf16[2048,1280]{1,0:T(8,128)(2,1)S(1)} copy-done((bf16[2048,1280]{1,0:T(8,128)(2,1)S(1)}, bf16[2048,1280]{1,0:T(8,128)(2,1)}, u32[]{:S(2)}) %copy-start.4) | copy-done | bytes 5242904
  121.2 4.9 %comb_dots.1 = (f32[512,2048]{1,0:T(8,128)S(1)}, f32[1,2048]{1,0:T(1,128)S(1)}) custom-call(s32[3]{0:T(128)S(1)} %pad_add_fusion.place_ref, bf16[512,2048]{1,0:T(8,128)(2,1)S(1)} %get-tuple-element.50.exp_ref, bf16[2048,1280]{1,0:T(8,128)(2,1)S(1)} %copy-done.4, f32[8,1,2048]{2,1,0:T(1,128)S(1)} %all-to-all-done.row_ref, ...), custom_call_target="tpu_custom_call" | custom-call | flops 2684354560 | bytes 5242880 | tf_op jit(solution)/shard_map/comb_dots/pallas_call | solution.py:421
  126.1 1.7 %collective-permute-start.5 = (f32[1,2048]{1,0:T(1,128)S(1)}, f32[1,2048]{1,0:T(1,128)S(1)}, u32[]{:S(2)}, u32[]{:S(2)}) collective-permute-start(f32[1,2048]{1,0:T(1,128)S(1)} %get-tuple-element.62.sum_ref), channel_id=1, source_target_pairs={{0,4},{4,0},{1,5},{5,1},{2,6},{6,2},{3,7},{7,3},{8,12},{12,8},{9,1... | collective-permute-start | bytes 24584 | tf_op jit(solution)/shard_map/ppermute | solution.py:565
  127.8 0.0 slice-done.1
  127.8 5.4 %disp_dots.1 = (f32[512,2048]{1,0:T(8,128)S(1)}, bf16[512,2048]{1,0:T(8,128)(2,1)S(1)}, bf16[2,160,512]{2,1,0:T(8,128)(2,1)S(1)}) custom-call(s32[3]{0:T(128)S(1)} %pad_add_fusion.place_ref, bf16[512,2048]{1,0:T(8,128)(2,1)S(1)} %get-tuple-element.50.exp_ref, f32[512,2048]{1,0:T(8,128)S(1)} %get-tuple-element.59.dot_ref, bf16[2048,1280]{1,0:T(8,128)(2,1)S(1)} %bitcast.8, ...), custom_call_target="tpu_custom_call" | custom-call | flops 2684354560 | bytes 5242880 | tf_op jit(solution)/shard_map/disp_dots/pallas_call | solution.py:464
  133.2 0.0 collective-permute-done.5.other_ref
  133.3 3.3 %logit_grads.1 = (bf16[1280,128]{1,0:T(8,128)(2,1)S(1)}, bf16[160,2048]{1,0:T(8,128)(2,1)S(1)}, f32[160,2048]{1,0:T(8,128)S(1)}) custom-call(s32[3]{0:T(128)S(1)} %pad_add_fusion.place_ref, bf16[512,2048]{1,0:T(8,128)(2,1)S(1)} %get-tuple-element.50.exp_ref, f32[512,2048]{1,0:T(8,128)S(1)} %get-tuple-element.60.terms_ref, ...), custom_call_target="tpu_custom_call" | custom-call | flops 671088640 | bytes 5242880 | tf_op jit(solution)/shard_map/logit_grads/pallas_call | solution.py:510
  136.6 1.4 collective-permute-start.6
  138.0 11.7 %all_to_all.32 = bf16[16,80,128]{2,1,0:T(8,128)(2,1)S(1)} all-to-all(bf16[16,80,128]{2,1,0:T(8,128)(2,1)S(1)} %bitcast.9), channel_id=1, replica_groups=mesh['zl'=2,'y'=4,'c'=2,'xa'=2,'xb'=2,'zh'=2] {'zl','y','c'}, dimensions={0} | all-to-all | bytes 655360 | tf_op jit(solution)/shard_map/all_to_all | solution.py:573
  149.7 0.7 convert_reduce_fusion
  150.4 3.4 %collective-permute-done.6 = bf16[160,2048]{1,0:T(8,128)(2,1)S(1)} collective-permute-done((bf16[160,2048]{1,0:T(8,128)(2,1)S(1)}, bf16[160,2048]{1,0:T(8,128)(2,1)S(1)}, u32[]{:S(2)}, u32[]{:S(2)}) %collective-permute-start.6) | collective-permute-done | bytes 655392 | tf_op jit(solution)/shard_map/ppermute | solution.py:572
  153.8 1.0 fusion
  (19 shorter events, 0.0 us)
Async XLA Ops:
  7.2 68.3 %all-gather.3.cloned.1.call-start = ((), (), s32[]{:S(2)}) async-start(), calls=%async_computation.6 | async-start | bytes 1638400 | tf_op jit(solution)/shard_map/all_gather | solution.py:539
  7.9 2.5 %copy-start = (bf16[2048,1280]{1,0:T(8,128)(2,1)S(1)}, bf16[2048,1280]{1,0:T(8,128)(2,1)}, u32[]{:S(2)}) copy-start(bf16[2048,1280]{1,0:T(8,128)(2,1)} %tokens_ref.9) | copy-start | bytes 15728644
  10.4 1.0 copy-start.10
  13.8 14.8 %all-to-all-start = ((f32[8,1,2048]{2,1,0:T(1,128)}), f32[8,1,2048]{2,1,0:T(1,128)S(1)}, u32[]{:S(2)}, u32[]{:S(2)}) async-start(f32[8,1,2048]{2,1,0:T(1,128)} %get-tuple-element.38), calls=%async_computation | async-start | bytes 131072 | tf_op jit(solution)/shard_map/all_to_all | solution.py:542
  22.0 1.9 %collective-permute-start = (f32[128,128]{1,0:T(8,128)S(1)}, f32[128,128]{1,0:T(8,128)S(1)}, u32[]{:S(2)}, u32[]{:S(2)}) collective-permute-start(f32[128,128]{1,0:T(8,128)S(1)} %get-tuple-element.39.column_ref), channel_id=1, source_target_pairs={{0,8},{8,0},{1,9},{9,1},{2,10},{10,2},{3,11},{11,3},{4,12},{12,4},... | collective-permute-start | bytes 196616 | tf_op jit(solution)/shard_map/ppermute | solution.py:541
  23.8 2.5 %copy-start.1 = (bf16[2048,1280]{1,0:T(8,128)(2,1)S(1)}, bf16[2048,1280]{1,0:T(8,128)(2,1)}, u32[]{:S(2)}) copy-start(bf16[2048,1280]{1,0:T(8,128)(2,1)} %tokens_ref.9) | copy-start | bytes 15728644
  28.6 2.5 %copy-start.3 = (bf16[2048,1280]{1,0:T(8,128)(2,1)S(1)}, bf16[2048,1280]{1,0:T(8,128)(2,1)}, u32[]{:S(2)}) copy-start(bf16[2048,1280]{1,0:T(8,128)(2,1)} %grad_ref.3) | copy-start | bytes 15728644
  31.1 35.4 %copy-start.6 = (bf16[8,192,1280]{2,1,0:T(8,128)(2,1)S(1)}, bf16[8,192,1280]{2,1,0:T(8,128)(2,1)}, u32[]{:S(2)}) copy-start(bf16[8,192,1280]{2,1,0:T(8,128)(2,1)} %w_in_ref.1) | copy-start | bytes 11796484
  31.1 35.4 %copy-start.7 = (bf16[8,192,1280]{2,1,0:T(8,128)(2,1)S(1)}, bf16[8,192,1280]{2,1,0:T(8,128)(2,1)}, u32[]{:S(2)}) copy-start(bf16[8,192,1280]{2,1,0:T(8,128)(2,1)} %w_out_ref.1) | copy-start | bytes 11796484
  32.6 3.6 %collective-permute-start.1 = (bf16[8,16,1280]{2,1,0:T(8,128)(2,1)S(1)}, bf16[8,16,1280]{2,1,0:T(8,128)(2,1)S(1)}, u32[]{:S(2)}, u32[]{:S(2)}) collective-permute-start(bf16[8,16,1280]{2,1,0:T(8,128)(2,1)S(1)} %get-tuple-element.41), channel_id=1, source_target_pairs={{0,8},{8,0},{1,9},{9,1},{2,10},{10,2},{3,11},{11,3},{4,12},{12,4},... | collective-permute-start | bytes 983048 | tf_op jit(solution)/shard_map/ppermute | solution.py:547
  64.2 2.3 %collective-permute-start.2 = (bf16[8,16,1280]{2,1,0:T(8,128)(2,1)S(1)}, bf16[8,16,1280]{2,1,0:T(8,128)(2,1)S(1)}, u32[]{:S(2)}, u32[]{:S(2)}) collective-permute-start(bf16[8,16,1280]{2,1,0:T(8,128)(2,1)S(1)} %all_to_all.31.mine_ref), channel_id=1, source_target_pairs={{0,8},{8,0},{1,9},{9,1},{2,10},{10,2},{3,11},{11,3},{4,12},{12,4},... | collective-permute-start | bytes 983048 | tf_op jit(solution)/shard_map/ppermute | solution.py:550
  66.6 5.2 %copy-start.8 = (bf16[8,16,1280]{2,1,0:T(8,128)(2,1)}, bf16[8,16,1280]{2,1,0:T(8,128)(2,1)S(1)}, u32[]{:S(2)}) copy-start(bf16[8,16,1280]{2,1,0:T(8,128)(2,1)S(1)} %collective-permute-done.2.other_ref) | copy-start | bytes 983044
  71.7 0.6 copy-start.13
  72.4 0.6 copy-start.15
  73.0 1.6 %collective-permute-start.3 = (bf16[8,16,1280]{2,1,0:T(8,128)(2,1)S(1)}, bf16[8,16,1280]{2,1,0:T(8,128)(2,1)S(1)}, u32[]{:S(2)}, u32[]{:S(2)}) collective-permute-start(bf16[8,16,1280]{2,1,0:T(8,128)(2,1)S(1)} %get-tuple-element.44), channel_id=1, source_target_pairs={{0,8},{8,0},{1,9},{9,1},{2,10},{10,2},{3,11},{11,3},{4,12},{12,4},... | collective-permute-start | bytes 983048 | tf_op jit(solution)/shard_map/ppermute | solution.py:553
  75.4 11.6 %all-to-all-start.3 = ((bf16[8,16,1280]{2,1,0:T(8,128)(2,1)}), bf16[8,16,1280]{2,1,0:T(8,128)(2,1)S(1)}, u32[]{:S(2)}, u32[]{:S(2)}) async-start(bf16[8,16,1280]{2,1,0:T(8,128)(2,1)} %pair_sum.3), calls=%async_computation.3 | async-start | bytes 655360 | tf_op jit(solution)/shard_map/all_to_all | solution.py:555
  78.9 2.5 %copy-start.2 = (bf16[2048,1280]{1,0:T(8,128)(2,1)S(1)}, bf16[2048,1280]{1,0:T(8,128)(2,1)}, u32[]{:S(2)}) copy-start(bf16[2048,1280]{1,0:T(8,128)(2,1)} %tokens_ref.9) | copy-start | bytes 15728644
  81.4 1.3 copy-start.17
  86.2 2.0 %copy-start.11 = (bf16[2,160,512]{2,1,0:T(8,128)(2,1)}, bf16[2,160,512]{2,1,0:T(8,128)(2,1)S(1)}, u32[]{:S(2)}) copy-start(bf16[2,160,512]{2,1,0:T(8,128)(2,1)S(1)} %get-tuple-element.63.keys_rows_ref) | copy-start | bytes 983044
  87.1 1.1 copy-start.5
  88.2 24.3 %all-to-all-start.4 = ((bf16[32,16,1408]{2,1,0:T(8,128)(2,1)}), bf16[32,16,1408]{2,1,0:T(8,128)(2,1)}, u32[]{:S(2)}, u32[]{:S(2)}) async-start(bf16[32,16,1408]{2,1,0:T(8,128)(2,1)} %copy-done.5), calls=%async_computation.4 | async-start | bytes 2883584 | tf_op jit(solution)/shard_map/all_to_all | solution.py:559
  93.6 1.0 copy-start.9
  94.6 0.8 copy-start.14
  95.4 0.8 copy-start.16
  96.3 31.5 %slice-start = ((s8[5242880]{0:T(1024)(128)(4,1)}), s8[1048576]{0:T(1024)(128)(4,1)S(1)}, s32[]{:S(2)}) async-start(s8[5242880]{0:T(1024)(128)(4,1)} %bitcast.7), calls=%async_computation.7 | async-start | bytes 2097152
  112.5 15.3 %slice-start.1 = ((s8[5242880]{0:T(1024)(128)(4,1)}), s8[4194304]{0:T(1024)(128)(4,1)S(1)}, s32[]{:S(2)}) async-start(s8[5242880]{0:T(1024)(128)(4,1)} %bitcast.7), calls=%async_computation.8 | async-start | bytes 8388608
  112.5 6.2 %collective-permute-start.4 = (bf16[32,16,1408]{2,1,0:T(8,128)(2,1)}, bf16[32,16,1408]{2,1,0:T(8,128)(2,1)S(1)}, u32[]{:S(2)}, u32[]{:S(2)}) collective-permute-start(bf16[32,16,1408]{2,1,0:T(8,128)(2,1)} %all-to-all-done.4.mine_ref), channel_id=1, source_target_pairs={{0,8},{8,0},{1,9},{9,1},{2,10},{10,2},{3,11},{11,3},{4,12},{12,4},... | collective-permute-start | bytes 4325384 | tf_op jit(solution)/shard_map/ppermute | solution.py:562
  118.7 2.5 %copy-start.4 = (bf16[2048,1280]{1,0:T(8,128)(2,1)S(1)}, bf16[2048,1280]{1,0:T(8,128)(2,1)}, u32[]{:S(2)}) copy-start(bf16[2048,1280]{1,0:T(8,128)(2,1)} %grad_ref.3) | copy-start | bytes 15728644
  126.1 7.2 %collective-permute-start.5 = (f32[1,2048]{1,0:T(1,128)S(1)}, f32[1,2048]{1,0:T(1,128)S(1)}, u32[]{:S(2)}, u32[]{:S(2)}) collective-permute-start(f32[1,2048]{1,0:T(1,128)S(1)} %get-tuple-element.62.sum_ref), channel_id=1, source_target_pairs={{0,4},{4,0},{1,5},{5,1},{2,6},{6,2},{3,7},{7,3},{8,12},{12,8},{9,1... | collective-permute-start | bytes 24584 | tf_op jit(solution)/shard_map/ppermute | solution.py:565
  127.8 5.5 %copy-start.12 = (bf16[2,160,512]{2,1,0:T(8,128)(2,1)S(1)}, bf16[2,160,512]{2,1,0:T(8,128)(2,1)}, u32[]{:S(2)}) copy-start(bf16[2,160,512]{2,1,0:T(8,128)(2,1)} %copy-done.11) | copy-start | bytes 983044
  136.6 17.2 %collective-permute-start.6 = (bf16[160,2048]{1,0:T(8,128)(2,1)S(1)}, bf16[160,2048]{1,0:T(8,128)(2,1)S(1)}, u32[]{:S(2)}, u32[]{:S(2)}) collective-permute-start(bf16[160,2048]{1,0:T(8,128)(2,1)S(1)} %get-tuple-element.66), channel_id=1, source_target_pairs={{0,4},{4,0},{1,5},{5,1},{2,6},{6,2},{3,7},{7,3},{8,12},{12,8},{9,1... | collective-permute-start | bytes 1966088 | tf_op jit(solution)/shard_map/ppermute | solution.py:572
Sparse Core Ops, SparseCore 0:
  9.7 43.1 all-gather.2

commit v5 on v4

--- a/solution.py
+++ b/solution.py
@@ -246,7 +246,7 @@
     block = mine.shape[1]
     half = features // 2
 
-    def kernel(place_ref, mine_ref, other_ref, w_in_ref, w_out_ref, keep_ref, give_ref, act_ref, pre_ref):
+    def kernel(place_ref, mine_ref, other_ref, w_in_ref, w_out_ref, keep_ref, give_ref, act_hbm, pre_hbm, act_ref, pre_ref, sems):
         here, there = halves(place_ref, half)
 
         def inward(at, weights_ref, e):
@@ -273,17 +273,24 @@
                 ).astype(bf16)
             act_ref[e] = act
             pre_ref[e] = pre
+        first = pltpu.make_async_copy(act_ref, act_hbm, sems.at[0])
+        second = pltpu.make_async_copy(pre_ref, pre_hbm, sems.at[1])
+        first.start()
+        second.start()
+        first.wait()
+        second.wait()
 
     return pl.pallas_call(
         kernel,
         in_specs=[in_smem()] + [whole_in_vmem()] * 4,
-        out_specs=[whole_in_vmem()] * 4,
+        out_specs=[whole_in_vmem()] * 2 + [pl.BlockSpec(memory_space=pltpu.HBM)] * 2,
         out_shape=[
             jax.ShapeDtypeStruct((experts, block, features), bf16),
             jax.ShapeDtypeStruct((experts, block, features), bf16),
             jax.ShapeDtypeStruct((experts, block, hidden), bf16),
             jax.ShapeDtypeStruct((experts, block, hidden), bf16),
         ],
+        scratch_shapes=[pltpu.VMEM((experts, block, hidden), bf16)] * 2 + [pltpu.SemaphoreType.DMA((2,))],
         compiler_params=params(GRANT),
         cost_estimate=cost(8 * experts * block * hidden * features, 4 * experts * hidden * features),
         name="experts_part",
@@ -350,19 +357,33 @@
     )(terms, slot_in, column)
 
 
-def all_exps(place, keys_all, tokens, width, tile=256):
-    blocks, features, block = keys_all.shape
-    slots = blocks * block
+def all_exps(place, slot_keys, near_keys, far_keys, tokens, width, tile=256):
+    features, block = slot_keys.shape
     count = tokens.shape[0]
     half = features // 2
-
-    def kernel(place_ref, keys_ref, tokens_ref, exp_ref, rows_ref, turned_ref):
-        for at in range(blocks):
-            cut = slice(at * block, (at + 1) * block)
-            turned_ref[cut, :] = keys_ref[at].T
-            for side in range(2):
-                first = pl.multiple_of(place_ref[1] * width + side * half, 16)
-                rows_ref[side, :, cut] = keys_ref[at, pl.ds(first, width), :]
+    others = len(near_keys)
+    slots = (others + 1) * block
+
+    def kernel(place_ref, own_ref, *refs):
+        near_refs, far_refs = refs[:others], refs[others : 2 * others]
+        tokens_ref, exp_ref, rows_ref, turned_ref = refs[2 * others :]
+        core, at_own = place_ref[0], place_ref[1]
+        here, there = halves(place_ref, half)
+
+        def spot(at):
+            return pl.ds(pl.multiple_of(at * block, block), block)
+
+        rows = pl.ds(pl.multiple_of(at_own * width, 16), width)
+        turned_ref[spot(at_own), :] = own_ref[...].T
+        for side in range(2):
+            first = pl.multiple_of(at_own * width + side * half, 16)
+            rows_ref[side, :, spot(at_own)] = own_ref[pl.ds(first, width), :]
+        for at in range(others):
+            place_at = spot(at_own ^ (at + 1))
+            turned_ref[place_at, here] = near_refs[at][...].T
+            turned_ref[place_at, there] = far_refs[at][...].T
+            rows_ref[core, :, place_at] = near_refs[at][rows, :]
+            rows_ref[1 - core, :, place_at] = far_refs[at][rows, :]
         for at in range(0, count, tile):
             exp_ref[:, at : at + tile] = jnp.exp(
                 lax.dot_general(
@@ -373,7 +394,7 @@
 
     return pl.pallas_call(
         kernel,
-        in_specs=[in_smem()] + [whole_in_vmem()] * 2,
+        in_specs=[in_smem()] + [whole_in_vmem()] * (2 * others + 2),
         out_specs=[whole_in_vmem()] * 2,
         out_shape=[
             jax.ShapeDtypeStruct((slots, count), bf16),
@@ -383,37 +404,49 @@
         compiler_params=params(GRANT),
         cost_estimate=cost(2 * slots * features * count, 2 * features * count),
         name="all_exps",
-    )(place, keys_all, tokens)
-
-
-def width_dot(place_ref, mine_ref, other_ref, ref, at, rows):
-    blocks, block, _unused = mine_ref.shape
+    )(place, slot_keys, *near_keys, *far_keys, tokens)
+
+
+def half_dot(place_ref, gathered_ref, ref, at, rows, own):
+    blocks, block, _unused = gathered_ref.shape
     half = ref.shape[1] // 2
     here, there = halves(place_ref, half)
-    near = lax.dot_general(
-        mine_ref[:, :, at * half : (at + 1) * half].reshape(blocks * block, half),
-        ref[rows, here],
+    return lax.dot_general(
+        gathered_ref[:, :, at * half : (at + 1) * half].reshape(blocks * block, half),
+        ref[rows, here if own else there],
         cols_contract,
         preferred_element_type=f32,
     )
-    far = lax.dot_general(
-        other_ref[:, :, at * half : (at + 1) * half].reshape(blocks * block, half),
-        ref[rows, there],
-        cols_contract,
-        preferred_element_type=f32,
-    )
-    return near + far
-
-
-def comb_dots(place, exps, out_grad, row_parts, mine, other, tile=256):
+
+
+def near_dots(place, out_grad, mine, slots, tile=256):
+    count, features = out_grad.shape
+
+    def kernel(place_ref, grad_ref, mine_ref, dot_ref):
+        for at in range(0, count, tile):
+            cut = slice(at, at + tile)
+            dot_ref[:, cut] = half_dot(place_ref, mine_ref, grad_ref, 0, cut, True)
+
+    return pl.pallas_call(
+        kernel,
+        in_specs=[in_smem()] + [whole_in_vmem()] * 2,
+        out_specs=whole_in_vmem(),
+        out_shape=jax.ShapeDtypeStruct((slots, count), f32),
+        compiler_params=params(GRANT),
+        cost_estimate=cost(slots * features * count, features * count),
+        name="near_dots",
+    )(place, out_grad, mine)
+
+
+def comb_dots(place, exps, near, out_grad, row_parts, other, tile=256):
     slots, count = exps.shape
     features = out_grad.shape[1]
 
-    def kernel(place_ref, exp_ref, grad_ref, row_ref, mine_ref, other_ref, dot_ref, sum_ref):
+    def kernel(place_ref, exp_ref, near_ref, grad_ref, row_ref, other_ref, dot_ref, sum_ref):
         for at in range(0, count, tile):
             cut = slice(at, at + tile)
             power, inverse = guarded(jnp.sum(row_ref[:, :, cut], axis=0))
-            dots = width_dot(place_ref, mine_ref, other_ref, grad_ref, 0, cut)
+            dots = near_ref[:, cut] + half_dot(place_ref, other_ref, grad_ref, 0, cut, False)
             dot_ref[:, cut] = dots
             terms = (exp_ref[:, cut].astype(f32) * power) * dots
             sum_ref[:, cut] = jnp.sum(terms, axis=0, keepdims=True) * inverse
@@ -427,9 +460,9 @@
             jax.ShapeDtypeStruct((1, count), f32),
         ],
         compiler_params=params(GRANT),
-        cost_estimate=cost(2 * slots * features * count, 2 * features * count),
+        cost_estimate=cost(slots * features * count, features * count),
         name="comb_dots",
-    )(place, exps, out_grad, row_parts, mine, other)
+    )(place, exps, near, out_grad, row_parts, other)
 
 
 def disp_dots(place, exps, dots, tokens, row_parts, mine, other, width, tile=256):
@@ -457,7 +490,8 @@
             exps_here = exp_ref[:, cut].astype(f32)
             dispatch = (exps_here * power_ref[...]) * inverse_ref[...]
             dispatch_ref[:, cut] = dispatch.astype(bf16)
-            disp_dot = width_dot(place_ref, mine_ref, other_ref, tokens_ref, 1, cut)
+            disp_dot = half_dot(place_ref, mine_ref, tokens_ref, 1, cut, True)
+            disp_dot = disp_dot + half_dot(place_ref, other_ref, tokens_ref, 1, cut, False)
             combine = (exps_here * power) * inverse
             terms_ref[:, cut] = combine * dot_ref[:, cut] + dispatch * (disp_dot - total_ref[...])
 
@@ -477,50 +511,72 @@
     )(place, exps, dots, tokens, row_parts, mine, other)
 
 
-def logit_grads(place, exps, terms, dispatch, tokens, row_parts, row, row_other, keys_rows, grad_rows, own_slots, tile=256):
+def columns_dot(place_ref, keys_rows_ref, grad_rows_ref, logit, dispatch, own):
+    core, half_at = place_ref[0], place_ref[2]
+    near = jnp.where(core == half_at, 0, 1)
+    at_keys, at_grad = (half_at, near) if own else (1 - half_at, 1 - near)
+    total = jnp.dot(keys_rows_ref[at_keys], logit, preferred_element_type=f32)
+    return total + jnp.dot(grad_rows_ref[at_grad], dispatch, preferred_element_type=f32)
+
+
+def logit_grads(place, exps, terms, dispatch, row_parts, row, row_other, keys_rows, grad_rows, tile=256):
     slots, count = exps.shape
-    features = tokens.shape[1]
     width = keys_rows.shape[1]
 
     def kernel(
-        place_ref, exp_ref, terms_ref, dispatch_ref, tokens_ref, row_ref, sum_ref, other_ref, keys_rows_ref, grad_rows_ref,
-        keys_ref, sent_ref, own_ref, logit_ref,
+        place_ref, exp_ref, terms_ref, dispatch_ref, row_ref, sum_ref, other_ref, keys_rows_ref, grad_rows_ref,
+        logit_ref, sent_ref,
     ):
-        core, half_at = place_ref[0], place_ref[2]
-        near = jnp.where(core == half_at, 0, 1)
         for at in range(0, count, tile):
             cut = slice(at, at + tile)
             power, inverse = guarded(jnp.sum(row_ref[:, :, cut], axis=0))
             weight = (sum_ref[:, cut] + other_ref[:, cut]) * inverse
             exps_here = exp_ref[:, cut].astype(f32)
             logit_ref[:, cut] = (terms_ref[:, cut] - (exps_here * power) * weight).astype(bf16)
-            for out_ref, at_keys, at_grad in (
-                (sent_ref, 1 - half_at, 1 - near),
-                (own_ref, half_at, near),
-            ):
-                total = jnp.dot(keys_rows_ref[at_keys], logit_ref[:, cut], preferred_element_type=f32)
-                total = total + jnp.dot(
-                    grad_rows_ref[at_grad], dispatch_ref[:, cut], preferred_element_type=f32
-                )
-                out_ref[:, cut] = total.astype(out_ref.dtype)
+            sent_ref[:, cut] = columns_dot(
+                place_ref, keys_rows_ref, grad_rows_ref, logit_ref[:, cut], dispatch_ref[:, cut], False
+            ).astype(bf16)
+
+    return pl.pallas_call(
+        kernel,
+        in_specs=[in_smem()] + [whole_in_vmem()] * 8,
+        out_specs=[whole_in_vmem()] * 2,
+        out_shape=[
+            jax.ShapeDtypeStruct((slots, count), bf16),
+            jax.ShapeDtypeStruct((width, count), bf16),
+        ],
+        compiler_params=params(GRANT),
+        cost_estimate=cost(4 * slots * width * count, 4 * slots * count),
+        name="logit_grads",
+    )(place, exps, terms, dispatch, row_parts, row, row_other, keys_rows, grad_rows)
+
+
+def own_parts(place, logit, dispatch, tokens, keys_rows, grad_rows, own_slots, tile=256):
+    count, features = tokens.shape
+    width = keys_rows.shape[1]
+
+    def kernel(place_ref, logit_ref, dispatch_ref, tokens_ref, keys_rows_ref, grad_rows_ref, keys_ref, own_ref):
         own = pl.ds(pl.multiple_of(place_ref[1] * own_slots, own_slots), own_slots)
         total = jnp.dot(logit_ref[own, :], tokens_ref[...], preferred_element_type=f32)
         keys_ref[...] = total.T.astype(bf16)
-
-    return pl.pallas_call(
-        kernel,
-        in_specs=[in_smem()] + [whole_in_vmem()] * 9,
-        out_specs=[whole_in_vmem()] * 3,
+        for at in range(0, count, tile):
+            cut = slice(at, at + tile)
+            own_ref[:, cut] = columns_dot(
+                place_ref, keys_rows_ref, grad_rows_ref, logit_ref[:, cut], dispatch_ref[:, cut], True
+            )
+
+    return pl.pallas_call(
+        kernel,
+        in_specs=[in_smem()] + [whole_in_vmem()] * 5,
+        out_specs=[whole_in_vmem()] * 2,
         out_shape=[
             jax.ShapeDtypeStruct((features, own_slots), bf16),
-            jax.ShapeDtypeStruct((width, count), bf16),
             jax.ShapeDtypeStruct((width, count), f32),
         ],
-        scratch_shapes=[pltpu.VMEM((slots, count), bf16)],
         compiler_params=params(GRANT),
         cost_estimate=cost(2 * own_slots * features * count, 2 * features * count),
-        name="logit_grads",
-    )(place, exps, terms, dispatch, tokens, row_parts, row, row_other, keys_rows, grad_rows)
+        name="own_parts",
+    )(place, logit, dispatch, tokens, keys_rows, grad_rows)
 
 
 def per_device(tokens, slot_keys, w_in, w_out, out_grad):
@@ -536,8 +592,16 @@
         [lax.axis_index("c"), lax.axis_index(KEYS), lax.axis_index("xa")]
     ).astype(jnp.int32)
 
-    keys_all = lax.all_gather(slot_keys, KEYS, axis=0, tiled=False)
+    half = features // 2
+    own_half = lax.dynamic_slice_in_dim(slot_keys, lax.axis_index("c") * half, half, 0)
+    blocks = lax.axis_size(KEYS)
+    near_keys = [
+        lax.ppermute(own_half, KEYS, [(at, at ^ other) for at in range(blocks)])
+        for other in range(1, blocks)
+    ]
     exps, own_row, column = own_logits(slot_keys, tokens, slot_devices)
+    own_row, near_keys = lax.optimization_barrier((own_row, near_keys))
+    far_keys = [lax.ppermute(keys, "c", swap) for keys in near_keys]
     column_other = lax.ppermute(column, "c", swap)
     row_parts = lax.all_to_all(own_row, SLOT, 0, 0)
     slot_in_part = dispatch_part(exps, column, column_other, tokens)
@@ -551,9 +615,9 @@
 
     keep, give, act, pre = experts_part(place, mine, other, w_in, w_out)
     sent = pair_sum(keep, lax.ppermute(give, "c", swap))
-    sent, keys_all = lax.optimization_barrier((sent, keys_all))
+    sent, near_keys, far_keys = lax.optimization_barrier((sent, near_keys, far_keys))
     terms = lax.all_to_all(sent, CHIPS, 0, 0)
-    all_exp, keys_rows = all_exps(place, keys_all, tokens, width)
+    all_exp, keys_rows = all_exps(place, slot_keys, near_keys, far_keys, tokens, width)
     terms, all_exp, act, pre = lax.optimization_barrier((terms, all_exp, act, pre))
     sent = sum_terms(terms, slot_in, column_total, everyone)
     gathered = lax.all_to_all(sent, GATHERED, 0, 0)
@@ -561,15 +625,20 @@
     gathered, grad_w_in, grad_w_out = lax.optimization_barrier((gathered, grad_w_in, grad_w_out))
     gathered_other = lax.ppermute(gathered, "c", swap)
 
-    dots, row = comb_dots(place, all_exp, out_grad, row_parts, gathered, gathered_other)
+    near = near_dots(place, out_grad, gathered, all_exp.shape[0])
+    gathered_other, near = lax.optimization_barrier((gathered_other, near))
+    dots, row = comb_dots(place, all_exp, near, out_grad, row_parts, gathered_other)
     row_other = lax.ppermute(row, "xa", swap)
     terms, dispatch, grad_rows = disp_dots(
         place, all_exp, dots, tokens, row_parts, gathered, gathered_other, width
     )
-    keys_part, sent, own_grads = logit_grads(
-        place, all_exp, terms, dispatch, tokens, row_parts, row, row_other, keys_rows, grad_rows, own_slots
+    logit, sent = logit_grads(
+        place, all_exp, terms, dispatch, row_parts, row, row_other, keys_rows, grad_rows
     )
     received = lax.ppermute(sent, "xa", swap)
+    keys_part, own_grads = own_parts(
+        place, logit, dispatch, tokens, keys_rows, grad_rows, own_slots
+    )
     keys_parts = lax.all_to_all(
         keys_part.reshape(seq_devices, features // seq_devices, own_slots), SEQ, 0, 0
     )

time: 163 us -> 149 us (0.914)
  between operations: 14.2 us -> 0.93 us
  starting transfers between devices: 28.1 us -> 34.9 us
  waiting for transfers between devices: 23.7 us -> 17.3 us
  blocking collectives: 39.4 us -> 33.1 us
  local copies, waits for them, and re-layouts: 19.8 us -> 25.6 us
    ppermute x0 -> x6, starting transfers between devices: none -> 6.44 us  [the longest x3 5.81 us: per_device(): lax.ppermute(own_half, KEYS, [(at, at ^ other) for at in range(blocks)])]
    unnamed x40 -> x58, local copies, waits for them, and re-layouts: 19.8 us -> 24.6 us
    all_to_all x1, blocking collectives: 12.5 us -> 9.05 us  [per_device(): mine = lax.all_to_all(sent, CHIPS, 0, 0)]
    pallas_call x2 -> x4, Pallas kernels: 6.86 us -> 10.1 us  [the longest x1 3.78 us: all_exps(): pl.pallas_call(kernel, in_specs=[in_smem()] + [whole_in_vmem()] * (2 * ot...]
    ppermute x1, waiting for transfers between devices: 3.06 us -> 0.01 us  [per_device(): gathered_other = lax.ppermute(gathered, 'c', swap)]
    all_to_all x1, blocking collectives: 15.1 us -> 12.6 us  [per_device(): lax.all_to_all(pair_sum(keep, lax.ppermute(give, 'c', swap)), CHIPS, 0, 0)]
    pallas_call x1, Pallas kernels: 4.85 us -> 2.43 us  [comb_dots(): pl.pallas_call(kernel, in_specs=[in_smem()] + [whole_in_vmem()] * 5, out_...]
    all_to_all x1, waiting for transfers between devices: 1.35 us -> 3.2 us  [per_device(): row_parts = lax.all_to_all(own_row, SLOT, 0, 0)]
  transfers between devices with their start and end apart: 11 -> 16, of which waited for: 9 -> 6; matrix products, arithmetic and copies ran while one was open for 0% -> 0% of each run, Pallas kernels for 16% -> 16%
where the time goes in v5:
time: 149 us; the launch traced here: 148 us
  starting transfers between devices  34.9 us (23%)
  Pallas kernels  34.8 us (23%)
  blocking collectives  33.1 us (22%)
  local copies, waits for them, and re-layouts  25.6 us (17%)
  waiting for transfers between devices  17.3 us (12%)
  other arithmetic  1.73 us (1%)
    unnamed x58, local copies, waits for them, and re-layouts  24.6 us
    all_to_all x1, blocking collectives, per_device(): lax.all_to_all(pair_sum(keep, lax.ppermute(give, 'c', swap)), CHIPS, 0, 0)  12.6 us
    all_to_all x1, blocking collectives, per_device(): lax.all_to_all(keys_part.reshape(seq_devices, features // seq_devices, ow...  11.4 us
    all_to_all x1, blocking collectives, per_device(): mine = lax.all_to_all(sent, CHIPS, 0, 0)  9.05 us
    all_to_all x1, waiting for transfers between devices, per_device(): gathered = lax.all_to_all(sent, GATHERED, 0, 0)  8.94 us
    all_to_all x1, starting transfers between devices, per_device(): row_parts = lax.all_to_all(own_row, SLOT, 0, 0)  7.22 us
    pallas_call x1, Pallas kernels, weight_grads(): pl.pallas_call(kernel, grid=(experts,), in_specs=[in_smem(), pl.BlockSpec...  6.31 us
    ppermute x3, starting transfers between devices, per_device(): lax.ppermute(own_half, KEYS, [(at, at ^ other) for at in range(blocks)])  5.81 us
  transfers between devices with their start and end apart: 16, of which 6 were waited for; matrix products, arithmetic and copies ran while one was open for 0% of the time, Pallas kernels for 16%

profile of v5, /device:TPU:1, one launch (start us, length us, event | category | flops | bytes accessed | tf_op | source)
XLA Modules:
  0.0 148.4 jit_solution(6020938705473905306)
XLA Ops:
  0.6 0.9 constant_dynamic-slice_fusion
  1.6 5.4 %collective-permute-start.2 = (bf16[640,128]{1,0:T(8,128)(2,1)S(1)}, bf16[640,128]{1,0:T(8,128)(2,1)S(1)}, u32[]{:S(2)}, u32[]{:S(2)}) collective-permute-start(bf16[640,128]{1,0:T(8,128)(2,1)S(1)} %constant_dynamic-slice_fusion), channel_id=1, source_target_pairs={{0,3},{1,2},{2,1},{3,0},{4,7},{5,6},{6,5},{7,4},{8,11},{9,10},{10,... | collective-permute-start | bytes 491528 | tf_op jit(solution)/shard_map/ppermute | solution.py:599
  7.0 0.3 collective-permute-start.1
  7.3 0.1 collective-permute-start
  7.4 2.5 %copy-done = bf16[2048,1280]{1,0:T(8,128)(2,1)S(1)} copy-done((bf16[2048,1280]{1,0:T(8,128)(2,1)S(1)}, bf16[2048,1280]{1,0:T(8,128)(2,1)}, u32[]{:S(2)}) %copy-start) | copy-done | bytes 5242904
  9.9 1.0 copy-done.17
  10.8 2.5 %own_logits.1 = (f32[128,2048]{1,0:T(8,128)S(1)}, f32[8,1,2048]{2,1,0:T(1,128)}, f32[128,128]{1,0:T(8,128)S(1)}) custom-call(bf16[1280,128]{1,0:T(8,128)(2,1)S(1)} %copy-done.17, bf16[2048,1280]{1,0:T(8,128)(2,1)S(1)} %copy-done), custom_call_target="tpu_custom_call" | custom-call | flops 671088640 | bytes 5242880 | tf_op jit(solution)/shard_map/own_logits/pallas_call | solution.py:102
  13.3 1.2 collective-permute-start.3
  14.5 0.1 pad_add_fusion.place_ref
  14.6 7.2 %all-to-all-start = ((f32[8,1,2048]{2,1,0:T(1,128)}), f32[8,1,2048]{2,1,0:T(1,128)S(1)}, u32[]{:S(2)}, u32[]{:S(2)}) async-start(f32[8,1,2048]{2,1,0:T(1,128)} %get-tuple-element.51), calls=%async_computation | async-start | bytes 131072 | tf_op jit(solution)/shard_map/all_to_all | solution.py:606
  21.9 2.5 %copy-done.1 = bf16[2048,1280]{1,0:T(8,128)(2,1)S(1)} copy-done((bf16[2048,1280]{1,0:T(8,128)(2,1)S(1)}, bf16[2048,1280]{1,0:T(8,128)(2,1)}, u32[]{:S(2)}) %copy-start.1) | copy-done | bytes 5242904
  24.3 0.9 dispatch_part.1.in_ref
  25.3 3.2 %all-to-all-done.row_ref = f32[8,1,2048]{2,1,0:T(1,128)S(1)} async-done(((f32[8,1,2048]{2,1,0:T(1,128)}), f32[8,1,2048]{2,1,0:T(1,128)S(1)}, u32[]{:S(2)}, u32[]{:S(2)}) %all-to-all-start) | async-done | bytes 65568 | tf_op jit(solution)/shard_map/all_to_all | solution.py:606
  28.5 2.5 %copy-done.3 = bf16[2048,1280]{1,0:T(8,128)(2,1)S(1)} copy-done((bf16[2048,1280]{1,0:T(8,128)(2,1)S(1)}, bf16[2048,1280]{1,0:T(8,128)(2,1)}, u32[]{:S(2)}) %copy-start.3) | copy-done | bytes 5242904
  31.0 1.5 combine_part.1
  32.4 2.0 %collective-permute-start.4 = (bf16[8,16,1280]{2,1,0:T(8,128)(2,1)S(1)}, bf16[8,16,1280]{2,1,0:T(8,128)(2,1)S(1)}, u32[]{:S(2)}, u32[]{:S(2)}) collective-permute-start(bf16[8,16,1280]{2,1,0:T(8,128)(2,1)S(1)} %get-tuple-element.54), channel_id=1, source_target_pairs={{0,8},{8,0},{1,9},{9,1},{2,10},{10,2},{3,11},{11,3},{4,12},{12,4},... | collective-permute-start | bytes 983048 | tf_op jit(solution)/shard_map/ppermute | solution.py:611
  34.4 1.3 collective-permute-done.4.received_ref
  35.7 0.1 pair_sum.2
  35.8 12.6 %all_to_all.30.parts_ref = bf16[8,16,1408]{2,1,0:T(8,128)(2,1)S(1)} all-to-all(bf16[8,16,1408]{2,1,0:T(8,128)(2,1)S(1)} %pair_sum.2), channel_id=1, replica_groups=mesh['zl'=2,'y'=4,'c'=2,'xa'=2,'xb'=2,'zh'=2] {'zl','y'}, dimensions={0} | all-to-all | bytes 720896 | tf_op jit(solution)/shard_map/all_to_all | solution.py:611
  48.4 0.2 sum_slots.1
  48.6 9.0 %all_to_all.31.mine_ref = bf16[8,16,1280]{2,1,0:T(8,128)(2,1)S(1)} all-to-all(bf16[8,16,1280]{2,1,0:T(8,128)(2,1)S(1)} %get-tuple-element.55), channel_id=1, replica_groups=mesh['zl'=2,'y'=4,'c'=2,'xa'=2,'xb'=2,'zh'=2] {'zl','y'}, dimensions={0} | all-to-all | bytes 655360 | tf_op jit(solution)/shard_map/all_to_all | solution.py:613
  57.7 2.4 %collective-permute-start.5 = (bf16[8,16,1280]{2,1,0:T(8,128)(2,1)S(1)}, bf16[8,16,1280]{2,1,0:T(8,128)(2,1)S(1)}, u32[]{:S(2)}, u32[]{:S(2)}) collective-permute-start(bf16[8,16,1280]{2,1,0:T(8,128)(2,1)S(1)} %all_to_all.31.mine_ref), channel_id=1, source_target_pairs={{0,8},{8,0},{1,9},{9,1},{2,10},{10,2},{3,11},{11,3},{4,12},{12,4},... | collective-permute-start | bytes 983048 | tf_op jit(solution)/shard_map/ppermute | solution.py:614
  60.1 1.3 collective-permute-done.5.other_ref
  61.3 5.3 %experts_part.1 = (bf16[8,16,1280]{2,1,0:T(8,128)(2,1)S(1)}, bf16[8,16,1280]{2,1,0:T(8,128)(2,1)S(1)}, bf16[8,16,192]{2,1,0:T(8,128)(2,1)S(1)}, bf16[8,16,192]{2,1,0:T(8,128)(2,1)S(1)}) custom-call(s32[3]{0:T(128)S(1)} %pad_add_fusion.place_ref, bf16[8,16,1280]{2,1,0:T(8,128)(2,1)S(1)} %all_to_all.31.mine_ref, ...), custom_call_target="tpu_custom_call" | custom-call | flops 251658240 | bytes 7864320 | tf_op jit(solution)/shard_map/experts_part/pallas_call | solution.py:283
  66.7 0.5 collective-permute-start.6
  67.2 0.1 collective-permute-start.7
  67.3 0.4 collective-permute-start.8
  67.7 0.1 collective-permute-start.9
  67.8 0.6 collective-permute-done.6.received_ref
  68.4 0.8 pair_sum.3
  69.3 0.7 copy-done.23
  69.9 0.7 copy-done.25
  70.6 3.4 %all-to-all-start.3 = ((bf16[8,16,1280]{2,1,0:T(8,128)(2,1)}), bf16[8,16,1280]{2,1,0:T(8,128)(2,1)S(1)}, u32[]{:S(2)}, u32[]{:S(2)}) async-start(bf16[8,16,1280]{2,1,0:T(8,128)(2,1)} %pair_sum.3), calls=%async_computation.3 | async-start | bytes 655360 | tf_op jit(solution)/shard_map/all_to_all | solution.py:619
  74.1 0.0 copy-start.2
  74.1 2.5 %copy-done.2 = bf16[2048,1280]{1,0:T(8,128)(2,1)S(1)} copy-done((bf16[2048,1280]{1,0:T(8,128)(2,1)S(1)}, bf16[2048,1280]{1,0:T(8,128)(2,1)}, u32[]{:S(2)}) %copy-start.2) | copy-done | bytes 5242904
  76.5 0.9 copy-done.24
  77.5 0.9 copy-done.26
  78.4 3.8 %all_exps.1 = (bf16[512,2048]{1,0:T(8,128)(2,1)S(1)}, bf16[2,160,512]{2,1,0:T(8,128)(2,1)S(1)}) custom-call(s32[3]{0:T(128)S(1)} %pad_add_fusion.place_ref, bf16[1280,128]{1,0:T(8,128)(2,1)S(1)} %copy-done.18, bf16[640,128]{1,0:T(8,128)(2,1)S(1)} %collective-permute-done.refs_0_, bf16[640,128]{1,0:T(8,128)(2,1)S(1)} %collective-permute-done.1.refs_1_, ...), custom_call_target="tpu_custom_call" | custom-call | flops 2684354560 | bytes 5242880 | tf_op jit(solution)/shard_map/all_exps/pallas_call | solution.py:395
  82.2 0.7 copy-done.13
  82.9 0.1 sum_terms.1
  83.0 1.1 copy-done.6
  84.2 5.5 %all-to-all-start.4 = ((bf16[32,16,1408]{2,1,0:T(8,128)(2,1)}), bf16[32,16,1408]{2,1,0:T(8,128)(2,1)S(1)}, u32[]{:S(2)}, u32[]{:S(2)}) async-start(bf16[32,16,1408]{2,1,0:T(8,128)(2,1)} %copy-done.6), calls=%async_computation.4 | async-start | bytes 2883584 | tf_op jit(solution)/shard_map/all_to_all | solution.py:623
  89.7 0.0 copy-start.10
  89.7 1.0 copy-done.10
  90.6 1.0 copy-done.16
  91.6 0.8 copy-done.20
  92.4 0.8 copy-done.22
  93.3 6.3 %weight_grads.1 = (bf16[8,192,1280]{2,1,0:T(8,128)(2,1)}, bf16[8,192,1280]{2,1,0:T(8,128)(2,1)}) custom-call(s32[3]{0:T(128)S(1)} %pad_add_fusion.place_ref, bf16[8,16,1280]{2,1,0:T(8,128)(2,1)S(1)} %copy-done.10, bf16[8,16,1280]{2,1,0:T(8,128)(2,1)S(1)} %copy-done.16, bf16[8,16,192]{2,1,0:T(8,128)(2,1)S(1)} %copy-done.20, bf16[8,16,192]{2,1,0:T(8,128)(2,1)S(1)} %copy-done.22), custom_call_target="tpu_custom_call" | custom-call | flops 125829120 | bytes 7864320 | tf_op jit(solution)/shard_map/weight_grads/pallas_call | solution.py:315
  99.6 8.9 %all-to-all-done.4.mine_ref = bf16[32,16,1408]{2,1,0:T(8,128)(2,1)S(1)} async-done(((bf16[32,16,1408]{2,1,0:T(8,128)(2,1)}), bf16[32,16,1408]{2,1,0:T(8,128)(2,1)S(1)}, u32[]{:S(2)}, u32[]{:S(2)}) %all-to-all-start.4) | async-done | bytes 1441824 | tf_op jit(solution)/shard_map/all_to_all | solution.py:623
  108.5 3.2 %collective-permute-start.10 = (bf16[32,16,1408]{2,1,0:T(8,128)(2,1)S(1)}, bf16[32,16,1408]{2,1,0:T(8,128)(2,1)S(1)}, u32[]{:S(2)}, u32[]{:S(2)}) collective-permute-start(bf16[32,16,1408]{2,1,0:T(8,128)(2,1)S(1)} %all-to-all-done.4.mine_ref), channel_id=1, source_target_pairs={{0,8},{8,0},{1,9},{9,1},{2,10},{10,2},{3,11},{11,3},{4,12},{12,4},... | collective-permute-start | bytes 4325384 | tf_op jit(solution)/shard_map/ppermute | solution.py:626
  111.7 2.5 %copy-done.4 = bf16[2048,1280]{1,0:T(8,128)(2,1)S(1)} copy-done((bf16[2048,1280]{1,0:T(8,128)(2,1)S(1)}, bf16[2048,1280]{1,0:T(8,128)(2,1)}, u32[]{:S(2)}) %copy-start.4) | copy-done | bytes 5242904
  114.2 2.4 %near_dots.1.near_ref = f32[512,2048]{1,0:T(8,128)S(1)} custom-call(s32[3]{0:T(128)S(1)} %pad_add_fusion.place_ref, bf16[2048,1280]{1,0:T(8,128)(2,1)S(1)} %copy-done.4, bf16[32,16,1408]{2,1,0:T(8,128)(2,1)S(1)} %all-to-all-done.4.mine_ref), custom_call_target="tpu_custom_call" | custom-call | flops 1342177280 | bytes 2621440 | tf_op jit(solution)/shard_map/near_dots/pallas_call | solution.py:430
  116.5 0.0 slice-start.1
  116.6 2.6 %copy-done.5 = bf16[2048,1280]{1,0:T(8,128)(2,1)S(1)} copy-done((bf16[2048,1280]{1,0:T(8,128)(2,1)S(1)}, bf16[2048,1280]{1,0:T(8,128)(2,1)}, u32[]{:S(2)}) %copy-start.5) | copy-done | bytes 5242904
  119.2 2.4 %comb_dots.1 = (f32[512,2048]{1,0:T(8,128)S(1)}, f32[1,2048]{1,0:T(1,128)S(1)}) custom-call(s32[3]{0:T(128)S(1)} %pad_add_fusion.place_ref, bf16[512,2048]{1,0:T(8,128)(2,1)S(1)} %get-tuple-element.71.exp_ref, f32[512,2048]{1,0:T(8,128)S(1)} %near_dots.1.near_ref, bf16[2048,1280]{1,0:T(8,128)(2,1)S(1)} %copy-done.5, f32[8,1,2048]{2,1,0:T(1,128)S(1)} %copy-done.12, ...), custom_call_target="tpu_custom_call" | custom-call | flops 1342177280 | bytes 2621440 | tf_op jit(solution)/shard_map/comb_dots/pallas_call | solution.py:454
  121.6 1.9 %collective-permute-start.11 = (f32[1,2048]{1,0:T(1,128)S(1)}, f32[1,2048]{1,0:T(1,128)S(1)}, u32[]{:S(2)}, u32[]{:S(2)}) collective-permute-start(f32[1,2048]{1,0:T(1,128)S(1)} %get-tuple-element.85.sum_ref), channel_id=1, source_target_pairs={{0,4},{4,0},{1,5},{5,1},{2,6},{6,2},{3,7},{7,3},{8,12},{12,8},{9,1... | collective-permute-start | bytes 24584 | tf_op jit(solution)/shard_map/ppermute | solution.py:631
  123.5 4.5 %disp_dots.1 = (f32[512,2048]{1,0:T(8,128)S(1)}, bf16[512,2048]{1,0:T(8,128)(2,1)S(1)}, bf16[2,160,512]{2,1,0:T(8,128)(2,1)S(1)}) custom-call(s32[3]{0:T(128)S(1)} %pad_add_fusion.place_ref, bf16[512,2048]{1,0:T(8,128)(2,1)S(1)} %get-tuple-element.71.exp_ref, f32[512,2048]{1,0:T(8,128)S(1)} %get-tuple-element.82.dot_ref, bf16[2048,1280]{1,0:T(8,128)(2,1)S(1)} %bitcast.7, ...), custom_call_target="tpu_custom_call" | custom-call | flops 2684354560 | bytes 5242880 | tf_op jit(solution)/shard_map/disp_dots/pallas_call | solution.py:498
  128.0 1.9 %logit_grads.1 = (bf16[512,2048]{1,0:T(8,128)(2,1)S(1)}, bf16[160,2048]{1,0:T(8,128)(2,1)S(1)}) custom-call(s32[3]{0:T(128)S(1)} %pad_add_fusion.place_ref, bf16[512,2048]{1,0:T(8,128)(2,1)S(1)} %get-tuple-element.71.exp_ref, f32[512,2048]{1,0:T(8,128)S(1)} %get-tuple-element.83.terms_ref, bf16[512,2048]{1,0:T(8,128)(2,1)S(1)} %get-tuple-element.84.dispatch_ref, ...), custom_call_target="tpu_custom_call" | custom-call | flops 671088640 | bytes 4194304 | tf_op jit(solution)/shard_map/logit_grads/pallas_call | solution.py:540
  129.9 1.3 collective-permute-start.12
  131.2 2.1 %own_parts.1 = (bf16[1280,128]{1,0:T(8,128)(2,1)S(1)}, f32[160,2048]{1,0:T(8,128)S(1)}) custom-call(s32[3]{0:T(128)S(1)} %pad_add_fusion.place_ref, bf16[512,2048]{1,0:T(8,128)(2,1)S(1)} %get-tuple-element.88.logit_ref, bf16[512,2048]{1,0:T(8,128)(2,1)S(1)} %get-tuple-element.84.dispatch_ref, bf16[2048,1280]{1,0:T(8,128)(2,1)S(1)} %bitcast.7, ...), custom_call_target="tpu_custom_call" | custom-call | flops 671088640 | bytes 5242880 | tf_op jit(solution)/shard_map/own_parts/pallas_call | solution.py:568
  133.2 11.4 %all_to_all.32 = bf16[16,80,128]{2,1,0:T(8,128)(2,1)S(1)} all-to-all(bf16[16,80,128]{2,1,0:T(8,128)(2,1)S(1)} %bitcast.8), channel_id=1, replica_groups=mesh['zl'=2,'y'=4,'c'=2,'xa'=2,'xb'=2,'zh'=2] {'zl','y','c'}, dimensions={0} | all-to-all | bytes 655360 | tf_op jit(solution)/shard_map/all_to_all | solution.py:642
  144.7 0.7 convert_reduce_fusion
  145.4 2.0 %collective-permute-done.12 = bf16[160,2048]{1,0:T(8,128)(2,1)S(1)} collective-permute-done((bf16[160,2048]{1,0:T(8,128)(2,1)S(1)}, bf16[160,2048]{1,0:T(8,128)(2,1)S(1)}, u32[]{:S(2)}, u32[]{:S(2)}) %collective-permute-start.12) | collective-permute-done | bytes 655392 | tf_op jit(solution)/shard_map/ppermute | solution.py:638
  147.4 1.0 fusion
  (49 shorter events, 0.1 us)
Async XLA Ops:
  1.6 13.0 %collective-permute-start.2 = (bf16[640,128]{1,0:T(8,128)(2,1)S(1)}, bf16[640,128]{1,0:T(8,128)(2,1)S(1)}, u32[]{:S(2)}, u32[]{:S(2)}) collective-permute-start(bf16[640,128]{1,0:T(8,128)(2,1)S(1)} %constant_dynamic-slice_fusion), channel_id=1, source_target_pairs={{0,3},{1,2},{2,1},{3,0},{4,7},{5,6},{6,5},{7,4},{8,11},{9,10},{10,... | collective-permute-start | bytes 491528 | tf_op jit(solution)/shard_map/ppermute | solution.py:599
  7.0 7.6 %collective-permute-start.1 = (bf16[640,128]{1,0:T(8,128)(2,1)S(1)}, bf16[640,128]{1,0:T(8,128)(2,1)S(1)}, u32[]{:S(2)}, u32[]{:S(2)}) collective-permute-start(bf16[640,128]{1,0:T(8,128)(2,1)S(1)} %constant_dynamic-slice_fusion), channel_id=1, source_target_pairs={{0,2},{1,3},{2,0},{3,1},{4,6},{5,7},{6,4},{7,5},{8,10},{9,11},{10,... | collective-permute-start | bytes 491528 | tf_op jit(solution)/shard_map/ppermute | solution.py:599
  7.3 7.4 %collective-permute-start = (bf16[640,128]{1,0:T(8,128)(2,1)S(1)}, bf16[640,128]{1,0:T(8,128)(2,1)S(1)}, u32[]{:S(2)}, u32[]{:S(2)}) collective-permute-start(bf16[640,128]{1,0:T(8,128)(2,1)S(1)} %constant_dynamic-slice_fusion), channel_id=1, source_target_pairs={{0,1},{1,0},{2,3},{3,2},{4,5},{5,4},{6,7},{7,6},{8,9},{9,8},{10,11... | collective-permute-start | bytes 491528 | tf_op jit(solution)/shard_map/ppermute | solution.py:599
  7.4 2.5 %copy-start = (bf16[2048,1280]{1,0:T(8,128)(2,1)S(1)}, bf16[2048,1280]{1,0:T(8,128)(2,1)}, u32[]{:S(2)}) copy-start(bf16[2048,1280]{1,0:T(8,128)(2,1)} %tokens_ref.7) | copy-start | bytes 15728644
  9.9 1.0 copy-start.17
  13.3 8.5 %collective-permute-start.3 = (f32[128,128]{1,0:T(8,128)S(1)}, f32[128,128]{1,0:T(8,128)S(1)}, u32[]{:S(2)}, u32[]{:S(2)}) collective-permute-start(f32[128,128]{1,0:T(8,128)S(1)} %get-tuple-element.52.column_ref), channel_id=1, source_target_pairs={{0,8},{8,0},{1,9},{9,1},{2,10},{10,2},{3,11},{11,3},{4,12},{12,4},... | collective-permute-start | bytes 196616 | tf_op jit(solution)/shard_map/ppermute | solution.py:605
  14.6 13.8 %all-to-all-start = ((f32[8,1,2048]{2,1,0:T(1,128)}), f32[8,1,2048]{2,1,0:T(1,128)S(1)}, u32[]{:S(2)}, u32[]{:S(2)}) async-start(f32[8,1,2048]{2,1,0:T(1,128)} %get-tuple-element.51), calls=%async_computation | async-start | bytes 131072 | tf_op jit(solution)/shard_map/all_to_all | solution.py:606
  21.9 2.5 %copy-start.1 = (bf16[2048,1280]{1,0:T(8,128)(2,1)S(1)}, bf16[2048,1280]{1,0:T(8,128)(2,1)}, u32[]{:S(2)}) copy-start(bf16[2048,1280]{1,0:T(8,128)(2,1)} %tokens_ref.7) | copy-start | bytes 15728644
  28.5 2.5 %copy-start.3 = (bf16[2048,1280]{1,0:T(8,128)(2,1)S(1)}, bf16[2048,1280]{1,0:T(8,128)(2,1)}, u32[]{:S(2)}) copy-start(bf16[2048,1280]{1,0:T(8,128)(2,1)} %grad_ref.5) | copy-start | bytes 15728644
  31.0 1.5 %copy-start.11 = (f32[8,1,2048]{2,1,0:T(1,128)}, f32[8,1,2048]{2,1,0:T(1,128)S(1)}, u32[]{:S(2)}) copy-start(f32[8,1,2048]{2,1,0:T(1,128)S(1)} %all-to-all-done.row_ref) | copy-start | bytes 196612
  31.0 30.4 %copy-start.7 = (bf16[8,192,1280]{2,1,0:T(8,128)(2,1)S(1)}, bf16[8,192,1280]{2,1,0:T(8,128)(2,1)}, u32[]{:S(2)}) copy-start(bf16[8,192,1280]{2,1,0:T(8,128)(2,1)} %w_in_ref.1) | copy-start | bytes 11796484
  31.0 30.4 %copy-start.8 = (bf16[8,192,1280]{2,1,0:T(8,128)(2,1)S(1)}, bf16[8,192,1280]{2,1,0:T(8,128)(2,1)}, u32[]{:S(2)}) copy-start(bf16[8,192,1280]{2,1,0:T(8,128)(2,1)} %w_out_ref.1) | copy-start | bytes 11796484
  32.4 3.3 %collective-permute-start.4 = (bf16[8,16,1280]{2,1,0:T(8,128)(2,1)S(1)}, bf16[8,16,1280]{2,1,0:T(8,128)(2,1)S(1)}, u32[]{:S(2)}, u32[]{:S(2)}) collective-permute-start(bf16[8,16,1280]{2,1,0:T(8,128)(2,1)S(1)} %get-tuple-element.54), channel_id=1, source_target_pairs={{0,8},{8,0},{1,9},{9,1},{2,10},{10,2},{3,11},{11,3},{4,12},{12,4},... | collective-permute-start | bytes 983048 | tf_op jit(solution)/shard_map/ppermute | solution.py:611
  57.7 9.0 %copy-start.9 = (bf16[8,16,1280]{2,1,0:T(8,128)(2,1)}, bf16[8,16,1280]{2,1,0:T(8,128)(2,1)S(1)}, u32[]{:S(2)}) copy-start(bf16[8,16,1280]{2,1,0:T(8,128)(2,1)S(1)} %all_to_all.31.mine_ref) | copy-start | bytes 983044
  57.7 16.4 %copy-start.18 = (bf16[1280,128]{1,0:T(8,128)(2,1)S(1)}, bf16[1280,128]{1,0:T(8,128)(2,1)}, u32[]{:S(2)}) copy-start(bf16[1280,128]{1,0:T(8,128)(2,1)} %own_ref.1) | copy-start | bytes 983044
  57.7 3.6 %collective-permute-start.5 = (bf16[8,16,1280]{2,1,0:T(8,128)(2,1)S(1)}, bf16[8,16,1280]{2,1,0:T(8,128)(2,1)S(1)}, u32[]{:S(2)}, u32[]{:S(2)}) collective-permute-start(bf16[8,16,1280]{2,1,0:T(8,128)(2,1)S(1)} %all_to_all.31.mine_ref), channel_id=1, source_target_pairs={{0,8},{8,0},{1,9},{9,1},{2,10},{10,2},{3,11},{11,3},{4,12},{12,4},... | collective-permute-start | bytes 983048 | tf_op jit(solution)/shard_map/ppermute | solution.py:614
  61.3 5.4 %copy-start.15 = (bf16[8,16,1280]{2,1,0:T(8,128)(2,1)}, bf16[8,16,1280]{2,1,0:T(8,128)(2,1)S(1)}, u32[]{:S(2)}) copy-start(bf16[8,16,1280]{2,1,0:T(8,128)(2,1)S(1)} %collective-permute-done.5.other_ref) | copy-start | bytes 983044
  66.7 2.5 %copy-start.19 = (bf16[8,16,192]{2,1,0:T(8,128)(2,1)}, bf16[8,16,192]{2,1,0:T(8,128)(2,1)S(1)}, u32[]{:S(2)}) copy-start(bf16[8,16,192]{2,1,0:T(8,128)(2,1)S(1)} %get-tuple-element.75.act_ref) | copy-start | bytes 147460
  66.7 2.5 %copy-start.21 = (bf16[8,16,192]{2,1,0:T(8,128)(2,1)}, bf16[8,16,192]{2,1,0:T(8,128)(2,1)S(1)}, u32[]{:S(2)}) copy-start(bf16[8,16,192]{2,1,0:T(8,128)(2,1)S(1)} %get-tuple-element.76.pre_ref) | copy-start | bytes 147460
  66.7 1.7 %collective-permute-start.6 = (bf16[8,16,1280]{2,1,0:T(8,128)(2,1)S(1)}, bf16[8,16,1280]{2,1,0:T(8,128)(2,1)S(1)}, u32[]{:S(2)}, u32[]{:S(2)}) collective-permute-start(bf16[8,16,1280]{2,1,0:T(8,128)(2,1)S(1)} %get-tuple-element.57), channel_id=1, source_target_pairs={{0,8},{8,0},{1,9},{9,1},{2,10},{10,2},{3,11},{11,3},{4,12},{12,4},... | collective-permute-start | bytes 983048 | tf_op jit(solution)/shard_map/ppermute | solution.py:617
  67.2 2.1 %collective-permute-start.7 = (bf16[640,128]{1,0:T(8,128)(2,1)S(1)}, bf16[640,128]{1,0:T(8,128)(2,1)S(1)}, u32[]{:S(2)}, u32[]{:S(2)}) collective-permute-start(bf16[640,128]{1,0:T(8,128)(2,1)S(1)} %collective-permute-done.refs_0_), channel_id=1, source_target_pairs={{0,8},{8,0},{1,9},{9,1},{2,10},{10,2},{3,11},{11,3},{4,12},{12,4},... | collective-permute-start | bytes 491528 | tf_op jit(solution)/shard_map/ppermute | solution.py:604
  67.3 1.9 %collective-permute-start.8 = (bf16[640,128]{1,0:T(8,128)(2,1)S(1)}, bf16[640,128]{1,0:T(8,128)(2,1)S(1)}, u32[]{:S(2)}, u32[]{:S(2)}) collective-permute-start(bf16[640,128]{1,0:T(8,128)(2,1)S(1)} %collective-permute-done.1.refs_1_), channel_id=1, source_target_pairs={{0,8},{8,0},{1,9},{9,1},{2,10},{10,2},{3,11},{11,3},{4,12},{12,4},... | collective-permute-start | bytes 491528 | tf_op jit(solution)/shard_map/ppermute | solution.py:604
  67.7 2.2 %collective-permute-start.9 = (bf16[640,128]{1,0:T(8,128)(2,1)S(1)}, bf16[640,128]{1,0:T(8,128)(2,1)S(1)}, u32[]{:S(2)}, u32[]{:S(2)}) collective-permute-start(bf16[640,128]{1,0:T(8,128)(2,1)S(1)} %collective-permute-done.2.refs_2_), channel_id=1, source_target_pairs={{0,8},{8,0},{1,9},{9,1},{2,10},{10,2},{3,11},{11,3},{4,12},{12,4},... | collective-permute-start | bytes 491528 | tf_op jit(solution)/shard_map/ppermute | solution.py:604
  69.3 0.7 copy-start.23
  69.9 0.7 copy-start.25
  70.6 12.3 %all-to-all-start.3 = ((bf16[8,16,1280]{2,1,0:T(8,128)(2,1)}), bf16[8,16,1280]{2,1,0:T(8,128)(2,1)S(1)}, u32[]{:S(2)}, u32[]{:S(2)}) async-start(bf16[8,16,1280]{2,1,0:T(8,128)(2,1)} %pair_sum.3), calls=%async_computation.3 | async-start | bytes 655360 | tf_op jit(solution)/shard_map/all_to_all | solution.py:619
  74.1 2.5 %copy-start.2 = (bf16[2048,1280]{1,0:T(8,128)(2,1)S(1)}, bf16[2048,1280]{1,0:T(8,128)(2,1)}, u32[]{:S(2)}) copy-start(bf16[2048,1280]{1,0:T(8,128)(2,1)} %tokens_ref.7) | copy-start | bytes 15728644
  76.5 0.9 copy-start.24
  77.5 0.9 copy-start.26
  82.2 0.7 copy-start.13
  83.0 1.1 copy-start.6
  84.2 24.3 %all-to-all-start.4 = ((bf16[32,16,1408]{2,1,0:T(8,128)(2,1)}), bf16[32,16,1408]{2,1,0:T(8,128)(2,1)S(1)}, u32[]{:S(2)}, u32[]{:S(2)}) async-start(bf16[32,16,1408]{2,1,0:T(8,128)(2,1)} %copy-done.6), calls=%async_computation.4 | async-start | bytes 2883584 | tf_op jit(solution)/shard_map/all_to_all | solution.py:623
  89.7 1.0 copy-start.10
  90.6 1.0 copy-start.16
  91.6 0.8 copy-start.20
  92.4 0.8 copy-start.22
  108.5 8.0 %collective-permute-start.10 = (bf16[32,16,1408]{2,1,0:T(8,128)(2,1)S(1)}, bf16[32,16,1408]{2,1,0:T(8,128)(2,1)S(1)}, u32[]{:S(2)}, u32[]{:S(2)}) collective-permute-start(bf16[32,16,1408]{2,1,0:T(8,128)(2,1)S(1)} %all-to-all-done.4.mine_ref), channel_id=1, source_target_pairs={{0,8},{8,0},{1,9},{9,1},{2,10},{10,2},{3,11},{11,3},{4,12},{12,4},... | collective-permute-start | bytes 4325384 | tf_op jit(solution)/shard_map/ppermute | solution.py:626
  111.7 2.5 %copy-start.4 = (bf16[2048,1280]{1,0:T(8,128)(2,1)S(1)}, bf16[2048,1280]{1,0:T(8,128)(2,1)}, u32[]{:S(2)}) copy-start(bf16[2048,1280]{1,0:T(8,128)(2,1)} %grad_ref.5) | copy-start | bytes 15728644
  114.2 2.4 %copy-start.12 = (f32[8,1,2048]{2,1,0:T(1,128)S(1)}, f32[8,1,2048]{2,1,0:T(1,128)}, u32[]{:S(2)}) copy-start(f32[8,1,2048]{2,1,0:T(1,128)} %copy-done.11) | copy-start | bytes 196612
  114.2 9.3 %slice-start = ((s8[5242880]{0:T(1024)(128)(4,1)}), s8[4194304]{0:T(1024)(128)(4,1)S(1)}, s32[]{:S(2)}) async-start(s8[5242880]{0:T(1024)(128)(4,1)} %bitcast.6), calls=%async_computation.6 | async-start | bytes 8388608
  116.5 6.9 %slice-start.1 = ((s8[5242880]{0:T(1024)(128)(4,1)}), s8[1048576]{0:T(1024)(128)(4,1)S(1)}, s32[]{:S(2)}) async-start(s8[5242880]{0:T(1024)(128)(4,1)} %bitcast.6), calls=%async_computation.7 | async-start | bytes 2097152
  116.6 2.6 %copy-start.5 = (bf16[2048,1280]{1,0:T(8,128)(2,1)S(1)}, bf16[2048,1280]{1,0:T(8,128)(2,1)}, u32[]{:S(2)}) copy-start(bf16[2048,1280]{1,0:T(8,128)(2,1)} %grad_ref.5) | copy-start | bytes 15728644
  121.6 6.4 %collective-permute-start.11 = (f32[1,2048]{1,0:T(1,128)S(1)}, f32[1,2048]{1,0:T(1,128)S(1)}, u32[]{:S(2)}, u32[]{:S(2)}) collective-permute-start(f32[1,2048]{1,0:T(1,128)S(1)} %get-tuple-element.85.sum_ref), channel_id=1, source_target_pairs={{0,4},{4,0},{1,5},{5,1},{2,6},{6,2},{3,7},{7,3},{8,12},{12,8},{9,1... | collective-permute-start | bytes 24584 | tf_op jit(solution)/shard_map/ppermute | solution.py:631
  123.5 4.5 %copy-start.14 = (bf16[2,160,512]{2,1,0:T(8,128)(2,1)S(1)}, bf16[2,160,512]{2,1,0:T(8,128)(2,1)}, u32[]{:S(2)}) copy-start(bf16[2,160,512]{2,1,0:T(8,128)(2,1)} %copy-done.13) | copy-start | bytes 983044
  129.9 17.5 %collective-permute-start.12 = (bf16[160,2048]{1,0:T(8,128)(2,1)S(1)}, bf16[160,2048]{1,0:T(8,128)(2,1)S(1)}, u32[]{:S(2)}, u32[]{:S(2)}) collective-permute-start(bf16[160,2048]{1,0:T(8,128)(2,1)S(1)} %get-tuple-element.90), channel_id=1, source_target_pairs={{0,4},{4,0},{1,5},{5,1},{2,6},{6,2},{3,7},{7,3},{8,12},{12,8},{9,1... | collective-permute-start | bytes 1966088 | tf_op jit(solution)/shard_map/ppermute | solution.py:638

commit v6 on v5

--- a/solution.py
+++ b/solution.py
@@ -79,41 +79,6 @@
     return here, there
 
 
-def own_logits(slot_keys, tokens, copies, tile=512):
-    features, slots = slot_keys.shape
-    count = tokens.shape[0]
-
-    def kernel(slot_keys_ref, tokens_ref, exp_ref, row_ref, column_ref):
-        keys = slot_keys_ref[...].T
-        by_lane = jnp.zeros((slots, LANES), f32)
-        for at in range(0, count, tile):
-            cut = slice(at, at + tile)
-            exps = jnp.exp(
-                lax.dot_general(keys, tokens_ref[cut, :], cols_contract, preferred_element_type=f32)
-            )
-            exp_ref[:, cut] = exps
-            row_ref[:, :, cut] = jnp.broadcast_to(
-                jnp.sum(exps, axis=0, keepdims=True)[None], (copies, 1, tile)
-            )
-            for lanes in range(0, tile, LANES):
-                by_lane = by_lane + exps[:, lanes : lanes + LANES]
-        column_ref[...] = by_lane
-
-    return pl.pallas_call(
-        kernel,
-        in_specs=[whole_in_vmem()] * 2,
-        out_specs=[whole_in_vmem()] * 3,
-        out_shape=[
-            jax.ShapeDtypeStruct((slots, count), f32),
-            jax.ShapeDtypeStruct((copies, 1, count), f32),
-            jax.ShapeDtypeStruct((slots, LANES), f32),
-        ],
-        compiler_params=params(GRANT),
-        cost_estimate=cost(2 * slots * features * count, 2 * features * count),
-        name="own_logits",
-    )(slot_keys, tokens)
-
-
 def dispatch_part(exps, column, column_other, tokens):
     slots, count = exps.shape
     features = tokens.shape[1]
@@ -138,17 +103,18 @@
     )(exps, column, column_other, tokens)
 
 
-def combine_part(place, exps, row_parts, column, column_other, slot_in_part, out_grad, groups):
+def combine_part(place, exps, row, row_other, column, column_other, slot_in_part, out_grad, groups):
     slots, count = exps.shape
     features = out_grad.shape[1]
     half = features // 2
     block = slots // groups
 
     def kernel(
-        place_ref, exp_ref, row_ref, column_ref, other_ref, in_ref, grad_ref,
-        keep_ref, give_ref, weights_ref, total_ref,
+        place_ref, exp_ref, row_ref, row_other_ref, column_ref, other_ref, in_ref, grad_ref,
+        keep_ref, give_ref, row_total_ref, weights_ref, total_ref,
     ):
-        power, inverse = guarded(jnp.sum(row_ref[...], axis=0))
+        row_total_ref[...] = row_ref[...] + row_other_ref[...]
+        power, inverse = guarded(row_total_ref[...])
         weights_ref[...] = ((exp_ref[...] * power) * inverse).astype(bf16)
         total = jnp.sum(column_ref[...] + other_ref[...], axis=1, keepdims=True)
         shift, _unused = guarded(total)
@@ -168,11 +134,12 @@
 
     return pl.pallas_call(
         kernel,
-        in_specs=[in_smem()] + [whole_in_vmem()] * 6,
-        out_specs=[whole_in_vmem()] * 2,
+        in_specs=[in_smem()] + [whole_in_vmem()] * 7,
+        out_specs=[whole_in_vmem()] * 3,
         out_shape=[
             jax.ShapeDtypeStruct((groups, block, features + LANES), bf16),
             jax.ShapeDtypeStruct((groups, block, features), bf16),
+            jax.ShapeDtypeStruct((1, count), f32),
         ],
         scratch_shapes=[
             pltpu.VMEM((slots, count), bf16),
@@ -181,7 +148,7 @@
         compiler_params=params(GRANT),
         cost_estimate=cost(2 * slots * features * count, 2 * features * count),
         name="combine_part",
-    )(place, exps, row_parts, column, column_other, slot_in_part, out_grad)
+    )(place, exps, row, row_other, column, column_other, slot_in_part, out_grad)
 
 
 def pair_sum(keep, received):
@@ -364,43 +331,73 @@
     others = len(near_keys)
     slots = (others + 1) * block
 
-    def kernel(place_ref, own_ref, *refs):
-        near_refs, far_refs = refs[:others], refs[others : 2 * others]
-        tokens_ref, exp_ref, rows_ref, turned_ref = refs[2 * others :]
+    def kernel(place_ref, *refs):
+        blocks_hbm = refs[: 2 * others + 1]
+        tokens_ref, all_ref, own_ref, row_ref, column_ref, rows_ref = refs[2 * others + 1 : 2 * others + 7]
+        turned_ref, found_ref, keys_ref, *block_refs = refs[2 * others + 7 : -1]
+        sems = refs[-1]
+        started = []
+        for at, target in enumerate([keys_ref] + block_refs):
+            started.append(pltpu.make_async_copy(blocks_hbm[at], target, sems.at[at]))
+            started[at].start()
+        near_refs, far_refs = block_refs[:others], block_refs[others:]
+        for copy in started:
+            copy.wait()
         core, at_own = place_ref[0], place_ref[1]
         here, there = halves(place_ref, half)
 
         def spot(at):
             return pl.ds(pl.multiple_of(at * block, block), block)
 
+        own = spot(at_own)
         rows = pl.ds(pl.multiple_of(at_own * width, 16), width)
-        turned_ref[spot(at_own), :] = own_ref[...].T
+        turned_ref[own, :] = keys_ref[...].T
         for side in range(2):
             first = pl.multiple_of(at_own * width + side * half, 16)
-            rows_ref[side, :, spot(at_own)] = own_ref[pl.ds(first, width), :]
+            rows_ref[side, :, own] = keys_ref[pl.ds(first, width), :]
         for at in range(others):
             place_at = spot(at_own ^ (at + 1))
             turned_ref[place_at, here] = near_refs[at][...].T
             turned_ref[place_at, there] = far_refs[at][...].T
             rows_ref[core, :, place_at] = near_refs[at][rows, :]
             rows_ref[1 - core, :, place_at] = far_refs[at][rows, :]
+        by_lane = jnp.zeros((block, LANES), f32)
         for at in range(0, count, tile):
-            exp_ref[:, at : at + tile] = jnp.exp(
+            cut = slice(at, at + tile)
+            found = jnp.exp(
                 lax.dot_general(
-                    turned_ref[...], tokens_ref[at : at + tile, :], cols_contract,
-                    preferred_element_type=f32,
+                    turned_ref[...], tokens_ref[cut, :], cols_contract, preferred_element_type=f32
                 )
-            ).astype(bf16)
-
-    return pl.pallas_call(
-        kernel,
-        in_specs=[in_smem()] + [whole_in_vmem()] * (2 * others + 2),
-        out_specs=[whole_in_vmem()] * 2,
+            )
+            found_ref[:, cut] = found
+            all_ref[:, cut] = found.astype(bf16)
+            row_ref[:, cut] = jnp.sum(found, axis=0, keepdims=True)
+            exps = found_ref[own, cut]
+            own_ref[:, cut] = exps
+            for lanes in range(0, tile, LANES):
+                by_lane = by_lane + exps[:, lanes : lanes + LANES]
+        column_ref[...] = by_lane
+
+    return pl.pallas_call(
+        kernel,
+        in_specs=[in_smem()]
+        + [pl.BlockSpec(memory_space=pltpu.HBM)] * (2 * others + 1)
+        + [whole_in_vmem()],
+        out_specs=[whole_in_vmem()] * 5,
         out_shape=[
             jax.ShapeDtypeStruct((slots, count), bf16),
+            jax.ShapeDtypeStruct((block, count), f32),
+            jax.ShapeDtypeStruct((1, count), f32),
+            jax.ShapeDtypeStruct((block, LANES), f32),
             jax.ShapeDtypeStruct((2, width, slots), bf16),
         ],
-        scratch_shapes=[pltpu.VMEM((slots, features), bf16)],
+        scratch_shapes=[
+            pltpu.VMEM((slots, features), bf16),
+            pltpu.VMEM((slots, count), f32),
+            pltpu.VMEM((features, block), bf16),
+        ]
+        + [pltpu.VMEM((half, block), bf16)] * (2 * others)
+        + [pltpu.SemaphoreType.DMA((2 * others + 1,))],
         compiler_params=params(GRANT),
         cost_estimate=cost(2 * slots * features * count, 2 * features * count),
         name="all_exps",
@@ -421,8 +418,11 @@
 
 def near_dots(place, out_grad, mine, slots, tile=256):
     count, features = out_grad.shape
-
-    def kernel(place_ref, grad_ref, mine_ref, dot_ref):
+    half = features // 2
+
+    def kernel(place_ref, grad_ref, mine_ref, dot_ref, far_ref):
+        _unused, there = halves(place_ref, half)
+        far_ref[...] = grad_ref[:, there]
         for at in range(0, count, tile):
             cut = slice(at, at + tile)
             dot_ref[:, cut] = half_dot(place_ref, mine_ref, grad_ref, 0, cut, True)
@@ -430,39 +430,45 @@
     return pl.pallas_call(
         kernel,
         in_specs=[in_smem()] + [whole_in_vmem()] * 2,
-        out_specs=whole_in_vmem(),
-        out_shape=jax.ShapeDtypeStruct((slots, count), f32),
+        out_specs=[whole_in_vmem()] * 2,
+        out_shape=[
+            jax.ShapeDtypeStruct((slots, count), f32),
+            jax.ShapeDtypeStruct((count, half), bf16),
+        ],
         compiler_params=params(GRANT),
         cost_estimate=cost(slots * features * count, features * count),
         name="near_dots",
     )(place, out_grad, mine)
 
 
-def comb_dots(place, exps, near, out_grad, row_parts, other, tile=256):
+def comb_dots(exps, near, grad_far, row_parts, other, tile=256):
     slots, count = exps.shape
-    features = out_grad.shape[1]
-
-    def kernel(place_ref, exp_ref, near_ref, grad_ref, row_ref, other_ref, dot_ref, sum_ref):
+    half = grad_far.shape[1]
+
+    def kernel(exp_ref, near_ref, grad_ref, row_ref, other_ref, dot_ref, sum_ref):
+        slot_out = other_ref[:, :, :half].reshape(slots, half)
         for at in range(0, count, tile):
             cut = slice(at, at + tile)
-            power, inverse = guarded(jnp.sum(row_ref[:, :, cut], axis=0))
-            dots = near_ref[:, cut] + half_dot(place_ref, other_ref, grad_ref, 0, cut, False)
+            power, inverse = guarded(row_ref[:, cut])
+            dots = near_ref[:, cut] + lax.dot_general(
+                slot_out, grad_ref[cut, :], cols_contract, preferred_element_type=f32
+            )
             dot_ref[:, cut] = dots
             terms = (exp_ref[:, cut].astype(f32) * power) * dots
             sum_ref[:, cut] = jnp.sum(terms, axis=0, keepdims=True) * inverse
 
     return pl.pallas_call(
         kernel,
-        in_specs=[in_smem()] + [whole_in_vmem()] * 5,
+        in_specs=[whole_in_vmem()] * 5,
         out_specs=[whole_in_vmem()] * 2,
         out_shape=[
             jax.ShapeDtypeStruct((slots, count), f32),
             jax.ShapeDtypeStruct((1, count), f32),
         ],
         compiler_params=params(GRANT),
-        cost_estimate=cost(slots * features * count, features * count),
+        cost_estimate=cost(2 * slots * half * count, 2 * half * count),
         name="comb_dots",
-    )(place, exps, near, out_grad, row_parts, other)
+    )(exps, near, grad_far, row_parts, other)
 
 
 def disp_dots(place, exps, dots, tokens, row_parts, mine, other, width, tile=256):
@@ -486,7 +492,7 @@
             rows_ref[at] = turned_ref[rows, :]
         for at in range(0, count, tile):
             cut = slice(at, at + tile)
-            power, inverse = guarded(jnp.sum(row_ref[:, :, cut], axis=0))
+            power, inverse = guarded(row_ref[:, cut])
             exps_here = exp_ref[:, cut].astype(f32)
             dispatch = (exps_here * power_ref[...]) * inverse_ref[...]
             dispatch_ref[:, cut] = dispatch.astype(bf16)
@@ -529,7 +535,7 @@
     ):
         for at in range(0, count, tile):
             cut = slice(at, at + tile)
-            power, inverse = guarded(jnp.sum(row_ref[:, :, cut], axis=0))
+            power, inverse = guarded(row_ref[:, cut])
             weight = (sum_ref[:, cut] + other_ref[:, cut]) * inverse
             exps_here = exp_ref[:, cut].astype(f32)
             logit_ref[:, cut] = (terms_ref[:, cut] - (exps_here * power) * weight).astype(bf16)
@@ -599,14 +605,15 @@
         lax.ppermute(own_half, KEYS, [(at, at ^ other) for at in range(blocks)])
         for other in range(1, blocks)
     ]
-    exps, own_row, column = own_logits(slot_keys, tokens, slot_devices)
-    own_row, near_keys = lax.optimization_barrier((own_row, near_keys))
     far_keys = [lax.ppermute(keys, "c", swap) for keys in near_keys]
+    all_exp, exps, row_sum, column, keys_rows = all_exps(
+        place, slot_keys, near_keys, far_keys, tokens, width
+    )
     column_other = lax.ppermute(column, "c", swap)
-    row_parts = lax.all_to_all(own_row, SLOT, 0, 0)
+    row_sum_other = lax.ppermute(row_sum, "xa", swap)
     slot_in_part = dispatch_part(exps, column, column_other, tokens)
-    keep, give = combine_part(
-        place, exps, row_parts, column, column_other, slot_in_part, out_grad, groups
+    keep, give, row_parts = combine_part(
+        place, exps, row_sum, row_sum_other, column, column_other, slot_in_part, out_grad, groups
     )
     parts = lax.all_to_all(pair_sum(keep, lax.ppermute(give, "c", swap)), CHIPS, 0, 0)
     sent, slot_in, column_total = sum_slots(parts, groups)
@@ -615,19 +622,17 @@
 
     keep, give, act, pre = experts_part(place, mine, other, w_in, w_out)
     sent = pair_sum(keep, lax.ppermute(give, "c", swap))
-    sent, near_keys, far_keys = lax.optimization_barrier((sent, near_keys, far_keys))
     terms = lax.all_to_all(sent, CHIPS, 0, 0)
-    all_exp, keys_rows = all_exps(place, slot_keys, near_keys, far_keys, tokens, width)
-    terms, all_exp, act, pre = lax.optimization_barrier((terms, all_exp, act, pre))
+    terms, act, pre = lax.optimization_barrier((terms, act, pre))
     sent = sum_terms(terms, slot_in, column_total, everyone)
     gathered = lax.all_to_all(sent, GATHERED, 0, 0)
     grad_w_in, grad_w_out = weight_grads(place, mine, other, act, pre)
     gathered, grad_w_in, grad_w_out = lax.optimization_barrier((gathered, grad_w_in, grad_w_out))
     gathered_other = lax.ppermute(gathered, "c", swap)
 
-    near = near_dots(place, out_grad, gathered, all_exp.shape[0])
+    near, grad_far = near_dots(place, out_grad, gathered, all_exp.shape[0])
     gathered_other, near = lax.optimization_barrier((gathered_other, near))
-    dots, row = comb_dots(place, all_exp, near, out_grad, row_parts, gathered_other)
+    dots, row = comb_dots(all_exp, near, grad_far, row_parts, gathered_other)
     row_other = lax.ppermute(row, "xa", swap)
     terms, dispatch, grad_rows = disp_dots(
         place, all_exp, dots, tokens, row_parts, gathered, gathered_other, width

time: 149 us -> 142 us (0.953)
  local copies, waits for them, and re-layouts: 25.6 us -> 13.6 us
  blocking collectives: 33.1 us -> 44 us
  starting transfers between devices: 34.9 us -> 27.7 us
  waiting for transfers between devices: 17.3 us -> 21.1 us
  Pallas kernels: 34.8 us -> 32.6 us
    unnamed x58 -> x40, local copies, waits for them, and re-layouts: 24.6 us -> 12.7 us
    all_to_all x2 -> x0, starting transfers between devices: 10.7 us -> none  [the longest x1 7.22 us: per_device(): row_parts = lax.all_to_all(own_row, SLOT, 0, 0)]
    all_to_all x0 -> x1, blocking collectives: none -> 10.4 us  [per_device(): terms = lax.all_to_all(sent, CHIPS, 0, 0)]
    ppermute x3, waiting for transfers between devices: 0.01 us -> 4.98 us  [per_device(): lax.ppermute(own_half, KEYS, [(at, at ^ other) for at in range(blocks)])]
    all_to_all x2 -> x0, waiting for transfers between devices: 3.2 us -> none  [the longest x1 3.2 us: per_device(): row_parts = lax.all_to_all(own_row, SLOT, 0, 0)]
    ppermute x3, starting transfers between devices: 0.63 us -> 3.61 us  [per_device(): far_keys = [lax.ppermute(keys, 'c', swap) for keys in near_keys]]
    ppermute x0 -> x1, starting transfers between devices: none -> 2.75 us  [per_device(): row_sum_other = lax.ppermute(row_sum, 'xa', swap)]
    pallas_call x4 -> x3, Pallas kernels: 10.2 us -> 8.8 us  [the longest x1 5.49 us: all_exps(): pl.pallas_call(kernel, in_specs=[in_smem()] + [pl.BlockSpec(memory_space=...]
  transfers between devices with their start and end apart: 16 -> 15, of which waited for: 6 -> 10; matrix products, arithmetic and copies ran while one was open for 0% -> 1% of each run, Pallas kernels for 16% -> 11%
where the time goes in v6:
time: 142 us
  blocking collectives  44 us (31%)
  Pallas kernels  32.6 us (23%)
  starting transfers between devices  27.7 us (20%)
  waiting for transfers between devices  21.1 us (15%)
  local copies, waits for them, and re-layouts  13.6 us (10%)
  other arithmetic  1.73 us (1%)
    unnamed x40, local copies, waits for them, and re-layouts  12.7 us
    all_to_all x1, blocking collectives, per_device(): lax.all_to_all(pair_sum(keep, lax.ppermute(give, 'c', swap)), CHIPS, 0, 0)  12.6 us
    all_to_all x1, blocking collectives, per_device(): lax.all_to_all(keys_part.reshape(seq_devices, features // seq_devices, ow...  12 us
    all_to_all x1, blocking collectives, per_device(): terms = lax.all_to_all(sent, CHIPS, 0, 0)  10.4 us
    all_to_all x1, blocking collectives, per_device(): mine = lax.all_to_all(sent, CHIPS, 0, 0)  9.05 us
    all_to_all x1, waiting for transfers between devices, per_device(): gathered = lax.all_to_all(sent, GATHERED, 0, 0)  8.45 us
    pallas_call x1, Pallas kernels, weight_grads(): pl.pallas_call(kernel, grid=(experts,), in_specs=[in_smem(), pl.BlockSpec...  6.32 us
    ppermute x3, starting transfers between devices, per_device(): lax.ppermute(own_half, KEYS, [(at, at ^ other) for at in range(blocks)])  5.81 us
  transfers between devices with their start and end apart: 15, of which 10 were waited for; matrix products, arithmetic and copies ran while one was open for 1% of the time, Pallas kernels for 11%

profile of v6, /device:TPU:1, one launch (start us, length us, event | category | flops | bytes accessed | tf_op | source)
XLA Modules:
  0.0 141.7 jit_solution(14515667870439337410)
XLA Ops:
  0.6 0.9 constant_dynamic-slice_fusion
  1.6 5.4 %collective-permute-start.2 = (bf16[640,128]{1,0:T(8,128)(2,1)S(1)}, bf16[640,128]{1,0:T(8,128)(2,1)S(1)}, u32[]{:S(2)}, u32[]{:S(2)}) collective-permute-start(bf16[640,128]{1,0:T(8,128)(2,1)S(1)} %constant_dynamic-slice_fusion), channel_id=1, source_target_pairs={{0,3},{1,2},{2,1},{3,0},{4,7},{5,6},{6,5},{7,4},{8,11},{9,10},{10,... | collective-permute-start | bytes 491528 | tf_op jit(solution)/shard_map/ppermute | solution.py:605
  7.0 0.3 collective-permute-start.1
  7.3 0.1 collective-permute-start
  7.4 3.5 %collective-permute-done.2.refs_3_ = bf16[640,128]{1,0:T(8,128)(2,1)S(1)} collective-permute-done((bf16[640,128]{1,0:T(8,128)(2,1)S(1)}, bf16[640,128]{1,0:T(8,128)(2,1)S(1)}, u32[]{:S(2)}, u32[]{:S(2)}) %collective-permute-start.2) | collective-permute-done | bytes 163872 | tf_op jit(solution)/shard_map/ppermute | solution.py:605
  10.9 2.1 %collective-permute-start.5 = (bf16[640,128]{1,0:T(8,128)(2,1)S(1)}, bf16[640,128]{1,0:T(8,128)(2,1)S(1)}, u32[]{:S(2)}, u32[]{:S(2)}) collective-permute-start(bf16[640,128]{1,0:T(8,128)(2,1)S(1)} %collective-permute-done.2.refs_3_), channel_id=1, source_target_pairs={{0,8},{8,0},{1,9},{9,1},{2,10},{10,2},{3,11},{11,3},{4,12},{12,4},... | collective-permute-start | bytes 491528 | tf_op jit(solution)/shard_map/ppermute | solution.py:608
  13.0 1.4 %collective-permute-done.1.refs_2_ = bf16[640,128]{1,0:T(8,128)(2,1)S(1)} collective-permute-done((bf16[640,128]{1,0:T(8,128)(2,1)S(1)}, bf16[640,128]{1,0:T(8,128)(2,1)S(1)}, u32[]{:S(2)}, u32[]{:S(2)}) %collective-permute-start.1) | collective-permute-done | bytes 163872 | tf_op jit(solution)/shard_map/ppermute | solution.py:605
  14.4 1.5 %collective-permute-start.4 = (bf16[640,128]{1,0:T(8,128)(2,1)S(1)}, bf16[640,128]{1,0:T(8,128)(2,1)S(1)}, u32[]{:S(2)}, u32[]{:S(2)}) collective-permute-start(bf16[640,128]{1,0:T(8,128)(2,1)S(1)} %collective-permute-done.1.refs_2_), channel_id=1, source_target_pairs={{0,8},{8,0},{1,9},{9,1},{2,10},{10,2},{3,11},{11,3},{4,12},{12,4},... | collective-permute-start | bytes 491528 | tf_op jit(solution)/shard_map/ppermute | solution.py:608
  16.0 0.0 collective-permute-done.refs_1_
  16.0 0.0 collective-permute-start.3
  16.0 0.1 pad_add_fusion.place_ref
  16.0 0.0 collective-permute-done.5.refs_6_
  16.0 0.9 collective-permute-done.4.refs_5_
  17.0 0.4 collective-permute-done.3.refs_4_
  17.4 2.5 %copy-done = bf16[2048,1280]{1,0:T(8,128)(2,1)S(1)} copy-done((bf16[2048,1280]{1,0:T(8,128)(2,1)S(1)}, bf16[2048,1280]{1,0:T(8,128)(2,1)}, u32[]{:S(2)}) %copy-start) | copy-done | bytes 5242904
  19.9 1.0 copy-done.13
  20.8 5.5 %all_exps.1 = (bf16[512,2048]{1,0:T(8,128)(2,1)S(1)}, f32[128,2048]{1,0:T(8,128)S(1)}, f32[1,2048]{1,0:T(1,128)S(1)}, f32[128,128]{1,0:T(8,128)S(1)}, bf16[2,160,512]{2,1,0:T(8,128)(2,1)S(1)}) custom-call(s32[3]{0:T(128)S(1)} %pad_add_fusion.place_ref, bf16[1280,128]{1,0:T(8,128)(2,1)S(1)} %copy-done.13, bf16[640,128]{1,0:T(8,128)(2,1)S(1)} %collective-permute-done.refs_1_, ...), custom_call_target="tpu_custom_call" | custom-call | flops 2684354560 | bytes 5242880 | tf_op jit(solution)/shard_map/all_exps/pallas_call | solution.py:381
  26.3 0.0 copy-start.11
  26.3 0.7 copy-done.11
  27.1 0.2 collective-permute-start.7
  27.3 2.7 %collective-permute-start.6 = (f32[1,2048]{1,0:T(1,128)S(1)}, f32[1,2048]{1,0:T(1,128)S(1)}, u32[]{:S(2)}, u32[]{:S(2)}) collective-permute-start(f32[1,2048]{1,0:T(1,128)S(1)} %get-tuple-element.42.row_ref), channel_id=1, source_target_pairs={{0,4},{4,0},{1,5},{5,1},{2,6},{6,2},{3,7},{7,3},{8,12},{12,8},{9,1... | collective-permute-start | bytes 24584 | tf_op jit(solution)/shard_map/ppermute | solution.py:613
  30.0 0.0 collective-permute-done.7.other_ref
  30.0 0.9 dispatch_part.1.in_ref
  31.0 0.3 collective-permute-done.6.row_other_ref
  31.3 1.2 copy-done.2
  32.5 1.4 combine_part.1
  34.0 0.6 collective-permute-start.8
  34.6 1.3 collective-permute-done.8.received_ref
  35.9 0.1 pair_sum.2
  35.9 12.6 %all_to_all.25.parts_ref = bf16[8,16,1408]{2,1,0:T(8,128)(2,1)S(1)} all-to-all(bf16[8,16,1408]{2,1,0:T(8,128)(2,1)S(1)} %pair_sum.2), channel_id=1, replica_groups=mesh['zl'=2,'y'=4,'c'=2,'xa'=2,'xb'=2,'zh'=2] {'zl','y'}, dimensions={0} | all-to-all | bytes 720896 | tf_op jit(solution)/shard_map/all_to_all | solution.py:618
  48.6 0.2 sum_slots.1
  48.8 9.0 %all_to_all.26.mine_ref = bf16[8,16,1280]{2,1,0:T(8,128)(2,1)S(1)} all-to-all(bf16[8,16,1280]{2,1,0:T(8,128)(2,1)S(1)} %get-tuple-element.46), channel_id=1, replica_groups=mesh['zl'=2,'y'=4,'c'=2,'xa'=2,'xb'=2,'zh'=2] {'zl','y'}, dimensions={0} | all-to-all | bytes 655360 | tf_op jit(solution)/shard_map/all_to_all | solution.py:620
  57.8 2.4 %collective-permute-start.9 = (bf16[8,16,1280]{2,1,0:T(8,128)(2,1)S(1)}, bf16[8,16,1280]{2,1,0:T(8,128)(2,1)S(1)}, u32[]{:S(2)}, u32[]{:S(2)}) collective-permute-start(bf16[8,16,1280]{2,1,0:T(8,128)(2,1)S(1)} %all_to_all.26.mine_ref), channel_id=1, source_target_pairs={{0,8},{8,0},{1,9},{9,1},{2,10},{10,2},{3,11},{11,3},{4,12},{12,4},... | collective-permute-start | bytes 983048 | tf_op jit(solution)/shard_map/ppermute | solution.py:621
  60.2 1.3 collective-permute-done.9.other_ref
  61.5 5.4 %experts_part.1 = (bf16[8,16,1280]{2,1,0:T(8,128)(2,1)S(1)}, bf16[8,16,1280]{2,1,0:T(8,128)(2,1)S(1)}, bf16[8,16,192]{2,1,0:T(8,128)(2,1)S(1)}, bf16[8,16,192]{2,1,0:T(8,128)(2,1)S(1)}) custom-call(s32[3]{0:T(128)S(1)} %pad_add_fusion.place_ref, bf16[8,16,1280]{2,1,0:T(8,128)(2,1)S(1)} %all_to_all.26.mine_ref, ...), custom_call_target="tpu_custom_call" | custom-call | flops 251658240 | bytes 7864320 | tf_op jit(solution)/shard_map/experts_part/pallas_call | solution.py:250
  66.9 0.4 collective-permute-start.10
  67.3 1.3 collective-permute-done.10.received_ref
  68.6 0.1 pair_sum.3
  68.7 10.4 %all_to_all.27.terms_ref = bf16[8,16,1280]{2,1,0:T(8,128)(2,1)S(1)} all-to-all(bf16[8,16,1280]{2,1,0:T(8,128)(2,1)S(1)} %pair_sum.3), channel_id=1, replica_groups=mesh['zl'=2,'y'=4,'c'=2,'xa'=2,'xb'=2,'zh'=2] {'zl','y'}, dimensions={0} | all-to-all | bytes 655360 | tf_op jit(solution)/shard_map/all_to_all | solution.py:625
  79.1 0.1 sum_terms.1
  79.2 1.1 copy-done.4
  80.3 5.6 %all-to-all-start.3 = ((bf16[32,16,1408]{2,1,0:T(8,128)(2,1)}), bf16[32,16,1408]{2,1,0:T(8,128)(2,1)S(1)}, u32[]{:S(2)}, u32[]{:S(2)}) async-start(bf16[32,16,1408]{2,1,0:T(8,128)(2,1)} %copy-done.4), calls=%async_computation.3 | async-start | bytes 2883584 | tf_op jit(solution)/shard_map/all_to_all | solution.py:628
  85.9 0.0 copy-start.8
  85.9 1.0 copy-done.8
  86.9 1.0 copy-done.10
  87.9 0.8 copy-done.15
  88.7 0.8 copy-done.17
  89.5 6.3 %weight_grads.1 = (bf16[8,192,1280]{2,1,0:T(8,128)(2,1)}, bf16[8,192,1280]{2,1,0:T(8,128)(2,1)}) custom-call(s32[3]{0:T(128)S(1)} %pad_add_fusion.place_ref, bf16[8,16,1280]{2,1,0:T(8,128)(2,1)S(1)} %copy-done.8, bf16[8,16,1280]{2,1,0:T(8,128)(2,1)S(1)} %copy-done.10, bf16[8,16,192]{2,1,0:T(8,128)(2,1)S(1)} %copy-done.15, bf16[8,16,192]{2,1,0:T(8,128)(2,1)S(1)} %copy-done.17), custom_call_target="tpu_custom_call" | custom-call | flops 125829120 | bytes 7864320 | tf_op jit(solution)/shard_map/weight_grads/pallas_call | solution.py:282
  95.9 8.4 %all-to-all-done.3.mine_ref = bf16[32,16,1408]{2,1,0:T(8,128)(2,1)S(1)} async-done(((bf16[32,16,1408]{2,1,0:T(8,128)(2,1)}), bf16[32,16,1408]{2,1,0:T(8,128)(2,1)S(1)}, u32[]{:S(2)}, u32[]{:S(2)}) %all-to-all-start.3) | async-done | bytes 1441824 | tf_op jit(solution)/shard_map/all_to_all | solution.py:628
  104.3 3.2 %collective-permute-start.11 = (bf16[32,16,1408]{2,1,0:T(8,128)(2,1)S(1)}, bf16[32,16,1408]{2,1,0:T(8,128)(2,1)S(1)}, u32[]{:S(2)}, u32[]{:S(2)}) collective-permute-start(bf16[32,16,1408]{2,1,0:T(8,128)(2,1)S(1)} %all-to-all-done.3.mine_ref), channel_id=1, source_target_pairs={{0,8},{8,0},{1,9},{9,1},{2,10},{10,2},{3,11},{11,3},{4,12},{12,4},... | collective-permute-start | bytes 4325384 | tf_op jit(solution)/shard_map/ppermute | solution.py:631
  107.5 2.5 %copy-done.3 = bf16[2048,1280]{1,0:T(8,128)(2,1)S(1)} copy-done((bf16[2048,1280]{1,0:T(8,128)(2,1)S(1)}, bf16[2048,1280]{1,0:T(8,128)(2,1)}, u32[]{:S(2)}) %copy-start.3) | copy-done | bytes 5242904
  110.0 2.6 %near_dots.1 = (f32[512,2048]{1,0:T(8,128)S(1)}, bf16[2048,640]{1,0:T(8,128)(2,1)S(1)}) custom-call(s32[3]{0:T(128)S(1)} %pad_add_fusion.place_ref, bf16[2048,1280]{1,0:T(8,128)(2,1)S(1)} %copy-done.3, bf16[32,16,1408]{2,1,0:T(8,128)(2,1)S(1)} %all-to-all-done.3.mine_ref), custom_call_target="tpu_custom_call" | custom-call | flops 1342177280 | bytes 2621440 | tf_op jit(solution)/shard_map/near_dots/pallas_call | solution.py:430
  112.6 0.0 slice-start
  112.6 0.0 slice-start.1
  112.6 1.9 %comb_dots.1 = (f32[512,2048]{1,0:T(8,128)S(1)}, f32[1,2048]{1,0:T(1,128)S(1)}) custom-call(bf16[512,2048]{1,0:T(8,128)(2,1)S(1)} %get-tuple-element.40.exp_ref, f32[512,2048]{1,0:T(8,128)S(1)} %get-tuple-element.60.near_ref, bf16[2048,640]{1,0:T(8,128)(2,1)S(1)} %get-tuple-element.61.grad_ref, f32[1,2048]{1,0:T(1,128)S(1)} %get-tuple-element.62.row_ref, ...), custom_call_target="tpu_custom_call" | custom-call | flops 1342177280 | bytes 2621440 | tf_op jit(solution)/shard_map/comb_dots/pallas_call | solution.py:460
  114.5 2.5 %collective-permute-start.12 = (f32[1,2048]{1,0:T(1,128)S(1)}, f32[1,2048]{1,0:T(1,128)S(1)}, u32[]{:S(2)}, u32[]{:S(2)}) collective-permute-start(f32[1,2048]{1,0:T(1,128)S(1)} %get-tuple-element.67.sum_ref), channel_id=1, source_target_pairs={{0,4},{4,0},{1,5},{5,1},{2,6},{6,2},{3,7},{7,3},{8,12},{12,8},{9,1... | collective-permute-start | bytes 24584 | tf_op jit(solution)/shard_map/ppermute | solution.py:636
  117.0 4.4 %disp_dots.1 = (f32[512,2048]{1,0:T(8,128)S(1)}, bf16[512,2048]{1,0:T(8,128)(2,1)S(1)}, bf16[2,160,512]{2,1,0:T(8,128)(2,1)S(1)}) custom-call(s32[3]{0:T(128)S(1)} %pad_add_fusion.place_ref, bf16[512,2048]{1,0:T(8,128)(2,1)S(1)} %get-tuple-element.40.exp_ref, f32[512,2048]{1,0:T(8,128)S(1)} %get-tuple-element.64.dot_ref, bf16[2048,1280]{1,0:T(8,128)(2,1)S(1)} %bitcast.7, ...), custom_call_target="tpu_custom_call" | custom-call | flops 2684354560 | bytes 5242880 | tf_op jit(solution)/shard_map/disp_dots/pallas_call | solution.py:504
  121.5 1.7 %logit_grads.1 = (bf16[512,2048]{1,0:T(8,128)(2,1)S(1)}, bf16[160,2048]{1,0:T(8,128)(2,1)S(1)}) custom-call(s32[3]{0:T(128)S(1)} %pad_add_fusion.place_ref, bf16[512,2048]{1,0:T(8,128)(2,1)S(1)} %get-tuple-element.40.exp_ref, f32[512,2048]{1,0:T(8,128)S(1)} %get-tuple-element.65.terms_ref, bf16[512,2048]{1,0:T(8,128)(2,1)S(1)} %get-tuple-element.66.dispatch_ref, ...), custom_call_target="tpu_custom_call" | custom-call | flops 671088640 | bytes 4194304 | tf_op jit(solution)/shard_map/logit_grads/pallas_call | solution.py:546
  123.2 0.6 collective-permute-start.13
  123.7 2.1 %own_parts.1 = (bf16[1280,128]{1,0:T(8,128)(2,1)S(1)}, f32[160,2048]{1,0:T(8,128)S(1)}) custom-call(s32[3]{0:T(128)S(1)} %pad_add_fusion.place_ref, bf16[512,2048]{1,0:T(8,128)(2,1)S(1)} %get-tuple-element.70.logit_ref, bf16[512,2048]{1,0:T(8,128)(2,1)S(1)} %get-tuple-element.66.dispatch_ref, bf16[2048,1280]{1,0:T(8,128)(2,1)S(1)} %bitcast.7, ...), custom_call_target="tpu_custom_call" | custom-call | flops 671088640 | bytes 5242880 | tf_op jit(solution)/shard_map/own_parts/pallas_call | solution.py:574
  125.8 12.0 %all_to_all.28 = bf16[16,80,128]{2,1,0:T(8,128)(2,1)S(1)} all-to-all(bf16[16,80,128]{2,1,0:T(8,128)(2,1)S(1)} %bitcast.8), channel_id=1, replica_groups=mesh['zl'=2,'y'=4,'c'=2,'xa'=2,'xb'=2,'zh'=2] {'zl','y','c'}, dimensions={0} | all-to-all | bytes 655360 | tf_op jit(solution)/shard_map/all_to_all | solution.py:647
  137.8 0.7 convert_reduce_fusion
  138.5 2.3 %collective-permute-done.13 = bf16[160,2048]{1,0:T(8,128)(2,1)S(1)} collective-permute-done((bf16[160,2048]{1,0:T(8,128)(2,1)S(1)}, bf16[160,2048]{1,0:T(8,128)(2,1)S(1)}, u32[]{:S(2)}, u32[]{:S(2)}) %collective-permute-start.13) | collective-permute-done | bytes 655392 | tf_op jit(solution)/shard_map/ppermute | solution.py:643
  140.7 1.0 fusion
  (29 shorter events, 0.1 us)
Async XLA Ops:
  1.6 9.4 %collective-permute-start.2 = (bf16[640,128]{1,0:T(8,128)(2,1)S(1)}, bf16[640,128]{1,0:T(8,128)(2,1)S(1)}, u32[]{:S(2)}, u32[]{:S(2)}) collective-permute-start(bf16[640,128]{1,0:T(8,128)(2,1)S(1)} %constant_dynamic-slice_fusion), channel_id=1, source_target_pairs={{0,3},{1,2},{2,1},{3,0},{4,7},{5,6},{6,5},{7,4},{8,11},{9,10},{10,... | collective-permute-start | bytes 491528 | tf_op jit(solution)/shard_map/ppermute | solution.py:605
  7.0 7.4 %collective-permute-start.1 = (bf16[640,128]{1,0:T(8,128)(2,1)S(1)}, bf16[640,128]{1,0:T(8,128)(2,1)S(1)}, u32[]{:S(2)}, u32[]{:S(2)}) collective-permute-start(bf16[640,128]{1,0:T(8,128)(2,1)S(1)} %constant_dynamic-slice_fusion), channel_id=1, source_target_pairs={{0,2},{1,3},{2,0},{3,1},{4,6},{5,7},{6,4},{7,5},{8,10},{9,11},{10,... | collective-permute-start | bytes 491528 | tf_op jit(solution)/shard_map/ppermute | solution.py:605
  7.3 8.7 %collective-permute-start = (bf16[640,128]{1,0:T(8,128)(2,1)S(1)}, bf16[640,128]{1,0:T(8,128)(2,1)S(1)}, u32[]{:S(2)}, u32[]{:S(2)}) collective-permute-start(bf16[640,128]{1,0:T(8,128)(2,1)S(1)} %constant_dynamic-slice_fusion), channel_id=1, source_target_pairs={{0,1},{1,0},{2,3},{3,2},{4,5},{5,4},{6,7},{7,6},{8,9},{9,8},{10,11... | collective-permute-start | bytes 491528 | tf_op jit(solution)/shard_map/ppermute | solution.py:605
  10.9 5.1 %collective-permute-start.5 = (bf16[640,128]{1,0:T(8,128)(2,1)S(1)}, bf16[640,128]{1,0:T(8,128)(2,1)S(1)}, u32[]{:S(2)}, u32[]{:S(2)}) collective-permute-start(bf16[640,128]{1,0:T(8,128)(2,1)S(1)} %collective-permute-done.2.refs_3_), channel_id=1, source_target_pairs={{0,8},{8,0},{1,9},{9,1},{2,10},{10,2},{3,11},{11,3},{4,12},{12,4},... | collective-permute-start | bytes 491528 | tf_op jit(solution)/shard_map/ppermute | solution.py:608
  14.4 2.6 %collective-permute-start.4 = (bf16[640,128]{1,0:T(8,128)(2,1)S(1)}, bf16[640,128]{1,0:T(8,128)(2,1)S(1)}, u32[]{:S(2)}, u32[]{:S(2)}) collective-permute-start(bf16[640,128]{1,0:T(8,128)(2,1)S(1)} %collective-permute-done.1.refs_2_), channel_id=1, source_target_pairs={{0,8},{8,0},{1,9},{9,1},{2,10},{10,2},{3,11},{11,3},{4,12},{12,4},... | collective-permute-start | bytes 491528 | tf_op jit(solution)/shard_map/ppermute | solution.py:608
  16.0 1.4 collective-permute-start.3
  17.4 2.5 %copy-start = (bf16[2048,1280]{1,0:T(8,128)(2,1)S(1)}, bf16[2048,1280]{1,0:T(8,128)(2,1)}, u32[]{:S(2)}) copy-start(bf16[2048,1280]{1,0:T(8,128)(2,1)} %tokens_ref.5) | copy-start | bytes 15728644
  19.8 1.0 copy-start.13
  20.8 9.2 %copy-start.1 = (bf16[2048,1280]{1,0:T(8,128)(2,1)S(1)}, bf16[2048,1280]{1,0:T(8,128)(2,1)}, u32[]{:S(2)}) copy-start(bf16[2048,1280]{1,0:T(8,128)(2,1)} %tokens_ref.5) | copy-start | bytes 15728644
  26.3 0.7 copy-start.11
  27.1 3.0 %collective-permute-start.7 = (f32[128,128]{1,0:T(8,128)S(1)}, f32[128,128]{1,0:T(8,128)S(1)}, u32[]{:S(2)}, u32[]{:S(2)}) collective-permute-start(f32[128,128]{1,0:T(8,128)S(1)} %get-tuple-element.43.column_ref), channel_id=1, source_target_pairs={{0,8},{8,0},{1,9},{9,1},{2,10},{10,2},{3,11},{11,3},{4,12},{12,4},... | collective-permute-start | bytes 196616 | tf_op jit(solution)/shard_map/ppermute | solution.py:612
  27.3 4.0 %collective-permute-start.6 = (f32[1,2048]{1,0:T(1,128)S(1)}, f32[1,2048]{1,0:T(1,128)S(1)}, u32[]{:S(2)}, u32[]{:S(2)}) collective-permute-start(f32[1,2048]{1,0:T(1,128)S(1)} %get-tuple-element.42.row_ref), channel_id=1, source_target_pairs={{0,4},{4,0},{1,5},{5,1},{2,6},{6,2},{3,7},{7,3},{8,12},{12,8},{9,1... | collective-permute-start | bytes 24584 | tf_op jit(solution)/shard_map/ppermute | solution.py:613
  30.0 2.5 %copy-start.2 = (bf16[2048,1280]{1,0:T(8,128)(2,1)S(1)}, bf16[2048,1280]{1,0:T(8,128)(2,1)}, u32[]{:S(2)}) copy-start(bf16[2048,1280]{1,0:T(8,128)(2,1)} %grad_ref.3) | copy-start | bytes 15728644
  32.5 28.9 %copy-start.5 = (bf16[8,192,1280]{2,1,0:T(8,128)(2,1)S(1)}, bf16[8,192,1280]{2,1,0:T(8,128)(2,1)}, u32[]{:S(2)}) copy-start(bf16[8,192,1280]{2,1,0:T(8,128)(2,1)} %w_in_ref.1) | copy-start | bytes 11796484
  32.5 28.9 %copy-start.6 = (bf16[8,192,1280]{2,1,0:T(8,128)(2,1)S(1)}, bf16[8,192,1280]{2,1,0:T(8,128)(2,1)}, u32[]{:S(2)}) copy-start(bf16[8,192,1280]{2,1,0:T(8,128)(2,1)} %w_out_ref.1) | copy-start | bytes 11796484
  34.0 1.9 %collective-permute-start.8 = (bf16[8,16,1280]{2,1,0:T(8,128)(2,1)S(1)}, bf16[8,16,1280]{2,1,0:T(8,128)(2,1)S(1)}, u32[]{:S(2)}, u32[]{:S(2)}) collective-permute-start(bf16[8,16,1280]{2,1,0:T(8,128)(2,1)S(1)} %get-tuple-element.45), channel_id=1, source_target_pairs={{0,8},{8,0},{1,9},{9,1},{2,10},{10,2},{3,11},{11,3},{4,12},{12,4},... | collective-permute-start | bytes 983048 | tf_op jit(solution)/shard_map/ppermute | solution.py:618
  57.8 9.0 %copy-start.7 = (bf16[8,16,1280]{2,1,0:T(8,128)(2,1)}, bf16[8,16,1280]{2,1,0:T(8,128)(2,1)S(1)}, u32[]{:S(2)}) copy-start(bf16[8,16,1280]{2,1,0:T(8,128)(2,1)S(1)} %all_to_all.26.mine_ref) | copy-start | bytes 983044
  57.8 3.6 %collective-permute-start.9 = (bf16[8,16,1280]{2,1,0:T(8,128)(2,1)S(1)}, bf16[8,16,1280]{2,1,0:T(8,128)(2,1)S(1)}, u32[]{:S(2)}, u32[]{:S(2)}) collective-permute-start(bf16[8,16,1280]{2,1,0:T(8,128)(2,1)S(1)} %all_to_all.26.mine_ref), channel_id=1, source_target_pairs={{0,8},{8,0},{1,9},{9,1},{2,10},{10,2},{3,11},{11,3},{4,12},{12,4},... | collective-permute-start | bytes 983048 | tf_op jit(solution)/shard_map/ppermute | solution.py:621
  61.5 5.4 %copy-start.9 = (bf16[8,16,1280]{2,1,0:T(8,128)(2,1)}, bf16[8,16,1280]{2,1,0:T(8,128)(2,1)S(1)}, u32[]{:S(2)}) copy-start(bf16[8,16,1280]{2,1,0:T(8,128)(2,1)S(1)} %collective-permute-done.9.other_ref) | copy-start | bytes 983044
  66.9 12.2 %copy-start.14 = (bf16[8,16,192]{2,1,0:T(8,128)(2,1)}, bf16[8,16,192]{2,1,0:T(8,128)(2,1)S(1)}, u32[]{:S(2)}) copy-start(bf16[8,16,192]{2,1,0:T(8,128)(2,1)S(1)} %get-tuple-element.54.act_ref) | copy-start | bytes 147460
  66.9 12.2 %copy-start.16 = (bf16[8,16,192]{2,1,0:T(8,128)(2,1)}, bf16[8,16,192]{2,1,0:T(8,128)(2,1)S(1)}, u32[]{:S(2)}) copy-start(bf16[8,16,192]{2,1,0:T(8,128)(2,1)S(1)} %get-tuple-element.55.pre_ref) | copy-start | bytes 147460
  66.9 1.7 %collective-permute-start.10 = (bf16[8,16,1280]{2,1,0:T(8,128)(2,1)S(1)}, bf16[8,16,1280]{2,1,0:T(8,128)(2,1)S(1)}, u32[]{:S(2)}, u32[]{:S(2)}) collective-permute-start(bf16[8,16,1280]{2,1,0:T(8,128)(2,1)S(1)} %get-tuple-element.48), channel_id=1, source_target_pairs={{0,8},{8,0},{1,9},{9,1},{2,10},{10,2},{3,11},{11,3},{4,12},{12,4},... | collective-permute-start | bytes 983048 | tf_op jit(solution)/shard_map/ppermute | solution.py:624
  79.2 1.1 copy-start.4
  80.3 24.0 %all-to-all-start.3 = ((bf16[32,16,1408]{2,1,0:T(8,128)(2,1)}), bf16[32,16,1408]{2,1,0:T(8,128)(2,1)S(1)}, u32[]{:S(2)}, u32[]{:S(2)}) async-start(bf16[32,16,1408]{2,1,0:T(8,128)(2,1)} %copy-done.4), calls=%async_computation.3 | async-start | bytes 2883584 | tf_op jit(solution)/shard_map/all_to_all | solution.py:628
  85.9 1.0 copy-start.8
  86.9 1.0 copy-start.10
  87.9 0.8 copy-start.15
  88.7 0.8 copy-start.17
  104.3 8.3 %collective-permute-start.11 = (bf16[32,16,1408]{2,1,0:T(8,128)(2,1)S(1)}, bf16[32,16,1408]{2,1,0:T(8,128)(2,1)S(1)}, u32[]{:S(2)}, u32[]{:S(2)}) collective-permute-start(bf16[32,16,1408]{2,1,0:T(8,128)(2,1)S(1)} %all-to-all-done.3.mine_ref), channel_id=1, source_target_pairs={{0,8},{8,0},{1,9},{9,1},{2,10},{10,2},{3,11},{11,3},{4,12},{12,4},... | collective-permute-start | bytes 4325384 | tf_op jit(solution)/shard_map/ppermute | solution.py:631
  107.5 2.5 %copy-start.3 = (bf16[2048,1280]{1,0:T(8,128)(2,1)S(1)}, bf16[2048,1280]{1,0:T(8,128)(2,1)}, u32[]{:S(2)}) copy-start(bf16[2048,1280]{1,0:T(8,128)(2,1)} %grad_ref.3) | copy-start | bytes 15728644
  112.6 4.5 %slice-start = ((s8[5242880]{0:T(1024)(128)(4,1)}), s8[4194304]{0:T(1024)(128)(4,1)S(1)}, s32[]{:S(2)}) async-start(s8[5242880]{0:T(1024)(128)(4,1)} %bitcast.6), calls=%async_computation.5 | async-start | bytes 8388608
  112.6 4.4 %slice-start.1 = ((s8[5242880]{0:T(1024)(128)(4,1)}), s8[1048576]{0:T(1024)(128)(4,1)S(1)}, s32[]{:S(2)}) async-start(s8[5242880]{0:T(1024)(128)(4,1)} %bitcast.6), calls=%async_computation.6 | async-start | bytes 2097152
  114.5 6.9 %collective-permute-start.12 = (f32[1,2048]{1,0:T(1,128)S(1)}, f32[1,2048]{1,0:T(1,128)S(1)}, u32[]{:S(2)}, u32[]{:S(2)}) collective-permute-start(f32[1,2048]{1,0:T(1,128)S(1)} %get-tuple-element.67.sum_ref), channel_id=1, source_target_pairs={{0,4},{4,0},{1,5},{5,1},{2,6},{6,2},{3,7},{7,3},{8,12},{12,8},{9,1... | collective-permute-start | bytes 24584 | tf_op jit(solution)/shard_map/ppermute | solution.py:636
  117.0 4.4 %copy-start.12 = (bf16[2,160,512]{2,1,0:T(8,128)(2,1)S(1)}, bf16[2,160,512]{2,1,0:T(8,128)(2,1)}, u32[]{:S(2)}) copy-start(bf16[2,160,512]{2,1,0:T(8,128)(2,1)} %copy-done.11) | copy-start | bytes 983044
  123.2 17.6 %collective-permute-start.13 = (bf16[160,2048]{1,0:T(8,128)(2,1)S(1)}, bf16[160,2048]{1,0:T(8,128)(2,1)S(1)}, u32[]{:S(2)}, u32[]{:S(2)}) collective-permute-start(bf16[160,2048]{1,0:T(8,128)(2,1)S(1)} %get-tuple-element.72), channel_id=1, source_target_pairs={{0,4},{4,0},{1,5},{5,1},{2,6},{6,2},{3,7},{7,3},{8,12},{12,8},{9,1... | collective-permute-start | bytes 1966088 | tf_op jit(solution)/shard_map/ppermute | solution.py:643

commit v7 on v6

--- a/solution.py
+++ b/solution.py
@@ -213,31 +213,27 @@
     block = mine.shape[1]
     half = features // 2
 
-    def kernel(place_ref, mine_ref, other_ref, w_in_ref, w_out_ref, keep_ref, give_ref, act_hbm, pre_hbm, act_ref, pre_ref, sems):
+    def kernel(place_ref, mine_ref, other_ref, w_in_ref, w_out_ref, keep_ref, give_ref, act_hbm, pre_hbm, act_ref, pre_ref, whole_ref, out_ref, sems):
         here, there = halves(place_ref, half)
 
         def inward(at, weights_ref, e):
             cut = slice(at * half, (at + 1) * half)
-            near = lax.dot_general(
-                mine_ref[e, :, cut], weights_ref[e, :, here], cols_contract, preferred_element_type=f32
+            whole_ref[e, at, :, here] = mine_ref[e, :, cut]
+            whole_ref[e, at, :, there] = other_ref[e, :, cut]
+            return lax.dot_general(
+                whole_ref[e, at], weights_ref[e], cols_contract, preferred_element_type=f32
             )
-            far = lax.dot_general(
-                other_ref[e, :, cut], weights_ref[e, :, there], cols_contract, preferred_element_type=f32
-            )
-            return near + far
 
         for e in range(experts):
             hidden_pre = inward(0, w_in_ref, e)
             act_grad = inward(1, w_out_ref, e)
             act = gelu_tanh(hidden_pre).astype(bf16)
             pre = (act_grad * gelu_slope(hidden_pre)).astype(bf16)
-            for cut, out_ref in ((here, keep_ref), (there, give_ref)):
-                out_ref[e, :, :half] = jnp.dot(
-                    act, w_out_ref[e, :, cut], preferred_element_type=f32
-                ).astype(bf16)
-                out_ref[e, :, half:] = jnp.dot(
-                    pre, w_in_ref[e, :, cut], preferred_element_type=f32
-                ).astype(bf16)
+            out_ref[e, 0] = jnp.dot(act, w_out_ref[e], preferred_element_type=f32).astype(bf16)
+            out_ref[e, 1] = jnp.dot(pre, w_in_ref[e], preferred_element_type=f32).astype(bf16)
+            for cut, sent_ref in ((here, keep_ref), (there, give_ref)):
+                sent_ref[e, :, :half] = out_ref[e, 0, :, cut]
+                sent_ref[e, :, half:] = out_ref[e, 1, :, cut]
             act_ref[e] = act
             pre_ref[e] = pre
         first = pltpu.make_async_copy(act_ref, act_hbm, sems.at[0])
@@ -257,7 +253,9 @@
             jax.ShapeDtypeStruct((experts, block, hidden), bf16),
             jax.ShapeDtypeStruct((experts, block, hidden), bf16),
         ],
-        scratch_shapes=[pltpu.VMEM((experts, block, hidden), bf16)] * 2 + [pltpu.SemaphoreType.DMA((2,))],
+        scratch_shapes=[pltpu.VMEM((experts, block, hidden), bf16)] * 2
+        + [pltpu.VMEM((experts, 2, block, features), bf16)] * 2
+        + [pltpu.SemaphoreType.DMA((2,))],
         compiler_params=params(GRANT),
         cost_estimate=cost(8 * experts * block * hidden * features, 4 * experts * hidden * features),
         name="experts_part",
@@ -331,18 +329,11 @@
     others = len(near_keys)
     slots = (others + 1) * block
 
-    def kernel(place_ref, *refs):
-        blocks_hbm = refs[: 2 * others + 1]
-        tokens_ref, all_ref, own_ref, row_ref, column_ref, rows_ref = refs[2 * others + 1 : 2 * others + 7]
-        turned_ref, found_ref, keys_ref, *block_refs = refs[2 * others + 7 : -1]
-        sems = refs[-1]
-        started = []
-        for at, target in enumerate([keys_ref] + block_refs):
-            started.append(pltpu.make_async_copy(blocks_hbm[at], target, sems.at[at]))
-            started[at].start()
-        near_refs, far_refs = block_refs[:others], block_refs[others:]
-        for copy in started:
-            copy.wait()
+    def kernel(place_ref, keys_ref, *refs):
+        near_refs, far_refs = refs[:others], refs[others : 2 * others]
+        (
+            tokens_ref, all_ref, own_ref, row_ref, column_ref, rows_ref, turned_ref, found_ref
+        ) = refs[2 * others :]
         core, at_own = place_ref[0], place_ref[1]
         here, there = halves(place_ref, half)
 
@@ -380,9 +371,7 @@
 
     return pl.pallas_call(
         kernel,
-        in_specs=[in_smem()]
-        + [pl.BlockSpec(memory_space=pltpu.HBM)] * (2 * others + 1)
-        + [whole_in_vmem()],
+        in_specs=[in_smem()] + [whole_in_vmem()] * (2 * others + 2),
         out_specs=[whole_in_vmem()] * 5,
         out_shape=[
             jax.ShapeDtypeStruct((slots, count), bf16),
@@ -394,10 +383,7 @@
         scratch_shapes=[
             pltpu.VMEM((slots, features), bf16),
             pltpu.VMEM((slots, count), f32),
-            pltpu.VMEM((features, block), bf16),
-        ]
-        + [pltpu.VMEM((half, block), bf16)] * (2 * others)
-        + [pltpu.SemaphoreType.DMA((2 * others + 1,))],
+        ],
         compiler_params=params(GRANT),
         cost_estimate=cost(2 * slots * features * count, 2 * features * count),
         name="all_exps",
@@ -557,14 +543,19 @@
     )(place, exps, terms, dispatch, row_parts, row, row_other, keys_rows, grad_rows)
 
 
-def own_parts(place, logit, dispatch, tokens, keys_rows, grad_rows, own_slots, tile=256):
+def own_parts(place, logit, dispatch, tokens, keys_rows, grad_rows, own_slots, chips, tile=256):
     count, features = tokens.shape
     width = keys_rows.shape[1]
-
-    def kernel(place_ref, logit_ref, dispatch_ref, tokens_ref, keys_rows_ref, grad_rows_ref, keys_ref, own_ref):
+    rows = features // (2 * chips)
+
+    def kernel(place_ref, logit_ref, dispatch_ref, tokens_ref, keys_rows_ref, grad_rows_ref, keep_ref, give_ref, own_ref, keys_ref):
         own = pl.ds(pl.multiple_of(place_ref[1] * own_slots, own_slots), own_slots)
         total = jnp.dot(logit_ref[own, :], tokens_ref[...], preferred_element_type=f32)
         keys_ref[...] = total.T.astype(bf16)
+        for chip in range(chips):
+            for core, out_ref in ((place_ref[0], keep_ref), (1 - place_ref[0], give_ref)):
+                first = pl.multiple_of(chip * 2 * rows + core * rows, 16)
+                out_ref[chip] = keys_ref[pl.ds(first, rows), :]
         for at in range(0, count, tile):
             cut = slice(at, at + tile)
             own_ref[:, cut] = columns_dot(
@@ -574,11 +565,13 @@
     return pl.pallas_call(
         kernel,
         in_specs=[in_smem()] + [whole_in_vmem()] * 5,
-        out_specs=[whole_in_vmem()] * 2,
-        out_shape=[
-            jax.ShapeDtypeStruct((features, own_slots), bf16),
+        out_specs=[whole_in_vmem()] * 3,
+        out_shape=[
+            jax.ShapeDtypeStruct((chips, rows, own_slots), bf16),
+            jax.ShapeDtypeStruct((chips, rows, own_slots), bf16),
             jax.ShapeDtypeStruct((width, count), f32),
         ],
+        scratch_shapes=[pltpu.VMEM((features, own_slots), bf16)],
         compiler_params=params(GRANT),
         cost_estimate=cost(2 * own_slots * features * count, 2 * features * count),
         name="own_parts",
@@ -589,7 +582,6 @@
     features = tokens.shape[1]
     own_slots = slot_keys.shape[1]
     slot_devices = lax.axis_size(SLOT)
-    seq_devices = lax.axis_size(SEQ)
     groups = lax.axis_size(CHIPS)
     everyone = lax.axis_size(GATHERED)
     width = features // slot_devices
@@ -641,11 +633,11 @@
         place, all_exp, terms, dispatch, row_parts, row, row_other, keys_rows, grad_rows
     )
     received = lax.ppermute(sent, "xa", swap)
-    keys_part, own_grads = own_parts(
-        place, logit, dispatch, tokens, keys_rows, grad_rows, own_slots
+    keep, give, own_grads = own_parts(
+        place, logit, dispatch, tokens, keys_rows, grad_rows, own_slots, groups
     )
     keys_parts = lax.all_to_all(
-        keys_part.reshape(seq_devices, features // seq_devices, own_slots), SEQ, 0, 0
+        pair_sum(keep, lax.ppermute(give, "c", swap)), CHIPS, 0, 0
     )
     grad_tokens = (own_grads + received.astype(f32)).astype(bf16).T
     grad_keys = jnp.sum(keys_parts.astype(f32), axis=0)

time: 142 us -> 140 us (0.986)
  blocking collectives: 44 us -> 41.2 us
  waiting for transfers between devices: 21.1 us -> 23.3 us
  Pallas kernels: 32.6 us -> 30.6 us
    all_to_all x1 -> x0, blocking collectives: 12 us -> none  [per_device(): lax.all_to_all(keys_part.reshape(seq_devices, features // seq_devices, ow...]
    all_to_all x1 -> x2, blocking collectives: 12.6 us -> 21.7 us  [per_device(): lax.all_to_all(pair_sum(keep, lax.ppermute(give, 'c', swap)), CHIPS, 0, 0)]
  transfers between devices with their start and end apart: 15 -> 16, of which waited for: 10 -> 11; matrix products, arithmetic and copies ran while one was open for 1% -> 1% of each run, Pallas kernels for 11% -> 12%
where the time goes in v7:
time: 140 us
  blocking collectives  41.2 us (29%)
  Pallas kernels  30.6 us (22%)
  starting transfers between devices  28.4 us (20%)
  waiting for transfers between devices  23.3 us (17%)
  local copies, waits for them, and re-layouts  13.6 us (10%)
  other arithmetic  1.7 us (1%)
    all_to_all x2, blocking collectives, per_device(): lax.all_to_all(pair_sum(keep, lax.ppermute(give, 'c', swap)), CHIPS, 0, 0)  21.7 us
    unnamed x40, local copies, waits for them, and re-layouts  12.7 us
    all_to_all x1, blocking collectives, per_device(): terms = lax.all_to_all(sent, CHIPS, 0, 0)  10.4 us
    all_to_all x1, blocking collectives, per_device(): mine = lax.all_to_all(sent, CHIPS, 0, 0)  9.05 us
    all_to_all x1, waiting for transfers between devices, per_device(): gathered = lax.all_to_all(sent, GATHERED, 0, 0)  8.47 us
    pallas_call x1, Pallas kernels, weight_grads(): pl.pallas_call(kernel, grid=(experts,), in_specs=[in_smem(), pl.BlockSpec...  6.3 us
    ppermute x3, starting transfers between devices, per_device(): lax.ppermute(own_half, KEYS, [(at, at ^ other) for at in range(blocks)])  5.81 us
    all_to_all x1, starting transfers between devices, per_device(): gathered = lax.all_to_all(sent, GATHERED, 0, 0)  5.53 us
  transfers between devices with their start and end apart: 16, of which 11 were waited for; matrix products, arithmetic and copies ran while one was open for 1% of the time, Pallas kernels for 12%

profile of v7, /device:TPU:1, one launch (start us, length us, event | category | flops | bytes accessed | tf_op | source)
XLA Modules:
  0.0 139.6 jit_solution(9266607835796002838)
XLA Ops:
  0.6 0.9 constant_dynamic-slice_fusion
  1.6 5.4 %collective-permute-start.2 = (bf16[640,128]{1,0:T(8,128)(2,1)S(1)}, bf16[640,128]{1,0:T(8,128)(2,1)S(1)}, u32[]{:S(2)}, u32[]{:S(2)}) collective-permute-start(bf16[640,128]{1,0:T(8,128)(2,1)S(1)} %constant_dynamic-slice_fusion), channel_id=1, source_target_pairs={{0,3},{1,2},{2,1},{3,0},{4,7},{5,6},{6,5},{7,4},{8,11},{9,10},{10,... | collective-permute-start | bytes 491528 | tf_op jit(solution)/shard_map/ppermute | solution.py:597
  7.0 0.3 collective-permute-start.1
  7.3 0.1 collective-permute-start
  7.4 3.5 %collective-permute-done.2.refs_2_ = bf16[640,128]{1,0:T(8,128)(2,1)S(1)} collective-permute-done((bf16[640,128]{1,0:T(8,128)(2,1)S(1)}, bf16[640,128]{1,0:T(8,128)(2,1)S(1)}, u32[]{:S(2)}, u32[]{:S(2)}) %collective-permute-start.2) | collective-permute-done | bytes 163872 | tf_op jit(solution)/shard_map/ppermute | solution.py:597
  10.9 2.1 %collective-permute-start.5 = (bf16[640,128]{1,0:T(8,128)(2,1)S(1)}, bf16[640,128]{1,0:T(8,128)(2,1)S(1)}, u32[]{:S(2)}, u32[]{:S(2)}) collective-permute-start(bf16[640,128]{1,0:T(8,128)(2,1)S(1)} %collective-permute-done.2.refs_2_), channel_id=1, source_target_pairs={{0,8},{8,0},{1,9},{9,1},{2,10},{10,2},{3,11},{11,3},{4,12},{12,4},... | collective-permute-start | bytes 491528 | tf_op jit(solution)/shard_map/ppermute | solution.py:600
  13.0 1.4 %collective-permute-done.1.refs_1_ = bf16[640,128]{1,0:T(8,128)(2,1)S(1)} collective-permute-done((bf16[640,128]{1,0:T(8,128)(2,1)S(1)}, bf16[640,128]{1,0:T(8,128)(2,1)S(1)}, u32[]{:S(2)}, u32[]{:S(2)}) %collective-permute-start.1) | collective-permute-done | bytes 163872 | tf_op jit(solution)/shard_map/ppermute | solution.py:597
  14.4 1.5 %collective-permute-start.4 = (bf16[640,128]{1,0:T(8,128)(2,1)S(1)}, bf16[640,128]{1,0:T(8,128)(2,1)S(1)}, u32[]{:S(2)}, u32[]{:S(2)}) collective-permute-start(bf16[640,128]{1,0:T(8,128)(2,1)S(1)} %collective-permute-done.1.refs_1_), channel_id=1, source_target_pairs={{0,8},{8,0},{1,9},{9,1},{2,10},{10,2},{3,11},{11,3},{4,12},{12,4},... | collective-permute-start | bytes 491528 | tf_op jit(solution)/shard_map/ppermute | solution.py:600
  16.0 0.0 collective-permute-start.3
  16.0 0.1 pad_add_fusion.place_ref
  16.0 0.0 collective-permute-done.5.refs_5_
  16.0 0.9 collective-permute-done.4.refs_4_
  17.0 0.4 collective-permute-done.3.refs_3_
  17.4 2.5 %copy-done = bf16[2048,1280]{1,0:T(8,128)(2,1)S(1)} copy-done((bf16[2048,1280]{1,0:T(8,128)(2,1)S(1)}, bf16[2048,1280]{1,0:T(8,128)(2,1)}, u32[]{:S(2)}) %copy-start) | copy-done | bytes 5242904
  19.9 1.0 copy-done.13
  20.8 4.1 %all_exps.1 = (bf16[512,2048]{1,0:T(8,128)(2,1)S(1)}, f32[128,2048]{1,0:T(8,128)S(1)}, f32[1,2048]{1,0:T(1,128)S(1)}, f32[128,128]{1,0:T(8,128)S(1)}, bf16[2,160,512]{2,1,0:T(8,128)(2,1)S(1)}) custom-call(s32[3]{0:T(128)S(1)} %pad_add_fusion.place_ref, bf16[1280,128]{1,0:T(8,128)(2,1)S(1)} %copy-done.13, bf16[640,128]{1,0:T(8,128)(2,1)S(1)} %collective-permute-done.refs_0_, ...), custom_call_target="tpu_custom_call" | custom-call | flops 2684354560 | bytes 5242880 | tf_op jit(solution)/shard_map/all_exps/pallas_call | solution.py:372
  24.9 0.0 copy-start.11
  24.9 0.7 copy-done.11
  25.6 0.2 collective-permute-start.7
  25.9 2.7 %collective-permute-start.6 = (f32[1,2048]{1,0:T(1,128)S(1)}, f32[1,2048]{1,0:T(1,128)S(1)}, u32[]{:S(2)}, u32[]{:S(2)}) collective-permute-start(f32[1,2048]{1,0:T(1,128)S(1)} %get-tuple-element.43.row_ref), channel_id=1, source_target_pairs={{0,4},{4,0},{1,5},{5,1},{2,6},{6,2},{3,7},{7,3},{8,12},{12,8},{9,1... | collective-permute-start | bytes 24584 | tf_op jit(solution)/shard_map/ppermute | solution.py:605
  28.6 0.9 dispatch_part.1.in_ref
  29.5 0.3 collective-permute-done.6.row_other_ref
  29.9 1.2 copy-done.2
  31.1 1.4 %combine_part.1 = (bf16[8,16,1408]{2,1,0:T(8,128)(2,1)S(1)}, bf16[8,16,1280]{2,1,0:T(8,128)(2,1)S(1)}, f32[1,2048]{1,0:T(1,128)S(1)}) custom-call(s32[3]{0:T(128)S(1)} %pad_add_fusion.place_ref, f32[128,2048]{1,0:T(8,128)S(1)} %get-tuple-element.42.exp_ref, f32[1,2048]{1,0:T(1,128)S(1)} %get-tuple-element.43.row_ref, ...), custom_call_target="tpu_custom_call" | custom-call | flops 671088640 | bytes 5242880 | tf_op jit(solution)/shard_map/combine_part/pallas_call | solution.py:135
  32.5 0.6 collective-permute-start.8
  33.2 1.3 collective-permute-done.8.received_ref
  34.4 0.1 pair_sum.3
  34.5 12.6 %all_to_all.25.parts_ref = bf16[8,16,1408]{2,1,0:T(8,128)(2,1)S(1)} all-to-all(bf16[8,16,1408]{2,1,0:T(8,128)(2,1)S(1)} %pair_sum.3), channel_id=1, replica_groups=mesh['zl'=2,'y'=4,'c'=2,'xa'=2,'xb'=2,'zh'=2] {'zl','y'}, dimensions={0} | all-to-all | bytes 720896 | tf_op jit(solution)/shard_map/all_to_all | solution.py:610
  47.1 0.2 sum_slots.1
  47.4 9.0 %all_to_all.26.mine_ref = bf16[8,16,1280]{2,1,0:T(8,128)(2,1)S(1)} all-to-all(bf16[8,16,1280]{2,1,0:T(8,128)(2,1)S(1)} %get-tuple-element.47), channel_id=1, replica_groups=mesh['zl'=2,'y'=4,'c'=2,'xa'=2,'xb'=2,'zh'=2] {'zl','y'}, dimensions={0} | all-to-all | bytes 655360 | tf_op jit(solution)/shard_map/all_to_all | solution.py:612
  56.4 2.4 %collective-permute-start.9 = (bf16[8,16,1280]{2,1,0:T(8,128)(2,1)S(1)}, bf16[8,16,1280]{2,1,0:T(8,128)(2,1)S(1)}, u32[]{:S(2)}, u32[]{:S(2)}) collective-permute-start(bf16[8,16,1280]{2,1,0:T(8,128)(2,1)S(1)} %all_to_all.26.mine_ref), channel_id=1, source_target_pairs={{0,8},{8,0},{1,9},{9,1},{2,10},{10,2},{3,11},{11,3},{4,12},{12,4},... | collective-permute-start | bytes 983048 | tf_op jit(solution)/shard_map/ppermute | solution.py:613
  58.8 1.3 collective-permute-done.9.other_ref
  60.0 4.8 %experts_part.1 = (bf16[8,16,1280]{2,1,0:T(8,128)(2,1)S(1)}, bf16[8,16,1280]{2,1,0:T(8,128)(2,1)S(1)}, bf16[8,16,192]{2,1,0:T(8,128)(2,1)S(1)}, bf16[8,16,192]{2,1,0:T(8,128)(2,1)S(1)}) custom-call(s32[3]{0:T(128)S(1)} %pad_add_fusion.place_ref, bf16[8,16,1280]{2,1,0:T(8,128)(2,1)S(1)} %all_to_all.26.mine_ref, ...), custom_call_target="tpu_custom_call" | custom-call | flops 251658240 | bytes 7864320 | tf_op jit(solution)/shard_map/experts_part/pallas_call | solution.py:246
  64.9 0.4 collective-permute-start.10
  65.3 1.3 collective-permute-done.10.received_ref
  66.6 0.1 pair_sum.4
  66.6 10.4 %all_to_all.27.terms_ref = bf16[8,16,1280]{2,1,0:T(8,128)(2,1)S(1)} all-to-all(bf16[8,16,1280]{2,1,0:T(8,128)(2,1)S(1)} %pair_sum.4), channel_id=1, replica_groups=mesh['zl'=2,'y'=4,'c'=2,'xa'=2,'xb'=2,'zh'=2] {'zl','y'}, dimensions={0} | all-to-all | bytes 655360 | tf_op jit(solution)/shard_map/all_to_all | solution.py:617
  77.0 0.1 sum_terms.1
  77.2 1.1 copy-done.4
  78.3 5.5 %all-to-all-start.3 = ((bf16[32,16,1408]{2,1,0:T(8,128)(2,1)}), bf16[32,16,1408]{2,1,0:T(8,128)(2,1)S(1)}, u32[]{:S(2)}, u32[]{:S(2)}) async-start(bf16[32,16,1408]{2,1,0:T(8,128)(2,1)} %copy-done.4), calls=%async_computation.3 | async-start | bytes 2883584 | tf_op jit(solution)/shard_map/all_to_all | solution.py:620
  83.9 0.0 copy-start.8
  83.9 1.0 copy-done.8
  84.8 1.0 copy-done.10
  85.8 0.8 copy-done.15
  86.7 0.8 copy-done.17
  87.5 6.3 %weight_grads.1 = (bf16[8,192,1280]{2,1,0:T(8,128)(2,1)}, bf16[8,192,1280]{2,1,0:T(8,128)(2,1)}) custom-call(s32[3]{0:T(128)S(1)} %pad_add_fusion.place_ref, bf16[8,16,1280]{2,1,0:T(8,128)(2,1)S(1)} %copy-done.8, bf16[8,16,1280]{2,1,0:T(8,128)(2,1)S(1)} %copy-done.10, bf16[8,16,192]{2,1,0:T(8,128)(2,1)S(1)} %copy-done.15, bf16[8,16,192]{2,1,0:T(8,128)(2,1)S(1)} %copy-done.17), custom_call_target="tpu_custom_call" | custom-call | flops 125829120 | bytes 7864320 | tf_op jit(solution)/shard_map/weight_grads/pallas_call | solution.py:280
  93.8 8.5 %all-to-all-done.3.mine_ref = bf16[32,16,1408]{2,1,0:T(8,128)(2,1)S(1)} async-done(((bf16[32,16,1408]{2,1,0:T(8,128)(2,1)}), bf16[32,16,1408]{2,1,0:T(8,128)(2,1)S(1)}, u32[]{:S(2)}, u32[]{:S(2)}) %all-to-all-start.3) | async-done | bytes 1441824 | tf_op jit(solution)/shard_map/all_to_all | solution.py:620
  102.3 3.2 %collective-permute-start.11 = (bf16[32,16,1408]{2,1,0:T(8,128)(2,1)S(1)}, bf16[32,16,1408]{2,1,0:T(8,128)(2,1)S(1)}, u32[]{:S(2)}, u32[]{:S(2)}) collective-permute-start(bf16[32,16,1408]{2,1,0:T(8,128)(2,1)S(1)} %all-to-all-done.3.mine_ref), channel_id=1, source_target_pairs={{0,8},{8,0},{1,9},{9,1},{2,10},{10,2},{3,11},{11,3},{4,12},{12,4},... | collective-permute-start | bytes 4325384 | tf_op jit(solution)/shard_map/ppermute | solution.py:623
  105.5 2.5 %copy-done.3 = bf16[2048,1280]{1,0:T(8,128)(2,1)S(1)} copy-done((bf16[2048,1280]{1,0:T(8,128)(2,1)S(1)}, bf16[2048,1280]{1,0:T(8,128)(2,1)}, u32[]{:S(2)}) %copy-start.3) | copy-done | bytes 5242904
  107.9 2.6 %near_dots.1 = (f32[512,2048]{1,0:T(8,128)S(1)}, bf16[2048,640]{1,0:T(8,128)(2,1)S(1)}) custom-call(s32[3]{0:T(128)S(1)} %pad_add_fusion.place_ref, bf16[2048,1280]{1,0:T(8,128)(2,1)S(1)} %copy-done.3, bf16[32,16,1408]{2,1,0:T(8,128)(2,1)S(1)} %all-to-all-done.3.mine_ref), custom_call_target="tpu_custom_call" | custom-call | flops 1342177280 | bytes 2621440 | tf_op jit(solution)/shard_map/near_dots/pallas_call | solution.py:416
  110.5 0.0 slice-start
  110.6 1.9 %comb_dots.1 = (f32[512,2048]{1,0:T(8,128)S(1)}, f32[1,2048]{1,0:T(1,128)S(1)}) custom-call(bf16[512,2048]{1,0:T(8,128)(2,1)S(1)} %get-tuple-element.41.exp_ref, f32[512,2048]{1,0:T(8,128)S(1)} %get-tuple-element.61.near_ref, bf16[2048,640]{1,0:T(8,128)(2,1)S(1)} %get-tuple-element.62.grad_ref, f32[1,2048]{1,0:T(1,128)S(1)} %get-tuple-element.63.row_ref, ...), custom_call_target="tpu_custom_call" | custom-call | flops 1342177280 | bytes 2621440 | tf_op jit(solution)/shard_map/comb_dots/pallas_call | solution.py:446
  112.4 2.5 %collective-permute-start.12 = (f32[1,2048]{1,0:T(1,128)S(1)}, f32[1,2048]{1,0:T(1,128)S(1)}, u32[]{:S(2)}, u32[]{:S(2)}) collective-permute-start(f32[1,2048]{1,0:T(1,128)S(1)} %get-tuple-element.68.sum_ref), channel_id=1, source_target_pairs={{0,4},{4,0},{1,5},{5,1},{2,6},{6,2},{3,7},{7,3},{8,12},{12,8},{9,1... | collective-permute-start | bytes 24584 | tf_op jit(solution)/shard_map/ppermute | solution.py:628
  115.0 4.4 %disp_dots.1 = (f32[512,2048]{1,0:T(8,128)S(1)}, bf16[512,2048]{1,0:T(8,128)(2,1)S(1)}, bf16[2,160,512]{2,1,0:T(8,128)(2,1)S(1)}) custom-call(s32[3]{0:T(128)S(1)} %pad_add_fusion.place_ref, bf16[512,2048]{1,0:T(8,128)(2,1)S(1)} %get-tuple-element.41.exp_ref, f32[512,2048]{1,0:T(8,128)S(1)} %get-tuple-element.65.dot_ref, bf16[2048,1280]{1,0:T(8,128)(2,1)S(1)} %bitcast.6, ...), custom_call_target="tpu_custom_call" | custom-call | flops 2684354560 | bytes 5242880 | tf_op jit(solution)/shard_map/disp_dots/pallas_call | solution.py:490
  119.4 0.0 collective-permute-done.12.other_ref
  119.4 1.7 %logit_grads.1 = (bf16[512,2048]{1,0:T(8,128)(2,1)S(1)}, bf16[160,2048]{1,0:T(8,128)(2,1)S(1)}) custom-call(s32[3]{0:T(128)S(1)} %pad_add_fusion.place_ref, bf16[512,2048]{1,0:T(8,128)(2,1)S(1)} %get-tuple-element.41.exp_ref, f32[512,2048]{1,0:T(8,128)S(1)} %get-tuple-element.66.terms_ref, bf16[512,2048]{1,0:T(8,128)(2,1)S(1)} %get-tuple-element.67.dispatch_ref, ...), custom_call_target="tpu_custom_call" | custom-call | flops 671088640 | bytes 4194304 | tf_op jit(solution)/shard_map/logit_grads/pallas_call | solution.py:532
  121.1 0.6 collective-permute-start.13
  121.7 2.1 %own_parts.1 = (bf16[8,80,128]{2,1,0:T(8,128)(2,1)S(1)}, bf16[8,80,128]{2,1,0:T(8,128)(2,1)S(1)}, f32[160,2048]{1,0:T(8,128)S(1)}) custom-call(s32[3]{0:T(128)S(1)} %pad_add_fusion.place_ref, bf16[512,2048]{1,0:T(8,128)(2,1)S(1)} %get-tuple-element.71.logit_ref, bf16[512,2048]{1,0:T(8,128)(2,1)S(1)} %get-tuple-element.67.dispatch_ref, ...), custom_call_target="tpu_custom_call" | custom-call | flops 671088640 | bytes 5242880 | tf_op jit(solution)/shard_map/own_parts/pallas_call | solution.py:565
  123.8 0.7 collective-permute-start.14
  124.5 1.0 collective-permute-done.14.received_ref
  125.6 9.1 %all_to_all.28 = bf16[8,80,128]{2,1,0:T(8,128)(2,1)S(1)} all-to-all(bf16[8,80,128]{2,1,0:T(8,128)(2,1)S(1)} %pair_sum.5), channel_id=1, replica_groups=mesh['zl'=2,'y'=4,'c'=2,'xa'=2,'xb'=2,'zh'=2] {'zl','y'}, dimensions={0} | all-to-all | bytes 327680 | tf_op jit(solution)/shard_map/all_to_all | solution.py:639
  134.6 0.6 convert_reduce_fusion
  135.3 3.4 %collective-permute-done.13 = bf16[160,2048]{1,0:T(8,128)(2,1)S(1)} collective-permute-done((bf16[160,2048]{1,0:T(8,128)(2,1)S(1)}, bf16[160,2048]{1,0:T(8,128)(2,1)S(1)}, u32[]{:S(2)}, u32[]{:S(2)}) %collective-permute-start.13) | collective-permute-done | bytes 655392 | tf_op jit(solution)/shard_map/ppermute | solution.py:635
  138.6 1.0 fusion
  (32 shorter events, 0.1 us)
Async XLA Ops:
  1.6 9.4 %collective-permute-start.2 = (bf16[640,128]{1,0:T(8,128)(2,1)S(1)}, bf16[640,128]{1,0:T(8,128)(2,1)S(1)}, u32[]{:S(2)}, u32[]{:S(2)}) collective-permute-start(bf16[640,128]{1,0:T(8,128)(2,1)S(1)} %constant_dynamic-slice_fusion), channel_id=1, source_target_pairs={{0,3},{1,2},{2,1},{3,0},{4,7},{5,6},{6,5},{7,4},{8,11},{9,10},{10,... | collective-permute-start | bytes 491528 | tf_op jit(solution)/shard_map/ppermute | solution.py:597
  7.0 7.4 %collective-permute-start.1 = (bf16[640,128]{1,0:T(8,128)(2,1)S(1)}, bf16[640,128]{1,0:T(8,128)(2,1)S(1)}, u32[]{:S(2)}, u32[]{:S(2)}) collective-permute-start(bf16[640,128]{1,0:T(8,128)(2,1)S(1)} %constant_dynamic-slice_fusion), channel_id=1, source_target_pairs={{0,2},{1,3},{2,0},{3,1},{4,6},{5,7},{6,4},{7,5},{8,10},{9,11},{10,... | collective-permute-start | bytes 491528 | tf_op jit(solution)/shard_map/ppermute | solution.py:597
  7.3 8.7 %collective-permute-start = (bf16[640,128]{1,0:T(8,128)(2,1)S(1)}, bf16[640,128]{1,0:T(8,128)(2,1)S(1)}, u32[]{:S(2)}, u32[]{:S(2)}) collective-permute-start(bf16[640,128]{1,0:T(8,128)(2,1)S(1)} %constant_dynamic-slice_fusion), channel_id=1, source_target_pairs={{0,1},{1,0},{2,3},{3,2},{4,5},{5,4},{6,7},{7,6},{8,9},{9,8},{10,11... | collective-permute-start | bytes 491528 | tf_op jit(solution)/shard_map/ppermute | solution.py:597
  10.9 5.1 %collective-permute-start.5 = (bf16[640,128]{1,0:T(8,128)(2,1)S(1)}, bf16[640,128]{1,0:T(8,128)(2,1)S(1)}, u32[]{:S(2)}, u32[]{:S(2)}) collective-permute-start(bf16[640,128]{1,0:T(8,128)(2,1)S(1)} %collective-permute-done.2.refs_2_), channel_id=1, source_target_pairs={{0,8},{8,0},{1,9},{9,1},{2,10},{10,2},{3,11},{11,3},{4,12},{12,4},... | collective-permute-start | bytes 491528 | tf_op jit(solution)/shard_map/ppermute | solution.py:600
  14.4 2.6 %collective-permute-start.4 = (bf16[640,128]{1,0:T(8,128)(2,1)S(1)}, bf16[640,128]{1,0:T(8,128)(2,1)S(1)}, u32[]{:S(2)}, u32[]{:S(2)}) collective-permute-start(bf16[640,128]{1,0:T(8,128)(2,1)S(1)} %collective-permute-done.1.refs_1_), channel_id=1, source_target_pairs={{0,8},{8,0},{1,9},{9,1},{2,10},{10,2},{3,11},{11,3},{4,12},{12,4},... | collective-permute-start | bytes 491528 | tf_op jit(solution)/shard_map/ppermute | solution.py:600
  16.0 1.4 collective-permute-start.3
  17.4 2.5 %copy-start = (bf16[2048,1280]{1,0:T(8,128)(2,1)S(1)}, bf16[2048,1280]{1,0:T(8,128)(2,1)}, u32[]{:S(2)}) copy-start(bf16[2048,1280]{1,0:T(8,128)(2,1)} %tokens_ref.5) | copy-start | bytes 15728644
  19.8 1.0 copy-start.13
  20.8 7.8 %copy-start.1 = (bf16[2048,1280]{1,0:T(8,128)(2,1)S(1)}, bf16[2048,1280]{1,0:T(8,128)(2,1)}, u32[]{:S(2)}) copy-start(bf16[2048,1280]{1,0:T(8,128)(2,1)} %tokens_ref.5) | copy-start | bytes 15728644
  24.9 0.7 copy-start.11
  25.6 3.0 %collective-permute-start.7 = (f32[128,128]{1,0:T(8,128)S(1)}, f32[128,128]{1,0:T(8,128)S(1)}, u32[]{:S(2)}, u32[]{:S(2)}) collective-permute-start(f32[128,128]{1,0:T(8,128)S(1)} %get-tuple-element.44.column_ref), channel_id=1, source_target_pairs={{0,8},{8,0},{1,9},{9,1},{2,10},{10,2},{3,11},{11,3},{4,12},{12,4},... | collective-permute-start | bytes 196616 | tf_op jit(solution)/shard_map/ppermute | solution.py:604
  25.9 4.0 %collective-permute-start.6 = (f32[1,2048]{1,0:T(1,128)S(1)}, f32[1,2048]{1,0:T(1,128)S(1)}, u32[]{:S(2)}, u32[]{:S(2)}) collective-permute-start(f32[1,2048]{1,0:T(1,128)S(1)} %get-tuple-element.43.row_ref), channel_id=1, source_target_pairs={{0,4},{4,0},{1,5},{5,1},{2,6},{6,2},{3,7},{7,3},{8,12},{12,8},{9,1... | collective-permute-start | bytes 24584 | tf_op jit(solution)/shard_map/ppermute | solution.py:605
  28.6 2.5 %copy-start.2 = (bf16[2048,1280]{1,0:T(8,128)(2,1)S(1)}, bf16[2048,1280]{1,0:T(8,128)(2,1)}, u32[]{:S(2)}) copy-start(bf16[2048,1280]{1,0:T(8,128)(2,1)} %grad_ref.3) | copy-start | bytes 15728644
  31.1 29.0 %copy-start.5 = (bf16[8,192,1280]{2,1,0:T(8,128)(2,1)S(1)}, bf16[8,192,1280]{2,1,0:T(8,128)(2,1)}, u32[]{:S(2)}) copy-start(bf16[8,192,1280]{2,1,0:T(8,128)(2,1)} %w_in_ref.1) | copy-start | bytes 11796484
  31.1 29.0 %copy-start.6 = (bf16[8,192,1280]{2,1,0:T(8,128)(2,1)S(1)}, bf16[8,192,1280]{2,1,0:T(8,128)(2,1)}, u32[]{:S(2)}) copy-start(bf16[8,192,1280]{2,1,0:T(8,128)(2,1)} %w_out_ref.1) | copy-start | bytes 11796484
  32.5 1.9 %collective-permute-start.8 = (bf16[8,16,1280]{2,1,0:T(8,128)(2,1)S(1)}, bf16[8,16,1280]{2,1,0:T(8,128)(2,1)S(1)}, u32[]{:S(2)}, u32[]{:S(2)}) collective-permute-start(bf16[8,16,1280]{2,1,0:T(8,128)(2,1)S(1)} %get-tuple-element.46), channel_id=1, source_target_pairs={{0,8},{8,0},{1,9},{9,1},{2,10},{10,2},{3,11},{11,3},{4,12},{12,4},... | collective-permute-start | bytes 983048 | tf_op jit(solution)/shard_map/ppermute | solution.py:610
  56.4 8.4 %copy-start.7 = (bf16[8,16,1280]{2,1,0:T(8,128)(2,1)}, bf16[8,16,1280]{2,1,0:T(8,128)(2,1)S(1)}, u32[]{:S(2)}) copy-start(bf16[8,16,1280]{2,1,0:T(8,128)(2,1)S(1)} %all_to_all.26.mine_ref) | copy-start | bytes 983044
  56.4 3.6 %collective-permute-start.9 = (bf16[8,16,1280]{2,1,0:T(8,128)(2,1)S(1)}, bf16[8,16,1280]{2,1,0:T(8,128)(2,1)S(1)}, u32[]{:S(2)}, u32[]{:S(2)}) collective-permute-start(bf16[8,16,1280]{2,1,0:T(8,128)(2,1)S(1)} %all_to_all.26.mine_ref), channel_id=1, source_target_pairs={{0,8},{8,0},{1,9},{9,1},{2,10},{10,2},{3,11},{11,3},{4,12},{12,4},... | collective-permute-start | bytes 983048 | tf_op jit(solution)/shard_map/ppermute | solution.py:613
  60.0 4.8 %copy-start.9 = (bf16[8,16,1280]{2,1,0:T(8,128)(2,1)}, bf16[8,16,1280]{2,1,0:T(8,128)(2,1)S(1)}, u32[]{:S(2)}) copy-start(bf16[8,16,1280]{2,1,0:T(8,128)(2,1)S(1)} %collective-permute-done.9.other_ref) | copy-start | bytes 983044
  64.8 12.2 %copy-start.14 = (bf16[8,16,192]{2,1,0:T(8,128)(2,1)}, bf16[8,16,192]{2,1,0:T(8,128)(2,1)S(1)}, u32[]{:S(2)}) copy-start(bf16[8,16,192]{2,1,0:T(8,128)(2,1)S(1)} %get-tuple-element.55.act_ref) | copy-start | bytes 147460
  64.8 12.2 %copy-start.16 = (bf16[8,16,192]{2,1,0:T(8,128)(2,1)}, bf16[8,16,192]{2,1,0:T(8,128)(2,1)S(1)}, u32[]{:S(2)}) copy-start(bf16[8,16,192]{2,1,0:T(8,128)(2,1)S(1)} %get-tuple-element.56.pre_ref) | copy-start | bytes 147460
  64.9 1.7 %collective-permute-start.10 = (bf16[8,16,1280]{2,1,0:T(8,128)(2,1)S(1)}, bf16[8,16,1280]{2,1,0:T(8,128)(2,1)S(1)}, u32[]{:S(2)}, u32[]{:S(2)}) collective-permute-start(bf16[8,16,1280]{2,1,0:T(8,128)(2,1)S(1)} %get-tuple-element.49), channel_id=1, source_target_pairs={{0,8},{8,0},{1,9},{9,1},{2,10},{10,2},{3,11},{11,3},{4,12},{12,4},... | collective-permute-start | bytes 983048 | tf_op jit(solution)/shard_map/ppermute | solution.py:616
  77.2 1.2 copy-start.4
  78.3 23.9 %all-to-all-start.3 = ((bf16[32,16,1408]{2,1,0:T(8,128)(2,1)}), bf16[32,16,1408]{2,1,0:T(8,128)(2,1)S(1)}, u32[]{:S(2)}, u32[]{:S(2)}) async-start(bf16[32,16,1408]{2,1,0:T(8,128)(2,1)} %copy-done.4), calls=%async_computation.3 | async-start | bytes 2883584 | tf_op jit(solution)/shard_map/all_to_all | solution.py:620
  83.9 1.0 copy-start.8
  84.8 1.0 copy-start.10
  85.8 0.8 copy-start.15
  86.7 0.8 copy-start.17
  102.3 8.3 %collective-permute-start.11 = (bf16[32,16,1408]{2,1,0:T(8,128)(2,1)S(1)}, bf16[32,16,1408]{2,1,0:T(8,128)(2,1)S(1)}, u32[]{:S(2)}, u32[]{:S(2)}) collective-permute-start(bf16[32,16,1408]{2,1,0:T(8,128)(2,1)S(1)} %all-to-all-done.3.mine_ref), channel_id=1, source_target_pairs={{0,8},{8,0},{1,9},{9,1},{2,10},{10,2},{3,11},{11,3},{4,12},{12,4},... | collective-permute-start | bytes 4325384 | tf_op jit(solution)/shard_map/ppermute | solution.py:623
  105.5 2.5 %copy-start.3 = (bf16[2048,1280]{1,0:T(8,128)(2,1)S(1)}, bf16[2048,1280]{1,0:T(8,128)(2,1)}, u32[]{:S(2)}) copy-start(bf16[2048,1280]{1,0:T(8,128)(2,1)} %grad_ref.3) | copy-start | bytes 15728644
  110.5 4.5 %slice-start = ((s8[5242880]{0:T(1024)(128)(4,1)}), s8[4194304]{0:T(1024)(128)(4,1)S(1)}, s32[]{:S(2)}) async-start(s8[5242880]{0:T(1024)(128)(4,1)} %bitcast.5), calls=%async_computation.5 | async-start | bytes 8388608
  110.5 4.5 %slice-start.1 = ((s8[5242880]{0:T(1024)(128)(4,1)}), s8[1048576]{0:T(1024)(128)(4,1)S(1)}, s32[]{:S(2)}) async-start(s8[5242880]{0:T(1024)(128)(4,1)} %bitcast.5), calls=%async_computation.6 | async-start | bytes 2097152
  112.4 6.9 %collective-permute-start.12 = (f32[1,2048]{1,0:T(1,128)S(1)}, f32[1,2048]{1,0:T(1,128)S(1)}, u32[]{:S(2)}, u32[]{:S(2)}) collective-permute-start(f32[1,2048]{1,0:T(1,128)S(1)} %get-tuple-element.68.sum_ref), channel_id=1, source_target_pairs={{0,4},{4,0},{1,5},{5,1},{2,6},{6,2},{3,7},{7,3},{8,12},{12,8},{9,1... | collective-permute-start | bytes 24584 | tf_op jit(solution)/shard_map/ppermute | solution.py:628
  115.0 4.4 %copy-start.12 = (bf16[2,160,512]{2,1,0:T(8,128)(2,1)S(1)}, bf16[2,160,512]{2,1,0:T(8,128)(2,1)}, u32[]{:S(2)}) copy-start(bf16[2,160,512]{2,1,0:T(8,128)(2,1)} %copy-done.11) | copy-start | bytes 983044
  121.1 17.5 %collective-permute-start.13 = (bf16[160,2048]{1,0:T(8,128)(2,1)S(1)}, bf16[160,2048]{1,0:T(8,128)(2,1)S(1)}, u32[]{:S(2)}, u32[]{:S(2)}) collective-permute-start(bf16[160,2048]{1,0:T(8,128)(2,1)S(1)} %get-tuple-element.73), channel_id=1, source_target_pairs={{0,4},{4,0},{1,5},{5,1},{2,6},{6,2},{3,7},{7,3},{8,12},{12,8},{9,1... | collective-permute-start | bytes 1966088 | tf_op jit(solution)/shard_map/ppermute | solution.py:635
  123.8 1.7 %collective-permute-start.14 = (bf16[8,80,128]{2,1,0:T(8,128)(2,1)S(1)}, bf16[8,80,128]{2,1,0:T(8,128)(2,1)S(1)}, u32[]{:S(2)}, u32[]{:S(2)}) collective-permute-start(bf16[8,80,128]{2,1,0:T(8,128)(2,1)S(1)} %get-tuple-element.75), channel_id=1, source_target_pairs={{0,8},{8,0},{1,9},{9,1},{2,10},{10,2},{3,11},{11,3},{4,12},{12,4},... | collective-permute-start | bytes 491528 | tf_op jit(solution)/shard_map/ppermute | solution.py:640

commit v8 on v7

--- a/solution.py
+++ b/solution.py
@@ -11,10 +11,10 @@
 cols_contract = (((1,), (1,)), ((), ()))
 
 SEQ = ("zl", "y", "c")
-SLOT = ("xa", "xb", "zh")
+SLOT = ("xb", "xa", "zh")
 KEYS = ("xb", "zh")
 CHIPS = ("zl", "y")
-GATHERED = ("xb", "zh", "zl", "y")
+GATHERED = ("xb", "xa", "zh", "zl", "y")
 f32 = jnp.float32
 bf16 = jnp.bfloat16
 LANES = 128
@@ -341,17 +341,21 @@
             return pl.ds(pl.multiple_of(at * block, block), block)
 
         own = spot(at_own)
-        rows = pl.ds(pl.multiple_of(at_own * width, 16), width)
+        near_here = core == place_ref[2]
+        firsts = [pl.multiple_of(place_ref[3 + whose] * width, 16) for whose in range(2)]
         turned_ref[own, :] = keys_ref[...].T
-        for side in range(2):
-            first = pl.multiple_of(at_own * width + side * half, 16)
-            rows_ref[side, :, own] = keys_ref[pl.ds(first, width), :]
+        for whose, first in enumerate(firsts):
+            first = pl.multiple_of(place_ref[2] * half + first, 16)
+            rows_ref[whose, :, own] = keys_ref[pl.ds(first, width), :]
         for at in range(others):
             place_at = spot(at_own ^ (at + 1))
             turned_ref[place_at, here] = near_refs[at][...].T
             turned_ref[place_at, there] = far_refs[at][...].T
-            rows_ref[core, :, place_at] = near_refs[at][rows, :]
-            rows_ref[1 - core, :, place_at] = far_refs[at][rows, :]
+            for whose, first in enumerate(firsts):
+                rows = pl.ds(first, width)
+                rows_ref[whose, :, place_at] = jnp.where(
+                    near_here, near_refs[at][rows, :], far_refs[at][rows, :]
+                )
         by_lane = jnp.zeros((block, LANES), f32)
         for at in range(0, count, tile):
             cut = slice(at, at + tile)
@@ -472,10 +476,12 @@
         power_ref[...] = jnp.broadcast_to(lanes[:, 2:3], (slots, tile))
         inverse_ref[...] = jnp.broadcast_to(lanes[:, 0:1] + lanes[:, 1:2], (slots, tile))
         total_ref[...] = jnp.broadcast_to(inner, (slots, tile))
-        rows = pl.ds(pl.multiple_of(place_ref[1] * width, 16), width)
-        for at, ref in enumerate((mine_ref, other_ref)):
-            turned_ref[...] = ref[:, :, half:features].reshape(slots, half).T
-            rows_ref[at] = turned_ref[rows, :]
+        turned_ref[...] = jnp.where(
+            place_ref[0] == place_ref[2], mine_ref[:, :, half:features], other_ref[:, :, half:features]
+        ).reshape(slots, half).T
+        for whose in range(2):
+            first = pl.multiple_of(place_ref[3 + whose] * width, 16)
+            rows_ref[whose] = turned_ref[pl.ds(first, width), :]
         for at in range(0, count, tile):
             cut = slice(at, at + tile)
             power, inverse = guarded(row_ref[:, cut])
@@ -503,12 +509,10 @@
     )(place, exps, dots, tokens, row_parts, mine, other)
 
 
-def columns_dot(place_ref, keys_rows_ref, grad_rows_ref, logit, dispatch, own):
-    core, half_at = place_ref[0], place_ref[2]
-    near = jnp.where(core == half_at, 0, 1)
-    at_keys, at_grad = (half_at, near) if own else (1 - half_at, 1 - near)
-    total = jnp.dot(keys_rows_ref[at_keys], logit, preferred_element_type=f32)
-    return total + jnp.dot(grad_rows_ref[at_grad], dispatch, preferred_element_type=f32)
+def columns_dot(keys_rows_ref, grad_rows_ref, logit, dispatch, own):
+    whose = 0 if own else 1
+    total = jnp.dot(keys_rows_ref[whose], logit, preferred_element_type=f32)
+    return total + jnp.dot(grad_rows_ref[whose], dispatch, preferred_element_type=f32)
 
 
 def logit_grads(place, exps, terms, dispatch, row_parts, row, row_other, keys_rows, grad_rows, tile=256):
@@ -526,7 +530,7 @@
             exps_here = exp_ref[:, cut].astype(f32)
             logit_ref[:, cut] = (terms_ref[:, cut] - (exps_here * power) * weight).astype(bf16)
             sent_ref[:, cut] = columns_dot(
-                place_ref, keys_rows_ref, grad_rows_ref, logit_ref[:, cut], dispatch_ref[:, cut], False
+                keys_rows_ref, grad_rows_ref, logit_ref[:, cut], dispatch_ref[:, cut], False
             ).astype(bf16)
 
     return pl.pallas_call(
@@ -559,7 +563,7 @@
         for at in range(0, count, tile):
             cut = slice(at, at + tile)
             own_ref[:, cut] = columns_dot(
-                place_ref, keys_rows_ref, grad_rows_ref, logit_ref[:, cut], dispatch_ref[:, cut], True
+                keys_rows_ref, grad_rows_ref, logit_ref[:, cut], dispatch_ref[:, cut], True
             )
 
     return pl.pallas_call(
@@ -583,19 +587,31 @@
     own_slots = slot_keys.shape[1]
     slot_devices = lax.axis_size(SLOT)
     groups = lax.axis_size(CHIPS)
-    everyone = lax.axis_size(GATHERED)
+    everyone = lax.axis_size(GATHERED) // 2
+    quarter = everyone // 2
+    across = [
+        [*range(first, first + quarter), *range(4 * quarter - first - quarter, 4 * quarter - first)]
+        for first in (0, quarter)
+    ]
     width = features // slot_devices
     swap = [(0, 1), (1, 0)]
+    pair_at, depth_at = lax.axis_index("xa"), lax.axis_index("zh")
     place = jnp.stack(
-        [lax.axis_index("c"), lax.axis_index(KEYS), lax.axis_index("xa")]
+        [
+            lax.axis_index("c"),
+            lax.axis_index(KEYS),
+            lax.axis_index("xb"),
+            2 * pair_at + depth_at,
+            2 * (1 - pair_at) + depth_at,
+        ]
     ).astype(jnp.int32)
 
     half = features // 2
     own_half = lax.dynamic_slice_in_dim(slot_keys, lax.axis_index("c") * half, half, 0)
     blocks = lax.axis_size(KEYS)
     near_keys = [
-        lax.ppermute(own_half, KEYS, [(at, at ^ other) for at in range(blocks)])
-        for other in range(1, blocks)
+        lax.ppermute(own_half, SLOT, [(at, at ^ other) for at in range(slot_devices)])
+        for other in (1, 6, 7)
     ]
     far_keys = [lax.ppermute(keys, "c", swap) for keys in near_keys]
     all_exp, exps, row_sum, column, keys_rows = all_exps(
@@ -617,7 +633,7 @@
     terms = lax.all_to_all(sent, CHIPS, 0, 0)
     terms, act, pre = lax.optimization_barrier((terms, act, pre))
     sent = sum_terms(terms, slot_in, column_total, everyone)
-    gathered = lax.all_to_all(sent, GATHERED, 0, 0)
+    gathered = lax.all_to_all(sent, GATHERED, 0, 0, axis_index_groups=across)
     grad_w_in, grad_w_out = weight_grads(place, mine, other, act, pre)
     gathered, grad_w_in, grad_w_out = lax.optimization_barrier((gathered, grad_w_in, grad_w_out))
     gathered_other = lax.ppermute(gathered, "c", swap)
@@ -645,7 +661,7 @@
 
 
 def solution(mesh):
-    fine = Mesh(mesh.devices.reshape(2, 4, 2, 2, 2, 2), ("zl", "y", "c", "xa", "xb", "zh"))
+    fine = Mesh(mesh.devices.reshape(2, 4, 2, 2, 2, 2), ("zl", "y", "c", "xb", "xa", "zh"))
     placed = (
         P(SEQ, None),
         P(None, SLOT),

time: 140 us -> 139 us (level)
  starting transfers between devices: 28.4 us -> 25.8 us
    ppermute x1, starting transfers between devices: 2.73 us -> 0.02 us  [per_device(): row_sum_other = lax.ppermute(row_sum, 'xa', swap)]
    ppermute x1, starting transfers between devices: 2.54 us -> 0.09 us  [per_device(): row_other = lax.ppermute(row, 'xa', swap)]
    all_to_all x1, starting transfers between devices: 5.53 us -> 7.21 us  [per_device(): gathered = lax.all_to_all(sent, GATHERED, 0, 0, axis_index_groups=across)]
    all_to_all x1, waiting for transfers between devices: 8.47 us -> 10.1 us  [per_device(): gathered = lax.all_to_all(sent, GATHERED, 0, 0, axis_index_groups=across)]
    ppermute x1, waiting for transfers between devices: 3.36 us -> 1.96 us  [per_device(): received = lax.ppermute(sent, 'xa', swap)]
  transfers between devices with their start and end apart: 16 -> 16, of which waited for: 11 -> 12; matrix products, arithmetic and copies ran while one was open for 1% -> 1% of each run, Pallas kernels for 12% -> 12%
where the time goes in v8:
time: 139 us
  blocking collectives  40.9 us (29%)
  Pallas kernels  30.6 us (22%)
  starting transfers between devices  25.8 us (19%)
  waiting for transfers between devices  24.7 us (18%)
  local copies, waits for them, and re-layouts  14 us (10%)
  other arithmetic  1.63 us (1%)
    all_to_all x2, blocking collectives, per_device(): lax.all_to_all(pair_sum(keep, lax.ppermute(give, 'c', swap)), CHIPS, 0, 0)  21.5 us
    unnamed x40, local copies, waits for them, and re-layouts  12.9 us
    all_to_all x1, blocking collectives, per_device(): terms = lax.all_to_all(sent, CHIPS, 0, 0)  10.4 us
    all_to_all x1, waiting for transfers between devices, per_device(): gathered = lax.all_to_all(sent, GATHERED, 0, 0, axis_index_groups=across)  10.1 us
    all_to_all x1, blocking collectives, per_device(): mine = lax.all_to_all(sent, CHIPS, 0, 0)  9.05 us
    all_to_all x1, starting transfers between devices, per_device(): gathered = lax.all_to_all(sent, GATHERED, 0, 0, axis_index_groups=across)  7.21 us
    ppermute x3, starting transfers between devices, per_device(): lax.ppermute(own_half, SLOT, [(at, at ^ other) for at in range(slot_devic...  7.08 us
    pallas_call x1, Pallas kernels, weight_grads(): pl.pallas_call(kernel, grid=(experts,), in_specs=[in_smem(), pl.BlockSpec...  6.3 us
  transfers between devices with their start and end apart: 16, of which 12 were waited for; matrix products, arithmetic and copies ran while one was open for 1% of the time, Pallas kernels for 12%

profile of v8, /device:TPU:1, one launch (start us, length us, event | category | flops | bytes accessed | tf_op | source)
XLA Modules:
  0.0 138.5 jit_solution(5978556129889283075)
XLA Ops:
  0.6 0.9 constant_dynamic-slice_fusion
  1.6 6.7 %collective-permute-start.2 = (bf16[640,128]{1,0:T(8,128)(2,1)S(1)}, bf16[640,128]{1,0:T(8,128)(2,1)S(1)}, u32[]{:S(2)}, u32[]{:S(2)}) collective-permute-start(bf16[640,128]{1,0:T(8,128)(2,1)S(1)} %constant_dynamic-slice_fusion), channel_id=1, source_target_pairs={{0,7},{1,6},{2,5},{3,4},{4,3},{5,2},{6,1},{7,0},{8,15},{9,14},{10,... | collective-permute-start | bytes 491528 | tf_op jit(solution)/shard_map/ppermute | solution.py:613
  8.3 0.2 collective-permute-start.1
  8.5 0.2 collective-permute-start
  8.6 3.5 %collective-permute-done.2.refs_2_ = bf16[640,128]{1,0:T(8,128)(2,1)S(1)} collective-permute-done((bf16[640,128]{1,0:T(8,128)(2,1)S(1)}, bf16[640,128]{1,0:T(8,128)(2,1)S(1)}, u32[]{:S(2)}, u32[]{:S(2)}) %collective-permute-start.2) | collective-permute-done | bytes 163872 | tf_op jit(solution)/shard_map/ppermute | solution.py:613
  12.2 2.1 %collective-permute-start.5 = (bf16[640,128]{1,0:T(8,128)(2,1)S(1)}, bf16[640,128]{1,0:T(8,128)(2,1)S(1)}, u32[]{:S(2)}, u32[]{:S(2)}) collective-permute-start(bf16[640,128]{1,0:T(8,128)(2,1)S(1)} %collective-permute-done.2.refs_2_), channel_id=1, source_target_pairs={{0,8},{8,0},{1,9},{9,1},{2,10},{10,2},{3,11},{11,3},{4,12},{12,4},... | collective-permute-start | bytes 491528 | tf_op jit(solution)/shard_map/ppermute | solution.py:616
  14.3 1.5 %collective-permute-done.1.refs_1_ = bf16[640,128]{1,0:T(8,128)(2,1)S(1)} collective-permute-done((bf16[640,128]{1,0:T(8,128)(2,1)S(1)}, bf16[640,128]{1,0:T(8,128)(2,1)S(1)}, u32[]{:S(2)}, u32[]{:S(2)}) %collective-permute-start.1) | collective-permute-done | bytes 163872 | tf_op jit(solution)/shard_map/ppermute | solution.py:613
  15.7 1.4 %collective-permute-start.4 = (bf16[640,128]{1,0:T(8,128)(2,1)S(1)}, bf16[640,128]{1,0:T(8,128)(2,1)S(1)}, u32[]{:S(2)}, u32[]{:S(2)}) collective-permute-start(bf16[640,128]{1,0:T(8,128)(2,1)S(1)} %collective-permute-done.1.refs_1_), channel_id=1, source_target_pairs={{0,8},{8,0},{1,9},{9,1},{2,10},{10,2},{3,11},{11,3},{4,12},{12,4},... | collective-permute-start | bytes 491528 | tf_op jit(solution)/shard_map/ppermute | solution.py:616
  17.1 0.0 collective-permute-start.3
  17.2 0.1 stack.23.place_ref
  17.3 0.9 collective-permute-done.4.refs_4_
  18.2 0.4 collective-permute-done.3.refs_3_
  18.5 2.5 %copy-done = bf16[2048,1280]{1,0:T(8,128)(2,1)S(1)} copy-done((bf16[2048,1280]{1,0:T(8,128)(2,1)S(1)}, bf16[2048,1280]{1,0:T(8,128)(2,1)}, u32[]{:S(2)}) %copy-start) | copy-done | bytes 5242904
  21.0 1.0 copy-done.13
  22.0 4.1 %all_exps.1 = (bf16[512,2048]{1,0:T(8,128)(2,1)S(1)}, f32[128,2048]{1,0:T(8,128)S(1)}, f32[1,2048]{1,0:T(1,128)S(1)}, f32[128,128]{1,0:T(8,128)S(1)}, bf16[2,160,512]{2,1,0:T(8,128)(2,1)S(1)}) custom-call(s32[5]{0:T(128)S(1)} %stack.23.place_ref, bf16[1280,128]{1,0:T(8,128)(2,1)S(1)} %copy-done.13, bf16[640,128]{1,0:T(8,128)(2,1)S(1)} %collective-permute-done.refs_0_, ...), custom_call_target="tpu_custom_call" | custom-call | flops 2684354560 | bytes 5242880 | tf_op jit(solution)/shard_map/all_exps/pallas_call | solution.py:376
  26.1 0.0 copy-start.11
  26.1 0.7 copy-done.11
  26.8 0.2 collective-permute-start.7
  27.0 0.0 collective-permute-start.6
  27.1 1.0 collective-permute-done.7.other_ref
  28.1 0.9 dispatch_part.1.in_ref
  29.0 0.6 collective-permute-done.6.row_other_ref
  29.6 1.0 copy-done.2
  30.6 1.4 %combine_part.1 = (bf16[8,16,1408]{2,1,0:T(8,128)(2,1)S(1)}, bf16[8,16,1280]{2,1,0:T(8,128)(2,1)S(1)}, f32[1,2048]{1,0:T(1,128)S(1)}) custom-call(s32[5]{0:T(128)S(1)} %stack.23.place_ref, f32[128,2048]{1,0:T(8,128)S(1)} %get-tuple-element.42.exp_ref, f32[1,2048]{1,0:T(1,128)S(1)} %get-tuple-element.43.row_ref, ...), custom_call_target="tpu_custom_call" | custom-call | flops 671088640 | bytes 5242880 | tf_op jit(solution)/shard_map/combine_part/pallas_call | solution.py:135
  32.0 0.5 collective-permute-start.8
  32.5 1.3 collective-permute-done.8.received_ref
  33.7 0.1 pair_sum.3
  33.8 12.6 %all_to_all.25.parts_ref = bf16[8,16,1408]{2,1,0:T(8,128)(2,1)S(1)} all-to-all(bf16[8,16,1408]{2,1,0:T(8,128)(2,1)S(1)} %pair_sum.3), channel_id=1, replica_groups=mesh['zl'=2,'y'=4,'c'=2,'xb'=2,'xa'=2,'zh'=2] {'zl','y'}, dimensions={0} | all-to-all | bytes 720896 | tf_op jit(solution)/shard_map/all_to_all | solution.py:626
  46.5 0.2 sum_slots.1
  46.7 9.0 %all_to_all.26.mine_ref = bf16[8,16,1280]{2,1,0:T(8,128)(2,1)S(1)} all-to-all(bf16[8,16,1280]{2,1,0:T(8,128)(2,1)S(1)} %get-tuple-element.47), channel_id=1, replica_groups=mesh['zl'=2,'y'=4,'c'=2,'xb'=2,'xa'=2,'zh'=2] {'zl','y'}, dimensions={0} | all-to-all | bytes 655360 | tf_op jit(solution)/shard_map/all_to_all | solution.py:628
  55.7 2.4 %collective-permute-start.9 = (bf16[8,16,1280]{2,1,0:T(8,128)(2,1)S(1)}, bf16[8,16,1280]{2,1,0:T(8,128)(2,1)S(1)}, u32[]{:S(2)}, u32[]{:S(2)}) collective-permute-start(bf16[8,16,1280]{2,1,0:T(8,128)(2,1)S(1)} %all_to_all.26.mine_ref), channel_id=1, source_target_pairs={{0,8},{8,0},{1,9},{9,1},{2,10},{10,2},{3,11},{11,3},{4,12},{12,4},... | collective-permute-start | bytes 983048 | tf_op jit(solution)/shard_map/ppermute | solution.py:629
  58.1 1.3 collective-permute-done.9.other_ref
  59.4 4.8 %experts_part.1 = (bf16[8,16,1280]{2,1,0:T(8,128)(2,1)S(1)}, bf16[8,16,1280]{2,1,0:T(8,128)(2,1)S(1)}, bf16[8,16,192]{2,1,0:T(8,128)(2,1)S(1)}, bf16[8,16,192]{2,1,0:T(8,128)(2,1)S(1)}) custom-call(s32[5]{0:T(128)S(1)} %stack.23.place_ref, bf16[8,16,1280]{2,1,0:T(8,128)(2,1)S(1)} %all_to_all.26.mine_ref, ...), custom_call_target="tpu_custom_call" | custom-call | flops 251658240 | bytes 7864320 | tf_op jit(solution)/shard_map/experts_part/pallas_call | solution.py:246
  64.2 0.4 collective-permute-start.10
  64.6 1.3 collective-permute-done.10.received_ref
  65.9 0.1 pair_sum.4
  66.0 10.4 %all_to_all.27.terms_ref = bf16[8,16,1280]{2,1,0:T(8,128)(2,1)S(1)} all-to-all(bf16[8,16,1280]{2,1,0:T(8,128)(2,1)S(1)} %pair_sum.4), channel_id=1, replica_groups=mesh['zl'=2,'y'=4,'c'=2,'xb'=2,'xa'=2,'zh'=2] {'zl','y'}, dimensions={0} | all-to-all | bytes 655360 | tf_op jit(solution)/shard_map/all_to_all | solution.py:633
  76.3 0.1 sum_terms.1
  76.5 1.1 copy-done.4
  77.6 7.2 %all-to-all-start.3 = ((bf16[32,16,1408]{2,1,0:T(8,128)(2,1)}), bf16[32,16,1408]{2,1,0:T(8,128)(2,1)S(1)}, u32[]{:S(2)}, u32[]{:S(2)}) async-start(bf16[32,16,1408]{2,1,0:T(8,128)(2,1)} %copy-done.4), calls=%async_computation.3 | async-start | bytes 2883584 | tf_op jit(solution)/shard_map/all_to_all | solution.py:636
  84.9 1.0 copy-done.8
  85.8 1.0 copy-done.10
  86.8 0.8 copy-done.15
  87.7 0.8 copy-done.17
  88.5 6.3 %weight_grads.1 = (bf16[8,192,1280]{2,1,0:T(8,128)(2,1)}, bf16[8,192,1280]{2,1,0:T(8,128)(2,1)}) custom-call(s32[5]{0:T(128)S(1)} %stack.23.place_ref, bf16[8,16,1280]{2,1,0:T(8,128)(2,1)S(1)} %copy-done.8, bf16[8,16,1280]{2,1,0:T(8,128)(2,1)S(1)} %copy-done.10, bf16[8,16,192]{2,1,0:T(8,128)(2,1)S(1)} %copy-done.15, bf16[8,16,192]{2,1,0:T(8,128)(2,1)S(1)} %copy-done.17), custom_call_target="tpu_custom_call" | custom-call | flops 125829120 | bytes 7864320 | tf_op jit(solution)/shard_map/weight_grads/pallas_call | solution.py:280
  94.8 10.1 %all-to-all-done.3.mine_ref = bf16[32,16,1408]{2,1,0:T(8,128)(2,1)S(1)} async-done(((bf16[32,16,1408]{2,1,0:T(8,128)(2,1)}), bf16[32,16,1408]{2,1,0:T(8,128)(2,1)S(1)}, u32[]{:S(2)}, u32[]{:S(2)}) %all-to-all-start.3) | async-done | bytes 1441824 | tf_op jit(solution)/shard_map/all_to_all | solution.py:636
  104.9 2.6 %collective-permute-start.11 = (bf16[32,16,1408]{2,1,0:T(8,128)(2,1)S(1)}, bf16[32,16,1408]{2,1,0:T(8,128)(2,1)S(1)}, u32[]{:S(2)}, u32[]{:S(2)}) collective-permute-start(bf16[32,16,1408]{2,1,0:T(8,128)(2,1)S(1)} %all-to-all-done.3.mine_ref), channel_id=1, source_target_pairs={{0,8},{8,0},{1,9},{9,1},{2,10},{10,2},{3,11},{11,3},{4,12},{12,4},... | collective-permute-start | bytes 4325384 | tf_op jit(solution)/shard_map/ppermute | solution.py:639
  107.5 2.5 %copy-done.3 = bf16[2048,1280]{1,0:T(8,128)(2,1)S(1)} copy-done((bf16[2048,1280]{1,0:T(8,128)(2,1)S(1)}, bf16[2048,1280]{1,0:T(8,128)(2,1)}, u32[]{:S(2)}) %copy-start.3) | copy-done | bytes 5242904
  109.9 2.6 %near_dots.1 = (f32[512,2048]{1,0:T(8,128)S(1)}, bf16[2048,640]{1,0:T(8,128)(2,1)S(1)}) custom-call(s32[5]{0:T(128)S(1)} %stack.23.place_ref, bf16[2048,1280]{1,0:T(8,128)(2,1)S(1)} %copy-done.3, bf16[32,16,1408]{2,1,0:T(8,128)(2,1)S(1)} %all-to-all-done.3.mine_ref), custom_call_target="tpu_custom_call" | custom-call | flops 1342177280 | bytes 2621440 | tf_op jit(solution)/shard_map/near_dots/pallas_call | solution.py:420
  112.5 0.0 slice-start
  112.6 1.9 %comb_dots.1 = (f32[512,2048]{1,0:T(8,128)S(1)}, f32[1,2048]{1,0:T(1,128)S(1)}) custom-call(bf16[512,2048]{1,0:T(8,128)(2,1)S(1)} %get-tuple-element.41.exp_ref, f32[512,2048]{1,0:T(8,128)S(1)} %get-tuple-element.61.near_ref, bf16[2048,640]{1,0:T(8,128)(2,1)S(1)} %get-tuple-element.62.grad_ref, f32[1,2048]{1,0:T(1,128)S(1)} %get-tuple-element.63.row_ref, ...), custom_call_target="tpu_custom_call" | custom-call | flops 1342177280 | bytes 2621440 | tf_op jit(solution)/shard_map/comb_dots/pallas_call | solution.py:450
  114.5 0.1 collective-permute-start.12
  114.5 0.2 slice-done
  114.7 0.3 slice-done.1
  115.0 4.4 %disp_dots.1 = (f32[512,2048]{1,0:T(8,128)S(1)}, bf16[512,2048]{1,0:T(8,128)(2,1)S(1)}, bf16[2,160,512]{2,1,0:T(8,128)(2,1)S(1)}) custom-call(s32[5]{0:T(128)S(1)} %stack.23.place_ref, bf16[512,2048]{1,0:T(8,128)(2,1)S(1)} %get-tuple-element.41.exp_ref, f32[512,2048]{1,0:T(8,128)S(1)} %get-tuple-element.65.dot_ref, bf16[2048,1280]{1,0:T(8,128)(2,1)S(1)} %bitcast.8, ...), custom_call_target="tpu_custom_call" | custom-call | flops 2684354560 | bytes 5242880 | tf_op jit(solution)/shard_map/disp_dots/pallas_call | solution.py:496
  119.4 1.7 %logit_grads.1 = (bf16[512,2048]{1,0:T(8,128)(2,1)S(1)}, bf16[160,2048]{1,0:T(8,128)(2,1)S(1)}) custom-call(s32[5]{0:T(128)S(1)} %stack.23.place_ref, bf16[512,2048]{1,0:T(8,128)(2,1)S(1)} %get-tuple-element.41.exp_ref, f32[512,2048]{1,0:T(8,128)S(1)} %get-tuple-element.66.terms_ref, bf16[512,2048]{1,0:T(8,128)(2,1)S(1)} %get-tuple-element.67.dispatch_ref, ...), custom_call_target="tpu_custom_call" | custom-call | flops 671088640 | bytes 4194304 | tf_op jit(solution)/shard_map/logit_grads/pallas_call | solution.py:536
  121.2 1.1 collective-permute-start.13
  122.2 2.1 %own_parts.1 = (bf16[8,80,128]{2,1,0:T(8,128)(2,1)S(1)}, bf16[8,80,128]{2,1,0:T(8,128)(2,1)S(1)}, f32[160,2048]{1,0:T(8,128)S(1)}) custom-call(s32[5]{0:T(128)S(1)} %stack.23.place_ref, bf16[512,2048]{1,0:T(8,128)(2,1)S(1)} %get-tuple-element.71.logit_ref, bf16[512,2048]{1,0:T(8,128)(2,1)S(1)} %get-tuple-element.67.dispatch_ref, ...), custom_call_target="tpu_custom_call" | custom-call | flops 671088640 | bytes 5242880 | tf_op jit(solution)/shard_map/own_parts/pallas_call | solution.py:569
  124.3 0.7 collective-permute-start.14
  125.0 1.0 collective-permute-done.14.received_ref
  126.1 8.9 %all_to_all.28 = bf16[8,80,128]{2,1,0:T(8,128)(2,1)S(1)} all-to-all(bf16[8,80,128]{2,1,0:T(8,128)(2,1)S(1)} %pair_sum.5), channel_id=1, replica_groups=mesh['zl'=2,'y'=4,'c'=2,'xb'=2,'xa'=2,'zh'=2] {'zl','y'}, dimensions={0} | all-to-all | bytes 327680 | tf_op jit(solution)/shard_map/all_to_all | solution.py:655
  135.0 0.6 convert_reduce_fusion
  135.6 2.0 %collective-permute-done.13 = bf16[160,2048]{1,0:T(8,128)(2,1)S(1)} collective-permute-done((bf16[160,2048]{1,0:T(8,128)(2,1)S(1)}, bf16[160,2048]{1,0:T(8,128)(2,1)S(1)}, u32[]{:S(2)}, u32[]{:S(2)}) %collective-permute-start.13) | collective-permute-done | bytes 655392 | tf_op jit(solution)/shard_map/ppermute | solution.py:651
  137.6 1.0 fusion
  (32 shorter events, 0.1 us)
Async XLA Ops:
  1.6 10.6 %collective-permute-start.2 = (bf16[640,128]{1,0:T(8,128)(2,1)S(1)}, bf16[640,128]{1,0:T(8,128)(2,1)S(1)}, u32[]{:S(2)}, u32[]{:S(2)}) collective-permute-start(bf16[640,128]{1,0:T(8,128)(2,1)S(1)} %constant_dynamic-slice_fusion), channel_id=1, source_target_pairs={{0,7},{1,6},{2,5},{3,4},{4,3},{5,2},{6,1},{7,0},{8,15},{9,14},{10,... | collective-permute-start | bytes 491528 | tf_op jit(solution)/shard_map/ppermute | solution.py:613
  8.3 7.5 %collective-permute-start.1 = (bf16[640,128]{1,0:T(8,128)(2,1)S(1)}, bf16[640,128]{1,0:T(8,128)(2,1)S(1)}, u32[]{:S(2)}, u32[]{:S(2)}) collective-permute-start(bf16[640,128]{1,0:T(8,128)(2,1)S(1)} %constant_dynamic-slice_fusion), channel_id=1, source_target_pairs={{0,6},{1,7},{2,4},{3,5},{4,2},{5,3},{6,0},{7,1},{8,14},{9,15},{10,... | collective-permute-start | bytes 491528 | tf_op jit(solution)/shard_map/ppermute | solution.py:613
  8.5 8.7 %collective-permute-start = (bf16[640,128]{1,0:T(8,128)(2,1)S(1)}, bf16[640,128]{1,0:T(8,128)(2,1)S(1)}, u32[]{:S(2)}, u32[]{:S(2)}) collective-permute-start(bf16[640,128]{1,0:T(8,128)(2,1)S(1)} %constant_dynamic-slice_fusion), channel_id=1, source_target_pairs={{0,1},{1,0},{2,3},{3,2},{4,5},{5,4},{6,7},{7,6},{8,9},{9,8},{10,11... | collective-permute-start | bytes 491528 | tf_op jit(solution)/shard_map/ppermute | solution.py:613
  12.2 5.1 %collective-permute-start.5 = (bf16[640,128]{1,0:T(8,128)(2,1)S(1)}, bf16[640,128]{1,0:T(8,128)(2,1)S(1)}, u32[]{:S(2)}, u32[]{:S(2)}) collective-permute-start(bf16[640,128]{1,0:T(8,128)(2,1)S(1)} %collective-permute-done.2.refs_2_), channel_id=1, source_target_pairs={{0,8},{8,0},{1,9},{9,1},{2,10},{10,2},{3,11},{11,3},{4,12},{12,4},... | collective-permute-start | bytes 491528 | tf_op jit(solution)/shard_map/ppermute | solution.py:616
  15.7 2.4 %collective-permute-start.4 = (bf16[640,128]{1,0:T(8,128)(2,1)S(1)}, bf16[640,128]{1,0:T(8,128)(2,1)S(1)}, u32[]{:S(2)}, u32[]{:S(2)}) collective-permute-start(bf16[640,128]{1,0:T(8,128)(2,1)S(1)} %collective-permute-done.1.refs_1_), channel_id=1, source_target_pairs={{0,8},{8,0},{1,9},{9,1},{2,10},{10,2},{3,11},{11,3},{4,12},{12,4},... | collective-permute-start | bytes 491528 | tf_op jit(solution)/shard_map/ppermute | solution.py:616
  17.1 1.4 %collective-permute-start.3 = (bf16[640,128]{1,0:T(8,128)(2,1)S(1)}, bf16[640,128]{1,0:T(8,128)(2,1)S(1)}, u32[]{:S(2)}, u32[]{:S(2)}) collective-permute-start(bf16[640,128]{1,0:T(8,128)(2,1)S(1)} %collective-permute-done.refs_0_), channel_id=1, source_target_pairs={{0,8},{8,0},{1,9},{9,1},{2,10},{10,2},{3,11},{11,3},{4,12},{12,4},... | collective-permute-start | bytes 491528 | tf_op jit(solution)/shard_map/ppermute | solution.py:616
  18.5 2.5 %copy-start = (bf16[2048,1280]{1,0:T(8,128)(2,1)S(1)}, bf16[2048,1280]{1,0:T(8,128)(2,1)}, u32[]{:S(2)}) copy-start(bf16[2048,1280]{1,0:T(8,128)(2,1)} %tokens_ref.5) | copy-start | bytes 15728644
  21.0 1.0 copy-start.13
  22.0 6.1 %copy-start.1 = (bf16[2048,1280]{1,0:T(8,128)(2,1)S(1)}, bf16[2048,1280]{1,0:T(8,128)(2,1)}, u32[]{:S(2)}) copy-start(bf16[2048,1280]{1,0:T(8,128)(2,1)} %tokens_ref.5) | copy-start | bytes 15728644
  26.1 0.7 copy-start.11
  26.8 1.3 collective-permute-start.7
  27.0 2.5 %collective-permute-start.6 = (f32[1,2048]{1,0:T(1,128)S(1)}, f32[1,2048]{1,0:T(1,128)S(1)}, u32[]{:S(2)}, u32[]{:S(2)}) collective-permute-start(f32[1,2048]{1,0:T(1,128)S(1)} %get-tuple-element.43.row_ref), channel_id=1, source_target_pairs={{0,2},{2,0},{1,3},{3,1},{4,6},{6,4},{5,7},{7,5},{8,10},{10,8},{9,1... | collective-permute-start | bytes 24584 | tf_op jit(solution)/shard_map/ppermute | solution.py:621
  28.1 2.5 %copy-start.2 = (bf16[2048,1280]{1,0:T(8,128)(2,1)S(1)}, bf16[2048,1280]{1,0:T(8,128)(2,1)}, u32[]{:S(2)}) copy-start(bf16[2048,1280]{1,0:T(8,128)(2,1)} %grad_ref.3) | copy-start | bytes 15728644
  30.6 28.8 %copy-start.5 = (bf16[8,192,1280]{2,1,0:T(8,128)(2,1)S(1)}, bf16[8,192,1280]{2,1,0:T(8,128)(2,1)}, u32[]{:S(2)}) copy-start(bf16[8,192,1280]{2,1,0:T(8,128)(2,1)} %w_in_ref.1) | copy-start | bytes 11796484
  30.6 28.8 %copy-start.6 = (bf16[8,192,1280]{2,1,0:T(8,128)(2,1)S(1)}, bf16[8,192,1280]{2,1,0:T(8,128)(2,1)}, u32[]{:S(2)}) copy-start(bf16[8,192,1280]{2,1,0:T(8,128)(2,1)} %w_out_ref.1) | copy-start | bytes 11796484
  32.0 1.8 %collective-permute-start.8 = (bf16[8,16,1280]{2,1,0:T(8,128)(2,1)S(1)}, bf16[8,16,1280]{2,1,0:T(8,128)(2,1)S(1)}, u32[]{:S(2)}, u32[]{:S(2)}) collective-permute-start(bf16[8,16,1280]{2,1,0:T(8,128)(2,1)S(1)} %get-tuple-element.46), channel_id=1, source_target_pairs={{0,8},{8,0},{1,9},{9,1},{2,10},{10,2},{3,11},{11,3},{4,12},{12,4},... | collective-permute-start | bytes 983048 | tf_op jit(solution)/shard_map/ppermute | solution.py:626
  55.7 8.4 %copy-start.7 = (bf16[8,16,1280]{2,1,0:T(8,128)(2,1)}, bf16[8,16,1280]{2,1,0:T(8,128)(2,1)S(1)}, u32[]{:S(2)}) copy-start(bf16[8,16,1280]{2,1,0:T(8,128)(2,1)S(1)} %all_to_all.26.mine_ref) | copy-start | bytes 983044
  55.7 3.6 %collective-permute-start.9 = (bf16[8,16,1280]{2,1,0:T(8,128)(2,1)S(1)}, bf16[8,16,1280]{2,1,0:T(8,128)(2,1)S(1)}, u32[]{:S(2)}, u32[]{:S(2)}) collective-permute-start(bf16[8,16,1280]{2,1,0:T(8,128)(2,1)S(1)} %all_to_all.26.mine_ref), channel_id=1, source_target_pairs={{0,8},{8,0},{1,9},{9,1},{2,10},{10,2},{3,11},{11,3},{4,12},{12,4},... | collective-permute-start | bytes 983048 | tf_op jit(solution)/shard_map/ppermute | solution.py:629
  59.4 4.8 %copy-start.9 = (bf16[8,16,1280]{2,1,0:T(8,128)(2,1)}, bf16[8,16,1280]{2,1,0:T(8,128)(2,1)S(1)}, u32[]{:S(2)}) copy-start(bf16[8,16,1280]{2,1,0:T(8,128)(2,1)S(1)} %collective-permute-done.9.other_ref) | copy-start | bytes 983044
  64.1 12.2 %copy-start.14 = (bf16[8,16,192]{2,1,0:T(8,128)(2,1)}, bf16[8,16,192]{2,1,0:T(8,128)(2,1)S(1)}, u32[]{:S(2)}) copy-start(bf16[8,16,192]{2,1,0:T(8,128)(2,1)S(1)} %get-tuple-element.55.act_ref) | copy-start | bytes 147460
  64.2 12.2 %copy-start.16 = (bf16[8,16,192]{2,1,0:T(8,128)(2,1)}, bf16[8,16,192]{2,1,0:T(8,128)(2,1)S(1)}, u32[]{:S(2)}) copy-start(bf16[8,16,192]{2,1,0:T(8,128)(2,1)S(1)} %get-tuple-element.56.pre_ref) | copy-start | bytes 147460
  64.2 1.7 %collective-permute-start.10 = (bf16[8,16,1280]{2,1,0:T(8,128)(2,1)S(1)}, bf16[8,16,1280]{2,1,0:T(8,128)(2,1)S(1)}, u32[]{:S(2)}, u32[]{:S(2)}) collective-permute-start(bf16[8,16,1280]{2,1,0:T(8,128)(2,1)S(1)} %get-tuple-element.49), channel_id=1, source_target_pairs={{0,8},{8,0},{1,9},{9,1},{2,10},{10,2},{3,11},{11,3},{4,12},{12,4},... | collective-permute-start | bytes 983048 | tf_op jit(solution)/shard_map/ppermute | solution.py:632
  76.5 1.2 copy-start.4
  77.6 27.2 %all-to-all-start.3 = ((bf16[32,16,1408]{2,1,0:T(8,128)(2,1)}), bf16[32,16,1408]{2,1,0:T(8,128)(2,1)S(1)}, u32[]{:S(2)}, u32[]{:S(2)}) async-start(bf16[32,16,1408]{2,1,0:T(8,128)(2,1)} %copy-done.4), calls=%async_computation.3 | async-start | bytes 2883584 | tf_op jit(solution)/shard_map/all_to_all | solution.py:636
  84.9 1.0 copy-start.8
  85.8 1.0 copy-start.10
  86.8 0.8 copy-start.15
  87.7 0.8 copy-start.17
  104.9 7.7 %collective-permute-start.11 = (bf16[32,16,1408]{2,1,0:T(8,128)(2,1)S(1)}, bf16[32,16,1408]{2,1,0:T(8,128)(2,1)S(1)}, u32[]{:S(2)}, u32[]{:S(2)}) collective-permute-start(bf16[32,16,1408]{2,1,0:T(8,128)(2,1)S(1)} %all-to-all-done.3.mine_ref), channel_id=1, source_target_pairs={{0,8},{8,0},{1,9},{9,1},{2,10},{10,2},{3,11},{11,3},{4,12},{12,4},... | collective-permute-start | bytes 4325384 | tf_op jit(solution)/shard_map/ppermute | solution.py:639
  107.5 2.5 %copy-start.3 = (bf16[2048,1280]{1,0:T(8,128)(2,1)S(1)}, bf16[2048,1280]{1,0:T(8,128)(2,1)}, u32[]{:S(2)}) copy-start(bf16[2048,1280]{1,0:T(8,128)(2,1)} %grad_ref.3) | copy-start | bytes 15728644
  112.5 2.2 %slice-start = ((s8[5242880]{0:T(1024)(128)(4,1)}), s8[4194304]{0:T(1024)(128)(4,1)S(1)}, s32[]{:S(2)}) async-start(s8[5242880]{0:T(1024)(128)(4,1)} %bitcast.7), calls=%async_computation.5 | async-start | bytes 8388608
  112.5 2.5 %slice-start.1 = ((s8[5242880]{0:T(1024)(128)(4,1)}), s8[1048576]{0:T(1024)(128)(4,1)S(1)}, s32[]{:S(2)}) async-start(s8[5242880]{0:T(1024)(128)(4,1)} %bitcast.7), calls=%async_computation.6 | async-start | bytes 2097152
  114.5 5.0 %collective-permute-start.12 = (f32[1,2048]{1,0:T(1,128)S(1)}, f32[1,2048]{1,0:T(1,128)S(1)}, u32[]{:S(2)}, u32[]{:S(2)}) collective-permute-start(f32[1,2048]{1,0:T(1,128)S(1)} %get-tuple-element.68.sum_ref), channel_id=1, source_target_pairs={{0,2},{2,0},{1,3},{3,1},{4,6},{6,4},{5,7},{7,5},{8,10},{10,8},{9,1... | collective-permute-start | bytes 24584 | tf_op jit(solution)/shard_map/ppermute | solution.py:644
  115.0 4.4 %copy-start.12 = (bf16[2,160,512]{2,1,0:T(8,128)(2,1)S(1)}, bf16[2,160,512]{2,1,0:T(8,128)(2,1)}, u32[]{:S(2)}) copy-start(bf16[2,160,512]{2,1,0:T(8,128)(2,1)} %copy-done.11) | copy-start | bytes 983044
  121.2 16.4 %collective-permute-start.13 = (bf16[160,2048]{1,0:T(8,128)(2,1)S(1)}, bf16[160,2048]{1,0:T(8,128)(2,1)S(1)}, u32[]{:S(2)}, u32[]{:S(2)}) collective-permute-start(bf16[160,2048]{1,0:T(8,128)(2,1)S(1)} %get-tuple-element.73), channel_id=1, source_target_pairs={{0,2},{2,0},{1,3},{3,1},{4,6},{6,4},{5,7},{7,5},{8,10},{10,8},{9,1... | collective-permute-start | bytes 1966088 | tf_op jit(solution)/shard_map/ppermute | solution.py:651
  124.3 1.7 %collective-permute-start.14 = (bf16[8,80,128]{2,1,0:T(8,128)(2,1)S(1)}, bf16[8,80,128]{2,1,0:T(8,128)(2,1)S(1)}, u32[]{:S(2)}, u32[]{:S(2)}) collective-permute-start(bf16[8,80,128]{2,1,0:T(8,128)(2,1)S(1)} %get-tuple-element.75), channel_id=1, source_target_pairs={{0,8},{8,0},{1,9},{9,1},{2,10},{10,2},{3,11},{11,3},{4,12},{12,4},... | collective-permute-start | bytes 491528 | tf_op jit(solution)/shard_map/ppermute | solution.py:656

commit v9 on v8

--- a/solution.py
+++ b/solution.py
@@ -443,9 +443,9 @@
             dots = near_ref[:, cut] + lax.dot_general(
                 slot_out, grad_ref[cut, :], cols_contract, preferred_element_type=f32
             )
-            dot_ref[:, cut] = dots
-            terms = (exp_ref[:, cut].astype(f32) * power) * dots
-            sum_ref[:, cut] = jnp.sum(terms, axis=0, keepdims=True) * inverse
+            terms = ((exp_ref[:, cut].astype(f32) * power) * inverse) * dots
+            dot_ref[:, cut] = terms
+            sum_ref[:, cut] = jnp.sum(terms, axis=0, keepdims=True)
 
     return pl.pallas_call(
         kernel,
@@ -461,13 +461,13 @@
     )(exps, near, grad_far, row_parts, other)
 
 
-def disp_dots(place, exps, dots, tokens, row_parts, mine, other, width, tile=256):
+def disp_dots(place, exps, dots, tokens, mine, other, width, tile=256):
     slots, count = exps.shape
     features = tokens.shape[1]
     half = features // 2
 
     def kernel(
-        place_ref, exp_ref, dot_ref, tokens_ref, row_ref, mine_ref, other_ref,
+        place_ref, exp_ref, dot_ref, tokens_ref, mine_ref, other_ref,
         terms_ref, dispatch_ref, rows_ref, power_ref, inverse_ref, total_ref, turned_ref,
     ):
         lanes = mine_ref[:, :, features:].reshape(slots, LANES).astype(f32)
@@ -484,18 +484,16 @@
             rows_ref[whose] = turned_ref[pl.ds(first, width), :]
         for at in range(0, count, tile):
             cut = slice(at, at + tile)
-            power, inverse = guarded(row_ref[:, cut])
             exps_here = exp_ref[:, cut].astype(f32)
             dispatch = (exps_here * power_ref[...]) * inverse_ref[...]
             dispatch_ref[:, cut] = dispatch.astype(bf16)
             disp_dot = half_dot(place_ref, mine_ref, tokens_ref, 1, cut, True)
             disp_dot = disp_dot + half_dot(place_ref, other_ref, tokens_ref, 1, cut, False)
-            combine = (exps_here * power) * inverse
-            terms_ref[:, cut] = combine * dot_ref[:, cut] + dispatch * (disp_dot - total_ref[...])
-
-    return pl.pallas_call(
-        kernel,
-        in_specs=[in_smem()] + [whole_in_vmem()] * 6,
+            terms_ref[:, cut] = dot_ref[:, cut] + dispatch * (disp_dot - total_ref[...])
+
+    return pl.pallas_call(
+        kernel,
+        in_specs=[in_smem()] + [whole_in_vmem()] * 5,
         out_specs=[whole_in_vmem()] * 3,
         out_shape=[
             jax.ShapeDtypeStruct((slots, count), f32),
@@ -506,7 +504,7 @@
         compiler_params=params(GRANT),
         cost_estimate=cost(2 * slots * features * count, 2 * features * count),
         name="disp_dots",
-    )(place, exps, dots, tokens, row_parts, mine, other)
+    )(place, exps, dots, tokens, mine, other)
 
 
 def columns_dot(keys_rows_ref, grad_rows_ref, logit, dispatch, own):
@@ -643,7 +641,7 @@
     dots, row = comb_dots(all_exp, near, grad_far, row_parts, gathered_other)
     row_other = lax.ppermute(row, "xa", swap)
     terms, dispatch, grad_rows = disp_dots(
-        place, all_exp, dots, tokens, row_parts, gathered, gathered_other, width
+        place, all_exp, dots, tokens, gathered, gathered_other, width
     )
     logit, sent = logit_grads(
         place, all_exp, terms, dispatch, row_parts, row, row_other, keys_rows, grad_rows

time: 139 us -> 139 us (level)
  no operation moved by 1% of the time
where the time goes in v9:
time: 139 us; the launch traced here: 138 us
  blocking collectives  40.9 us (29%)
  Pallas kernels  30.3 us (22%)
  starting transfers between devices  25.8 us (19%)
  waiting for transfers between devices  24.7 us (18%)
  local copies, waits for them, and re-layouts  14 us (10%)
  other arithmetic  1.63 us (1%)
    all_to_all x2, blocking collectives, per_device(): lax.all_to_all(pair_sum(keep, lax.ppermute(give, 'c', swap)), CHIPS, 0, 0)  21.5 us
    unnamed x40, local copies, waits for them, and re-layouts  13 us
    all_to_all x1, blocking collectives, per_device(): terms = lax.all_to_all(sent, CHIPS, 0, 0)  10.4 us
    all_to_all x1, waiting for transfers between devices, per_device(): gathered = lax.all_to_all(sent, GATHERED, 0, 0, axis_index_groups=across)  10.1 us
    all_to_all x1, blocking collectives, per_device(): mine = lax.all_to_all(sent, CHIPS, 0, 0)  9.05 us
    all_to_all x1, starting transfers between devices, per_device(): gathered = lax.all_to_all(sent, GATHERED, 0, 0, axis_index_groups=across)  7.21 us
    ppermute x3, starting transfers between devices, per_device(): lax.ppermute(own_half, SLOT, [(at, at ^ other) for at in range(slot_devic...  7.08 us
    pallas_call x1, Pallas kernels, weight_grads(): pl.pallas_call(kernel, grid=(experts,), in_specs=[in_smem(), pl.BlockSpec...  6.3 us
  transfers between devices with their start and end apart: 16, of which 12 were waited for; matrix products, arithmetic and copies ran while one was open for 1% of the time, Pallas kernels for 12%

profile of v9, /device:TPU:1, one launch (start us, length us, event | category | flops | bytes accessed | tf_op | source)
XLA Modules:
  0.0 138.2 jit_solution(13107067367907739425)
XLA Ops:
  0.6 0.9 constant_dynamic-slice_fusion
  1.6 6.7 %collective-permute-start.2 = (bf16[640,128]{1,0:T(8,128)(2,1)S(1)}, bf16[640,128]{1,0:T(8,128)(2,1)S(1)}, u32[]{:S(2)}, u32[]{:S(2)}) collective-permute-start(bf16[640,128]{1,0:T(8,128)(2,1)S(1)} %constant_dynamic-slice_fusion), channel_id=1, source_target_pairs={{0,7},{1,6},{2,5},{3,4},{4,3},{5,2},{6,1},{7,0},{8,15},{9,14},{10,... | collective-permute-start | bytes 491528 | tf_op jit(solution)/shard_map/ppermute | solution.py:611
  8.3 0.2 collective-permute-start.1
  8.5 0.2 collective-permute-start
  8.6 3.5 %collective-permute-done.2.refs_2_ = bf16[640,128]{1,0:T(8,128)(2,1)S(1)} collective-permute-done((bf16[640,128]{1,0:T(8,128)(2,1)S(1)}, bf16[640,128]{1,0:T(8,128)(2,1)S(1)}, u32[]{:S(2)}, u32[]{:S(2)}) %collective-permute-start.2) | collective-permute-done | bytes 163872 | tf_op jit(solution)/shard_map/ppermute | solution.py:611
  12.2 2.1 %collective-permute-start.5 = (bf16[640,128]{1,0:T(8,128)(2,1)S(1)}, bf16[640,128]{1,0:T(8,128)(2,1)S(1)}, u32[]{:S(2)}, u32[]{:S(2)}) collective-permute-start(bf16[640,128]{1,0:T(8,128)(2,1)S(1)} %collective-permute-done.2.refs_2_), channel_id=1, source_target_pairs={{0,8},{8,0},{1,9},{9,1},{2,10},{10,2},{3,11},{11,3},{4,12},{12,4},... | collective-permute-start | bytes 491528 | tf_op jit(solution)/shard_map/ppermute | solution.py:614
  14.3 1.5 %collective-permute-done.1.refs_1_ = bf16[640,128]{1,0:T(8,128)(2,1)S(1)} collective-permute-done((bf16[640,128]{1,0:T(8,128)(2,1)S(1)}, bf16[640,128]{1,0:T(8,128)(2,1)S(1)}, u32[]{:S(2)}, u32[]{:S(2)}) %collective-permute-start.1) | collective-permute-done | bytes 163872 | tf_op jit(solution)/shard_map/ppermute | solution.py:611
  15.7 1.4 %collective-permute-start.4 = (bf16[640,128]{1,0:T(8,128)(2,1)S(1)}, bf16[640,128]{1,0:T(8,128)(2,1)S(1)}, u32[]{:S(2)}, u32[]{:S(2)}) collective-permute-start(bf16[640,128]{1,0:T(8,128)(2,1)S(1)} %collective-permute-done.1.refs_1_), channel_id=1, source_target_pairs={{0,8},{8,0},{1,9},{9,1},{2,10},{10,2},{3,11},{11,3},{4,12},{12,4},... | collective-permute-start | bytes 491528 | tf_op jit(solution)/shard_map/ppermute | solution.py:614
  17.1 0.0 collective-permute-start.3
  17.2 0.1 stack.23.place_ref
  17.3 0.9 collective-permute-done.4.refs_4_
  18.2 0.4 collective-permute-done.3.refs_3_
  18.5 2.5 %copy-done = bf16[2048,1280]{1,0:T(8,128)(2,1)S(1)} copy-done((bf16[2048,1280]{1,0:T(8,128)(2,1)S(1)}, bf16[2048,1280]{1,0:T(8,128)(2,1)}, u32[]{:S(2)}) %copy-start) | copy-done | bytes 5242904
  21.0 1.0 copy-done.13
  22.0 4.1 %all_exps.1 = (bf16[512,2048]{1,0:T(8,128)(2,1)S(1)}, f32[128,2048]{1,0:T(8,128)S(1)}, f32[1,2048]{1,0:T(1,128)S(1)}, f32[128,128]{1,0:T(8,128)S(1)}, bf16[2,160,512]{2,1,0:T(8,128)(2,1)S(1)}) custom-call(s32[5]{0:T(128)S(1)} %stack.23.place_ref, bf16[1280,128]{1,0:T(8,128)(2,1)S(1)} %copy-done.13, bf16[640,128]{1,0:T(8,128)(2,1)S(1)} %collective-permute-done.refs_0_, ...), custom_call_target="tpu_custom_call" | custom-call | flops 2684354560 | bytes 5242880 | tf_op jit(solution)/shard_map/all_exps/pallas_call | solution.py:376
  26.1 0.0 copy-start.11
  26.1 0.7 copy-done.11
  26.8 0.2 collective-permute-start.7
  27.0 0.0 collective-permute-start.6
  27.1 1.0 collective-permute-done.7.other_ref
  28.1 0.9 dispatch_part.1.in_ref
  29.0 0.6 collective-permute-done.6.row_other_ref
  29.6 1.0 copy-done.2
  30.6 1.4 %combine_part.1 = (bf16[8,16,1408]{2,1,0:T(8,128)(2,1)S(1)}, bf16[8,16,1280]{2,1,0:T(8,128)(2,1)S(1)}, f32[1,2048]{1,0:T(1,128)S(1)}) custom-call(s32[5]{0:T(128)S(1)} %stack.23.place_ref, f32[128,2048]{1,0:T(8,128)S(1)} %get-tuple-element.42.exp_ref, f32[1,2048]{1,0:T(1,128)S(1)} %get-tuple-element.43.row_ref, ...), custom_call_target="tpu_custom_call" | custom-call | flops 671088640 | bytes 5242880 | tf_op jit(solution)/shard_map/combine_part/pallas_call | solution.py:135
  32.0 0.5 collective-permute-start.8
  32.5 1.3 collective-permute-done.8.received_ref
  33.7 0.1 pair_sum.3
  33.8 12.6 %all_to_all.25.parts_ref = bf16[8,16,1408]{2,1,0:T(8,128)(2,1)S(1)} all-to-all(bf16[8,16,1408]{2,1,0:T(8,128)(2,1)S(1)} %pair_sum.3), channel_id=1, replica_groups=mesh['zl'=2,'y'=4,'c'=2,'xb'=2,'xa'=2,'zh'=2] {'zl','y'}, dimensions={0} | all-to-all | bytes 720896 | tf_op jit(solution)/shard_map/all_to_all | solution.py:624
  46.5 0.2 sum_slots.1
  46.7 9.0 %all_to_all.26.mine_ref = bf16[8,16,1280]{2,1,0:T(8,128)(2,1)S(1)} all-to-all(bf16[8,16,1280]{2,1,0:T(8,128)(2,1)S(1)} %get-tuple-element.47), channel_id=1, replica_groups=mesh['zl'=2,'y'=4,'c'=2,'xb'=2,'xa'=2,'zh'=2] {'zl','y'}, dimensions={0} | all-to-all | bytes 655360 | tf_op jit(solution)/shard_map/all_to_all | solution.py:626
  55.7 2.4 %collective-permute-start.9 = (bf16[8,16,1280]{2,1,0:T(8,128)(2,1)S(1)}, bf16[8,16,1280]{2,1,0:T(8,128)(2,1)S(1)}, u32[]{:S(2)}, u32[]{:S(2)}) collective-permute-start(bf16[8,16,1280]{2,1,0:T(8,128)(2,1)S(1)} %all_to_all.26.mine_ref), channel_id=1, source_target_pairs={{0,8},{8,0},{1,9},{9,1},{2,10},{10,2},{3,11},{11,3},{4,12},{12,4},... | collective-permute-start | bytes 983048 | tf_op jit(solution)/shard_map/ppermute | solution.py:627
  58.1 1.3 collective-permute-done.9.other_ref
  59.4 4.8 %experts_part.1 = (bf16[8,16,1280]{2,1,0:T(8,128)(2,1)S(1)}, bf16[8,16,1280]{2,1,0:T(8,128)(2,1)S(1)}, bf16[8,16,192]{2,1,0:T(8,128)(2,1)S(1)}, bf16[8,16,192]{2,1,0:T(8,128)(2,1)S(1)}) custom-call(s32[5]{0:T(128)S(1)} %stack.23.place_ref, bf16[8,16,1280]{2,1,0:T(8,128)(2,1)S(1)} %all_to_all.26.mine_ref, ...), custom_call_target="tpu_custom_call" | custom-call | flops 251658240 | bytes 7864320 | tf_op jit(solution)/shard_map/experts_part/pallas_call | solution.py:246
  64.2 0.4 collective-permute-start.10
  64.6 1.3 collective-permute-done.10.received_ref
  65.9 0.1 pair_sum.4
  66.0 10.4 %all_to_all.27.terms_ref = bf16[8,16,1280]{2,1,0:T(8,128)(2,1)S(1)} all-to-all(bf16[8,16,1280]{2,1,0:T(8,128)(2,1)S(1)} %pair_sum.4), channel_id=1, replica_groups=mesh['zl'=2,'y'=4,'c'=2,'xb'=2,'xa'=2,'zh'=2] {'zl','y'}, dimensions={0} | all-to-all | bytes 655360 | tf_op jit(solution)/shard_map/all_to_all | solution.py:631
  76.3 0.1 sum_terms.1
  76.5 1.1 copy-done.4
  77.6 7.2 %all-to-all-start.3 = ((bf16[32,16,1408]{2,1,0:T(8,128)(2,1)}), bf16[32,16,1408]{2,1,0:T(8,128)(2,1)S(1)}, u32[]{:S(2)}, u32[]{:S(2)}) async-start(bf16[32,16,1408]{2,1,0:T(8,128)(2,1)} %copy-done.4), calls=%async_computation.3 | async-start | bytes 2883584 | tf_op jit(solution)/shard_map/all_to_all | solution.py:634
  84.9 1.0 copy-done.8
  85.8 1.0 copy-done.10
  86.8 0.8 copy-done.15
  87.7 0.8 copy-done.17
  88.5 6.3 %weight_grads.1 = (bf16[8,192,1280]{2,1,0:T(8,128)(2,1)}, bf16[8,192,1280]{2,1,0:T(8,128)(2,1)}) custom-call(s32[5]{0:T(128)S(1)} %stack.23.place_ref, bf16[8,16,1280]{2,1,0:T(8,128)(2,1)S(1)} %copy-done.8, bf16[8,16,1280]{2,1,0:T(8,128)(2,1)S(1)} %copy-done.10, bf16[8,16,192]{2,1,0:T(8,128)(2,1)S(1)} %copy-done.15, bf16[8,16,192]{2,1,0:T(8,128)(2,1)S(1)} %copy-done.17), custom_call_target="tpu_custom_call" | custom-call | flops 125829120 | bytes 7864320 | tf_op jit(solution)/shard_map/weight_grads/pallas_call | solution.py:280
  94.8 10.1 %all-to-all-done.3.mine_ref = bf16[32,16,1408]{2,1,0:T(8,128)(2,1)S(1)} async-done(((bf16[32,16,1408]{2,1,0:T(8,128)(2,1)}), bf16[32,16,1408]{2,1,0:T(8,128)(2,1)S(1)}, u32[]{:S(2)}, u32[]{:S(2)}) %all-to-all-start.3) | async-done | bytes 1441824 | tf_op jit(solution)/shard_map/all_to_all | solution.py:634
  104.9 2.6 %collective-permute-start.11 = (bf16[32,16,1408]{2,1,0:T(8,128)(2,1)S(1)}, bf16[32,16,1408]{2,1,0:T(8,128)(2,1)S(1)}, u32[]{:S(2)}, u32[]{:S(2)}) collective-permute-start(bf16[32,16,1408]{2,1,0:T(8,128)(2,1)S(1)} %all-to-all-done.3.mine_ref), channel_id=1, source_target_pairs={{0,8},{8,0},{1,9},{9,1},{2,10},{10,2},{3,11},{11,3},{4,12},{12,4},... | collective-permute-start | bytes 4325384 | tf_op jit(solution)/shard_map/ppermute | solution.py:637
  107.5 2.5 %copy-done.3 = bf16[2048,1280]{1,0:T(8,128)(2,1)S(1)} copy-done((bf16[2048,1280]{1,0:T(8,128)(2,1)S(1)}, bf16[2048,1280]{1,0:T(8,128)(2,1)}, u32[]{:S(2)}) %copy-start.3) | copy-done | bytes 5242904
  109.9 2.6 %near_dots.1 = (f32[512,2048]{1,0:T(8,128)S(1)}, bf16[2048,640]{1,0:T(8,128)(2,1)S(1)}) custom-call(s32[5]{0:T(128)S(1)} %stack.23.place_ref, bf16[2048,1280]{1,0:T(8,128)(2,1)S(1)} %copy-done.3, bf16[32,16,1408]{2,1,0:T(8,128)(2,1)S(1)} %all-to-all-done.3.mine_ref), custom_call_target="tpu_custom_call" | custom-call | flops 1342177280 | bytes 2621440 | tf_op jit(solution)/shard_map/near_dots/pallas_call | solution.py:420
  112.5 0.0 slice-start
  112.6 1.9 %comb_dots.1 = (f32[512,2048]{1,0:T(8,128)S(1)}, f32[1,2048]{1,0:T(1,128)S(1)}) custom-call(bf16[512,2048]{1,0:T(8,128)(2,1)S(1)} %get-tuple-element.41.exp_ref, f32[512,2048]{1,0:T(8,128)S(1)} %get-tuple-element.61.near_ref, bf16[2048,640]{1,0:T(8,128)(2,1)S(1)} %get-tuple-element.62.grad_ref, f32[1,2048]{1,0:T(1,128)S(1)} %get-tuple-element.63.row_ref, ...), custom_call_target="tpu_custom_call" | custom-call | flops 1342177280 | bytes 2621440 | tf_op jit(solution)/shard_map/comb_dots/pallas_call | solution.py:450
  114.4 0.1 collective-permute-start.12
  114.5 0.2 slice-done
  114.7 0.3 slice-done.1
  115.0 4.1 %disp_dots.1 = (f32[512,2048]{1,0:T(8,128)S(1)}, bf16[512,2048]{1,0:T(8,128)(2,1)S(1)}, bf16[2,160,512]{2,1,0:T(8,128)(2,1)S(1)}) custom-call(s32[5]{0:T(128)S(1)} %stack.23.place_ref, bf16[512,2048]{1,0:T(8,128)(2,1)S(1)} %get-tuple-element.41.exp_ref, f32[512,2048]{1,0:T(8,128)S(1)} %get-tuple-element.65.dot_ref, bf16[2048,1280]{1,0:T(8,128)(2,1)S(1)} %bitcast.8, ...), custom_call_target="tpu_custom_call" | custom-call | flops 2684354560 | bytes 5242880 | tf_op jit(solution)/shard_map/disp_dots/pallas_call | solution.py:494
  119.1 1.7 %logit_grads.1 = (bf16[512,2048]{1,0:T(8,128)(2,1)S(1)}, bf16[160,2048]{1,0:T(8,128)(2,1)S(1)}) custom-call(s32[5]{0:T(128)S(1)} %stack.23.place_ref, bf16[512,2048]{1,0:T(8,128)(2,1)S(1)} %get-tuple-element.41.exp_ref, f32[512,2048]{1,0:T(8,128)S(1)} %get-tuple-element.66.terms_ref, bf16[512,2048]{1,0:T(8,128)(2,1)S(1)} %get-tuple-element.67.dispatch_ref, ...), custom_call_target="tpu_custom_call" | custom-call | flops 671088640 | bytes 4194304 | tf_op jit(solution)/shard_map/logit_grads/pallas_call | solution.py:534
  120.9 1.1 collective-permute-start.13
  121.9 2.1 %own_parts.1 = (bf16[8,80,128]{2,1,0:T(8,128)(2,1)S(1)}, bf16[8,80,128]{2,1,0:T(8,128)(2,1)S(1)}, f32[160,2048]{1,0:T(8,128)S(1)}) custom-call(s32[5]{0:T(128)S(1)} %stack.23.place_ref, bf16[512,2048]{1,0:T(8,128)(2,1)S(1)} %get-tuple-element.71.logit_ref, bf16[512,2048]{1,0:T(8,128)(2,1)S(1)} %get-tuple-element.67.dispatch_ref, ...), custom_call_target="tpu_custom_call" | custom-call | flops 671088640 | bytes 5242880 | tf_op jit(solution)/shard_map/own_parts/pallas_call | solution.py:567
  124.0 0.7 collective-permute-start.14
  124.7 1.0 collective-permute-done.14.received_ref
  125.8 8.9 %all_to_all.28 = bf16[8,80,128]{2,1,0:T(8,128)(2,1)S(1)} all-to-all(bf16[8,80,128]{2,1,0:T(8,128)(2,1)S(1)} %pair_sum.5), channel_id=1, replica_groups=mesh['zl'=2,'y'=4,'c'=2,'xb'=2,'xa'=2,'zh'=2] {'zl','y'}, dimensions={0} | all-to-all | bytes 327680 | tf_op jit(solution)/shard_map/all_to_all | solution.py:653
  134.6 0.6 convert_reduce_fusion
  135.3 1.9 %collective-permute-done.13 = bf16[160,2048]{1,0:T(8,128)(2,1)S(1)} collective-permute-done((bf16[160,2048]{1,0:T(8,128)(2,1)S(1)}, bf16[160,2048]{1,0:T(8,128)(2,1)S(1)}, u32[]{:S(2)}, u32[]{:S(2)}) %collective-permute-start.13) | collective-permute-done | bytes 655392 | tf_op jit(solution)/shard_map/ppermute | solution.py:649
  137.2 1.0 fusion
  (32 shorter events, 0.1 us)
Async XLA Ops:
  1.6 10.6 %collective-permute-start.2 = (bf16[640,128]{1,0:T(8,128)(2,1)S(1)}, bf16[640,128]{1,0:T(8,128)(2,1)S(1)}, u32[]{:S(2)}, u32[]{:S(2)}) collective-permute-start(bf16[640,128]{1,0:T(8,128)(2,1)S(1)} %constant_dynamic-slice_fusion), channel_id=1, source_target_pairs={{0,7},{1,6},{2,5},{3,4},{4,3},{5,2},{6,1},{7,0},{8,15},{9,14},{10,... | collective-permute-start | bytes 491528 | tf_op jit(solution)/shard_map/ppermute | solution.py:611
  8.3 7.5 %collective-permute-start.1 = (bf16[640,128]{1,0:T(8,128)(2,1)S(1)}, bf16[640,128]{1,0:T(8,128)(2,1)S(1)}, u32[]{:S(2)}, u32[]{:S(2)}) collective-permute-start(bf16[640,128]{1,0:T(8,128)(2,1)S(1)} %constant_dynamic-slice_fusion), channel_id=1, source_target_pairs={{0,6},{1,7},{2,4},{3,5},{4,2},{5,3},{6,0},{7,1},{8,14},{9,15},{10,... | collective-permute-start | bytes 491528 | tf_op jit(solution)/shard_map/ppermute | solution.py:611
  8.5 8.7 %collective-permute-start = (bf16[640,128]{1,0:T(8,128)(2,1)S(1)}, bf16[640,128]{1,0:T(8,128)(2,1)S(1)}, u32[]{:S(2)}, u32[]{:S(2)}) collective-permute-start(bf16[640,128]{1,0:T(8,128)(2,1)S(1)} %constant_dynamic-slice_fusion), channel_id=1, source_target_pairs={{0,1},{1,0},{2,3},{3,2},{4,5},{5,4},{6,7},{7,6},{8,9},{9,8},{10,11... | collective-permute-start | bytes 491528 | tf_op jit(solution)/shard_map/ppermute | solution.py:611
  12.2 5.1 %collective-permute-start.5 = (bf16[640,128]{1,0:T(8,128)(2,1)S(1)}, bf16[640,128]{1,0:T(8,128)(2,1)S(1)}, u32[]{:S(2)}, u32[]{:S(2)}) collective-permute-start(bf16[640,128]{1,0:T(8,128)(2,1)S(1)} %collective-permute-done.2.refs_2_), channel_id=1, source_target_pairs={{0,8},{8,0},{1,9},{9,1},{2,10},{10,2},{3,11},{11,3},{4,12},{12,4},... | collective-permute-start | bytes 491528 | tf_op jit(solution)/shard_map/ppermute | solution.py:614
  15.7 2.4 %collective-permute-start.4 = (bf16[640,128]{1,0:T(8,128)(2,1)S(1)}, bf16[640,128]{1,0:T(8,128)(2,1)S(1)}, u32[]{:S(2)}, u32[]{:S(2)}) collective-permute-start(bf16[640,128]{1,0:T(8,128)(2,1)S(1)} %collective-permute-done.1.refs_1_), channel_id=1, source_target_pairs={{0,8},{8,0},{1,9},{9,1},{2,10},{10,2},{3,11},{11,3},{4,12},{12,4},... | collective-permute-start | bytes 491528 | tf_op jit(solution)/shard_map/ppermute | solution.py:614
  17.1 1.4 %collective-permute-start.3 = (bf16[640,128]{1,0:T(8,128)(2,1)S(1)}, bf16[640,128]{1,0:T(8,128)(2,1)S(1)}, u32[]{:S(2)}, u32[]{:S(2)}) collective-permute-start(bf16[640,128]{1,0:T(8,128)(2,1)S(1)} %collective-permute-done.refs_0_), channel_id=1, source_target_pairs={{0,8},{8,0},{1,9},{9,1},{2,10},{10,2},{3,11},{11,3},{4,12},{12,4},... | collective-permute-start | bytes 491528 | tf_op jit(solution)/shard_map/ppermute | solution.py:614
  18.5 2.5 %copy-start = (bf16[2048,1280]{1,0:T(8,128)(2,1)S(1)}, bf16[2048,1280]{1,0:T(8,128)(2,1)}, u32[]{:S(2)}) copy-start(bf16[2048,1280]{1,0:T(8,128)(2,1)} %tokens_ref.5) | copy-start | bytes 15728644
  21.0 1.0 copy-start.13
  22.0 6.1 %copy-start.1 = (bf16[2048,1280]{1,0:T(8,128)(2,1)S(1)}, bf16[2048,1280]{1,0:T(8,128)(2,1)}, u32[]{:S(2)}) copy-start(bf16[2048,1280]{1,0:T(8,128)(2,1)} %tokens_ref.5) | copy-start | bytes 15728644
  26.1 0.7 copy-start.11
  26.8 1.3 collective-permute-start.7
  27.0 2.5 %collective-permute-start.6 = (f32[1,2048]{1,0:T(1,128)S(1)}, f32[1,2048]{1,0:T(1,128)S(1)}, u32[]{:S(2)}, u32[]{:S(2)}) collective-permute-start(f32[1,2048]{1,0:T(1,128)S(1)} %get-tuple-element.43.row_ref), channel_id=1, source_target_pairs={{0,2},{2,0},{1,3},{3,1},{4,6},{6,4},{5,7},{7,5},{8,10},{10,8},{9,1... | collective-permute-start | bytes 24584 | tf_op jit(solution)/shard_map/ppermute | solution.py:619
  28.1 2.5 %copy-start.2 = (bf16[2048,1280]{1,0:T(8,128)(2,1)S(1)}, bf16[2048,1280]{1,0:T(8,128)(2,1)}, u32[]{:S(2)}) copy-start(bf16[2048,1280]{1,0:T(8,128)(2,1)} %grad_ref.3) | copy-start | bytes 15728644
  30.6 28.8 %copy-start.5 = (bf16[8,192,1280]{2,1,0:T(8,128)(2,1)S(1)}, bf16[8,192,1280]{2,1,0:T(8,128)(2,1)}, u32[]{:S(2)}) copy-start(bf16[8,192,1280]{2,1,0:T(8,128)(2,1)} %w_in_ref.1) | copy-start | bytes 11796484
  30.6 28.8 %copy-start.6 = (bf16[8,192,1280]{2,1,0:T(8,128)(2,1)S(1)}, bf16[8,192,1280]{2,1,0:T(8,128)(2,1)}, u32[]{:S(2)}) copy-start(bf16[8,192,1280]{2,1,0:T(8,128)(2,1)} %w_out_ref.1) | copy-start | bytes 11796484
  32.0 1.8 %collective-permute-start.8 = (bf16[8,16,1280]{2,1,0:T(8,128)(2,1)S(1)}, bf16[8,16,1280]{2,1,0:T(8,128)(2,1)S(1)}, u32[]{:S(2)}, u32[]{:S(2)}) collective-permute-start(bf16[8,16,1280]{2,1,0:T(8,128)(2,1)S(1)} %get-tuple-element.46), channel_id=1, source_target_pairs={{0,8},{8,0},{1,9},{9,1},{2,10},{10,2},{3,11},{11,3},{4,12},{12,4},... | collective-permute-start | bytes 983048 | tf_op jit(solution)/shard_map/ppermute | solution.py:624
  55.7 8.4 %copy-start.7 = (bf16[8,16,1280]{2,1,0:T(8,128)(2,1)}, bf16[8,16,1280]{2,1,0:T(8,128)(2,1)S(1)}, u32[]{:S(2)}) copy-start(bf16[8,16,1280]{2,1,0:T(8,128)(2,1)S(1)} %all_to_all.26.mine_ref) | copy-start | bytes 983044
  55.7 3.6 %collective-permute-start.9 = (bf16[8,16,1280]{2,1,0:T(8,128)(2,1)S(1)}, bf16[8,16,1280]{2,1,0:T(8,128)(2,1)S(1)}, u32[]{:S(2)}, u32[]{:S(2)}) collective-permute-start(bf16[8,16,1280]{2,1,0:T(8,128)(2,1)S(1)} %all_to_all.26.mine_ref), channel_id=1, source_target_pairs={{0,8},{8,0},{1,9},{9,1},{2,10},{10,2},{3,11},{11,3},{4,12},{12,4},... | collective-permute-start | bytes 983048 | tf_op jit(solution)/shard_map/ppermute | solution.py:627
  59.4 4.8 %copy-start.9 = (bf16[8,16,1280]{2,1,0:T(8,128)(2,1)}, bf16[8,16,1280]{2,1,0:T(8,128)(2,1)S(1)}, u32[]{:S(2)}) copy-start(bf16[8,16,1280]{2,1,0:T(8,128)(2,1)S(1)} %collective-permute-done.9.other_ref) | copy-start | bytes 983044
  64.1 12.2 %copy-start.14 = (bf16[8,16,192]{2,1,0:T(8,128)(2,1)}, bf16[8,16,192]{2,1,0:T(8,128)(2,1)S(1)}, u32[]{:S(2)}) copy-start(bf16[8,16,192]{2,1,0:T(8,128)(2,1)S(1)} %get-tuple-element.55.act_ref) | copy-start | bytes 147460
  64.2 12.2 %copy-start.16 = (bf16[8,16,192]{2,1,0:T(8,128)(2,1)}, bf16[8,16,192]{2,1,0:T(8,128)(2,1)S(1)}, u32[]{:S(2)}) copy-start(bf16[8,16,192]{2,1,0:T(8,128)(2,1)S(1)} %get-tuple-element.56.pre_ref) | copy-start | bytes 147460
  64.2 1.7 %collective-permute-start.10 = (bf16[8,16,1280]{2,1,0:T(8,128)(2,1)S(1)}, bf16[8,16,1280]{2,1,0:T(8,128)(2,1)S(1)}, u32[]{:S(2)}, u32[]{:S(2)}) collective-permute-start(bf16[8,16,1280]{2,1,0:T(8,128)(2,1)S(1)} %get-tuple-element.49), channel_id=1, source_target_pairs={{0,8},{8,0},{1,9},{9,1},{2,10},{10,2},{3,11},{11,3},{4,12},{12,4},... | collective-permute-start | bytes 983048 | tf_op jit(solution)/shard_map/ppermute | solution.py:630
  76.5 1.2 copy-start.4
  77.6 27.2 %all-to-all-start.3 = ((bf16[32,16,1408]{2,1,0:T(8,128)(2,1)}), bf16[32,16,1408]{2,1,0:T(8,128)(2,1)S(1)}, u32[]{:S(2)}, u32[]{:S(2)}) async-start(bf16[32,16,1408]{2,1,0:T(8,128)(2,1)} %copy-done.4), calls=%async_computation.3 | async-start | bytes 2883584 | tf_op jit(solution)/shard_map/all_to_all | solution.py:634
  84.9 1.0 copy-start.8
  85.8 1.0 copy-start.10
  86.8 0.8 copy-start.15
  87.7 0.8 copy-start.17
  104.9 7.7 %collective-permute-start.11 = (bf16[32,16,1408]{2,1,0:T(8,128)(2,1)S(1)}, bf16[32,16,1408]{2,1,0:T(8,128)(2,1)S(1)}, u32[]{:S(2)}, u32[]{:S(2)}) collective-permute-start(bf16[32,16,1408]{2,1,0:T(8,128)(2,1)S(1)} %all-to-all-done.3.mine_ref), channel_id=1, source_target_pairs={{0,8},{8,0},{1,9},{9,1},{2,10},{10,2},{3,11},{11,3},{4,12},{12,4},... | collective-permute-start | bytes 4325384 | tf_op jit(solution)/shard_map/ppermute | solution.py:637
  107.5 2.5 %copy-start.3 = (bf16[2048,1280]{1,0:T(8,128)(2,1)S(1)}, bf16[2048,1280]{1,0:T(8,128)(2,1)}, u32[]{:S(2)}) copy-start(bf16[2048,1280]{1,0:T(8,128)(2,1)} %grad_ref.3) | copy-start | bytes 15728644
  112.5 2.2 %slice-start = ((s8[5242880]{0:T(1024)(128)(4,1)}), s8[4194304]{0:T(1024)(128)(4,1)S(1)}, s32[]{:S(2)}) async-start(s8[5242880]{0:T(1024)(128)(4,1)} %bitcast.7), calls=%async_computation.5 | async-start | bytes 8388608
  112.5 2.5 %slice-start.1 = ((s8[5242880]{0:T(1024)(128)(4,1)}), s8[1048576]{0:T(1024)(128)(4,1)S(1)}, s32[]{:S(2)}) async-start(s8[5242880]{0:T(1024)(128)(4,1)} %bitcast.7), calls=%async_computation.6 | async-start | bytes 2097152
  114.4 4.7 %collective-permute-start.12 = (f32[1,2048]{1,0:T(1,128)S(1)}, f32[1,2048]{1,0:T(1,128)S(1)}, u32[]{:S(2)}, u32[]{:S(2)}) collective-permute-start(f32[1,2048]{1,0:T(1,128)S(1)} %get-tuple-element.68.sum_ref), channel_id=1, source_target_pairs={{0,2},{2,0},{1,3},{3,1},{4,6},{6,4},{5,7},{7,5},{8,10},{10,8},{9,1... | collective-permute-start | bytes 24584 | tf_op jit(solution)/shard_map/ppermute | solution.py:642
  115.0 4.1 %copy-start.12 = (bf16[2,160,512]{2,1,0:T(8,128)(2,1)S(1)}, bf16[2,160,512]{2,1,0:T(8,128)(2,1)}, u32[]{:S(2)}) copy-start(bf16[2,160,512]{2,1,0:T(8,128)(2,1)} %copy-done.11) | copy-start | bytes 983044
  120.9 16.4 %collective-permute-start.13 = (bf16[160,2048]{1,0:T(8,128)(2,1)S(1)}, bf16[160,2048]{1,0:T(8,128)(2,1)S(1)}, u32[]{:S(2)}, u32[]{:S(2)}) collective-permute-start(bf16[160,2048]{1,0:T(8,128)(2,1)S(1)} %get-tuple-element.73), channel_id=1, source_target_pairs={{0,2},{2,0},{1,3},{3,1},{4,6},{6,4},{5,7},{7,5},{8,10},{10,8},{9,1... | collective-permute-start | bytes 1966088 | tf_op jit(solution)/shard_map/ppermute | solution.py:649
  124.0 1.7 %collective-permute-start.14 = (bf16[8,80,128]{2,1,0:T(8,128)(2,1)S(1)}, bf16[8,80,128]{2,1,0:T(8,128)(2,1)S(1)}, u32[]{:S(2)}, u32[]{:S(2)}) collective-permute-start(bf16[8,80,128]{2,1,0:T(8,128)(2,1)S(1)} %get-tuple-element.75), channel_id=1, source_target_pairs={{0,8},{8,0},{1,9},{9,1},{2,10},{10,2},{3,11},{11,3},{4,12},{12,4},... | collective-permute-start | bytes 491528 | tf_op jit(solution)/shard_map/ppermute | solution.py:654
